TPU v7x, 768 devices: a whole 4x8x12 slice. The times are simulated.
768 devices in a mesh: lat: 96 (over x, z, core), lon: 8 (over y).
Axes of the slice: x: 4, y: 8, z: 12, core: 2. Of those that a mesh axis runs over, the one named last changes fastest.
Arguments:
- departures: float32 [196608, 128], P(('lat', 'lon')), may hold values from -6 to 6
- obs_weight: float32 [196608, 128], P(('lat', 'lon')), may hold values from 0.2 to 4
- obs_columns: int32 [196608], P(('lat', 'lon')), may hold values from 0 to 127
- obs_owner: int32 [196608, 1], P(('lat', 'lon')), may hold values from 0 to 7; in each aligned block of 256 rows (0 to 255, 256 to 511, ...) at most 64 rows name the same one
- obs_counts: int32 [768], P(('lat', 'lon')), may hold values from 128 to 256
- background_std: float32 [768, 128, 128], P('lat', 'lon'), may hold values from 0.5 to 2
- diffusion: float32 [768, 128], P('lat', 'lon'), may hold values from 0.15 to 0.45
- level_factor: float32 [128, 128], replicated, may hold values from -0.5 to 0.5
- model_mixing: float32 [128, 128], replicated, may hold values from -0.5 to 0.5
Outputs:
- solution: float32 [768, 128, 128], P('lat', 'lon')
- residual: float32 [768, 128, 128], P('lat', 'lon')
Inputs may be any that keep to these rules, and one draw needn't show every extreme that they name: `obs_owner`: among the 256 rows of one shard no tile is named by more than 64 rows.
All inputs are finite; a program needn't handle non-finite values.
Results may differ from a plain program's by a relative error of at most 0.025.
Values sent between devices are 32-bit elements; how exact they have to be, the bound alone decides.
No kernel may reach another device: no remote copies, remote signals or barrier semaphores. Data moves between devices by JAX's collectives and lax.ppermute only.
A program may use at most 32 MiB of HBM per device.

v0:
```python
import jax
import jax.numpy as jnp
from jax import lax
from jax.sharding import PartitionSpec as P

STEPS = 3
ITERS = 2


HIGH = lax.Precision.HIGHEST


def with_halo(shard, sides, width):
    for axis, dim in sides:
        size, length = (lax.axis_size(axis), shard.shape[dim])
        up = [(i, (i + 1) % size) for i in range(size)]
        down = [(j, i) for i, j in up]
        last = lax.slice_in_dim(shard, length - width, length, axis=dim)
        first = lax.slice_in_dim(shard, 0, width, axis=dim)
        before = lax.ppermute(last, axis, up)
        after = lax.ppermute(first, axis, down)
        shard = jnp.concatenate([before, shard, after], axis=dim)
    return shard


def level_mix(field, matrix):
    return jnp.einsum("abl,lm->abm", field, matrix, precision=HIGH)


def level_mix_t(field, matrix):
    return jnp.einsum("abl,ml->abm", field, matrix, precision=HIGH)


def smooth(field, diffusion):
    scaled = diffusion[:, :, None] * field
    padded = with_halo(scaled, (("lat", 0), ("lon", 1)), 1)
    lat_index = lax.axis_index("lat")
    last_index = lax.axis_size("lat") - 1
    keep_low = jnp.where(lat_index == 0, 0.0, 1.0).astype(jnp.float32)
    keep_high = jnp.where(lat_index == last_index, 0.0, 1.0).astype(jnp.float32)
    south_rows = padded[:-2, 1:-1].at[0].multiply(keep_low)
    north_rows = padded[2:, 1:-1].at[-1].multiply(keep_high)
    centre = padded[1:-1, 1:-1]
    laplace = south_rows + north_rows + padded[1:-1, :-2] + padded[1:-1, 2:] - 4.0 * centre
    return field + diffusion[:, :, None] * laplace


def squares(residual):
    return lax.psum(jnp.sum(residual * residual), ("lat", "lon"))


def shards(
    departures,
    obs_weight,
    obs_columns,
    obs_owner,
    obs_counts,
    background_std,
    diffusion,
    level_factor,
    model_mixing,
):
    lat_cells, lon_cells, levels = background_std.shape
    lon_devices = lax.axis_size("lon")
    slot_index = jnp.arange(obs_columns.shape[0], dtype=jnp.int32)
    is_used = (slot_index < obs_counts[0]).astype(jnp.float32)
    obs_time = slot_index % STEPS
    weights = obs_weight * is_used[:, None]
    owners = obs_owner[:, 0]

    def backward(forcings):
        adjoint = forcings[STEPS - 1]
        for section in range(STEPS - 1, -1, -1):
            adjoint = smooth(adjoint + 0.5 * level_mix_t(adjoint, model_mixing), diffusion)
            if section > 0:
                adjoint = adjoint + forcings[section - 1]
        scaled = background_std * adjoint
        return scaled + 0.5 * level_mix_t(scaled, level_factor)

    row_width = lon_cells * lon_devices
    row_index = (
        obs_time * (lat_cells * row_width)
        + obs_columns // lon_cells * row_width
        + owners * lon_cells
        + obs_columns % lon_cells
    )

    def spread_forcing(values):
        forcing_rows = (
            jnp.zeros((STEPS * lat_cells * row_width, levels), jnp.float32)
            .at[row_index]
            .add(values)
        )
        forcing_rows = forcing_rows.reshape(STEPS, lat_cells, row_width, levels)
        return lax.psum_scatter(forcing_rows, "lon", scatter_dimension=2, tiled=True)

    right_side = backward(spread_forcing(weights * departures))
    solution = jnp.zeros_like(right_side)
    residual = right_side
    direction = right_side
    norm_now = squares(residual)
    for section in range(ITERS):
        current = background_std * (direction + 0.5 * level_mix(direction, level_factor))
        forward_states = []
        for forward_section in range(STEPS):
            smoothed = smooth(current, diffusion)
            current = smoothed + 0.5 * level_mix(smoothed, model_mixing)
            forward_states.append(current)
        stacked = jnp.stack(forward_states, axis=0)
        gathered = lax.all_gather(stacked, "lon", axis=2, tiled=True)
        hessian_forcings = spread_forcing(
            weights * gathered.reshape(STEPS * lat_cells * row_width, levels)[row_index]
        )
        hess_dir = direction + backward(hessian_forcings)
        curve = lax.psum(jnp.sum(direction * hess_dir), ("lat", "lon"))
        step_size = norm_now / curve
        solution = solution + step_size * direction
        residual = residual - step_size * hess_dir
        if section + 1 < ITERS:
            norm_next = squares(residual)
            direction = residual + norm_next / norm_now * direction
            norm_now = norm_next
    return (solution, residual)


def solution(mesh):
    placed = (
        P(("lat", "lon"), None),
        P(("lat", "lon"), None),
        P(("lat", "lon")),
        P(("lat", "lon"), None),
        P(("lat", "lon")),
        P("lat", "lon", None),
        P("lat", "lon"),
        P(),
        P(),
    )
    return jax.shard_map(
        shards,
        mesh=mesh,
        in_specs=placed,
        out_specs=(P("lat", "lon", None), P("lat", "lon", None)),
        check_vma=False,
    )
```

profile of v0, /device:TPU:1, one launch (start us, length us, event | category | flops | bytes accessed | tf_op | source)
XLA Modules:
  0.0 875.7 jit_solution(1455031991967042187)
XLA Ops:
  9.3 3.2 scatter_custom_fusion
  12.5 49.3 %reduce-scatter.4.cloned.1.call-done = f32[3,8,16,128]{3,2,1,0:T(8,128)} async-done(((f32[3,8,128,128]{3,2,1,0:T(8,128)}), f32[3,8,16,128]{3,2,1,0:T(8,128)}) %reduce-scatter.4.cloned.1.call-update) | async-done | bytes 196624 | tf_op jit(solution)/shard_map/reduce_scatter | solution.py:95
  63.0 7.5 collective-permute-start
  78.4 3.7 collective-permute-start.3
  84.1 3.3 collective-permute-start.4
  87.3 4.0 collective-permute-start.5
  95.2 4.0 collective-permute-start.7
  104.2 7.3 collective-permute-start.9
  112.3 3.6 collective-permute-start.10
  115.9 3.2 collective-permute-start.11
  122.8 8.9 %collective-permute-start.13 = (f32[1,16,128]{2,1,0:T(8,128)S(1)}, f32[1,16,128]{2,1,0:T(8,128)S(1)}, u32[]{:S(2)}, u32[]{:S(2)}) collective-permute-start(f32[1,16,128]{2,1,0:T(8,128)S(1)} %get-tuple-element.445), channel_id=1, source_target_pairs={{8,0},{16,8},{24,16},{32,24},{40,32},{48,40},{56,48},{64,56},{72,6... | collective-permute-start | bytes 24584 | tf_op jit(solution)/shard_map/ppermute | solution.py:21
  132.5 3.4 collective-permute-start.14
  135.9 3.1 collective-permute-start.15
  142.6 8.9 %collective-permute-start.17 = (f32[1,16,128]{2,1,0:T(8,128)S(1)}, f32[1,16,128]{2,1,0:T(8,128)S(1)}, u32[]{:S(2)}, u32[]{:S(2)}) collective-permute-start(f32[1,16,128]{2,1,0:T(8,128)S(1)} %get-tuple-element.441), channel_id=1, source_target_pairs={{8,0},{16,8},{24,16},{32,24},{40,32},{48,40},{56,48},{64,56},{72,6... | collective-permute-start | bytes 24584 | tf_op jit(solution)/shard_map/ppermute | solution.py:21
  155.5 3.4 collective-permute-start.19
  162.1 8.9 %collective-permute-start.21 = (f32[1,16,128]{2,1,0:T(8,128)S(1)}, f32[1,16,128]{2,1,0:T(8,128)S(1)}, u32[]{:S(2)}, u32[]{:S(2)}) collective-permute-start(f32[1,16,128]{2,1,0:T(8,128)S(1)} %get-tuple-element.437), channel_id=1, source_target_pairs={{8,0},{16,8},{24,16},{32,24},{40,32},{48,40},{56,48},{64,56},{72,6... | collective-permute-start | bytes 24584 | tf_op jit(solution)/shard_map/ppermute | solution.py:21
  174.7 3.7 collective-permute-start.23
  180.2 39.1 %all-gather.3.cloned.1.call-done = f32[3,8,128,128]{3,2,1,0:T(8,128)} async-done(((f32[3,8,16,128]{3,2,1,0:T(8,128)}), f32[3,8,128,128]{3,2,1,0:T(8,128)}) %all-gather.3.cloned.1.call-update) | async-done | bytes 1572880 | tf_op jit(solution)/shard_map/all_gather | solution.py:110
  219.3 4.5 scatter_custom_fusion.1
  223.9 44.8 %reduce-scatter.6.cloned.1.call-done = f32[3,8,16,128]{3,2,1,0:T(8,128)} async-done(((f32[3,8,128,128]{3,2,1,0:T(8,128)}), f32[3,8,16,128]{3,2,1,0:T(8,128)}) %reduce-scatter.6.cloned.1.call-update) | async-done | bytes 196624 | tf_op jit(solution)/shard_map/reduce_scatter | solution.py:95
  269.9 7.6 collective-permute-start.24
  285.2 3.8 collective-permute-start.27
  290.9 3.2 collective-permute-start.28
  294.1 4.0 collective-permute-start.29
  302.0 4.0 collective-permute-start.31
  311.0 7.3 collective-permute-start.33
  319.1 3.6 collective-permute-start.34
  322.8 3.3 collective-permute-start.35
  328.1 114.5 %all-reduce = (f32[]{:T(128)}, f32[]{:T(128)}) all-reduce(f32[]{:T(128)} %get-tuple-element.363, f32[]{:T(128)} %get-tuple-element.362), channel_id=1, replica_groups=mesh['lat'=96,'lon'=8] {'lat','lon'}, use_global_device_ids=true, to_apply=%region_3.4 | all-reduce | flops 2 | bytes 16 | tf_op jit(solution)/shard_map/psum | solution.py:49
  444.6 103.7 %psum.30 = f32[]{:T(128)} all-reduce(f32[]{:T(128)} %multiply_reduce_fusion.1), channel_id=1, replica_groups=mesh['lat'=96,'lon'=8] {'lat','lon'}, use_global_device_ids=true, to_apply=%region_9.10 | all-reduce | flops 1 | bytes 8 | tf_op jit(solution)/shard_map/psum | solution.py:49
  549.9 4.2 collective-permute-start.36
  561.0 4.6 collective-permute-start.39
  569.7 3.6 collective-permute-start.41
  576.6 5.1 collective-permute-start.43
  586.3 6.9 collective-permute-start.45
  594.1 4.9 collective-permute-start.46
  604.8 39.0 %all-gather.5.cloned.1.call-done = f32[3,8,128,128]{3,2,1,0:T(8,128)} async-done(((f32[3,8,16,128]{3,2,1,0:T(8,128)}), f32[3,8,128,128]{3,2,1,0:T(8,128)}) %all-gather.5.cloned.1.call-update) | async-done | bytes 1572880 | tf_op jit(solution)/shard_map/all_gather | solution.py:110
  643.8 4.5 scatter_custom_fusion.2
  648.4 44.8 %reduce-scatter.8.cloned.1.call-done = f32[3,8,16,128]{3,2,1,0:T(8,128)} async-done(((f32[3,8,128,128]{3,2,1,0:T(8,128)}), f32[3,8,16,128]{3,2,1,0:T(8,128)}) %reduce-scatter.8.cloned.1.call-update) | async-done | bytes 196624 | tf_op jit(solution)/shard_map/reduce_scatter | solution.py:95
  694.4 7.6 collective-permute-start.48
  709.7 3.8 collective-permute-start.51
  715.5 3.2 collective-permute-start.52
  718.7 4.0 collective-permute-start.53
  726.6 4.0 collective-permute-start.55
  735.6 7.3 collective-permute-start.57
  743.7 3.6 collective-permute-start.58
  747.3 3.3 collective-permute-start.59
  752.7 114.5 %psum.31 = f32[]{:T(128)} all-reduce(f32[]{:T(128)} %get-tuple-element.489), channel_id=1, replica_groups=mesh['lat'=96,'lon'=8] {'lat','lon'}, use_global_device_ids=true, to_apply=%region_13.14 | all-reduce | flops 1 | bytes 8 | tf_op jit(solution)/shard_map/psum | solution.py:115
  (206 shorter events, 114.0 us)
Async XLA Ops:
  7.2 54.6 %reduce-scatter.4.cloned.1.call-start = ((), (), s32[]{:S(2)}) async-start(), calls=%async_computation.3 | async-start | bytes 1769472 | tf_op jit(solution)/shard_map/reduce_scatter | solution.py:95
  12.5 206.8 %all-gather.3.cloned.1.call-start = ((), (), s32[]{:S(2)}) async-start(), calls=%async_computation.4 | async-start | bytes 1769472 | tf_op jit(solution)/shard_map/all_gather | solution.py:110
  63.0 9.5 %collective-permute-start = (f32[1,16,128]{2,1,0:T(8,128)S(1)}, f32[1,16,128]{2,1,0:T(8,128)S(1)}, u32[]{:S(2)}, u32[]{:S(2)}) collective-permute-start(f32[1,16,128]{2,1,0:T(8,128)S(1)} %get-tuple-element.456), channel_id=1, source_target_pairs={{0,8},{8,16},{16,24},{24,32},{32,40},{40,48},{48,56},{56,64},{64,7... | collective-permute-start | bytes 24584 | tf_op jit(solution)/shard_map/ppermute | solution.py:20
  70.6 5.0 collective-permute-start.1
  75.6 6.5 collective-permute-start.2
  84.1 7.3 collective-permute-start.4
  87.3 5.0 collective-permute-start.5
  92.3 6.9 collective-permute-start.6
  101.2 10.3 %collective-permute-start.8 = (f32[1,16,128]{2,1,0:T(8,128)S(1)}, f32[1,16,128]{2,1,0:T(8,128)S(1)}, u32[]{:S(2)}, u32[]{:S(2)}) collective-permute-start(f32[1,16,128]{2,1,0:T(8,128)S(1)} %get-tuple-element.448), channel_id=1, source_target_pairs={{0,8},{8,16},{16,24},{24,32},{32,40},{40,48},{48,56},{56,64},{64,7... | collective-permute-start | bytes 24584 | tf_op jit(solution)/shard_map/ppermute | solution.py:20
  104.2 8.1 collective-permute-start.9
  112.3 6.9 collective-permute-start.10
  120.9 10.8 %collective-permute-start.12 = (f32[1,16,128]{2,1,0:T(8,128)S(1)}, f32[1,16,128]{2,1,0:T(8,128)S(1)}, u32[]{:S(2)}, u32[]{:S(2)}) collective-permute-start(f32[1,16,128]{2,1,0:T(8,128)S(1)} %get-tuple-element.444), channel_id=1, source_target_pairs={{0,8},{8,16},{16,24},{24,32},{32,40},{40,48},{48,56},{56,64},{64,7... | collective-permute-start | bytes 24584 | tf_op jit(solution)/shard_map/ppermute | solution.py:20
  122.8 9.7 %collective-permute-start.13 = (f32[1,16,128]{2,1,0:T(8,128)S(1)}, f32[1,16,128]{2,1,0:T(8,128)S(1)}, u32[]{:S(2)}, u32[]{:S(2)}) collective-permute-start(f32[1,16,128]{2,1,0:T(8,128)S(1)} %get-tuple-element.445), channel_id=1, source_target_pairs={{8,0},{16,8},{24,16},{32,24},{40,32},{48,40},{56,48},{64,56},{72,6... | collective-permute-start | bytes 24584 | tf_op jit(solution)/shard_map/ppermute | solution.py:21
  132.5 6.6 collective-permute-start.14
  140.6 11.0 %collective-permute-start.16 = (f32[1,16,128]{2,1,0:T(8,128)S(1)}, f32[1,16,128]{2,1,0:T(8,128)S(1)}, u32[]{:S(2)}, u32[]{:S(2)}) collective-permute-start(f32[1,16,128]{2,1,0:T(8,128)S(1)} %get-tuple-element.440), channel_id=1, source_target_pairs={{0,8},{8,16},{16,24},{24,32},{32,40},{40,48},{48,56},{56,64},{64,7... | collective-permute-start | bytes 24584 | tf_op jit(solution)/shard_map/ppermute | solution.py:20
  142.6 9.7 %collective-permute-start.17 = (f32[1,16,128]{2,1,0:T(8,128)S(1)}, f32[1,16,128]{2,1,0:T(8,128)S(1)}, u32[]{:S(2)}, u32[]{:S(2)}) collective-permute-start(f32[1,16,128]{2,1,0:T(8,128)S(1)} %get-tuple-element.441), channel_id=1, source_target_pairs={{8,0},{16,8},{24,16},{32,24},{40,32},{48,40},{56,48},{64,56},{72,6... | collective-permute-start | bytes 24584 | tf_op jit(solution)/shard_map/ppermute | solution.py:21
  152.4 6.6 collective-permute-start.18
  160.1 10.9 %collective-permute-start.20 = (f32[1,16,128]{2,1,0:T(8,128)S(1)}, f32[1,16,128]{2,1,0:T(8,128)S(1)}, u32[]{:S(2)}, u32[]{:S(2)}) collective-permute-start(f32[1,16,128]{2,1,0:T(8,128)S(1)} %get-tuple-element.436), channel_id=1, source_target_pairs={{0,8},{8,16},{16,24},{24,32},{32,40},{40,48},{48,56},{56,64},{64,7... | collective-permute-start | bytes 24584 | tf_op jit(solution)/shard_map/ppermute | solution.py:20
  162.1 9.7 %collective-permute-start.21 = (f32[1,16,128]{2,1,0:T(8,128)S(1)}, f32[1,16,128]{2,1,0:T(8,128)S(1)}, u32[]{:S(2)}, u32[]{:S(2)}) collective-permute-start(f32[1,16,128]{2,1,0:T(8,128)S(1)} %get-tuple-element.437), channel_id=1, source_target_pairs={{8,0},{16,8},{24,16},{32,24},{40,32},{48,40},{56,48},{64,56},{72,6... | collective-permute-start | bytes 24584 | tf_op jit(solution)/shard_map/ppermute | solution.py:21
  171.8 6.6 collective-permute-start.22
  180.1 88.5 %reduce-scatter.6.cloned.1.call-start = ((), (), s32[]{:S(2)}) async-start(), calls=%async_computation.5 | async-start | bytes 1769472 | tf_op jit(solution)/shard_map/reduce_scatter | solution.py:95
  223.8 420.0 %all-gather.5.cloned.1.call-start = ((), (), s32[]{:S(2)}) async-start(), calls=%async_computation.6 | async-start | bytes 1769472 | tf_op jit(solution)/shard_map/all_gather | solution.py:110
  269.9 9.5 %collective-permute-start.24 = (f32[1,16,128]{2,1,0:T(8,128)S(1)}, f32[1,16,128]{2,1,0:T(8,128)S(1)}, u32[]{:S(2)}, u32[]{:S(2)}) collective-permute-start(f32[1,16,128]{2,1,0:T(8,128)S(1)} %get-tuple-element.432), channel_id=1, source_target_pairs={{0,8},{8,16},{16,24},{24,32},{32,40},{40,48},{48,56},{56,64},{64,7... | collective-permute-start | bytes 24584 | tf_op jit(solution)/shard_map/ppermute | solution.py:20
  277.5 5.0 collective-permute-start.25
  282.4 6.6 collective-permute-start.26
  290.9 7.3 collective-permute-start.28
  294.1 5.0 collective-permute-start.29
  299.1 7.0 collective-permute-start.30
  308.0 10.3 %collective-permute-start.32 = (f32[1,16,128]{2,1,0:T(8,128)S(1)}, f32[1,16,128]{2,1,0:T(8,128)S(1)}, u32[]{:S(2)}, u32[]{:S(2)}) collective-permute-start(f32[1,16,128]{2,1,0:T(8,128)S(1)} %get-tuple-element.424), channel_id=1, source_target_pairs={{0,8},{8,16},{16,24},{24,32},{32,40},{40,48},{48,56},{56,64},{64,7... | collective-permute-start | bytes 24584 | tf_op jit(solution)/shard_map/ppermute | solution.py:20
  311.0 8.1 collective-permute-start.33
  319.1 7.0 collective-permute-start.34
  549.9 6.2 collective-permute-start.36
  559.1 6.6 collective-permute-start.38
  561.0 5.3 collective-permute-start.39
  566.6 6.7 collective-permute-start.40
  574.7 7.1 collective-permute-start.42
  576.6 6.3 collective-permute-start.43
  583.2 10.0 %collective-permute-start.44 = (f32[1,16,128]{2,1,0:T(8,128)S(1)}, f32[1,16,128]{2,1,0:T(8,128)S(1)}, u32[]{:S(2)}, u32[]{:S(2)}) collective-permute-start(f32[1,16,128]{2,1,0:T(8,128)S(1)} %get-tuple-element.412), channel_id=1, source_target_pairs={{0,8},{8,16},{16,24},{24,32},{32,40},{40,48},{48,56},{56,64},{64,7... | collective-permute-start | bytes 24584 | tf_op jit(solution)/shard_map/ppermute | solution.py:20
  586.3 7.7 collective-permute-start.45
  594.1 6.8 collective-permute-start.46
  604.6 88.6 %reduce-scatter.8.cloned.1.call-start = ((), (), s32[]{:S(2)}) async-start(), calls=%async_computation.7 | async-start | bytes 1769472 | tf_op jit(solution)/shard_map/reduce_scatter | solution.py:95
  694.4 9.5 %collective-permute-start.48 = (f32[1,16,128]{2,1,0:T(8,128)S(1)}, f32[1,16,128]{2,1,0:T(8,128)S(1)}, u32[]{:S(2)}, u32[]{:S(2)}) collective-permute-start(f32[1,16,128]{2,1,0:T(8,128)S(1)} %get-tuple-element.408), channel_id=1, source_target_pairs={{0,8},{8,16},{16,24},{24,32},{32,40},{40,48},{48,56},{56,64},{64,7... | collective-permute-start | bytes 24584 | tf_op jit(solution)/shard_map/ppermute | solution.py:20
  707.0 6.6 collective-permute-start.50
  715.5 7.3 collective-permute-start.52
  723.7 7.0 collective-permute-start.54
  732.6 10.3 %collective-permute-start.56 = (f32[1,16,128]{2,1,0:T(8,128)S(1)}, f32[1,16,128]{2,1,0:T(8,128)S(1)}, u32[]{:S(2)}, u32[]{:S(2)}) collective-permute-start(f32[1,16,128]{2,1,0:T(8,128)S(1)} %get-tuple-element.400), channel_id=1, source_target_pairs={{0,8},{8,16},{16,24},{24,32},{32,40},{40,48},{48,56},{56,64},{64,7... | collective-permute-start | bytes 24584 | tf_op jit(solution)/shard_map/ppermute | solution.py:20
  735.6 8.1 collective-permute-start.57
  743.7 7.0 collective-permute-start.58
  (22 other events, 480.4 us)
Sparse Core Ops, SparseCore 0:
  12.6 49.2 reduce-scatter.3
  180.2 39.0 all-gather.2
  223.9 44.6 reduce-scatter.5
  604.7 39.0 all-gather.4
  648.5 44.6 reduce-scatter.7
where the time goes:
time: 878 us; the launch traced here: 876 us
  blocking collectives  333 us (38%)
  waiting for transfers between devices  254 us (29%)
  starting transfers between devices  238 us (27%)
  between operations  19.8 us (2%)
  other arithmetic  16.7 us (2%)
  matrix products  15 us (2%)
    psum x2, blocking collectives, squares(): return lax.psum(jnp.sum(residual * residual), ('lat', 'lon'))  218 us
    reduce_scatter x3, waiting for transfers between devices, spread_forcing(): lax.psum_scatter(forcing_rows, 'lon', scatter_dimension=2, tiled=True)  139 us
    ppermute x30, starting transfers between devices, with_halo(): after = lax.ppermute(first, axis, down)  134 us
    psum x1, blocking collectives, shards(): curve = lax.psum(jnp.sum(direction * hess_dir), ('lat', 'lon'))  115 us
    ppermute x30, starting transfers between devices, with_halo(): before = lax.ppermute(last, axis, up)  104 us
    all_gather x2, waiting for transfers between devices, shards(): gathered = lax.all_gather(stacked, 'lon', axis=2, tiled=True)  78.1 us
    ppermute x30, waiting for transfers between devices, with_halo(): after = lax.ppermute(first, axis, down)  36.5 us
  transfers between devices with their start and end apart: 65, of which 35 were waited for; matrix products, arithmetic and copies ran while one was open for 0% of the time, Pallas kernels for 0%

commit v1 on v0

v1 whole, which is shorter than its diff:
```python
import functools
import jax
import jax.numpy as jnp
from jax import lax
from jax.experimental import pallas as pl
from jax.experimental.pallas import tpu as pltpu
from jax.sharding import PartitionSpec as P

F32 = jnp.float32
BF16 = jnp.bfloat16
L = 128
ROWS = 8
COLS = 16
CELLS = ROWS * COLS
STEPS = 3
SLOTS = 256
CAP = 64
WIDE = 3 * COLS
HALO = 2 * STEPS
BUCKET = 2 * CAP + 8
TILE_ROWS = 2 * STEPS * CELLS + CELLS + COLS
SIDE = 13

PARAMS = pltpu.CompilerParams(vmem_limit_bytes=40 * 1024 * 1024)


def call(kernel, name, outs, scratch=(), smem=()):
    def run(*args):
        specs = [
            pl.BlockSpec(memory_space=pltpu.SMEM if i in smem else pltpu.VMEM) for i in range(len(args))
        ]
        return pl.pallas_call(
            kernel,
            name=name,
            out_shape=outs,
            in_specs=specs,
            out_specs=jax.tree.map(lambda _: pl.BlockSpec(memory_space=pltpu.VMEM), outs),
            scratch_shapes=scratch,
            compiler_params=PARAMS,
        )(*args)

    return run


def shape(*dims, dtype=F32):
    return jax.ShapeDtypeStruct(dims, dtype)


def halves(x):
    high = x.astype(BF16)
    return high, (x - high.astype(F32)).astype(BF16)


def dot(a, b):
    return jnp.dot(a, b, preferred_element_type=F32)


def matrices_kernel(factor_ref, mixing_ref, out_ref):
    for i, ref in enumerate((mixing_ref, factor_ref)):
        for j in range(2):
            m = 0.5 * ref[...]
            high, low = halves(m.T if j else m)
            row = jnp.concatenate([high, low], axis=1)
            out_ref[2 * i + j] = jnp.concatenate([row, row], axis=0)


MIX, MIX_T, FACTOR, FACTOR_T = range(4)


def bucket_kernel(departures_ref, weight_ref, columns_ref, owner_ref, counts_ref, parity_ref, out_ref):
    sub = lax.broadcasted_iota(jnp.int32, (SLOTS, SLOTS), 0)
    lane = lax.broadcasted_iota(jnp.int32, (SLOTS, SLOTS), 1)
    owner_row = owner_ref[...].astype(F32)
    owner_col = jnp.sum(jnp.where(sub == lane, owner_row, 0.0), axis=1, keepdims=True)
    same = owner_row == owner_col
    rank_row = jnp.sum(jnp.where(same & (sub < lane), 1.0, 0.0), axis=0, keepdims=True)
    rank_col = jnp.sum(jnp.where(same & (lane < sub), 1.0, 0.0), axis=1, keepdims=True)
    place = (owner_row * CAP + rank_row).astype(jnp.int32)
    pick = lax.broadcasted_iota(jnp.int32, (8 * CAP, SLOTS), 0) == place
    pick = jnp.where(pick, 1.0, 0.0).astype(BF16)
    slot = lax.broadcasted_iota(jnp.int32, (SLOTS, L), 0)
    weights = jnp.where(slot < counts_ref[0], weight_ref[...], 0.0)
    parts = halves(weights * departures_ref[...]) + halves(weights)
    moved = dot(pick, jnp.concatenate(parts, axis=1))
    forcing = moved[:, :L] + moved[:, L : 2 * L]
    weights = moved[:, 2 * L : 3 * L] + moved[:, 3 * L :]
    number = lax.broadcasted_iota(jnp.int32, (1, SLOTS), 1)
    time = (number - STEPS * ((number * 171) >> 9)).astype(F32)
    tile = lax.broadcasted_iota(jnp.int32, (8, SLOTS), 0).astype(F32)
    here = tile == owner_row
    marks = jnp.concatenate(
        [jnp.where(here, time, 0.0), jnp.where(here, columns_ref[...].astype(F32), 0.0)], axis=0
    )
    target = rank_col + (CAP * parity_ref[0]).astype(F32)
    spread = jnp.where(lax.broadcasted_iota(jnp.int32, (SLOTS, L), 1).astype(F32) == target, 1.0, 0.0)
    codes = dot(marks.astype(BF16), spread.astype(BF16))
    codes = CELLS * codes[:8] + codes[8:]
    for d in range(8):
        out_ref[d, :CAP] = forcing[d * CAP : (d + 1) * CAP]
        out_ref[d, CAP : 2 * CAP] = weights[d * CAP : (d + 1) * CAP]
        out_ref[d, 2 * CAP :] = jnp.broadcast_to(codes[d : d + 1], (8, L))


def tile_kernel(received_ref, std_ref, diffusion_ref, out_ref):
    ones, data = [], []
    cell = lax.broadcasted_iota(jnp.int32, (STEPS * CELLS, L), 0)
    for j in range(4):
        pair = (2 * j, 2 * j + 1)
        codes = sum(received_ref[s, 2 * CAP : 2 * CAP + 1] for s in pair).astype(jnp.int32)
        ones.append(jnp.where(cell == codes, 1.0, 0.0).astype(BF16))
        for s in pair:
            parts = halves(received_ref[s, :CAP]) + halves(received_ref[s, CAP : 2 * CAP])
            data.append(jnp.concatenate(parts, axis=1))
    total = dot(jnp.concatenate(ones, axis=1), jnp.concatenate(data, axis=0))
    size = STEPS * CELLS
    out_ref[:size] = total[:, :L] + total[:, L : 2 * L]
    out_ref[size : 2 * size] = total[:, 2 * L : 3 * L] + total[:, 3 * L :]
    out_ref[2 * size : 2 * size + CELLS] = std_ref[...]
    sub = lax.broadcasted_iota(jnp.int32, (COLS, L), 0)
    lane = lax.broadcasted_iota(jnp.int32, (COLS, L), 1)
    turned = jnp.zeros((COLS, L), F32)
    for r in range(ROWS):
        row = diffusion_ref[r : r + 1]
        column = jnp.sum(jnp.where(sub == lane, row, 0.0), axis=1, keepdims=True)
        turned = turned + jnp.where(lane == r, column, 0.0)
    out_ref[2 * size + CELLS :] = turned


def wide(refs, start):
    return jnp.concatenate([ref[start : start + COLS] for ref in refs], axis=0)


def forcing_row(refs, t, r):
    return wide(refs, t * CELLS + r * COLS)


def weight_row(refs, t, r):
    return wide(refs, (STEPS + t) * CELLS + r * COLS)


def std_row(refs, r):
    return wide(refs, 2 * STEPS * CELLS + r * COLS)


def turned_row(refs):
    return wide(refs, 2 * STEPS * CELLS + CELLS)


def side_index(kind, t, k):
    return 6 * kind + (0, 3, 5)[2 - t] + k


def sides_kernel(left_ref, own_ref, right_ref, low_ref, high_ref):
    refs = (left_ref, own_ref, right_ref)
    for kind, row in enumerate((forcing_row, weight_row)):
        for t in range(STEPS):
            for k in range(t + 1):
                at = side_index(kind, t, k) * WIDE
                low_ref[at : at + WIDE] = row(refs, t, k)
                high_ref[at : at + WIDE] = row(refs, t, ROWS - 1 - t + k)
    last = (SIDE - 1) * WIDE
    low_ref[last:] = turned_row(refs)
    high_ref[last:] = turned_row(refs)


def side_or_own(refs, below_ref, above_ref, kind, t, r):
    if 0 <= r < ROWS:
        return (forcing_row, weight_row)[kind](refs, t, r)
    ref, k = (below_ref, r + t + 1) if r < 0 else (above_ref, r - ROWS)
    at = side_index(kind, t, k) * WIDE
    return ref[at : at + WIDE]


def fill_diffusion(refs, below_ref, above_ref, d_ref, first, stop):
    last = (SIDE - 1) * WIDE
    own, below, above = turned_row(refs), below_ref[last:], above_ref[last:]
    for r in range(first, stop):
        source = below if r < 0 else above if r >= ROWS else own
        column = source[:, r % ROWS : r % ROWS + 1]
        at = (r + HALO) * WIDE
        d_ref[at : at + WIDE] = jnp.broadcast_to(column, (WIDE, L))


def at(r):
    return pl.ds((r + HALO) * WIDE, WIDE)


def smooth_rows(first, stop, get, d_ref, put):
    held = []
    for r in range(first, stop):
        value, d = get(r), d_ref[at(r)]
        held.append((value, d, d * value))
        if len(held) == 3:
            value, d, u = held[1]
            laplace = held[0][2] + held[2][2] + pltpu.roll(u, 1, 0) + pltpu.roll(u, WIDE - 1, 0) - 4.0 * u
            put(r - 1, value + d * laplace)
            held.pop(0)


class Field:
    def __init__(self, v_ref, x_ref, y_ref, m_ref):
        self.v_ref, self.x_ref, self.y_ref, self.m_ref = v_ref, x_ref, y_ref, m_ref

    def put(self, r, value):
        self.v_ref[at(r)] = value
        high, low = halves(value)
        self.x_ref[at(r), :L] = high
        self.x_ref[at(r), L:] = low

    def mix(self, first, stop, which):
        rows = pl.ds((first + HALO) * WIDE, (stop - first) * WIDE)
        self.y_ref[rows] = dot(self.x_ref[rows], self.m_ref[which])

    def get(self, r):
        return self.v_ref[at(r)] + self.y_ref[at(r), :L] + self.y_ref[at(r), L:]


def adjoint(field, d_ref, forcing, std):
    for t in range(STEPS - 1, -1, -1):
        field.mix(-t - 1, ROWS + t + 1, MIX_T)
        if t > 0:
            put = lambda r, value, t=t: field.put(r, value + forcing(t - 1, r))
        else:
            put = lambda r, value: field.put(r, std(r) * value)
        smooth_rows(-t - 1, ROWS + t + 1, field.get, d_ref, put)
    field.mix(0, ROWS, FACTOR_T)


def right_side_kernel(
    left_ref, own_ref, right_ref, below_ref, above_ref, m_ref, b_ref, y_ref, low_ref, high_ref,
    v_ref, x_ref, p_ref, d_ref,
):
    refs = (left_ref, own_ref, right_ref)
    fill_diffusion(refs, below_ref, above_ref, d_ref, -STEPS, ROWS + STEPS)
    field = Field(v_ref, x_ref, p_ref, m_ref)
    forcing = lambda t, r: side_or_own(refs, below_ref, above_ref, 0, t, r)
    std = lambda r: std_row(refs, r)
    for r in range(-STEPS, ROWS + STEPS):
        field.put(r, forcing(STEPS - 1, r))
    adjoint(field, d_ref, forcing, std)
    for r in range(ROWS):
        value = field.get(r)
        b_ref[r] = value
        field.put(r, value)
    send_states(field, std, y_ref, low_ref, high_ref, slice(None))


def send_states(field, std, y_ref, low_ref, high_ref, columns):
    field.mix(0, ROWS, FACTOR)
    for r in range(ROWS):
        state = (std(r) * field.get(r))[columns]
        y_ref[r] = state
        if r < HALO:
            low_ref[r] = state
        if r >= ROWS - HALO:
            high_ref[r - (ROWS - HALO)] = state


def image(field, d_ref, weights, std, start, tops):
    smooth_rows(-HALO, ROWS + HALO, start, d_ref, field.put)
    for t in range(STEPS):
        first, stop = -HALO + t + 1, ROWS + HALO - t - 1
        field.mix(first, stop, MIX)
        if t == STEPS - 1:
            for r in range(first, stop):
                field.put(r, kept(field.get(r), weights, t, r, tops))
            break

        def get(r, t=t):
            value = field.get(r)
            if -t - 1 <= r < ROWS + t + 1:
                tops[t][at(r)] = kept(value, weights, t, r, tops)
            return value

        smooth_rows(first, stop, get, d_ref, field.put)
    adjoint(field, d_ref, lambda t, r: tops[t][at(r)], std)


def kept(value, weights, t, r, tops):
    forced = weights(t, r) * value
    if tops[2] is not None and 0 <= r < ROWS:
        own = slice(COLS, 2 * COLS)
        tops[2].append(forced[own] * value[own])
    return forced


INNER = slice(COLS // 2, WIDE - COLS // 2)
OWN = slice(COLS, 2 * COLS)


def first_image_kernel(
    left_ref, own_ref, right_ref, below_ref, above_ref, m_ref, b_ref, y_ref, south_ref, north_ref,
    q_ref, z_ref, low_ref, high_ref,
    v_ref, x_ref, p_ref, d_ref, g0_ref, g1_ref,
):
    refs = (left_ref, own_ref, right_ref)
    fill_diffusion(refs, below_ref, above_ref, d_ref, -HALO, ROWS + HALO)
    field = Field(v_ref, x_ref, p_ref, m_ref)
    weights = lambda t, r: side_or_own(refs, below_ref, above_ref, 1, t, r)
    std = lambda r: std_row(refs, r)

    def start(r):
        if r < 0:
            return south_ref[r + HALO]
        return north_ref[r - ROWS] if r >= ROWS else y_ref[r]

    image(field, d_ref, weights, std, start, (g0_ref, g1_ref, None))
    for r in range(ROWS):
        value = b_ref[r] + field.get(r)
        q_ref[r] = value[INNER]
        field.put(r, value)
    send_states(field, std, z_ref, low_ref, high_ref, INNER)


def second_image_kernel(
    left_ref, own_ref, right_ref, below_ref, above_ref, m_ref, b_ref, q_ref, y_ref, south_ref, north_ref,
    u_ref, sums_ref,
    v_ref, x_ref, p_ref, d_ref, g0_ref, g1_ref,
):
    refs = (left_ref, own_ref, right_ref)
    fill_diffusion(refs, below_ref, above_ref, d_ref, -HALO, ROWS + HALO)
    field = Field(v_ref, x_ref, p_ref, m_ref)
    weights = lambda t, r: side_or_own(refs, below_ref, above_ref, 1, t, r)
    std = lambda r: std_row(refs, r)
    edge = jnp.zeros((COLS // 2, L), F32)

    def start(r):
        state = south_ref[r + HALO] if r < 0 else north_ref[r - ROWS] if r >= ROWS else y_ref[r]
        return jnp.concatenate([edge, state, edge], axis=0)

    image(field, d_ref, weights, std, start, (g0_ref, g1_ref, None))
    sums = [jnp.zeros((COLS, L), F32) for _ in range(4)]
    middle = slice(COLS // 2, COLS // 2 + COLS)
    for r in range(ROWS):
        b, q = b_ref[r, OWN], q_ref[r, middle]
        u = q + field.get(r)[OWN]
        u_ref[r * COLS : (r + 1) * COLS] = u
        for i, term in enumerate((b * b, b * q, q * q, q * u)):
            sums[i] = sums[i] + term
    lane = lax.broadcasted_iota(jnp.int32, (1, L), 1)
    row = jnp.zeros((1, L), F32)
    for i, term in enumerate(sums):
        total = jnp.sum(jnp.sum(term, axis=0, keepdims=True), axis=1, keepdims=True)
        row = row + jnp.where(lane == i, total, 0.0)
    sums_ref[...] = jnp.broadcast_to(row, sums_ref.shape)


def add_kernel(parts_ref, out_ref):
    out_ref[...] = jnp.broadcast_to(jnp.sum(parts_ref[...], axis=0, keepdims=True), out_ref.shape)


def finish_kernel(parts_ref, b_ref, q_ref, u_ref, solution_ref, residual_ref):
    total = jnp.sum(parts_ref[...], axis=0, keepdims=True)
    bb, bq, qq, qu = (total[:, i : i + 1] for i in range(4))
    first = bb / bq
    norm = first * first * qq - bb
    gain = 1.0 + norm / bb
    curve = gain * gain * bq - 2.0 * first * gain * qq + first * first * qu
    second = norm / curve
    along_b = first + second * gain
    along_q = first * second
    middle = slice(COLS // 2, COLS // 2 + COLS)
    for r in range(ROWS):
        rows = slice(r * COLS, (r + 1) * COLS)
        b, q = b_ref[r, OWN], q_ref[r, middle]
        solution_ref[rows] = along_b * b - along_q * q
        residual_ref[rows] = b - along_b * q + along_q * u_ref[rows]


def exchange(to_before, to_after, axis, wrap):
    size = lax.axis_size(axis)
    up = [(i, (i + 1) % size) for i in range(size if wrap else size - 1)]
    down = [(j, i) for i, j in up]
    return lax.ppermute(to_after, axis, up), lax.ppermute(to_before, axis, down)


def shards(
    departures, obs_weight, obs_columns, obs_owner, obs_counts, background_std, diffusion, level_factor, model_mixing
):
    parity = (lax.axis_index("lon") % 2).astype(jnp.int32).reshape(1)
    mats = call(matrices_kernel, "matrices", shape(4, 2 * L, 2 * L, dtype=BF16))(level_factor, model_mixing)
    buckets = call(bucket_kernel, "bucket", shape(8, BUCKET, L), smem=(4, 5))(
        departures, obs_weight, obs_columns.reshape(1, SLOTS), obs_owner.reshape(1, SLOTS), obs_counts, parity
    )
    received = lax.all_to_all(buckets, "lon", 0, 0)
    own = call(tile_kernel, "tile", shape(TILE_ROWS, L))(
        received, background_std.reshape(CELLS, L), jnp.pad(diffusion, ((0, 0), (0, L - COLS)))
    )
    left, right = exchange(own, own, "lon", True)
    refs = (left, own, right)
    side = shape(SIDE * WIDE, L)
    low, high = call(sides_kernel, "sides", (side, side))(*refs)
    below, above = exchange(low, high, "lat", False)
    tall = (ROWS + 2 * HALO) * WIDE
    scratch = [
        pltpu.VMEM((tall, L), F32),
        pltpu.VMEM((tall, 2 * L), BF16),
        pltpu.VMEM((tall, 2 * L), F32),
        pltpu.VMEM((tall, L), F32),
    ]
    tops = [pltpu.VMEM((tall, L), F32)] * 2
    send = shape(HALO, WIDE, L)
    b, y, low, high = call(
        right_side_kernel, "right_side", (shape(ROWS, WIDE, L), shape(ROWS, WIDE, L), send, send), scratch
    )(*refs, below, above, mats)
    south, north = exchange(low, high, "lat", False)
    inner = 2 * COLS
    send = shape(HALO, inner, L)
    q, z, low, high = call(
        first_image_kernel, "first_image", (shape(ROWS, inner, L), shape(ROWS, inner, L), send, send), scratch + tops
    )(*refs, below, above, mats, b, y, south, north)
    south, north = exchange(low, high, "lat", False)
    lat = lax.axis_size("lat")
    u, sums = call(second_image_kernel, "second_image", (shape(CELLS, L), shape(lat, L)), scratch + tops)(
        *refs, below, above, mats, b, q, z, south, north
    )
    sums = lax.all_to_all(sums, "lat", 0, 0, tiled=True)
    sums = call(add_kernel, "add", shape(8, L))(sums)
    sums = lax.all_to_all(sums, "lon", 0, 0, tiled=True)
    out = shape(CELLS, L)
    solution, residual = call(finish_kernel, "finish", (out, out))(sums, b, q, u)
    return solution.reshape(ROWS, COLS, L), residual.reshape(ROWS, COLS, L)


def solution(mesh):
    placed = (
        P(("lat", "lon"), None),
        P(("lat", "lon"), None),
        P(("lat", "lon")),
        P(("lat", "lon"), None),
        P(("lat", "lon")),
        P("lat", "lon", None),
        P("lat", "lon"),
        P(),
        P(),
    )
    return jax.shard_map(
        shards,
        mesh=mesh,
        in_specs=placed,
        out_specs=(P("lat", "lon", None), P("lat", "lon", None)),
        check_vma=False,
    )
```

time: 878 us -> 127 us (0.14)
  blocking collectives: 333 us -> 40.8 us
  waiting for transfers between devices: 254 us -> 35.1 us
  starting transfers between devices: 238 us -> 39.4 us
  between operations: 19.8 us -> 1.46 us
  other arithmetic: 16.7 us -> 0 us
  matrix products: 15 us -> 0 us
    psum x3 -> x0, blocking collectives: 333 us -> none  [the longest x2 218 us: squares(): return lax.psum(jnp.sum(residual * residual), ('lat', 'lon'))]
    ppermute x60 -> x8, starting transfers between devices: 237 us -> 31.6 us  [the longest x4 22.8 us: exchange(): lax.ppermute(to_after, axis, up)]
    reduce_scatter x3 -> x0, waiting for transfers between devices: 139 us -> none  [spread_forcing(): lax.psum_scatter(forcing_rows, 'lon', scatter_dimension=2, tiled=True)]
    all_gather x2 -> x0, waiting for transfers between devices: 78.1 us -> none  [shards(): gathered = lax.all_gather(stacked, 'lon', axis=2, tiled=True)]
    all_to_all x0 -> x2, blocking collectives: none -> 40.8 us  [the longest x1 31.9 us: shards(): sums = lax.all_to_all(sums, 'lat', 0, 0, tiled=True)]
    dot_general x20 -> x0, matrix products: 15 us -> none  [the longest x12 13 us: level_mix_t(): return jnp.einsum('abl,ml->abm', field, matrix, precision=HIGH)]
    ppermute x60 -> x8, waiting for transfers between devices: 36.6 us -> 22.4 us  [the longest x4 17.4 us: exchange(): lax.ppermute(to_before, axis, down)]
    all_to_all x0 -> x1, waiting for transfers between devices: none -> 12.6 us  [shards(): received = lax.all_to_all(buckets, 'lon', 0, 0)]
  transfers between devices with their start and end apart: 65 -> 9, of which waited for: 35 -> 7; matrix products, arithmetic and copies ran while one was open for 0% -> 0% of each run, Pallas kernels for 0% -> 0%
where the time goes in v1:
time: 127 us
  blocking collectives  40.8 us (32%)
  starting transfers between devices  39.4 us (31%)
  waiting for transfers between devices  35.1 us (28%)
  Pallas kernels  7.7 us (6%)
  local copies, waits for them, and re-layouts  2.51 us (2%)
  between operations  1.46 us (1%)
    all_to_all x1, blocking collectives, shards(): sums = lax.all_to_all(sums, 'lat', 0, 0, tiled=True)  31.9 us
    ppermute x4, starting transfers between devices, exchange(): lax.ppermute(to_after, axis, up)  22.8 us
    ppermute x4, waiting for transfers between devices, exchange(): lax.ppermute(to_before, axis, down)  17.4 us
    all_to_all x1, waiting for transfers between devices, shards(): received = lax.all_to_all(buckets, 'lon', 0, 0)  12.6 us
    all_to_all x1, blocking collectives, shards(): sums = lax.all_to_all(sums, 'lon', 0, 0, tiled=True)  8.89 us
    ppermute x4, starting transfers between devices, exchange(): lax.ppermute(to_before, axis, down)  8.79 us
    all_to_all x1, starting transfers between devices, shards(): received = lax.all_to_all(buckets, 'lon', 0, 0)  7.79 us
    pallas_call x9, Pallas kernels, run(): pl.pallas_call(kernel, name=name, out_shape=outs, in_specs=specs, out_spe...  7.7 us
  transfers between devices with their start and end apart: 9, of which 7 were waited for; matrix products, arithmetic and copies ran while one was open for 0% of the time, Pallas kernels for 0%

profile of v1, /device:TPU:1, one launch (start us, length us, event | category | flops | bytes accessed | tf_op | source)
XLA Modules:
  0.0 126.9 jit_solution(9751214126718922267)
XLA Ops:
  1.3 0.0 copy-start.6
  1.3 0.0 copy-start.5
  1.3 0.7 copy-done.6
  2.0 0.0 copy-done.5
  2.0 0.0 copy-start
  2.0 0.9 copy-done
  2.9 0.0 copy-start.1
  2.9 0.9 copy-done.1
  3.8 1.2 bucket.1
  5.0 0.0 copy-start.7
  5.0 0.0 copy-start.2
  5.0 7.8 %all-to-all-start = ((f32[8,136,128]{2,1,0:T(8,128)}), f32[8,136,128]{2,1,0:T(8,128)S(1)}, u32[]{:S(2)}, u32[]{:S(2)}) async-start(f32[8,136,128]{2,1,0:T(8,128)} %bucket.1), calls=%async_computation | async-start | bytes 1114112 | tf_op jit(solution)/shard_map/all_to_all | solution.py:385
  12.8 0.0 copy-done.7
  12.8 12.6 %all-to-all-done.received_ref = f32[8,136,128]{2,1,0:T(8,128)S(1)} async-done(((f32[8,136,128]{2,1,0:T(8,128)}), f32[8,136,128]{2,1,0:T(8,128)S(1)}, u32[]{:S(2)}, u32[]{:S(2)}) %all-to-all-start) | async-done | bytes 557088 | tf_op jit(solution)/shard_map/all_to_all | solution.py:385
  25.5 0.0 copy-done.2
  25.5 0.4 tile.1.own_ref
  25.9 0.0 copy-start.3
  25.9 0.0 copy-start.4
  25.9 2.1 %collective-permute-start.1 = (f32[912,128]{1,0:T(8,128)S(1)}, f32[912,128]{1,0:T(8,128)S(1)}, u32[]{:S(2)}, u32[]{:S(2)}) collective-permute-start(f32[912,128]{1,0:T(8,128)S(1)} %tile.1.own_ref), channel_id=1, source_target_pairs={{1,0},{2,1},{3,2},{4,3},{5,4},{6,5},{7,6},{0,7},{9,8},{10,9},{11,1... | collective-permute-start | bytes 1400840 | tf_op jit(solution)/shard_map/ppermute | solution.py:374
  27.9 3.4 %collective-permute-start = (f32[912,128]{1,0:T(8,128)S(1)}, f32[912,128]{1,0:T(8,128)S(1)}, u32[]{:S(2)}, u32[]{:S(2)}) collective-permute-start(f32[912,128]{1,0:T(8,128)S(1)} %tile.1.own_ref), channel_id=1, source_target_pairs={{0,1},{1,2},{2,3},{3,4},{4,5},{5,6},{6,7},{7,0},{8,9},{9,10},{10,1... | collective-permute-start | bytes 1400840 | tf_op jit(solution)/shard_map/ppermute | solution.py:374
  31.3 4.0 %collective-permute-done.1.right_ref = f32[912,128]{1,0:T(8,128)S(1)} collective-permute-done((f32[912,128]{1,0:T(8,128)S(1)}, f32[912,128]{1,0:T(8,128)S(1)}, u32[]{:S(2)}, u32[]{:S(2)}) %collective-permute-start.1) | collective-permute-done | bytes 466976 | tf_op jit(solution)/shard_map/ppermute | solution.py:374
  35.3 3.1 %collective-permute-done.left_ref = f32[912,128]{1,0:T(8,128)S(1)} collective-permute-done((f32[912,128]{1,0:T(8,128)S(1)}, f32[912,128]{1,0:T(8,128)S(1)}, u32[]{:S(2)}, u32[]{:S(2)}) %collective-permute-start) | collective-permute-done | bytes 466976 | tf_op jit(solution)/shard_map/ppermute | solution.py:374
  38.5 15.6 %collective-permute-start.2 = (f32[624,128]{1,0:T(8,128)S(1)}, f32[624,128]{1,0:T(8,128)S(1)}, u32[]{:S(2)}, u32[]{:S(2)}) collective-permute-start(f32[624,128]{1,0:T(8,128)S(1)} %get-tuple-element.16), channel_id=1, source_target_pairs={{0,8},{8,16},{16,24},{24,32},{32,40},{40,48},{48,56},{56,64},{64,7... | collective-permute-start | bytes 958472 | tf_op jit(solution)/shard_map/ppermute | solution.py:374
  54.1 1.9 %collective-permute-start.3 = (f32[624,128]{1,0:T(8,128)S(1)}, f32[624,128]{1,0:T(8,128)S(1)}, u32[]{:S(2)}, u32[]{:S(2)}) collective-permute-start(f32[624,128]{1,0:T(8,128)S(1)} %get-tuple-element.17), channel_id=1, source_target_pairs={{8,0},{16,8},{24,16},{32,24},{40,32},{48,40},{56,48},{64,56},{72,6... | collective-permute-start | bytes 958472 | tf_op jit(solution)/shard_map/ppermute | solution.py:374
  56.0 0.0 copy-done.3
  56.0 0.0 copy-done.4
  56.0 0.1 matrices.1.m_ref
  56.2 1.8 %collective-permute-done.2.below_ref = f32[624,128]{1,0:T(8,128)S(1)} collective-permute-done((f32[624,128]{1,0:T(8,128)S(1)}, f32[624,128]{1,0:T(8,128)S(1)}, u32[]{:S(2)}, u32[]{:S(2)}) %collective-permute-start.2) | collective-permute-done | bytes 319520 | tf_op jit(solution)/shard_map/ppermute | solution.py:374
  58.0 4.4 %collective-permute-done.3.above_ref = f32[624,128]{1,0:T(8,128)S(1)} collective-permute-done((f32[624,128]{1,0:T(8,128)S(1)}, f32[624,128]{1,0:T(8,128)S(1)}, u32[]{:S(2)}, u32[]{:S(2)}) %collective-permute-start.3) | collective-permute-done | bytes 319520 | tf_op jit(solution)/shard_map/ppermute | solution.py:374
  62.4 1.1 right_side.1
  63.5 1.9 %collective-permute-start.4 = (f32[6,48,128]{2,1,0:T(8,128)S(1)}, f32[6,48,128]{2,1,0:T(8,128)S(1)}, u32[]{:S(2)}, u32[]{:S(2)}) collective-permute-start(f32[6,48,128]{2,1,0:T(8,128)S(1)} %get-tuple-element.20), channel_id=1, source_target_pairs={{0,8},{8,16},{16,24},{24,32},{32,40},{40,48},{48,56},{56,64},{64,7... | collective-permute-start | bytes 442376 | tf_op jit(solution)/shard_map/ppermute | solution.py:374
  65.4 2.4 %collective-permute-start.5 = (f32[6,48,128]{2,1,0:T(8,128)S(1)}, f32[6,48,128]{2,1,0:T(8,128)S(1)}, u32[]{:S(2)}, u32[]{:S(2)}) collective-permute-start(f32[6,48,128]{2,1,0:T(8,128)S(1)} %get-tuple-element.21), channel_id=1, source_target_pairs={{8,0},{16,8},{24,16},{32,24},{40,32},{48,40},{56,48},{64,56},{72,6... | collective-permute-start | bytes 442376 | tf_op jit(solution)/shard_map/ppermute | solution.py:374
  67.9 0.0 collective-permute-done.4.south_ref
  67.9 4.8 %collective-permute-done.5.north_ref = f32[6,48,128]{2,1,0:T(8,128)S(1)} collective-permute-done((f32[6,48,128]{2,1,0:T(8,128)S(1)}, f32[6,48,128]{2,1,0:T(8,128)S(1)}, u32[]{:S(2)}, u32[]{:S(2)}) %collective-permute-start.5) | collective-permute-done | bytes 147488 | tf_op jit(solution)/shard_map/ppermute | solution.py:374
  72.6 2.0 %first_image.1 = (f32[8,32,128]{2,1,0:T(8,128)S(1)}, f32[8,32,128]{2,1,0:T(8,128)S(1)}, f32[6,32,128]{2,1,0:T(8,128)S(1)}, f32[6,32,128]{2,1,0:T(8,128)S(1)}) custom-call(f32[912,128]{1,0:T(8,128)S(1)} %collective-permute-done.left_ref, f32[912,128]{1,0:T(8,128)S(1)} %tile.1.own_ref, f32[912,128]{1,0:T(8,128)S(1)} %collective-permute-done.1.right_ref, ...), custom_call_target="tpu_custom_call" | custom-call | tf_op jit(solution)/shard_map/first_image/pallas_call | solution.py:32
  74.7 1.9 %collective-permute-start.6 = (f32[6,32,128]{2,1,0:T(8,128)S(1)}, f32[6,32,128]{2,1,0:T(8,128)S(1)}, u32[]{:S(2)}, u32[]{:S(2)}) collective-permute-start(f32[6,32,128]{2,1,0:T(8,128)S(1)} %get-tuple-element.24), channel_id=1, source_target_pairs={{0,8},{8,16},{16,24},{24,32},{32,40},{40,48},{48,56},{56,64},{64,7... | collective-permute-start | bytes 294920 | tf_op jit(solution)/shard_map/ppermute | solution.py:374
  76.6 2.4 %collective-permute-start.7 = (f32[6,32,128]{2,1,0:T(8,128)S(1)}, f32[6,32,128]{2,1,0:T(8,128)S(1)}, u32[]{:S(2)}, u32[]{:S(2)}) collective-permute-start(f32[6,32,128]{2,1,0:T(8,128)S(1)} %get-tuple-element.25), channel_id=1, source_target_pairs={{8,0},{16,8},{24,16},{32,24},{40,32},{48,40},{56,48},{64,56},{72,6... | collective-permute-start | bytes 294920 | tf_op jit(solution)/shard_map/ppermute | solution.py:374
  79.0 0.0 collective-permute-done.6.south_ref
  79.1 4.2 %collective-permute-done.7.north_ref = f32[6,32,128]{2,1,0:T(8,128)S(1)} collective-permute-done((f32[6,32,128]{2,1,0:T(8,128)S(1)}, f32[6,32,128]{2,1,0:T(8,128)S(1)}, u32[]{:S(2)}, u32[]{:S(2)}) %collective-permute-start.7) | collective-permute-done | bytes 98336 | tf_op jit(solution)/shard_map/ppermute | solution.py:374
  83.3 2.0 %second_image.1 = (f32[128,128]{1,0:T(8,128)S(1)}, f32[96,128]{1,0:T(8,128)S(1)}) custom-call(f32[912,128]{1,0:T(8,128)S(1)} %collective-permute-done.left_ref, f32[912,128]{1,0:T(8,128)S(1)} %tile.1.own_ref, f32[912,128]{1,0:T(8,128)S(1)} %collective-permute-done.1.right_ref, f32[624,128]{1,0:T(8,128)S(1)} %collective-permute-done.2.below_ref, ...), custom_call_target="tpu_custom_call" | custom-call | tf_op jit(solution)/shard_map/second_image/pallas_call | solution.py:32
  85.3 31.9 %all_to_all.27 = f32[96,1,128]{2,1,0:T(1,128)S(1)} all-to-all(f32[96,1,128]{2,1,0:T(1,128)S(1)} %bitcast.16), channel_id=1, replica_groups=mesh['lat'=96,'lon'=8] {'lat'}, dimensions={0} | all-to-all | bytes 98304 | tf_op jit(solution)/shard_map/all_to_all | solution.py:417
  117.2 8.9 %all_to_all.28 = f32[8,1,128]{2,1,0:T(1,128)S(1)} all-to-all(f32[8,1,128]{2,1,0:T(1,128)S(1)} %bitcast.18), channel_id=1, replica_groups=mesh['lat'=96,'lon'=8] {'lon'}, dimensions={0} | all-to-all | bytes 8192 | tf_op jit(solution)/shard_map/all_to_all | solution.py:419
  126.1 0.8 finish.1
  (3 shorter events, 0.1 us)
Async XLA Ops:
  1.3 0.7 copy-start.6
  1.3 0.7 copy-start.5
  2.0 0.9 copy-start
  2.9 0.9 copy-start.1
  5.0 7.8 %copy-start.7 = (f32[8,16]{1,0:T(8,128)S(1)}, f32[8,16]{1,0:T(8,128)}, u32[]{:S(2)}) copy-start(f32[8,16]{1,0:T(8,128)} %param.15) | copy-start | bytes 1540
  5.0 20.5 %copy-start.2 = (f32[8,16,128]{2,1,0:T(8,128)S(1)}, f32[8,16,128]{2,1,0:T(8,128)}, u32[]{:S(2)}) copy-start(f32[8,16,128]{2,1,0:T(8,128)} %param.14) | copy-start | bytes 196612
  5.0 20.4 %all-to-all-start = ((f32[8,136,128]{2,1,0:T(8,128)}), f32[8,136,128]{2,1,0:T(8,128)S(1)}, u32[]{:S(2)}, u32[]{:S(2)}) async-start(f32[8,136,128]{2,1,0:T(8,128)} %bucket.1), calls=%async_computation | async-start | bytes 1114112 | tf_op jit(solution)/shard_map/all_to_all | solution.py:385
  25.9 30.2 %copy-start.3 = (f32[128,128]{1,0:T(8,128)S(1)}, f32[128,128]{1,0:T(8,128)}, u32[]{:S(2)}) copy-start(f32[128,128]{1,0:T(8,128)} %factor_ref.1) | copy-start | bytes 196612
  25.9 30.2 %copy-start.4 = (f32[128,128]{1,0:T(8,128)S(1)}, f32[128,128]{1,0:T(8,128)}, u32[]{:S(2)}) copy-start(f32[128,128]{1,0:T(8,128)} %mixing_ref.1) | copy-start | bytes 196612
  25.9 9.4 %collective-permute-start.1 = (f32[912,128]{1,0:T(8,128)S(1)}, f32[912,128]{1,0:T(8,128)S(1)}, u32[]{:S(2)}, u32[]{:S(2)}) collective-permute-start(f32[912,128]{1,0:T(8,128)S(1)} %tile.1.own_ref), channel_id=1, source_target_pairs={{1,0},{2,1},{3,2},{4,3},{5,4},{6,5},{7,6},{0,7},{9,8},{10,9},{11,1... | collective-permute-start | bytes 1400840 | tf_op jit(solution)/shard_map/ppermute | solution.py:374
  27.9 10.5 %collective-permute-start = (f32[912,128]{1,0:T(8,128)S(1)}, f32[912,128]{1,0:T(8,128)S(1)}, u32[]{:S(2)}, u32[]{:S(2)}) collective-permute-start(f32[912,128]{1,0:T(8,128)S(1)} %tile.1.own_ref), channel_id=1, source_target_pairs={{0,1},{1,2},{2,3},{3,4},{4,5},{5,6},{6,7},{7,0},{8,9},{9,10},{10,1... | collective-permute-start | bytes 1400840 | tf_op jit(solution)/shard_map/ppermute | solution.py:374
  38.5 19.5 %collective-permute-start.2 = (f32[624,128]{1,0:T(8,128)S(1)}, f32[624,128]{1,0:T(8,128)S(1)}, u32[]{:S(2)}, u32[]{:S(2)}) collective-permute-start(f32[624,128]{1,0:T(8,128)S(1)} %get-tuple-element.16), channel_id=1, source_target_pairs={{0,8},{8,16},{16,24},{24,32},{32,40},{40,48},{48,56},{56,64},{64,7... | collective-permute-start | bytes 958472 | tf_op jit(solution)/shard_map/ppermute | solution.py:374
  54.1 8.3 %collective-permute-start.3 = (f32[624,128]{1,0:T(8,128)S(1)}, f32[624,128]{1,0:T(8,128)S(1)}, u32[]{:S(2)}, u32[]{:S(2)}) collective-permute-start(f32[624,128]{1,0:T(8,128)S(1)} %get-tuple-element.17), channel_id=1, source_target_pairs={{8,0},{16,8},{24,16},{32,24},{40,32},{48,40},{56,48},{64,56},{72,6... | collective-permute-start | bytes 958472 | tf_op jit(solution)/shard_map/ppermute | solution.py:374
  63.5 4.3 %collective-permute-start.4 = (f32[6,48,128]{2,1,0:T(8,128)S(1)}, f32[6,48,128]{2,1,0:T(8,128)S(1)}, u32[]{:S(2)}, u32[]{:S(2)}) collective-permute-start(f32[6,48,128]{2,1,0:T(8,128)S(1)} %get-tuple-element.20), channel_id=1, source_target_pairs={{0,8},{8,16},{16,24},{24,32},{32,40},{40,48},{48,56},{56,64},{64,7... | collective-permute-start | bytes 442376 | tf_op jit(solution)/shard_map/ppermute | solution.py:374
  65.4 7.2 %collective-permute-start.5 = (f32[6,48,128]{2,1,0:T(8,128)S(1)}, f32[6,48,128]{2,1,0:T(8,128)S(1)}, u32[]{:S(2)}, u32[]{:S(2)}) collective-permute-start(f32[6,48,128]{2,1,0:T(8,128)S(1)} %get-tuple-element.21), channel_id=1, source_target_pairs={{8,0},{16,8},{24,16},{32,24},{40,32},{48,40},{56,48},{64,56},{72,6... | collective-permute-start | bytes 442376 | tf_op jit(solution)/shard_map/ppermute | solution.py:374
  74.7 4.3 %collective-permute-start.6 = (f32[6,32,128]{2,1,0:T(8,128)S(1)}, f32[6,32,128]{2,1,0:T(8,128)S(1)}, u32[]{:S(2)}, u32[]{:S(2)}) collective-permute-start(f32[6,32,128]{2,1,0:T(8,128)S(1)} %get-tuple-element.24), channel_id=1, source_target_pairs={{0,8},{8,16},{16,24},{24,32},{32,40},{40,48},{48,56},{56,64},{64,7... | collective-permute-start | bytes 294920 | tf_op jit(solution)/shard_map/ppermute | solution.py:374
  76.6 6.7 %collective-permute-start.7 = (f32[6,32,128]{2,1,0:T(8,128)S(1)}, f32[6,32,128]{2,1,0:T(8,128)S(1)}, u32[]{:S(2)}, u32[]{:S(2)}) collective-permute-start(f32[6,32,128]{2,1,0:T(8,128)S(1)} %get-tuple-element.25), channel_id=1, source_target_pairs={{8,0},{16,8},{24,16},{32,24},{40,32},{48,40},{56,48},{64,56},{72,6... | collective-permute-start | bytes 294920 | tf_op jit(solution)/shard_map/ppermute | solution.py:374

commit v2 on v0

v2 whole, which is shorter than its diff:
```python
import jax
import jax.numpy as jnp
from jax import lax
from jax.experimental import pallas as pl
from jax.experimental.pallas import tpu as pltpu
from jax.sharding import PartitionSpec as P

F32 = jnp.float32
BF16 = jnp.bfloat16
L = 128
ROWS = 8
COLS = 16
CELLS = ROWS * COLS
STEPS = 3
SLOTS = 256
CAP = 64
WIDE = 3 * COLS
INNER = 2 * COLS
EDGE = COLS // 2
BUCKET = 2 * CAP + 8
REACH = 3 * STEPS

MIB = 1024 * 1024


def call(kernel, name, outs, scratch=(), smem=(), hbm=(), vmem=40):
    def run(*args):
        spaces = [pltpu.SMEM if i in smem else pltpu.HBM if i in hbm else pltpu.VMEM for i in range(len(args))]
        specs = [pl.BlockSpec(memory_space=space) for space in spaces]
        return pl.pallas_call(
            kernel,
            name=name,
            out_shape=outs,
            in_specs=specs,
            out_specs=jax.tree.map(lambda _: pl.BlockSpec(memory_space=pltpu.VMEM), outs),
            scratch_shapes=scratch,
            compiler_params=pltpu.CompilerParams(vmem_limit_bytes=vmem * MIB),
        )(*args)

    return run


def shape(*dims, dtype=F32):
    return jax.ShapeDtypeStruct(dims, dtype)


def halves(x):
    high = x.astype(BF16)
    return high, (x - high.astype(F32)).astype(BF16)


def dot(a, b):
    return jnp.dot(a, b, preferred_element_type=F32)


def matrices_kernel(factor_ref, mixing_ref, out_ref):
    for i, ref in enumerate((mixing_ref, factor_ref)):
        for j in range(2):
            m = 0.5 * ref[...]
            high, low = halves(m.T if j else m)
            row = jnp.concatenate([high, low], axis=1)
            out_ref[2 * i + j] = jnp.concatenate([row, row], axis=0)


MIX, MIX_T, FACTOR, FACTOR_T = range(4)


def bucket_kernel(
    departures_hbm, weight_hbm, columns_ref, owner_ref, counts_ref, parity_ref, out_ref, departures_ref, weight_ref, sems
):
    copies = [
        pltpu.make_async_copy(departures_hbm, departures_ref, sems.at[0]),
        pltpu.make_async_copy(weight_hbm, weight_ref, sems.at[1]),
    ]
    for copy in copies:
        copy.start()
    sub = lax.broadcasted_iota(jnp.int32, (SLOTS, SLOTS), 0)
    lane = lax.broadcasted_iota(jnp.int32, (SLOTS, SLOTS), 1)
    owner_row = owner_ref[...].astype(F32)
    owner_col = jnp.sum(jnp.where(sub == lane, owner_row, 0.0), axis=1, keepdims=True)
    same = owner_row == owner_col
    rank_row = jnp.sum(jnp.where(same & (sub < lane), 1.0, 0.0), axis=0, keepdims=True)
    rank_col = jnp.sum(jnp.where(same & (lane < sub), 1.0, 0.0), axis=1, keepdims=True)
    place = (owner_row * CAP + rank_row).astype(jnp.int32)
    pick = lax.broadcasted_iota(jnp.int32, (8 * CAP, SLOTS), 0) == place
    pick = jnp.where(pick, 1.0, 0.0).astype(BF16)
    slot = lax.broadcasted_iota(jnp.int32, (SLOTS, L), 0)
    for copy in copies:
        copy.wait()
    weights = jnp.where(slot < counts_ref[0], weight_ref[...], 0.0)
    parts = halves(weights * departures_ref[...]) + halves(weights)
    moved = dot(pick, jnp.concatenate(parts, axis=1))
    forcing = moved[:, :L] + moved[:, L : 2 * L]
    weights = moved[:, 2 * L : 3 * L] + moved[:, 3 * L :]
    number = lax.broadcasted_iota(jnp.int32, (1, SLOTS), 1)
    time = (number - STEPS * ((number * 171) >> 9)).astype(F32)
    tile = lax.broadcasted_iota(jnp.int32, (8, SLOTS), 0).astype(F32)
    here = tile == owner_row
    marks = jnp.concatenate(
        [jnp.where(here, time, 0.0), jnp.where(here, columns_ref[...].astype(F32), 0.0)], axis=0
    )
    target = rank_col + (CAP * parity_ref[0]).astype(F32)
    spread = jnp.where(lax.broadcasted_iota(jnp.int32, (SLOTS, L), 1).astype(F32) == target, 1.0, 0.0)
    codes = dot(marks.astype(BF16), spread.astype(BF16))
    codes = CELLS * codes[:8] + codes[8:]
    for d in range(8):
        out_ref[d, :CAP] = forcing[d * CAP : (d + 1) * CAP]
        out_ref[d, CAP : 2 * CAP] = weights[d * CAP : (d + 1) * CAP]
        out_ref[d, 2 * CAP :] = jnp.broadcast_to(codes[d : d + 1], (8, L))


def fixed_kernel(std_ref, diffusion_ref, out_ref):
    out_ref[:CELLS] = std_ref[...]
    sub = lax.broadcasted_iota(jnp.int32, (COLS, COLS), 0)
    lane = lax.broadcasted_iota(jnp.int32, (COLS, COLS), 1)
    place = lax.broadcasted_iota(jnp.int32, (COLS, L), 1)
    turned = jnp.zeros((COLS, L), F32)
    for r in range(ROWS):
        row = diffusion_ref[r : r + 1]
        column = jnp.sum(jnp.where(sub == lane, row, 0.0), axis=1, keepdims=True)
        turned = turned + jnp.where(place == r, column, 0.0)
    out_ref[CELLS:] = turned


SIZE = STEPS * CELLS
PACKED = SIZE + STEPS * ROWS * EDGE


def tile_kernel(received_ref, fixed_left_ref, fixed_right_ref, own_ref, to_left_ref, to_right_ref):
    ones, data = [], []
    cell = lax.broadcasted_iota(jnp.int32, (SIZE, L), 0)
    for j in range(4):
        pair = (2 * j, 2 * j + 1)
        codes = sum(received_ref[s, 2 * CAP : 2 * CAP + 1] for s in pair).astype(jnp.int32)
        ones.append(jnp.where(cell == codes, 1.0, 0.0).astype(BF16))
        for s in pair:
            parts = halves(received_ref[s, :CAP]) + halves(received_ref[s, CAP : 2 * CAP])
            data.append(jnp.concatenate(parts, axis=1))
    total = dot(jnp.concatenate(ones, axis=1), jnp.concatenate(data, axis=0))
    forcing = total[:, :L] + total[:, L : 2 * L]
    weights = total[:, 2 * L : 3 * L] + total[:, 3 * L :]
    for ref in (own_ref, to_left_ref, to_right_ref):
        ref[:SIZE] = forcing
    own_ref[SIZE:] = weights
    for k in range(STEPS * ROWS):
        to = pl.ds(SIZE + k * EDGE, EDGE)
        to_left_ref[to] = weights[k * COLS : k * COLS + EDGE]
        to_right_ref[to] = weights[k * COLS + EDGE : (k + 1) * COLS]
    for r in range(ROWS):
        first = (STEPS - 1) * CELLS + r * COLS
        to_left_ref[PACKED + r : PACKED + r + 1] = weights[first + EDGE : first + EDGE + 1]
        to_right_ref[PACKED + r : PACKED + r + 1] = weights[first + EDGE - 1 : first + EDGE]


def wide(refs, start):
    return jnp.concatenate([ref[start : start + COLS] for ref in refs], axis=0)


class Tile:
    def __init__(self, left_ref, own_ref, right_ref, fixed_left_ref, fixed_ref, fixed_right_ref):
        self.left, self.own, self.right = left_ref, own_ref, right_ref
        self.fixed = (fixed_left_ref, fixed_ref, fixed_right_ref)

    def forcing(self, t, r):
        return wide((self.left, self.own, self.right), t * CELLS + r * COLS)

    def inner_weights(self, t, r):
        start = SIZE + t * CELLS + r * COLS
        packed = pl.ds(SIZE + (t * ROWS + r) * EDGE, EDGE)
        return [self.left[packed], self.own[start : start + COLS], self.right[packed]]

    def weights(self, t, r):
        inner = self.inner_weights(t, r)
        if t < STEPS - 1:
            edges = [jnp.zeros((EDGE, L), F32)] * 2
        else:
            edges = [jnp.broadcast_to(ref[PACKED + r : PACKED + r + 1], (EDGE, L)) for ref in (self.left, self.right)]
        return jnp.concatenate([edges[0], *inner, edges[1]], axis=0)

    def std(self, r):
        return wide(self.fixed, r * COLS)

    def turned(self):
        return wide(self.fixed, CELLS)


def inside(row):
    return row[EDGE : EDGE + INNER]


def padded(row):
    edge = jnp.zeros((EDGE, L), F32)
    return jnp.concatenate([edge, row, edge], axis=0)


def places(rows):
    found, total = {}, 0
    for kind, h, width in rows:
        found[kind, h] = (total, width)
        total += width
    return found, total


FIRST, FIRST_ROWS = places(
    [(("f", t), h, WIDE) for t in range(STEPS) for h in range(1, t + 3)]
    + [("std", h, WIDE) for h in range(1, STEPS + 1)]
    + [("diffusion", 1, WIDE)]
)
SECOND, SECOND_ROWS = places(
    [("state", h, WIDE if h <= STEPS else INNER) for h in range(1, REACH + 1)]
    + [("b", h, INNER) for h in range(1, STEPS + 1)]
    + [(("w", t), h, INNER) for t in range(STEPS) for h in range(1, t + 5)]
)
THIRD, THIRD_ROWS = places([(("g", t), h, INNER) for t in range(STEPS) for h in range(1, t + 2)])


def send(low_ref, high_ref, found, kind, h, row):
    start, width = found[kind, h]
    for ref, r in ((low_ref, h - 1), (high_ref, ROWS - h)):
        ref[start : start + width] = row(r)


def taken(sides, found, kind, r):
    below_ref, above_ref = sides
    ref, h = (below_ref, -r) if r < 0 else (above_ref, r - ROWS + 1)
    start, width = found[kind, h]
    return ref[start : start + width]


def sides_kernel(*refs):
    tile, (low_ref, high_ref) = Tile(*refs[:6]), refs[6:]
    for kind, h in FIRST:
        if kind == "std":
            row = tile.std
        elif kind == "diffusion":
            row = lambda r: tile.turned()
        else:
            row = lambda r, t=kind[1]: tile.forcing(t, r)
        send(low_ref, high_ref, FIRST, kind, h, row)


def own(r):
    return 0 <= r < ROWS


class Field:
    def __init__(self, width, reach, v_ref, x_ref, y_ref, d_ref, m_ref):
        self.width, self.reach = width, reach
        self.v_ref, self.x_ref, self.y_ref, self.d_ref, self.m_ref = v_ref, x_ref, y_ref, d_ref, m_ref

    def at(self, r):
        return pl.ds((r + self.reach) * self.width, self.width)

    def put(self, r, value):
        self.v_ref[self.at(r)] = value
        high, low = halves(value)
        self.x_ref[self.at(r), :L] = high
        self.x_ref[self.at(r), L:] = low

    def mix(self, first, stop, which):
        rows = pl.ds((first + self.reach) * self.width, (stop - first) * self.width)
        self.y_ref[rows] = dot(self.x_ref[rows], self.m_ref[which])

    def get(self, r):
        return self.v_ref[self.at(r)] + self.y_ref[self.at(r), :L] + self.y_ref[self.at(r), L:]

    def fill_diffusion(self, tile, sides, reach):
        values = {0: tile.turned(), -1: taken(sides, FIRST, "diffusion", -1), 1: taken(sides, FIRST, "diffusion", ROWS)}
        skip = (WIDE - self.width) // 2
        for r in range(-reach, ROWS + reach):
            column = values[r // ROWS][skip : skip + self.width, r % ROWS : r % ROWS + 1]
            self.d_ref[self.at(r)] = jnp.broadcast_to(column, (self.width, L))

    def smooth(self, first, stop, get, put, scaled=False):
        held = []
        for r in range(first, stop):
            value = get(r)
            if scaled and r in (first, stop - 1):
                held.append((value, None, value))
            else:
                d = self.d_ref[self.at(r)]
                held.append((value, d, d * value))
            if len(held) == 3:
                value, d, u = held[1]
                around = held[0][2] + held[2][2] + pltpu.roll(u, 1, 0) + pltpu.roll(u, self.width - 1, 0)
                put(r - 1, value + d * (around - 4.0 * u))
                held.pop(0)

    def forward(self, h, start, seen, scaled=False):
        self.smooth(-h, ROWS + h, start, self.put, scaled)
        for t in range(STEPS):
            first, stop = -h + t + 1, ROWS + h - t - 1
            self.mix(first, stop, MIX)

            def get(r, t=t):
                value = self.get(r)
                seen(t, r, value)
                return value

            if t < STEPS - 1:
                self.smooth(first, stop, get, self.put)
            else:
                for r in range(first, stop):
                    get(r)

    def adjoint(self, h, forcing, std):
        for t in range(STEPS - 1, -1, -1):
            first, stop = -h - t - 1, ROWS + h + t + 1
            self.mix(first, stop, MIX_T)
            if t > 0:
                put = lambda r, value, t=t: self.put(r, value + forcing(t - 1, r))
            else:
                put = lambda r, value: self.put(r, std(r) * value)
            self.smooth(first, stop, self.get, put)
        self.mix(-h, ROWS + h, FACTOR_T)


def scratch(width, reach):
    tall = (ROWS + 2 * reach) * width
    return [
        pltpu.VMEM((tall, L), F32),
        pltpu.VMEM((tall, 2 * L), BF16),
        pltpu.VMEM((tall, 2 * L), F32),
        pltpu.VMEM((tall, L), F32),
    ]


def std_rows(tile, sides):
    return lambda r: tile.std(r) if own(r) else taken(sides, FIRST, "std", r)


def right_side_kernel(*refs):
    tile, sides, m_ref = Tile(*refs[:6]), refs[6:8], refs[8]
    b_ref, y_ref, low_ref, high_ref = refs[9:13]
    field = Field(WIDE, STEPS + 1, *refs[13:17], m_ref)
    field.fill_diffusion(tile, sides, STEPS + 1)
    forcing = lambda t, r: tile.forcing(t, r) if own(r) else taken(sides, FIRST, ("f", t), r)
    std = std_rows(tile, sides)
    for r in range(-STEPS - 1, ROWS + STEPS + 1):
        field.put(r, forcing(STEPS - 1, r))
    field.adjoint(1, forcing, std)
    for r in range(-1, ROWS + 1):
        value = field.get(r)
        field.put(r, value)
        if own(r):
            b_ref[r] = value
    field.mix(-1, ROWS + 1, FACTOR)
    for r in range(-1, ROWS + 1):
        state = std(r) * field.get(r)
        if own(r):
            y_ref[r] = state
        else:
            state = field.d_ref[field.at(r)] * state
        for ref, h in ((low_ref, r + 1), (high_ref, ROWS - r)):
            if 1 <= h <= REACH and own(r) == (h < REACH):
                start, width = SECOND["state", h]
                ref[start : start + width] = state if width == WIDE else inside(state)
    for kind, h in SECOND:
        if kind == "b":
            send(low_ref, high_ref, SECOND, kind, h, lambda r: inside(b_ref[r]))
        elif kind != "state":
            row = lambda r, t=kind[1]: jnp.concatenate(tile.inner_weights(t, r), axis=0)
            send(low_ref, high_ref, SECOND, kind, h, row)


MIDDLE = slice(COLS, 2 * COLS)


def first_image_kernel(*refs):
    tile, sides, m_ref = Tile(*refs[:6]), refs[6:8], refs[8]
    b_ref, y_ref = refs[9:11]
    more = refs[11:13]
    q_ref, g_ref, low_ref, high_ref, sums_ref = refs[13:18]
    field = Field(WIDE, REACH, *refs[18:22], m_ref)
    tops = refs[22:24]
    field.fill_diffusion(tile, sides, REACH - 1)
    std = std_rows(tile, sides)

    def weights(t, r):
        return tile.weights(t, r) if own(r) else padded(taken(more, SECOND, ("w", t), r))

    def start(r):
        if own(r):
            return y_ref[r]
        row = taken(more, SECOND, "state", r)
        return row if row.shape[0] == WIDE else padded(row)

    def force(t, r, value):
        if -t - 4 <= r < ROWS + t + 4:
            if t < STEPS - 1:
                tops[t][field.at(r)] = weights(t, r) * value
            else:
                field.put(r, weights(t, r) * value)

    field.forward(REACH, start, force, scaled=True)
    field.adjoint(STEPS, lambda t, r: tops[t][field.at(r)], std)
    sums = [jnp.zeros((COLS, L), F32) for _ in range(4)]
    for r in range(-STEPS, ROWS + STEPS):
        b = b_ref[r] if own(r) else padded(taken(more, SECOND, "b", r))
        q = b + field.get(r)
        field.put(r, q)
        if own(r):
            b, q = b[MIDDLE], q[MIDDLE]
            q_ref[r] = q
            for i, term in enumerate((b * b, b * q, q * q, q * q)):
                sums[i] = sums[i] + term
    field.mix(-STEPS, ROWS + STEPS, FACTOR)

    def keep(t, r, value):
        if own(r):
            forced = tile.weights(t, r) * value
            sums[3] = sums[3] + forced[MIDDLE] * value[MIDDLE]
            forced = inside(forced)
            g_ref[t, r] = forced
            for ref, h in ((low_ref, r + 1), (high_ref, ROWS - r)):
                if h <= t + 1:
                    begin, width = THIRD[("g", t), h]
                    ref[begin : begin + width] = forced

    field.forward(STEPS, lambda r: std(r) * field.get(r), keep)
    lane = lax.broadcasted_iota(jnp.int32, (1, L), 1)
    row = jnp.zeros((1, L), F32)
    for i, term in enumerate(sums):
        total = jnp.sum(jnp.sum(term, axis=0, keepdims=True), axis=1, keepdims=True)
        row = row + jnp.where(lane == i, total, 0.0)
    sums_ref[...] = jnp.broadcast_to(row, sums_ref.shape)


def second_image_kernel(*refs):
    tile, sides, m_ref = Tile(*refs[:6]), refs[6:8], refs[8]
    q_ref, g_ref = refs[9:11]
    more = refs[11:13]
    u_ref = refs[13]
    field = Field(INNER, STEPS, *refs[14:18], m_ref)
    field.fill_diffusion(tile, sides, STEPS)
    forcing = lambda t, r: g_ref[t, r] if own(r) else taken(more, THIRD, ("g", t), r)
    for r in range(-STEPS, ROWS + STEPS):
        field.put(r, forcing(STEPS - 1, r))
    field.adjoint(0, forcing, lambda r: inside(tile.std(r)))
    for r in range(ROWS):
        u_ref[r] = q_ref[r] + field.get(r)[EDGE : EDGE + COLS]


def add_kernel(parts_ref, out_ref):
    out_ref[...] = jnp.broadcast_to(jnp.sum(parts_ref[...], axis=0, keepdims=True), out_ref.shape)


def finish_kernel(parts_ref, b_ref, q_ref, u_ref, solution_ref, residual_ref):
    total = jnp.sum(parts_ref[...], axis=0, keepdims=True)
    bb, bq, qq, qu = (total[:, i : i + 1] for i in range(4))
    first = bb / bq
    norm = first * first * qq - bb
    gain = 1.0 + norm / bb
    curve = gain * gain * bq - 2.0 * first * gain * qq + first * first * qu
    second = norm / curve
    along_b = first + second * gain
    along_q = first * second
    for r in range(ROWS):
        b, q = b_ref[r, MIDDLE], q_ref[r]
        solution_ref[r] = along_b * b - along_q * q
        residual_ref[r] = b - along_b * q + along_q * u_ref[r]


def exchange(to_before, to_after, axis, wrap):
    size = lax.axis_size(axis)
    up = [(i, (i + 1) % size) for i in range(size if wrap else size - 1)]
    down = [(j, i) for i, j in up]
    return lax.ppermute(to_after, axis, up), lax.ppermute(to_before, axis, down)


def shards(
    departures, obs_weight, obs_columns, obs_owner, obs_counts, background_std, diffusion, level_factor, model_mixing
):
    parity = (lax.axis_index("lon") % 2).astype(jnp.int32).reshape(1)
    slots = pltpu.VMEM((SLOTS, L), F32)
    buckets = call(
        bucket_kernel,
        "bucket",
        shape(8, BUCKET, L),
        [slots, slots, pltpu.SemaphoreType.DMA((2,))],
        smem=(4, 5),
        hbm=(0, 1),
        vmem=60,
    )(departures, obs_weight, obs_columns.reshape(1, SLOTS), obs_owner.reshape(1, SLOTS), obs_counts, parity)
    received = lax.all_to_all(buckets, "lon", 0, 0)
    mats = call(matrices_kernel, "matrices", shape(4, 2 * L, 2 * L, dtype=BF16))(level_factor, model_mixing)
    fixed = call(fixed_kernel, "fixed", shape(CELLS + COLS, L))(background_std.reshape(CELLS, L), diffusion)
    fixed_left, fixed_right = exchange(fixed, fixed, "lon", True)
    beside = shape(PACKED + ROWS, L)
    tile, to_left, to_right = call(tile_kernel, "tile", (shape(2 * SIZE, L), beside, beside))(
        received, fixed_left, fixed_right
    )
    left, right = exchange(to_left, to_right, "lon", True)
    refs = (left, tile, right, fixed_left, fixed, fixed_right)
    side = shape(FIRST_ROWS, L)
    below, above = exchange(*call(sides_kernel, "sides", (side, side))(*refs), "lat", False)
    refs = (*refs, below, above, mats)
    field, side = shape(ROWS, WIDE, L), shape(SECOND_ROWS, L)
    b, y, low, high = call(right_side_kernel, "right_side", (field, field, side, side), scratch(WIDE, STEPS + 1))(*refs)
    south, north = exchange(low, high, "lat", False)
    lat = lax.axis_size("lat")
    small, side = shape(ROWS, COLS, L), shape(THIRD_ROWS, L)
    space = scratch(WIDE, REACH)
    q, g, low, high, sums = call(
        first_image_kernel,
        "first_image",
        (small, shape(STEPS, ROWS, INNER, L), side, side, shape(lat, L)),
        space + [space[0]] * 2,
    )(*refs, b, y, south, north)
    sums = lax.all_to_all(sums, "lat", 0, 0, tiled=True)
    south, north = exchange(low, high, "lat", False)
    u = call(second_image_kernel, "second_image", small, scratch(INNER, STEPS))(*refs, q, g, south, north)
    sums = call(add_kernel, "add", shape(8, L))(sums)
    sums = lax.all_to_all(sums, "lon", 0, 0, tiled=True)
    return call(finish_kernel, "finish", (small, small))(sums, b, q, u)


def solution(mesh):
    placed = (
        P(("lat", "lon"), None),
        P(("lat", "lon"), None),
        P(("lat", "lon")),
        P(("lat", "lon"), None),
        P(("lat", "lon")),
        P("lat", "lon", None),
        P("lat", "lon"),
        P(),
        P(),
    )
    return jax.shard_map(
        shards,
        mesh=mesh,
        in_specs=placed,
        out_specs=(P("lat", "lon", None), P("lat", "lon", None)),
        check_vma=False,
    )
```

time: 878 us -> 119 us (0.14)
  blocking collectives: 333 us -> 0 us
  waiting for transfers between devices: 254 us -> 38 us
  starting transfers between devices: 238 us -> 68.1 us
  between operations: 19.8 us -> 1.48 us
  other arithmetic: 16.7 us -> 0 us
  matrix products: 15 us -> 0 us
  Pallas kernels: 0 us -> 11 us
    psum x3 -> x0, blocking collectives: 333 us -> none  [the longest x2 218 us: squares(): return lax.psum(jnp.sum(residual * residual), ('lat', 'lon'))]
    ppermute x60 -> x10, starting transfers between devices: 237 us -> 36.2 us  [the longest x5 20.8 us: exchange(): lax.ppermute(to_after, axis, up)]
    reduce_scatter x3 -> x0, waiting for transfers between devices: 139 us -> none  [spread_forcing(): lax.psum_scatter(forcing_rows, 'lon', scatter_dimension=2, tiled=True)]
    all_gather x2 -> x0, waiting for transfers between devices: 78.1 us -> none  [shards(): gathered = lax.all_gather(stacked, 'lon', axis=2, tiled=True)]
    all_to_all x0 -> x3, starting transfers between devices: none -> 31.9 us  [the longest x1 19.4 us: shards(): sums = lax.all_to_all(sums, 'lat', 0, 0, tiled=True)]
    dot_general x20 -> x0, matrix products: 15 us -> none  [the longest x12 13 us: level_mix_t(): return jnp.einsum('abl,ml->abm', field, matrix, precision=HIGH)]
    all_to_all x0 -> x3, waiting for transfers between devices: none -> 12.3 us  [the longest x1 6.64 us: shards(): sums = lax.all_to_all(sums, 'lat', 0, 0, tiled=True)]
    scatter-add x3 -> x0, other arithmetic: 12.1 us -> none  [spread_forcing(): forcing_rows = jnp.zeros((STEPS * lat_cells * row_width, levels), jnp.flo...]
  transfers between devices with their start and end apart: 65 -> 13, of which waited for: 35 -> 10; matrix products, arithmetic and copies ran while one was open for 0% -> 0% of each run, Pallas kernels for 0% -> 1%
where the time goes in v2:
time: 119 us
  starting transfers between devices  68.1 us (57%)
  waiting for transfers between devices  38 us (32%)
  Pallas kernels  11 us (9%)
  between operations  1.48 us (1%)
    ppermute x5, starting transfers between devices, exchange(): lax.ppermute(to_after, axis, up)  20.8 us
    all_to_all x1, starting transfers between devices, shards(): sums = lax.all_to_all(sums, 'lat', 0, 0, tiled=True)  19.4 us
    ppermute x5, starting transfers between devices, exchange(): lax.ppermute(to_before, axis, down)  15.4 us
    ppermute x5, waiting for transfers between devices, exchange(): lax.ppermute(to_before, axis, down)  13.8 us
    ppermute x5, waiting for transfers between devices, exchange(): lax.ppermute(to_after, axis, up)  12 us
    pallas_call x10, Pallas kernels, run(): pl.pallas_call(kernel, name=name, out_shape=outs, in_specs=specs, out_spe...  11 us
    all_to_all x1, starting transfers between devices, shards(): received = lax.all_to_all(buckets, 'lon', 0, 0)  7.79 us
    all_to_all x1, waiting for transfers between devices, shards(): sums = lax.all_to_all(sums, 'lat', 0, 0, tiled=True)  6.64 us
  transfers between devices with their start and end apart: 13, of which 10 were waited for; matrix products, arithmetic and copies ran while one was open for 0% of the time, Pallas kernels for 1%

profile of v2, /device:TPU:1, one launch (start us, length us, event | category | flops | bytes accessed | tf_op | source)
XLA Modules:
  0.0 118.7 jit_solution(6574867150160621585)
XLA Ops:
  1.3 2.8 %bucket.1 = f32[8,136,128]{2,1,0:T(8,128)} custom-call(f32[256,128]{1,0:T(8,128)} %departures_hbm.1, f32[256,128]{1,0:T(8,128)} %weight_hbm.1, s32[1,256]{1,0:T(1,128)} %bitcast.15, s32[1,256]{1,0:T(1,128)} %bitcast.16, s32[1]{0:T(128)S(6)} %copy.13.counts_ref, s32[1]{0:T(128)} %bitcast.2.parity_ref), custom_call_target="tpu_custom_call" | custom-call | tf_op jit(solution)/shard_map/bucket/pallas_call | solution.py:30
  4.1 0.0 copy-start.2
  4.1 0.0 copy-start.3
  4.1 7.8 %all-to-all-start = ((f32[8,136,128]{2,1,0:T(8,128)}), f32[8,136,128]{2,1,0:T(8,128)S(1)}, u32[]{:S(2)}, u32[]{:S(2)}) async-start(f32[8,136,128]{2,1,0:T(8,128)} %bucket.1), calls=%async_computation | async-start | bytes 1114112 | tf_op jit(solution)/shard_map/all_to_all | solution.py:485
  11.9 0.0 copy-done.2
  11.9 0.0 copy-done.3
  11.9 0.1 fixed.1.refs_4_
  12.0 4.6 %collective-permute-start.1 = (f32[144,128]{1,0:T(8,128)S(1)}, f32[144,128]{1,0:T(8,128)S(1)}, u32[]{:S(2)}, u32[]{:S(2)}) collective-permute-start(f32[144,128]{1,0:T(8,128)S(1)} %fixed.1.refs_4_), channel_id=1, source_target_pairs={{1,0},{2,1},{3,2},{4,3},{5,4},{6,5},{7,6},{0,7},{9,8},{10,9},{11,1... | collective-permute-start | bytes 221192 | tf_op jit(solution)/shard_map/ppermute | solution.py:468
  16.6 1.9 %collective-permute-start = (f32[144,128]{1,0:T(8,128)S(1)}, f32[144,128]{1,0:T(8,128)S(1)}, u32[]{:S(2)}, u32[]{:S(2)}) collective-permute-start(f32[144,128]{1,0:T(8,128)S(1)} %fixed.1.refs_4_), channel_id=1, source_target_pairs={{0,1},{1,2},{2,3},{3,4},{4,5},{5,6},{6,7},{7,0},{8,9},{9,10},{10,1... | collective-permute-start | bytes 221192 | tf_op jit(solution)/shard_map/ppermute | solution.py:468
  18.6 2.8 %collective-permute-done.1.fixed_right_ref.refs_5_ = f32[144,128]{1,0:T(8,128)S(1)} collective-permute-done((f32[144,128]{1,0:T(8,128)S(1)}, f32[144,128]{1,0:T(8,128)S(1)}, u32[]{:S(2)}, u32[]{:S(2)}) %collective-permute-start.1) | collective-permute-done | bytes 73760 | tf_op jit(solution)/shard_map/ppermute | solution.py:468
  21.3 4.9 %collective-permute-done.fixed_left_ref.refs_3_ = f32[144,128]{1,0:T(8,128)S(1)} collective-permute-done((f32[144,128]{1,0:T(8,128)S(1)}, f32[144,128]{1,0:T(8,128)S(1)}, u32[]{:S(2)}, u32[]{:S(2)}) %collective-permute-start) | collective-permute-done | bytes 73760 | tf_op jit(solution)/shard_map/ppermute | solution.py:468
  26.2 0.0 all-to-all-done.received_ref
  26.2 0.4 tile.1
  26.5 1.9 %collective-permute-start.2 = (f32[584,128]{1,0:T(8,128)S(1)}, f32[584,128]{1,0:T(8,128)S(1)}, u32[]{:S(2)}, u32[]{:S(2)}) collective-permute-start(f32[584,128]{1,0:T(8,128)S(1)} %get-tuple-element.16), channel_id=1, source_target_pairs={{0,1},{1,2},{2,3},{3,4},{4,5},{5,6},{6,7},{7,0},{8,9},{9,10},{10,1... | collective-permute-start | bytes 897032 | tf_op jit(solution)/shard_map/ppermute | solution.py:468
  28.5 4.6 %collective-permute-start.3 = (f32[584,128]{1,0:T(8,128)S(1)}, f32[584,128]{1,0:T(8,128)S(1)}, u32[]{:S(2)}, u32[]{:S(2)}) collective-permute-start(f32[584,128]{1,0:T(8,128)S(1)} %get-tuple-element.18), channel_id=1, source_target_pairs={{1,0},{2,1},{3,2},{4,3},{5,4},{6,5},{7,6},{0,7},{9,8},{10,9},{11,1... | collective-permute-start | bytes 897032 | tf_op jit(solution)/shard_map/ppermute | solution.py:468
  33.1 2.2 %collective-permute-done.2.refs_0_ = f32[584,128]{1,0:T(8,128)S(1)} collective-permute-done((f32[584,128]{1,0:T(8,128)S(1)}, f32[584,128]{1,0:T(8,128)S(1)}, u32[]{:S(2)}, u32[]{:S(2)}) %collective-permute-start.2) | collective-permute-done | bytes 299040 | tf_op jit(solution)/shard_map/ppermute | solution.py:468
  35.3 1.5 %collective-permute-done.3.refs_2_ = f32[584,128]{1,0:T(8,128)S(1)} collective-permute-done((f32[584,128]{1,0:T(8,128)S(1)}, f32[584,128]{1,0:T(8,128)S(1)}, u32[]{:S(2)}, u32[]{:S(2)}) %collective-permute-start.3) | collective-permute-done | bytes 299040 | tf_op jit(solution)/shard_map/ppermute | solution.py:468
  36.7 0.0 copy-start
  36.7 0.0 copy-start.1
  36.8 0.1 sides.1
  36.8 11.5 %collective-permute-start.4 = (f32[624,128]{1,0:T(8,128)S(1)}, f32[624,128]{1,0:T(8,128)S(1)}, u32[]{:S(2)}, u32[]{:S(2)}) collective-permute-start(f32[624,128]{1,0:T(8,128)S(1)} %get-tuple-element.19), channel_id=1, source_target_pairs={{0,8},{8,16},{16,24},{24,32},{32,40},{40,48},{48,56},{56,64},{64,7... | collective-permute-start | bytes 958472 | tf_op jit(solution)/shard_map/ppermute | solution.py:468
  48.3 1.9 %collective-permute-start.5 = (f32[624,128]{1,0:T(8,128)S(1)}, f32[624,128]{1,0:T(8,128)S(1)}, u32[]{:S(2)}, u32[]{:S(2)}) collective-permute-start(f32[624,128]{1,0:T(8,128)S(1)} %get-tuple-element.20), channel_id=1, source_target_pairs={{8,0},{16,8},{24,16},{32,24},{40,32},{48,40},{56,48},{64,56},{72,6... | collective-permute-start | bytes 958472 | tf_op jit(solution)/shard_map/ppermute | solution.py:468
  50.2 0.0 copy-done
  50.2 0.0 copy-done.1
  50.2 0.1 matrices.1.refs_8_
  50.3 1.8 %collective-permute-done.4.refs_6_ = f32[624,128]{1,0:T(8,128)S(1)} collective-permute-done((f32[624,128]{1,0:T(8,128)S(1)}, f32[624,128]{1,0:T(8,128)S(1)}, u32[]{:S(2)}, u32[]{:S(2)}) %collective-permute-start.4) | collective-permute-done | bytes 319520 | tf_op jit(solution)/shard_map/ppermute | solution.py:468
  52.2 4.4 %collective-permute-done.5.refs_7_ = f32[624,128]{1,0:T(8,128)S(1)} collective-permute-done((f32[624,128]{1,0:T(8,128)S(1)}, f32[624,128]{1,0:T(8,128)S(1)}, u32[]{:S(2)}, u32[]{:S(2)}) %collective-permute-start.5) | collective-permute-done | bytes 319520 | tf_op jit(solution)/shard_map/ppermute | solution.py:468
  56.6 1.2 %right_side.1 = (f32[8,48,128]{2,1,0:T(8,128)S(1)}, f32[8,48,128]{2,1,0:T(8,128)S(1)}, f32[912,128]{1,0:T(8,128)S(1)}, f32[912,128]{1,0:T(8,128)S(1)}) custom-call(f32[584,128]{1,0:T(8,128)S(1)} %collective-permute-done.2.refs_0_, f32[768,128]{1,0:T(8,128)S(1)} %get-tuple-element.17.refs_1_, f32[584,128]{1,0:T(8,128)S(1)} %collective-permute-done.3.refs_2_, ...), custom_call_target="tpu_custom_call" | custom-call | tf_op jit(solution)/shard_map/right_side/pallas_call | solution.py:30
  57.8 1.9 %collective-permute-start.6 = (f32[912,128]{1,0:T(8,128)S(1)}, f32[912,128]{1,0:T(8,128)S(1)}, u32[]{:S(2)}, u32[]{:S(2)}) collective-permute-start(f32[912,128]{1,0:T(8,128)S(1)} %get-tuple-element.23), channel_id=1, source_target_pairs={{0,8},{8,16},{16,24},{24,32},{32,40},{40,48},{48,56},{56,64},{64,7... | collective-permute-start | bytes 1400840 | tf_op jit(solution)/shard_map/ppermute | solution.py:468
  59.7 2.4 %collective-permute-start.7 = (f32[912,128]{1,0:T(8,128)S(1)}, f32[912,128]{1,0:T(8,128)S(1)}, u32[]{:S(2)}, u32[]{:S(2)}) collective-permute-start(f32[912,128]{1,0:T(8,128)S(1)} %get-tuple-element.24), channel_id=1, source_target_pairs={{8,0},{16,8},{24,16},{32,24},{40,32},{48,40},{56,48},{64,56},{72,6... | collective-permute-start | bytes 1400840 | tf_op jit(solution)/shard_map/ppermute | solution.py:468
  62.2 3.1 %collective-permute-done.6.refs_11_ = f32[912,128]{1,0:T(8,128)S(1)} collective-permute-done((f32[912,128]{1,0:T(8,128)S(1)}, f32[912,128]{1,0:T(8,128)S(1)}, u32[]{:S(2)}, u32[]{:S(2)}) %collective-permute-start.6) | collective-permute-done | bytes 466976 | tf_op jit(solution)/shard_map/ppermute | solution.py:468
  65.2 5.1 %collective-permute-done.7.refs_12_ = f32[912,128]{1,0:T(8,128)S(1)} collective-permute-done((f32[912,128]{1,0:T(8,128)S(1)}, f32[912,128]{1,0:T(8,128)S(1)}, u32[]{:S(2)}, u32[]{:S(2)}) %collective-permute-start.7) | collective-permute-done | bytes 466976 | tf_op jit(solution)/shard_map/ppermute | solution.py:468
  70.4 4.2 %first_image.1 = (f32[8,16,128]{2,1,0:T(8,128)S(1)}, f32[3,8,32,128]{3,2,1,0:T(8,128)S(1)}, f32[192,128]{1,0:T(8,128)S(1)}, f32[192,128]{1,0:T(8,128)S(1)}, f32[96,128]{1,0:T(8,128)}) custom-call(f32[584,128]{1,0:T(8,128)S(1)} %collective-permute-done.2.refs_0_, f32[768,128]{1,0:T(8,128)S(1)} %get-tuple-element.17.refs_1_, ...), custom_call_target="tpu_custom_call" | custom-call | tf_op jit(solution)/shard_map/first_image/pallas_call | solution.py:30
  74.6 19.4 %all-to-all-start.1 = ((f32[96,1,128]{2,1,0:T(1,128)}), f32[96,1,128]{2,1,0:T(1,128)S(1)}, u32[]{:S(2)}, u32[]{:S(2)}) async-start(f32[96,1,128]{2,1,0:T(1,128)} %bitcast.5), calls=%async_computation.1 | async-start | bytes 98304 | tf_op jit(solution)/shard_map/all_to_all | solution.py:510
  94.0 3.5 %collective-permute-start.8 = (f32[192,128]{1,0:T(8,128)S(1)}, f32[192,128]{1,0:T(8,128)S(1)}, u32[]{:S(2)}, u32[]{:S(2)}) collective-permute-start(f32[192,128]{1,0:T(8,128)S(1)} %get-tuple-element.28), channel_id=1, source_target_pairs={{0,8},{8,16},{16,24},{24,32},{32,40},{40,48},{48,56},{56,64},{64,7... | collective-permute-start | bytes 294920 | tf_op jit(solution)/shard_map/ppermute | solution.py:468
  97.5 1.9 %collective-permute-start.9 = (f32[192,128]{1,0:T(8,128)S(1)}, f32[192,128]{1,0:T(8,128)S(1)}, u32[]{:S(2)}, u32[]{:S(2)}) collective-permute-start(f32[192,128]{1,0:T(8,128)S(1)} %get-tuple-element.29), channel_id=1, source_target_pairs={{8,0},{16,8},{24,16},{32,24},{40,32},{48,40},{56,48},{64,56},{72,6... | collective-permute-start | bytes 294920 | tf_op jit(solution)/shard_map/ppermute | solution.py:468
  99.5 6.6 %all-to-all-done.1 = f32[96,1,128]{2,1,0:T(1,128)S(1)} async-done(((f32[96,1,128]{2,1,0:T(1,128)}), f32[96,1,128]{2,1,0:T(1,128)S(1)}, u32[]{:S(2)}, u32[]{:S(2)}) %all-to-all-start.1) | async-done | bytes 49184 | tf_op jit(solution)/shard_map/all_to_all | solution.py:510
  106.1 0.6 add.6
  106.7 4.7 %all-to-all-start.2 = ((f32[8,1,128]{2,1,0:T(1,128)}), f32[8,1,128]{2,1,0:T(1,128)S(1)}, u32[]{:S(2)}, u32[]{:S(2)}) async-start(f32[8,1,128]{2,1,0:T(1,128)} %bitcast.8), calls=%async_computation.2 | async-start | bytes 8192 | tf_op jit(solution)/shard_map/all_to_all | solution.py:514
  111.4 0.0 collective-permute-done.8.refs_11_
  111.4 0.0 collective-permute-done.9.refs_12_
  111.4 0.8 second_image.1.u_ref
  112.2 5.7 %all-to-all-done.2 = f32[8,1,128]{2,1,0:T(1,128)S(1)} async-done(((f32[8,1,128]{2,1,0:T(1,128)}), f32[8,1,128]{2,1,0:T(1,128)S(1)}, u32[]{:S(2)}, u32[]{:S(2)}) %all-to-all-start.2) | async-done | bytes 4128 | tf_op jit(solution)/shard_map/all_to_all | solution.py:514
  117.9 0.8 finish.1
Async XLA Ops:
  4.1 7.8 %copy-start.2 = (f32[8,16,128]{2,1,0:T(8,128)S(1)}, f32[8,16,128]{2,1,0:T(8,128)}, u32[]{:S(2)}) copy-start(f32[8,16,128]{2,1,0:T(8,128)} %param.14) | copy-start | bytes 196612
  4.1 7.8 %copy-start.3 = (f32[8,16]{1,0:T(8,128)S(1)}, f32[8,16]{1,0:T(8,128)}, u32[]{:S(2)}) copy-start(f32[8,16]{1,0:T(8,128)} %diffusion_ref.1) | copy-start | bytes 1540
  4.1 22.0 %all-to-all-start = ((f32[8,136,128]{2,1,0:T(8,128)}), f32[8,136,128]{2,1,0:T(8,128)S(1)}, u32[]{:S(2)}, u32[]{:S(2)}) async-start(f32[8,136,128]{2,1,0:T(8,128)} %bucket.1), calls=%async_computation | async-start | bytes 1114112 | tf_op jit(solution)/shard_map/all_to_all | solution.py:485
  12.0 9.3 %collective-permute-start.1 = (f32[144,128]{1,0:T(8,128)S(1)}, f32[144,128]{1,0:T(8,128)S(1)}, u32[]{:S(2)}, u32[]{:S(2)}) collective-permute-start(f32[144,128]{1,0:T(8,128)S(1)} %fixed.1.refs_4_), channel_id=1, source_target_pairs={{1,0},{2,1},{3,2},{4,3},{5,4},{6,5},{7,6},{0,7},{9,8},{10,9},{11,1... | collective-permute-start | bytes 221192 | tf_op jit(solution)/shard_map/ppermute | solution.py:468
  16.6 9.5 %collective-permute-start = (f32[144,128]{1,0:T(8,128)S(1)}, f32[144,128]{1,0:T(8,128)S(1)}, u32[]{:S(2)}, u32[]{:S(2)}) collective-permute-start(f32[144,128]{1,0:T(8,128)S(1)} %fixed.1.refs_4_), channel_id=1, source_target_pairs={{0,1},{1,2},{2,3},{3,4},{4,5},{5,6},{6,7},{7,0},{8,9},{9,10},{10,1... | collective-permute-start | bytes 221192 | tf_op jit(solution)/shard_map/ppermute | solution.py:468
  26.5 8.7 %collective-permute-start.2 = (f32[584,128]{1,0:T(8,128)S(1)}, f32[584,128]{1,0:T(8,128)S(1)}, u32[]{:S(2)}, u32[]{:S(2)}) collective-permute-start(f32[584,128]{1,0:T(8,128)S(1)} %get-tuple-element.16), channel_id=1, source_target_pairs={{0,1},{1,2},{2,3},{3,4},{4,5},{5,6},{6,7},{7,0},{8,9},{9,10},{10,1... | collective-permute-start | bytes 897032 | tf_op jit(solution)/shard_map/ppermute | solution.py:468
  28.5 8.3 %collective-permute-start.3 = (f32[584,128]{1,0:T(8,128)S(1)}, f32[584,128]{1,0:T(8,128)S(1)}, u32[]{:S(2)}, u32[]{:S(2)}) collective-permute-start(f32[584,128]{1,0:T(8,128)S(1)} %get-tuple-element.18), channel_id=1, source_target_pairs={{1,0},{2,1},{3,2},{4,3},{5,4},{6,5},{7,6},{0,7},{9,8},{10,9},{11,1... | collective-permute-start | bytes 897032 | tf_op jit(solution)/shard_map/ppermute | solution.py:468
  36.7 13.5 %copy-start = (f32[128,128]{1,0:T(8,128)S(1)}, f32[128,128]{1,0:T(8,128)}, u32[]{:S(2)}) copy-start(f32[128,128]{1,0:T(8,128)} %factor_ref.1) | copy-start | bytes 196612
  36.7 13.5 %copy-start.1 = (f32[128,128]{1,0:T(8,128)S(1)}, f32[128,128]{1,0:T(8,128)}, u32[]{:S(2)}) copy-start(f32[128,128]{1,0:T(8,128)} %mixing_ref.1) | copy-start | bytes 196612
  36.8 15.4 %collective-permute-start.4 = (f32[624,128]{1,0:T(8,128)S(1)}, f32[624,128]{1,0:T(8,128)S(1)}, u32[]{:S(2)}, u32[]{:S(2)}) collective-permute-start(f32[624,128]{1,0:T(8,128)S(1)} %get-tuple-element.19), channel_id=1, source_target_pairs={{0,8},{8,16},{16,24},{24,32},{32,40},{40,48},{48,56},{56,64},{64,7... | collective-permute-start | bytes 958472 | tf_op jit(solution)/shard_map/ppermute | solution.py:468
  48.3 8.3 %collective-permute-start.5 = (f32[624,128]{1,0:T(8,128)S(1)}, f32[624,128]{1,0:T(8,128)S(1)}, u32[]{:S(2)}, u32[]{:S(2)}) collective-permute-start(f32[624,128]{1,0:T(8,128)S(1)} %get-tuple-element.20), channel_id=1, source_target_pairs={{8,0},{16,8},{24,16},{32,24},{40,32},{48,40},{56,48},{64,56},{72,6... | collective-permute-start | bytes 958472 | tf_op jit(solution)/shard_map/ppermute | solution.py:468
  57.8 7.4 %collective-permute-start.6 = (f32[912,128]{1,0:T(8,128)S(1)}, f32[912,128]{1,0:T(8,128)S(1)}, u32[]{:S(2)}, u32[]{:S(2)}) collective-permute-start(f32[912,128]{1,0:T(8,128)S(1)} %get-tuple-element.23), channel_id=1, source_target_pairs={{0,8},{8,16},{16,24},{24,32},{32,40},{40,48},{48,56},{56,64},{64,7... | collective-permute-start | bytes 1400840 | tf_op jit(solution)/shard_map/ppermute | solution.py:468
  59.7 10.6 %collective-permute-start.7 = (f32[912,128]{1,0:T(8,128)S(1)}, f32[912,128]{1,0:T(8,128)S(1)}, u32[]{:S(2)}, u32[]{:S(2)}) collective-permute-start(f32[912,128]{1,0:T(8,128)S(1)} %get-tuple-element.24), channel_id=1, source_target_pairs={{8,0},{16,8},{24,16},{32,24},{40,32},{48,40},{56,48},{64,56},{72,6... | collective-permute-start | bytes 1400840 | tf_op jit(solution)/shard_map/ppermute | solution.py:468
  74.6 31.5 %all-to-all-start.1 = ((f32[96,1,128]{2,1,0:T(1,128)}), f32[96,1,128]{2,1,0:T(1,128)S(1)}, u32[]{:S(2)}, u32[]{:S(2)}) async-start(f32[96,1,128]{2,1,0:T(1,128)} %bitcast.5), calls=%async_computation.1 | async-start | bytes 98304 | tf_op jit(solution)/shard_map/all_to_all | solution.py:510
  94.0 17.4 %collective-permute-start.8 = (f32[192,128]{1,0:T(8,128)S(1)}, f32[192,128]{1,0:T(8,128)S(1)}, u32[]{:S(2)}, u32[]{:S(2)}) collective-permute-start(f32[192,128]{1,0:T(8,128)S(1)} %get-tuple-element.28), channel_id=1, source_target_pairs={{0,8},{8,16},{16,24},{24,32},{32,40},{40,48},{48,56},{56,64},{64,7... | collective-permute-start | bytes 294920 | tf_op jit(solution)/shard_map/ppermute | solution.py:468
  97.5 13.9 %collective-permute-start.9 = (f32[192,128]{1,0:T(8,128)S(1)}, f32[192,128]{1,0:T(8,128)S(1)}, u32[]{:S(2)}, u32[]{:S(2)}) collective-permute-start(f32[192,128]{1,0:T(8,128)S(1)} %get-tuple-element.29), channel_id=1, source_target_pairs={{8,0},{16,8},{24,16},{32,24},{40,32},{48,40},{56,48},{64,56},{72,6... | collective-permute-start | bytes 294920 | tf_op jit(solution)/shard_map/ppermute | solution.py:468
  106.7 11.1 %all-to-all-start.2 = ((f32[8,1,128]{2,1,0:T(1,128)}), f32[8,1,128]{2,1,0:T(1,128)S(1)}, u32[]{:S(2)}, u32[]{:S(2)}) async-start(f32[8,1,128]{2,1,0:T(1,128)} %bitcast.8), calls=%async_computation.2 | async-start | bytes 8192 | tf_op jit(solution)/shard_map/all_to_all | solution.py:514

commit v3 on v2

--- a/solution.py
+++ b/solution.py
@@ -189,6 +189,8 @@
 
 
 def padded(row):
+    if row.shape[0] == WIDE:
+        return row
     edge = jnp.zeros((EDGE, L), F32)
     return jnp.concatenate([edge, row, edge], axis=0)
 
@@ -202,22 +204,23 @@
 
 
 FIRST, FIRST_ROWS = places(
-    [(("f", t), h, WIDE) for t in range(STEPS) for h in range(1, t + 3)]
-    + [("std", h, WIDE) for h in range(1, STEPS + 1)]
+    [(("f", t), h, WIDE if h < t + 2 else INNER) for t in range(STEPS) for h in range(1, t + 3)]
+    + [("std", h, INNER) for h in range(1, STEPS + 1)]
     + [("diffusion", 1, WIDE)]
 )
 SECOND, SECOND_ROWS = places(
     [("state", h, WIDE if h <= STEPS else INNER) for h in range(1, REACH + 1)]
     + [("b", h, INNER) for h in range(1, STEPS + 1)]
-    + [(("w", t), h, INNER) for t in range(STEPS) for h in range(1, t + 5)]
 )
+WEIGHTS, WEIGHTS_ROWS = places([(("w", t), h, INNER) for t in range(STEPS) for h in range(1, t + 5)])
 THIRD, THIRD_ROWS = places([(("g", t), h, INNER) for t in range(STEPS) for h in range(1, t + 2)])
 
 
 def send(low_ref, high_ref, found, kind, h, row):
     start, width = found[kind, h]
     for ref, r in ((low_ref, h - 1), (high_ref, ROWS - h)):
-        ref[start : start + width] = row(r)
+        value = row(r)
+        ref[start : start + width] = inside(value) if width < value.shape[0] else value
 
 
 def taken(sides, found, kind, r):
@@ -237,6 +240,12 @@
         else:
             row = lambda r, t=kind[1]: tile.forcing(t, r)
         send(low_ref, high_ref, FIRST, kind, h, row)
+
+
+def weights_kernel(*refs):
+    tile, (low_ref, high_ref) = Tile(*refs[:6]), refs[6:]
+    for kind, h in WEIGHTS:
+        send(low_ref, high_ref, WEIGHTS, kind, h, lambda r: jnp.concatenate(tile.inner_weights(kind[1], r), axis=0))
 
 
 def own(r):
@@ -326,7 +335,7 @@
 
 
 def std_rows(tile, sides):
-    return lambda r: tile.std(r) if own(r) else taken(sides, FIRST, "std", r)
+    return lambda r: tile.std(r) if own(r) else padded(taken(sides, FIRST, "std", r))
 
 
 def right_side_kernel(*refs):
@@ -334,7 +343,7 @@
     b_ref, y_ref, low_ref, high_ref = refs[9:13]
     field = Field(WIDE, STEPS + 1, *refs[13:17], m_ref)
     field.fill_diffusion(tile, sides, STEPS + 1)
-    forcing = lambda t, r: tile.forcing(t, r) if own(r) else taken(sides, FIRST, ("f", t), r)
+    forcing = lambda t, r: tile.forcing(t, r) if own(r) else padded(taken(sides, FIRST, ("f", t), r))
     std = std_rows(tile, sides)
     for r in range(-STEPS - 1, ROWS + STEPS + 1):
         field.put(r, forcing(STEPS - 1, r))
@@ -355,12 +364,8 @@
             if 1 <= h <= REACH and own(r) == (h < REACH):
                 start, width = SECOND["state", h]
                 ref[start : start + width] = state if width == WIDE else inside(state)
-    for kind, h in SECOND:
-        if kind == "b":
-            send(low_ref, high_ref, SECOND, kind, h, lambda r: inside(b_ref[r]))
-        elif kind != "state":
-            row = lambda r, t=kind[1]: jnp.concatenate(tile.inner_weights(t, r), axis=0)
-            send(low_ref, high_ref, SECOND, kind, h, row)
+    for h in range(1, STEPS + 1):
+        send(low_ref, high_ref, SECOND, "b", h, lambda r: b_ref[r])
 
 
 MIDDLE = slice(COLS, 2 * COLS)
@@ -369,21 +374,20 @@
 def first_image_kernel(*refs):
     tile, sides, m_ref = Tile(*refs[:6]), refs[6:8], refs[8]
     b_ref, y_ref = refs[9:11]
-    more = refs[11:13]
-    q_ref, g_ref, low_ref, high_ref, sums_ref = refs[13:18]
-    field = Field(WIDE, REACH, *refs[18:22], m_ref)
-    tops = refs[22:24]
+    more, forced = refs[11:13], refs[13:15]
+    q_ref, g_ref, low_ref, high_ref, sums_ref = refs[15:20]
+    field = Field(WIDE, REACH, *refs[20:24], m_ref)
+    tops = refs[24:26]
     field.fill_diffusion(tile, sides, REACH - 1)
     std = std_rows(tile, sides)
 
     def weights(t, r):
-        return tile.weights(t, r) if own(r) else padded(taken(more, SECOND, ("w", t), r))
+        return tile.weights(t, r) if own(r) else padded(taken(forced, WEIGHTS, ("w", t), r))
 
     def start(r):
         if own(r):
             return y_ref[r]
-        row = taken(more, SECOND, "state", r)
-        return row if row.shape[0] == WIDE else padded(row)
+        return padded(taken(more, SECOND, "state", r))
 
     def force(t, r, value):
         if -t - 4 <= r < ROWS + t + 4:
@@ -439,6 +443,13 @@
     field.adjoint(0, forcing, lambda r: inside(tile.std(r)))
     for r in range(ROWS):
         u_ref[r] = q_ref[r] + field.get(r)[EDGE : EDGE + COLS]
+
+
+def levels(lat, lon):
+    quarter = lat // 4
+    near = [[i * quarter + k for k in range(quarter)] for i in range(4)]
+    far = [[(i * quarter + k) * lon + j for i in range(4) for j in range(lon)] for k in range(quarter)]
+    return near, far
 
 
 def add_kernel(parts_ref, out_ref):
@@ -494,24 +505,27 @@
     refs = (left, tile, right, fixed_left, fixed, fixed_right)
     side = shape(FIRST_ROWS, L)
     below, above = exchange(*call(sides_kernel, "sides", (side, side))(*refs), "lat", False)
+    side = shape(WEIGHTS_ROWS, L)
+    weights = exchange(*call(weights_kernel, "weights", (side, side))(*refs), "lat", False)
     refs = (*refs, below, above, mats)
     field, side = shape(ROWS, WIDE, L), shape(SECOND_ROWS, L)
     b, y, low, high = call(right_side_kernel, "right_side", (field, field, side, side), scratch(WIDE, STEPS + 1))(*refs)
     south, north = exchange(low, high, "lat", False)
-    lat = lax.axis_size("lat")
+    lat, lon = lax.axis_size("lat"), lax.axis_size("lon")
+    near, far = levels(lat, lon)
     small, side = shape(ROWS, COLS, L), shape(THIRD_ROWS, L)
     space = scratch(WIDE, REACH)
     q, g, low, high, sums = call(
         first_image_kernel,
         "first_image",
-        (small, shape(STEPS, ROWS, INNER, L), side, side, shape(lat, L)),
+        (small, shape(STEPS, ROWS, INNER, L), side, side, shape(4 * lon, L)),
         space + [space[0]] * 2,
-    )(*refs, b, y, south, north)
-    sums = lax.all_to_all(sums, "lat", 0, 0, tiled=True)
+    )(*refs, b, y, south, north, *weights)
+    sums = lax.all_to_all(sums, ("lat", "lon"), 0, 0, axis_index_groups=far, tiled=True)
     south, north = exchange(low, high, "lat", False)
     u = call(second_image_kernel, "second_image", small, scratch(INNER, STEPS))(*refs, q, g, south, north)
-    sums = call(add_kernel, "add", shape(8, L))(sums)
-    sums = lax.all_to_all(sums, "lon", 0, 0, tiled=True)
+    sums = call(add_kernel, "add", shape(lat // 4, L))(sums)
+    sums = lax.all_to_all(sums, "lat", 0, 0, axis_index_groups=near, tiled=True)
     return call(finish_kernel, "finish", (small, small))(sums, b, q, u)
 
 

time: 119 us -> 123 us (1.034)
  blocking collectives: 0 us -> 26.7 us
  waiting for transfers between devices: 38 us -> 25.4 us
  starting transfers between devices: 68.1 us -> 58.6 us
    all_to_all x0 -> x1, blocking collectives: none -> 26.7 us  [shards(): lax.all_to_all(sums, ('lat', 'lon'), 0, 0, axis_index_groups=far, tiled=T...]
    all_to_all x2 -> x1, starting transfers between devices: 24.1 us -> 8.94 us  [shards(): sums = lax.all_to_all(sums, 'lat', 0, 0, axis_index_groups=near, tiled=True)]
    ppermute x5 -> x6, waiting for transfers between devices: 13.8 us -> 8.71 us  [exchange(): lax.ppermute(to_before, axis, down)]
    ppermute x5 -> x6, waiting for transfers between devices: 12 us -> 7.99 us  [exchange(): lax.ppermute(to_after, axis, up)]
    ppermute x5 -> x6, starting transfers between devices: 20.8 us -> 24.4 us  [exchange(): lax.ppermute(to_after, axis, up)]
    all_to_all x2 -> x1, waiting for transfers between devices: 12.3 us -> 8.67 us  [shards(): sums = lax.all_to_all(sums, 'lat', 0, 0, axis_index_groups=near, tiled=True)]
    ppermute x5 -> x6, starting transfers between devices: 15.4 us -> 17.4 us  [exchange(): lax.ppermute(to_before, axis, down)]
    pallas_call x10 -> x11, Pallas kernels: 11 us -> 10.4 us  [run(): pl.pallas_call(kernel, name=name, out_shape=outs, in_specs=specs, out_spe...]
  transfers between devices with their start and end apart: 13 -> 14, of which waited for: 10 -> 8; matrix products, arithmetic and copies ran while one was open for 0% -> 0% of each run, Pallas kernels for 1% -> 2%
where the time goes in v3:
time: 123 us
  starting transfers between devices  58.6 us (48%)
  blocking collectives  26.7 us (22%)
  waiting for transfers between devices  25.4 us (21%)
  Pallas kernels  10.4 us (8%)
  between operations  1.54 us (1%)
    all_to_all x1, blocking collectives, shards(): lax.all_to_all(sums, ('lat', 'lon'), 0, 0, axis_index_groups=far, tiled=T...  26.7 us
    ppermute x6, starting transfers between devices, exchange(): lax.ppermute(to_after, axis, up)  24.4 us
    ppermute x6, starting transfers between devices, exchange(): lax.ppermute(to_before, axis, down)  17.4 us
    pallas_call x11, Pallas kernels, run(): pl.pallas_call(kernel, name=name, out_shape=outs, in_specs=specs, out_spe...  10.4 us
    all_to_all x1, starting transfers between devices, shards(): sums = lax.all_to_all(sums, 'lat', 0, 0, axis_index_groups=near, tiled=True)  8.94 us
    ppermute x6, waiting for transfers between devices, exchange(): lax.ppermute(to_before, axis, down)  8.71 us
    all_to_all x1, waiting for transfers between devices, shards(): sums = lax.all_to_all(sums, 'lat', 0, 0, axis_index_groups=near, tiled=True)  8.67 us
    ppermute x6, waiting for transfers between devices, exchange(): lax.ppermute(to_after, axis, up)  7.99 us
  transfers between devices with their start and end apart: 14, of which 8 were waited for; matrix products, arithmetic and copies ran while one was open for 0% of the time, Pallas kernels for 2%

profile of v3, /device:TPU:1, one launch (start us, length us, event | category | flops | bytes accessed | tf_op | source)
XLA Modules:
  0.0 122.7 jit_solution(13418811332604079912)
XLA Ops:
  1.3 2.8 %bucket.1 = f32[8,136,128]{2,1,0:T(8,128)} custom-call(f32[256,128]{1,0:T(8,128)} %departures_hbm.1, f32[256,128]{1,0:T(8,128)} %weight_hbm.1, s32[1,256]{1,0:T(1,128)} %bitcast.16, s32[1,256]{1,0:T(1,128)} %bitcast.17, s32[1]{0:T(128)S(6)} %copy.13.counts_ref, s32[1]{0:T(128)} %bitcast.2.parity_ref), custom_call_target="tpu_custom_call" | custom-call | tf_op jit(solution)/shard_map/bucket/pallas_call | solution.py:30
  4.1 0.0 copy-start.2
  4.1 0.0 copy-start.3
  4.1 7.8 %all-to-all-start = ((f32[8,136,128]{2,1,0:T(8,128)}), f32[8,136,128]{2,1,0:T(8,128)S(1)}, u32[]{:S(2)}, u32[]{:S(2)}) async-start(f32[8,136,128]{2,1,0:T(8,128)} %bucket.1), calls=%async_computation | async-start | bytes 1114112 | tf_op jit(solution)/shard_map/all_to_all | solution.py:496
  11.9 0.0 copy-done.2
  11.9 0.0 copy-done.3
  11.9 0.1 fixed.1.refs_4_
  12.0 4.6 %collective-permute-start.1 = (f32[144,128]{1,0:T(8,128)S(1)}, f32[144,128]{1,0:T(8,128)S(1)}, u32[]{:S(2)}, u32[]{:S(2)}) collective-permute-start(f32[144,128]{1,0:T(8,128)S(1)} %fixed.1.refs_4_), channel_id=1, source_target_pairs={{1,0},{2,1},{3,2},{4,3},{5,4},{6,5},{7,6},{0,7},{9,8},{10,9},{11,1... | collective-permute-start | bytes 221192 | tf_op jit(solution)/shard_map/ppermute | solution.py:479
  16.6 1.9 %collective-permute-start = (f32[144,128]{1,0:T(8,128)S(1)}, f32[144,128]{1,0:T(8,128)S(1)}, u32[]{:S(2)}, u32[]{:S(2)}) collective-permute-start(f32[144,128]{1,0:T(8,128)S(1)} %fixed.1.refs_4_), channel_id=1, source_target_pairs={{0,1},{1,2},{2,3},{3,4},{4,5},{5,6},{6,7},{7,0},{8,9},{9,10},{10,1... | collective-permute-start | bytes 221192 | tf_op jit(solution)/shard_map/ppermute | solution.py:479
  18.5 2.8 %collective-permute-done.1.fixed_right_ref.refs_5_ = f32[144,128]{1,0:T(8,128)S(1)} collective-permute-done((f32[144,128]{1,0:T(8,128)S(1)}, f32[144,128]{1,0:T(8,128)S(1)}, u32[]{:S(2)}, u32[]{:S(2)}) %collective-permute-start.1) | collective-permute-done | bytes 73760 | tf_op jit(solution)/shard_map/ppermute | solution.py:479
  21.3 4.9 %collective-permute-done.fixed_left_ref.refs_3_ = f32[144,128]{1,0:T(8,128)S(1)} collective-permute-done((f32[144,128]{1,0:T(8,128)S(1)}, f32[144,128]{1,0:T(8,128)S(1)}, u32[]{:S(2)}, u32[]{:S(2)}) %collective-permute-start) | collective-permute-done | bytes 73760 | tf_op jit(solution)/shard_map/ppermute | solution.py:479
  26.2 0.0 all-to-all-done.received_ref
  26.2 0.4 tile.1
  26.5 1.9 %collective-permute-start.2 = (f32[584,128]{1,0:T(8,128)S(1)}, f32[584,128]{1,0:T(8,128)S(1)}, u32[]{:S(2)}, u32[]{:S(2)}) collective-permute-start(f32[584,128]{1,0:T(8,128)S(1)} %get-tuple-element.18), channel_id=1, source_target_pairs={{0,1},{1,2},{2,3},{3,4},{4,5},{5,6},{6,7},{7,0},{8,9},{9,10},{10,1... | collective-permute-start | bytes 897032 | tf_op jit(solution)/shard_map/ppermute | solution.py:479
  28.5 4.6 %collective-permute-start.3 = (f32[584,128]{1,0:T(8,128)S(1)}, f32[584,128]{1,0:T(8,128)S(1)}, u32[]{:S(2)}, u32[]{:S(2)}) collective-permute-start(f32[584,128]{1,0:T(8,128)S(1)} %get-tuple-element.20), channel_id=1, source_target_pairs={{1,0},{2,1},{3,2},{4,3},{5,4},{6,5},{7,6},{0,7},{9,8},{10,9},{11,1... | collective-permute-start | bytes 897032 | tf_op jit(solution)/shard_map/ppermute | solution.py:479
  33.1 2.2 %collective-permute-done.2.refs_0_ = f32[584,128]{1,0:T(8,128)S(1)} collective-permute-done((f32[584,128]{1,0:T(8,128)S(1)}, f32[584,128]{1,0:T(8,128)S(1)}, u32[]{:S(2)}, u32[]{:S(2)}) %collective-permute-start.2) | collective-permute-done | bytes 299040 | tf_op jit(solution)/shard_map/ppermute | solution.py:479
  35.3 1.5 %collective-permute-done.3.refs_2_ = f32[584,128]{1,0:T(8,128)S(1)} collective-permute-done((f32[584,128]{1,0:T(8,128)S(1)}, f32[584,128]{1,0:T(8,128)S(1)}, u32[]{:S(2)}, u32[]{:S(2)}) %collective-permute-start.3) | collective-permute-done | bytes 299040 | tf_op jit(solution)/shard_map/ppermute | solution.py:479
  36.8 11.5 %collective-permute-start.4 = (f32[528,128]{1,0:T(8,128)S(1)}, f32[528,128]{1,0:T(8,128)S(1)}, u32[]{:S(2)}, u32[]{:S(2)}) collective-permute-start(f32[528,128]{1,0:T(8,128)S(1)} %get-tuple-element.21), channel_id=1, source_target_pairs={{0,8},{8,16},{16,24},{24,32},{32,40},{40,48},{48,56},{56,64},{64,7... | collective-permute-start | bytes 811016 | tf_op jit(solution)/shard_map/ppermute | solution.py:479
  48.3 0.0 copy-start
  48.3 0.0 copy-start.1
  48.3 2.1 %collective-permute-start.5 = (f32[528,128]{1,0:T(8,128)S(1)}, f32[528,128]{1,0:T(8,128)S(1)}, u32[]{:S(2)}, u32[]{:S(2)}) collective-permute-start(f32[528,128]{1,0:T(8,128)S(1)} %get-tuple-element.22), channel_id=1, source_target_pairs={{8,0},{16,8},{24,16},{32,24},{40,32},{48,40},{56,48},{64,56},{72,6... | collective-permute-start | bytes 811016 | tf_op jit(solution)/shard_map/ppermute | solution.py:479
  50.4 3.6 %collective-permute-start.8 = (f32[480,128]{1,0:T(8,128)S(1)}, f32[480,128]{1,0:T(8,128)S(1)}, u32[]{:S(2)}, u32[]{:S(2)}) collective-permute-start(f32[480,128]{1,0:T(8,128)S(1)} %get-tuple-element.27), channel_id=1, source_target_pairs={{0,8},{8,16},{16,24},{24,32},{32,40},{40,48},{48,56},{56,64},{64,7... | collective-permute-start | bytes 737288 | tf_op jit(solution)/shard_map/ppermute | solution.py:479
  54.0 1.9 %collective-permute-start.9 = (f32[480,128]{1,0:T(8,128)S(1)}, f32[480,128]{1,0:T(8,128)S(1)}, u32[]{:S(2)}, u32[]{:S(2)}) collective-permute-start(f32[480,128]{1,0:T(8,128)S(1)} %get-tuple-element.28), channel_id=1, source_target_pairs={{8,0},{16,8},{24,16},{32,24},{40,32},{48,40},{56,48},{64,56},{72,6... | collective-permute-start | bytes 737288 | tf_op jit(solution)/shard_map/ppermute | solution.py:479
  56.0 0.0 copy-done
  56.0 0.0 copy-done.1
  56.0 0.1 matrices.1.refs_8_
  56.1 0.0 collective-permute-done.4.refs_6_
  56.1 0.1 collective-permute-done.5.refs_7_
  56.2 1.2 right_side.1
  57.4 3.6 %collective-permute-start.6 = (f32[432,128]{1,0:T(8,128)S(1)}, f32[432,128]{1,0:T(8,128)S(1)}, u32[]{:S(2)}, u32[]{:S(2)}) collective-permute-start(f32[432,128]{1,0:T(8,128)S(1)} %get-tuple-element.25), channel_id=1, source_target_pairs={{0,8},{8,16},{16,24},{24,32},{32,40},{40,48},{48,56},{56,64},{64,7... | collective-permute-start | bytes 663560 | tf_op jit(solution)/shard_map/ppermute | solution.py:479
  61.0 1.9 %collective-permute-start.7 = (f32[432,128]{1,0:T(8,128)S(1)}, f32[432,128]{1,0:T(8,128)S(1)}, u32[]{:S(2)}, u32[]{:S(2)}) collective-permute-start(f32[432,128]{1,0:T(8,128)S(1)} %get-tuple-element.26), channel_id=1, source_target_pairs={{8,0},{16,8},{24,16},{32,24},{40,32},{48,40},{56,48},{64,56},{72,6... | collective-permute-start | bytes 663560 | tf_op jit(solution)/shard_map/ppermute | solution.py:479
  62.9 0.0 collective-permute-done.8.refs_13_
  62.9 0.0 collective-permute-done.9.refs_14_
  62.9 0.9 collective-permute-done.6.refs_11_
  63.8 4.4 %collective-permute-done.7.refs_12_ = f32[432,128]{1,0:T(8,128)S(1)} collective-permute-done((f32[432,128]{1,0:T(8,128)S(1)}, f32[432,128]{1,0:T(8,128)S(1)}, u32[]{:S(2)}, u32[]{:S(2)}) %collective-permute-start.7) | collective-permute-done | bytes 221216 | tf_op jit(solution)/shard_map/ppermute | solution.py:479
  68.2 3.6 %first_image.1 = (f32[8,16,128]{2,1,0:T(8,128)S(1)}, f32[3,8,32,128]{3,2,1,0:T(8,128)S(1)}, f32[192,128]{1,0:T(8,128)S(1)}, f32[192,128]{1,0:T(8,128)S(1)}, f32[32,128]{1,0:T(8,128)S(1)}) custom-call(f32[584,128]{1,0:T(8,128)S(1)} %collective-permute-done.2.refs_0_, f32[768,128]{1,0:T(8,128)S(1)} %get-tuple-element.19.refs_1_, ...), custom_call_target="tpu_custom_call" | custom-call | tf_op jit(solution)/shard_map/first_image/pallas_call | solution.py:30
  71.8 1.9 %collective-permute-start.10 = (f32[192,128]{1,0:T(8,128)S(1)}, f32[192,128]{1,0:T(8,128)S(1)}, u32[]{:S(2)}, u32[]{:S(2)}) collective-permute-start(f32[192,128]{1,0:T(8,128)S(1)} %get-tuple-element.32), channel_id=1, source_target_pairs={{0,8},{8,16},{16,24},{24,32},{32,40},{40,48},{48,56},{56,64},{64,7... | collective-permute-start | bytes 294920 | tf_op jit(solution)/shard_map/ppermute | solution.py:479
  73.7 2.4 %collective-permute-start.11 = (f32[192,128]{1,0:T(8,128)S(1)}, f32[192,128]{1,0:T(8,128)S(1)}, u32[]{:S(2)}, u32[]{:S(2)}) collective-permute-start(f32[192,128]{1,0:T(8,128)S(1)} %get-tuple-element.33), channel_id=1, source_target_pairs={{8,0},{16,8},{24,16},{32,24},{40,32},{48,40},{56,48},{64,56},{72,6... | collective-permute-start | bytes 294920 | tf_op jit(solution)/shard_map/ppermute | solution.py:479
  76.1 26.7 %all_to_all.27 = f32[32,1,128]{2,1,0:T(1,128)S(1)} all-to-all(f32[32,1,128]{2,1,0:T(1,128)S(1)} %bitcast.15), channel_id=1, replica_groups={{0,1,2,3,4,5,6,7,192,193,194,195,196,197,198,199,384,385,386,387,388,38..., dimensions={0} | all-to-all | bytes 32768 | tf_op jit(solution)/shard_map/all_to_all | solution.py:524
  102.8 0.6 add.6
  103.4 8.9 %all-to-all-start.2 = ((f32[24,1,128]{2,1,0:T(1,128)}), f32[24,1,128]{2,1,0:T(1,128)S(1)}, u32[]{:S(2)}, u32[]{:S(2)}) async-start(f32[24,1,128]{2,1,0:T(1,128)} %bitcast.8), calls=%async_computation.2 | async-start | bytes 24576 | tf_op jit(solution)/shard_map/all_to_all | solution.py:528
  112.4 0.0 collective-permute-done.10.refs_11_
  112.4 0.0 collective-permute-done.11.refs_12_
  112.4 0.8 second_image.1.u_ref
  113.2 8.7 %all-to-all-done.2 = f32[24,1,128]{2,1,0:T(1,128)S(1)} async-done(((f32[24,1,128]{2,1,0:T(1,128)}), f32[24,1,128]{2,1,0:T(1,128)S(1)}, u32[]{:S(2)}, u32[]{:S(2)}) %all-to-all-start.2) | async-done | bytes 12320 | tf_op jit(solution)/shard_map/all_to_all | solution.py:528
  121.9 0.8 finish.1
  (2 shorter events, 0.1 us)
Async XLA Ops:
  4.1 7.8 %copy-start.2 = (f32[8,16,128]{2,1,0:T(8,128)S(1)}, f32[8,16,128]{2,1,0:T(8,128)}, u32[]{:S(2)}) copy-start(f32[8,16,128]{2,1,0:T(8,128)} %param.14) | copy-start | bytes 196612
  4.1 7.8 %copy-start.3 = (f32[8,16]{1,0:T(8,128)S(1)}, f32[8,16]{1,0:T(8,128)}, u32[]{:S(2)}) copy-start(f32[8,16]{1,0:T(8,128)} %diffusion_ref.1) | copy-start | bytes 1540
  4.1 22.0 %all-to-all-start = ((f32[8,136,128]{2,1,0:T(8,128)}), f32[8,136,128]{2,1,0:T(8,128)S(1)}, u32[]{:S(2)}, u32[]{:S(2)}) async-start(f32[8,136,128]{2,1,0:T(8,128)} %bucket.1), calls=%async_computation | async-start | bytes 1114112 | tf_op jit(solution)/shard_map/all_to_all | solution.py:496
  12.0 9.3 %collective-permute-start.1 = (f32[144,128]{1,0:T(8,128)S(1)}, f32[144,128]{1,0:T(8,128)S(1)}, u32[]{:S(2)}, u32[]{:S(2)}) collective-permute-start(f32[144,128]{1,0:T(8,128)S(1)} %fixed.1.refs_4_), channel_id=1, source_target_pairs={{1,0},{2,1},{3,2},{4,3},{5,4},{6,5},{7,6},{0,7},{9,8},{10,9},{11,1... | collective-permute-start | bytes 221192 | tf_op jit(solution)/shard_map/ppermute | solution.py:479
  16.6 9.5 %collective-permute-start = (f32[144,128]{1,0:T(8,128)S(1)}, f32[144,128]{1,0:T(8,128)S(1)}, u32[]{:S(2)}, u32[]{:S(2)}) collective-permute-start(f32[144,128]{1,0:T(8,128)S(1)} %fixed.1.refs_4_), channel_id=1, source_target_pairs={{0,1},{1,2},{2,3},{3,4},{4,5},{5,6},{6,7},{7,0},{8,9},{9,10},{10,1... | collective-permute-start | bytes 221192 | tf_op jit(solution)/shard_map/ppermute | solution.py:479
  26.5 8.7 %collective-permute-start.2 = (f32[584,128]{1,0:T(8,128)S(1)}, f32[584,128]{1,0:T(8,128)S(1)}, u32[]{:S(2)}, u32[]{:S(2)}) collective-permute-start(f32[584,128]{1,0:T(8,128)S(1)} %get-tuple-element.18), channel_id=1, source_target_pairs={{0,1},{1,2},{2,3},{3,4},{4,5},{5,6},{6,7},{7,0},{8,9},{9,10},{10,1... | collective-permute-start | bytes 897032 | tf_op jit(solution)/shard_map/ppermute | solution.py:479
  28.5 8.3 %collective-permute-start.3 = (f32[584,128]{1,0:T(8,128)S(1)}, f32[584,128]{1,0:T(8,128)S(1)}, u32[]{:S(2)}, u32[]{:S(2)}) collective-permute-start(f32[584,128]{1,0:T(8,128)S(1)} %get-tuple-element.20), channel_id=1, source_target_pairs={{1,0},{2,1},{3,2},{4,3},{5,4},{6,5},{7,6},{0,7},{9,8},{10,9},{11,1... | collective-permute-start | bytes 897032 | tf_op jit(solution)/shard_map/ppermute | solution.py:479
  36.8 19.3 %collective-permute-start.4 = (f32[528,128]{1,0:T(8,128)S(1)}, f32[528,128]{1,0:T(8,128)S(1)}, u32[]{:S(2)}, u32[]{:S(2)}) collective-permute-start(f32[528,128]{1,0:T(8,128)S(1)} %get-tuple-element.21), channel_id=1, source_target_pairs={{0,8},{8,16},{16,24},{24,32},{32,40},{40,48},{48,56},{56,64},{64,7... | collective-permute-start | bytes 811016 | tf_op jit(solution)/shard_map/ppermute | solution.py:479
  48.3 7.7 %copy-start = (f32[128,128]{1,0:T(8,128)S(1)}, f32[128,128]{1,0:T(8,128)}, u32[]{:S(2)}) copy-start(f32[128,128]{1,0:T(8,128)} %factor_ref.1) | copy-start | bytes 196612
  48.3 7.7 %copy-start.1 = (f32[128,128]{1,0:T(8,128)S(1)}, f32[128,128]{1,0:T(8,128)}, u32[]{:S(2)}) copy-start(f32[128,128]{1,0:T(8,128)} %mixing_ref.1) | copy-start | bytes 196612
  48.3 7.9 %collective-permute-start.5 = (f32[528,128]{1,0:T(8,128)S(1)}, f32[528,128]{1,0:T(8,128)S(1)}, u32[]{:S(2)}, u32[]{:S(2)}) collective-permute-start(f32[528,128]{1,0:T(8,128)S(1)} %get-tuple-element.22), channel_id=1, source_target_pairs={{8,0},{16,8},{24,16},{32,24},{40,32},{48,40},{56,48},{64,56},{72,6... | collective-permute-start | bytes 811016 | tf_op jit(solution)/shard_map/ppermute | solution.py:479
  50.4 12.5 %collective-permute-start.8 = (f32[480,128]{1,0:T(8,128)S(1)}, f32[480,128]{1,0:T(8,128)S(1)}, u32[]{:S(2)}, u32[]{:S(2)}) collective-permute-start(f32[480,128]{1,0:T(8,128)S(1)} %get-tuple-element.27), channel_id=1, source_target_pairs={{0,8},{8,16},{16,24},{24,32},{32,40},{40,48},{48,56},{56,64},{64,7... | collective-permute-start | bytes 737288 | tf_op jit(solution)/shard_map/ppermute | solution.py:479
  54.0 8.9 %collective-permute-start.9 = (f32[480,128]{1,0:T(8,128)S(1)}, f32[480,128]{1,0:T(8,128)S(1)}, u32[]{:S(2)}, u32[]{:S(2)}) collective-permute-start(f32[480,128]{1,0:T(8,128)S(1)} %get-tuple-element.28), channel_id=1, source_target_pairs={{8,0},{16,8},{24,16},{32,24},{40,32},{48,40},{56,48},{64,56},{72,6... | collective-permute-start | bytes 737288 | tf_op jit(solution)/shard_map/ppermute | solution.py:479
  57.4 6.4 %collective-permute-start.6 = (f32[432,128]{1,0:T(8,128)S(1)}, f32[432,128]{1,0:T(8,128)S(1)}, u32[]{:S(2)}, u32[]{:S(2)}) collective-permute-start(f32[432,128]{1,0:T(8,128)S(1)} %get-tuple-element.25), channel_id=1, source_target_pairs={{0,8},{8,16},{16,24},{24,32},{32,40},{40,48},{48,56},{56,64},{64,7... | collective-permute-start | bytes 663560 | tf_op jit(solution)/shard_map/ppermute | solution.py:479
  61.0 7.3 %collective-permute-start.7 = (f32[432,128]{1,0:T(8,128)S(1)}, f32[432,128]{1,0:T(8,128)S(1)}, u32[]{:S(2)}, u32[]{:S(2)}) collective-permute-start(f32[432,128]{1,0:T(8,128)S(1)} %get-tuple-element.26), channel_id=1, source_target_pairs={{8,0},{16,8},{24,16},{32,24},{40,32},{48,40},{56,48},{64,56},{72,6... | collective-permute-start | bytes 663560 | tf_op jit(solution)/shard_map/ppermute | solution.py:479
  71.8 40.6 %collective-permute-start.10 = (f32[192,128]{1,0:T(8,128)S(1)}, f32[192,128]{1,0:T(8,128)S(1)}, u32[]{:S(2)}, u32[]{:S(2)}) collective-permute-start(f32[192,128]{1,0:T(8,128)S(1)} %get-tuple-element.32), channel_id=1, source_target_pairs={{0,8},{8,16},{16,24},{24,32},{32,40},{40,48},{48,56},{56,64},{64,7... | collective-permute-start | bytes 294920 | tf_op jit(solution)/shard_map/ppermute | solution.py:479
  73.7 38.7 %collective-permute-start.11 = (f32[192,128]{1,0:T(8,128)S(1)}, f32[192,128]{1,0:T(8,128)S(1)}, u32[]{:S(2)}, u32[]{:S(2)}) collective-permute-start(f32[192,128]{1,0:T(8,128)S(1)} %get-tuple-element.33), channel_id=1, source_target_pairs={{8,0},{16,8},{24,16},{32,24},{40,32},{48,40},{56,48},{64,56},{72,6... | collective-permute-start | bytes 294920 | tf_op jit(solution)/shard_map/ppermute | solution.py:479
  103.4 18.4 %all-to-all-start.2 = ((f32[24,1,128]{2,1,0:T(1,128)}), f32[24,1,128]{2,1,0:T(1,128)S(1)}, u32[]{:S(2)}, u32[]{:S(2)}) async-start(f32[24,1,128]{2,1,0:T(1,128)} %bitcast.8), calls=%async_computation.2 | async-start | bytes 24576 | tf_op jit(solution)/shard_map/all_to_all | solution.py:528

commit v4 on v3

--- a/solution.py
+++ b/solution.py
@@ -453,7 +453,7 @@
 
 
 def add_kernel(parts_ref, out_ref):
-    out_ref[...] = jnp.broadcast_to(jnp.sum(parts_ref[...], axis=0, keepdims=True), out_ref.shape)
+    out_ref[...] = jnp.broadcast_to(0.25 * jnp.sum(parts_ref[...], axis=0, keepdims=True), out_ref.shape)
 
 
 def finish_kernel(parts_ref, b_ref, q_ref, u_ref, solution_ref, residual_ref):
@@ -518,14 +518,14 @@
     q, g, low, high, sums = call(
         first_image_kernel,
         "first_image",
-        (small, shape(STEPS, ROWS, INNER, L), side, side, shape(4 * lon, L)),
+        (small, shape(STEPS, ROWS, INNER, L), side, side, shape(lat, L)),
         space + [space[0]] * 2,
     )(*refs, b, y, south, north, *weights)
-    sums = lax.all_to_all(sums, ("lat", "lon"), 0, 0, axis_index_groups=far, tiled=True)
+    sums = lax.all_to_all(sums, "lat", 0, 0, axis_index_groups=near, tiled=True)
     south, north = exchange(low, high, "lat", False)
     u = call(second_image_kernel, "second_image", small, scratch(INNER, STEPS))(*refs, q, g, south, north)
-    sums = call(add_kernel, "add", shape(lat // 4, L))(sums)
-    sums = lax.all_to_all(sums, "lat", 0, 0, axis_index_groups=near, tiled=True)
+    sums = call(add_kernel, "add", shape(4 * lon, L))(sums)
+    sums = lax.all_to_all(sums, ("lat", "lon"), 0, 0, axis_index_groups=far, tiled=True)
     return call(finish_kernel, "finish", (small, small))(sums, b, q, u)
 
 

time: 123 us -> 119 us (0.967)
  blocking collectives: 26.7 us -> 0 us
  starting transfers between devices: 58.6 us -> 76.4 us
  waiting for transfers between devices: 25.4 us -> 29.1 us
    all_to_all x1 -> x0, blocking collectives: 26.7 us -> none  [shards(): lax.all_to_all(sums, ('lat', 'lon'), 0, 0, axis_index_groups=far, tiled=T...]
    all_to_all x1, starting transfers between devices: 8.94 us -> 18 us  [shards(): sums = lax.all_to_all(sums, 'lat', 0, 0, axis_index_groups=near, tiled=True)]
    all_to_all x0 -> x1, waiting for transfers between devices: none -> 7.77 us  [shards(): lax.all_to_all(sums, ('lat', 'lon'), 0, 0, axis_index_groups=far, tiled=T...]
    all_to_all x0 -> x1, starting transfers between devices: none -> 7.53 us  [shards(): lax.all_to_all(sums, ('lat', 'lon'), 0, 0, axis_index_groups=far, tiled=T...]
    all_to_all x1, waiting for transfers between devices: 8.67 us -> 4.61 us  [shards(): sums = lax.all_to_all(sums, 'lat', 0, 0, axis_index_groups=near, tiled=True)]
    ppermute x6, starting transfers between devices: 24.4 us -> 26.1 us  [exchange(): lax.ppermute(to_after, axis, up)]
  transfers between devices with their start and end apart: 14 -> 15, of which waited for: 8 -> 9; matrix products, arithmetic and copies ran while one was open for 0% -> 0% of each run, Pallas kernels for 2% -> 2%
where the time goes in v4:
time: 119 us; the launch traced here: 118 us
  starting transfers between devices  76.4 us (64%)
  waiting for transfers between devices  29.1 us (24%)
  Pallas kernels  11.1 us (9%)
  between operations  1.55 us (1%)
    ppermute x6, starting transfers between devices, exchange(): lax.ppermute(to_after, axis, up)  26.1 us
    all_to_all x1, starting transfers between devices, shards(): sums = lax.all_to_all(sums, 'lat', 0, 0, axis_index_groups=near, tiled=True)  18 us
    ppermute x6, starting transfers between devices, exchange(): lax.ppermute(to_before, axis, down)  17 us
    pallas_call x11, Pallas kernels, run(): pl.pallas_call(kernel, name=name, out_shape=outs, in_specs=specs, out_spe...  11.1 us
    ppermute x6, waiting for transfers between devices, exchange(): lax.ppermute(to_before, axis, down)  8.71 us
    ppermute x6, waiting for transfers between devices, exchange(): lax.ppermute(to_after, axis, up)  7.99 us
    all_to_all x1, starting transfers between devices, shards(): received = lax.all_to_all(buckets, 'lon', 0, 0)  7.79 us
    all_to_all x1, waiting for transfers between devices, shards(): lax.all_to_all(sums, ('lat', 'lon'), 0, 0, axis_index_groups=far, tiled=T...  7.77 us
  transfers between devices with their start and end apart: 15, of which 9 were waited for; matrix products, arithmetic and copies ran while one was open for 0% of the time, Pallas kernels for 2%

profile of v4, /device:TPU:1, one launch (start us, length us, event | category | flops | bytes accessed | tf_op | source)
XLA Modules:
  0.0 118.1 jit_solution(11732186446167441729)
XLA Ops:
  1.3 2.8 %bucket.1 = f32[8,136,128]{2,1,0:T(8,128)} custom-call(f32[256,128]{1,0:T(8,128)} %departures_hbm.1, f32[256,128]{1,0:T(8,128)} %weight_hbm.1, s32[1,256]{1,0:T(1,128)} %bitcast.13, s32[1,256]{1,0:T(1,128)} %bitcast.14, s32[1]{0:T(128)S(6)} %copy.12.counts_ref, s32[1]{0:T(128)} %bitcast.2.parity_ref), custom_call_target="tpu_custom_call" | custom-call | tf_op jit(solution)/shard_map/bucket/pallas_call | solution.py:30
  4.1 0.0 copy-start.2
  4.1 0.0 copy-start.3
  4.1 7.8 %all-to-all-start = ((f32[8,136,128]{2,1,0:T(8,128)}), f32[8,136,128]{2,1,0:T(8,128)S(1)}, u32[]{:S(2)}, u32[]{:S(2)}) async-start(f32[8,136,128]{2,1,0:T(8,128)} %bucket.1), calls=%async_computation | async-start | bytes 1114112 | tf_op jit(solution)/shard_map/all_to_all | solution.py:496
  11.9 0.0 copy-done.2
  11.9 0.0 copy-done.3
  11.9 0.1 fixed.1.refs_4_
  12.0 4.6 %collective-permute-start.1 = (f32[144,128]{1,0:T(8,128)S(1)}, f32[144,128]{1,0:T(8,128)S(1)}, u32[]{:S(2)}, u32[]{:S(2)}) collective-permute-start(f32[144,128]{1,0:T(8,128)S(1)} %fixed.1.refs_4_), channel_id=1, source_target_pairs={{1,0},{2,1},{3,2},{4,3},{5,4},{6,5},{7,6},{0,7},{9,8},{10,9},{11,1... | collective-permute-start | bytes 221192 | tf_op jit(solution)/shard_map/ppermute | solution.py:479
  16.6 1.9 %collective-permute-start = (f32[144,128]{1,0:T(8,128)S(1)}, f32[144,128]{1,0:T(8,128)S(1)}, u32[]{:S(2)}, u32[]{:S(2)}) collective-permute-start(f32[144,128]{1,0:T(8,128)S(1)} %fixed.1.refs_4_), channel_id=1, source_target_pairs={{0,1},{1,2},{2,3},{3,4},{4,5},{5,6},{6,7},{7,0},{8,9},{9,10},{10,1... | collective-permute-start | bytes 221192 | tf_op jit(solution)/shard_map/ppermute | solution.py:479
  18.6 2.8 %collective-permute-done.1.fixed_right_ref.refs_5_ = f32[144,128]{1,0:T(8,128)S(1)} collective-permute-done((f32[144,128]{1,0:T(8,128)S(1)}, f32[144,128]{1,0:T(8,128)S(1)}, u32[]{:S(2)}, u32[]{:S(2)}) %collective-permute-start.1) | collective-permute-done | bytes 73760 | tf_op jit(solution)/shard_map/ppermute | solution.py:479
  21.3 4.9 %collective-permute-done.fixed_left_ref.refs_3_ = f32[144,128]{1,0:T(8,128)S(1)} collective-permute-done((f32[144,128]{1,0:T(8,128)S(1)}, f32[144,128]{1,0:T(8,128)S(1)}, u32[]{:S(2)}, u32[]{:S(2)}) %collective-permute-start) | collective-permute-done | bytes 73760 | tf_op jit(solution)/shard_map/ppermute | solution.py:479
  26.2 0.0 all-to-all-done.received_ref
  26.2 0.4 tile.1
  26.6 1.9 %collective-permute-start.2 = (f32[584,128]{1,0:T(8,128)S(1)}, f32[584,128]{1,0:T(8,128)S(1)}, u32[]{:S(2)}, u32[]{:S(2)}) collective-permute-start(f32[584,128]{1,0:T(8,128)S(1)} %get-tuple-element.18), channel_id=1, source_target_pairs={{0,1},{1,2},{2,3},{3,4},{4,5},{5,6},{6,7},{7,0},{8,9},{9,10},{10,1... | collective-permute-start | bytes 897032 | tf_op jit(solution)/shard_map/ppermute | solution.py:479
  28.5 4.6 %collective-permute-start.3 = (f32[584,128]{1,0:T(8,128)S(1)}, f32[584,128]{1,0:T(8,128)S(1)}, u32[]{:S(2)}, u32[]{:S(2)}) collective-permute-start(f32[584,128]{1,0:T(8,128)S(1)} %get-tuple-element.20), channel_id=1, source_target_pairs={{1,0},{2,1},{3,2},{4,3},{5,4},{6,5},{7,6},{0,7},{9,8},{10,9},{11,1... | collective-permute-start | bytes 897032 | tf_op jit(solution)/shard_map/ppermute | solution.py:479
  33.1 2.2 %collective-permute-done.2.refs_0_ = f32[584,128]{1,0:T(8,128)S(1)} collective-permute-done((f32[584,128]{1,0:T(8,128)S(1)}, f32[584,128]{1,0:T(8,128)S(1)}, u32[]{:S(2)}, u32[]{:S(2)}) %collective-permute-start.2) | collective-permute-done | bytes 299040 | tf_op jit(solution)/shard_map/ppermute | solution.py:479
  35.3 1.5 %collective-permute-done.3.refs_2_ = f32[584,128]{1,0:T(8,128)S(1)} collective-permute-done((f32[584,128]{1,0:T(8,128)S(1)}, f32[584,128]{1,0:T(8,128)S(1)}, u32[]{:S(2)}, u32[]{:S(2)}) %collective-permute-start.3) | collective-permute-done | bytes 299040 | tf_op jit(solution)/shard_map/ppermute | solution.py:479
  36.8 11.5 %collective-permute-start.4 = (f32[528,128]{1,0:T(8,128)S(1)}, f32[528,128]{1,0:T(8,128)S(1)}, u32[]{:S(2)}, u32[]{:S(2)}) collective-permute-start(f32[528,128]{1,0:T(8,128)S(1)} %get-tuple-element.21), channel_id=1, source_target_pairs={{0,8},{8,16},{16,24},{24,32},{32,40},{40,48},{48,56},{56,64},{64,7... | collective-permute-start | bytes 811016 | tf_op jit(solution)/shard_map/ppermute | solution.py:479
  48.3 0.0 copy-start
  48.3 0.0 copy-start.1
  48.3 2.1 %collective-permute-start.5 = (f32[528,128]{1,0:T(8,128)S(1)}, f32[528,128]{1,0:T(8,128)S(1)}, u32[]{:S(2)}, u32[]{:S(2)}) collective-permute-start(f32[528,128]{1,0:T(8,128)S(1)} %get-tuple-element.22), channel_id=1, source_target_pairs={{8,0},{16,8},{24,16},{32,24},{40,32},{48,40},{56,48},{64,56},{72,6... | collective-permute-start | bytes 811016 | tf_op jit(solution)/shard_map/ppermute | solution.py:479
  50.4 3.6 %collective-permute-start.8 = (f32[480,128]{1,0:T(8,128)S(1)}, f32[480,128]{1,0:T(8,128)S(1)}, u32[]{:S(2)}, u32[]{:S(2)}) collective-permute-start(f32[480,128]{1,0:T(8,128)S(1)} %get-tuple-element.27), channel_id=1, source_target_pairs={{0,8},{8,16},{16,24},{24,32},{32,40},{40,48},{48,56},{56,64},{64,7... | collective-permute-start | bytes 737288 | tf_op jit(solution)/shard_map/ppermute | solution.py:479
  54.0 1.9 %collective-permute-start.9 = (f32[480,128]{1,0:T(8,128)S(1)}, f32[480,128]{1,0:T(8,128)S(1)}, u32[]{:S(2)}, u32[]{:S(2)}) collective-permute-start(f32[480,128]{1,0:T(8,128)S(1)} %get-tuple-element.28), channel_id=1, source_target_pairs={{8,0},{16,8},{24,16},{32,24},{40,32},{48,40},{56,48},{64,56},{72,6... | collective-permute-start | bytes 737288 | tf_op jit(solution)/shard_map/ppermute | solution.py:479
  56.0 0.0 copy-done
  56.0 0.0 copy-done.1
  56.0 0.1 matrices.1.refs_8_
  56.1 0.0 collective-permute-done.4.refs_6_
  56.1 0.1 collective-permute-done.5.refs_7_
  56.2 1.2 %right_side.1 = (f32[8,48,128]{2,1,0:T(8,128)S(1)}, f32[8,48,128]{2,1,0:T(8,128)S(1)}, f32[432,128]{1,0:T(8,128)S(1)}, f32[432,128]{1,0:T(8,128)S(1)}) custom-call(f32[584,128]{1,0:T(8,128)S(1)} %collective-permute-done.2.refs_0_, f32[768,128]{1,0:T(8,128)S(1)} %get-tuple-element.19.refs_1_, f32[584,128]{1,0:T(8,128)S(1)} %collective-permute-done.3.refs_2_, ...), custom_call_target="tpu_custom_call" | custom-call | tf_op jit(solution)/shard_map/right_side/pallas_call | solution.py:30
  57.4 3.6 %collective-permute-start.6 = (f32[432,128]{1,0:T(8,128)S(1)}, f32[432,128]{1,0:T(8,128)S(1)}, u32[]{:S(2)}, u32[]{:S(2)}) collective-permute-start(f32[432,128]{1,0:T(8,128)S(1)} %get-tuple-element.25), channel_id=1, source_target_pairs={{0,8},{8,16},{16,24},{24,32},{32,40},{40,48},{48,56},{56,64},{64,7... | collective-permute-start | bytes 663560 | tf_op jit(solution)/shard_map/ppermute | solution.py:479
  61.0 1.9 %collective-permute-start.7 = (f32[432,128]{1,0:T(8,128)S(1)}, f32[432,128]{1,0:T(8,128)S(1)}, u32[]{:S(2)}, u32[]{:S(2)}) collective-permute-start(f32[432,128]{1,0:T(8,128)S(1)} %get-tuple-element.26), channel_id=1, source_target_pairs={{8,0},{16,8},{24,16},{32,24},{40,32},{48,40},{56,48},{64,56},{72,6... | collective-permute-start | bytes 663560 | tf_op jit(solution)/shard_map/ppermute | solution.py:479
  62.9 0.0 collective-permute-done.8.refs_13_
  62.9 0.0 collective-permute-done.9.refs_14_
  63.0 0.9 collective-permute-done.6.refs_11_
  63.9 4.4 %collective-permute-done.7.refs_12_ = f32[432,128]{1,0:T(8,128)S(1)} collective-permute-done((f32[432,128]{1,0:T(8,128)S(1)}, f32[432,128]{1,0:T(8,128)S(1)}, u32[]{:S(2)}, u32[]{:S(2)}) %collective-permute-start.7) | collective-permute-done | bytes 221216 | tf_op jit(solution)/shard_map/ppermute | solution.py:479
  68.3 4.2 %first_image.1 = (f32[8,16,128]{2,1,0:T(8,128)S(1)}, f32[3,8,32,128]{3,2,1,0:T(8,128)S(1)}, f32[192,128]{1,0:T(8,128)S(1)}, f32[192,128]{1,0:T(8,128)S(1)}, f32[96,128]{1,0:T(8,128)}) custom-call(f32[584,128]{1,0:T(8,128)S(1)} %collective-permute-done.2.refs_0_, f32[768,128]{1,0:T(8,128)S(1)} %get-tuple-element.19.refs_1_, ...), custom_call_target="tpu_custom_call" | custom-call | tf_op jit(solution)/shard_map/first_image/pallas_call | solution.py:30
  72.4 18.0 %all-to-all-start.1 = ((f32[24,4,128]{2,1,0:T(4,128)}), f32[24,4,128]{2,1,0:T(4,128)S(1)}, u32[]{:S(2)}, u32[]{:S(2)}) async-start(f32[24,4,128]{2,1,0:T(4,128)} %bitcast.4), calls=%async_computation.1 | async-start | bytes 98304 | tf_op jit(solution)/shard_map/all_to_all | solution.py:524
  90.5 3.5 %collective-permute-start.10 = (f32[192,128]{1,0:T(8,128)S(1)}, f32[192,128]{1,0:T(8,128)S(1)}, u32[]{:S(2)}, u32[]{:S(2)}) collective-permute-start(f32[192,128]{1,0:T(8,128)S(1)} %get-tuple-element.32), channel_id=1, source_target_pairs={{0,8},{8,16},{16,24},{24,32},{32,40},{40,48},{48,56},{56,64},{64,7... | collective-permute-start | bytes 294920 | tf_op jit(solution)/shard_map/ppermute | solution.py:479
  94.0 1.9 %collective-permute-start.11 = (f32[192,128]{1,0:T(8,128)S(1)}, f32[192,128]{1,0:T(8,128)S(1)}, u32[]{:S(2)}, u32[]{:S(2)}) collective-permute-start(f32[192,128]{1,0:T(8,128)S(1)} %get-tuple-element.33), channel_id=1, source_target_pairs={{8,0},{16,8},{24,16},{32,24},{40,32},{48,40},{56,48},{64,56},{72,6... | collective-permute-start | bytes 294920 | tf_op jit(solution)/shard_map/ppermute | solution.py:479
  95.9 4.6 %all-to-all-done.1 = f32[24,4,128]{2,1,0:T(4,128)S(1)} async-done(((f32[24,4,128]{2,1,0:T(4,128)}), f32[24,4,128]{2,1,0:T(4,128)S(1)}, u32[]{:S(2)}, u32[]{:S(2)}) %all-to-all-start.1) | async-done | bytes 49184 | tf_op jit(solution)/shard_map/all_to_all | solution.py:524
  100.6 0.6 add.6
  101.2 7.5 %all-to-all-start.2 = ((f32[32,1,128]{2,1,0:T(1,128)}), f32[32,1,128]{2,1,0:T(1,128)S(1)}, u32[]{:S(2)}, u32[]{:S(2)}) async-start(f32[32,1,128]{2,1,0:T(1,128)} %bitcast.7), calls=%async_computation.2 | async-start | bytes 32768 | tf_op jit(solution)/shard_map/all_to_all | solution.py:528
  108.7 0.0 collective-permute-done.10.refs_11_
  108.7 0.0 collective-permute-done.11.refs_12_
  108.8 0.8 second_image.1.u_ref
  109.5 7.8 %all-to-all-done.2 = f32[32,1,128]{2,1,0:T(1,128)S(1)} async-done(((f32[32,1,128]{2,1,0:T(1,128)}), f32[32,1,128]{2,1,0:T(1,128)S(1)}, u32[]{:S(2)}, u32[]{:S(2)}) %all-to-all-start.2) | async-done | bytes 16416 | tf_op jit(solution)/shard_map/all_to_all | solution.py:528
  117.3 0.8 finish.1
  (2 shorter events, 0.1 us)
Async XLA Ops:
  4.1 7.8 %copy-start.2 = (f32[8,16,128]{2,1,0:T(8,128)S(1)}, f32[8,16,128]{2,1,0:T(8,128)}, u32[]{:S(2)}) copy-start(f32[8,16,128]{2,1,0:T(8,128)} %param.14) | copy-start | bytes 196612
  4.1 7.8 %copy-start.3 = (f32[8,16]{1,0:T(8,128)S(1)}, f32[8,16]{1,0:T(8,128)}, u32[]{:S(2)}) copy-start(f32[8,16]{1,0:T(8,128)} %diffusion_ref.1) | copy-start | bytes 1540
  4.1 22.0 %all-to-all-start = ((f32[8,136,128]{2,1,0:T(8,128)}), f32[8,136,128]{2,1,0:T(8,128)S(1)}, u32[]{:S(2)}, u32[]{:S(2)}) async-start(f32[8,136,128]{2,1,0:T(8,128)} %bucket.1), calls=%async_computation | async-start | bytes 1114112 | tf_op jit(solution)/shard_map/all_to_all | solution.py:496
  12.0 9.3 %collective-permute-start.1 = (f32[144,128]{1,0:T(8,128)S(1)}, f32[144,128]{1,0:T(8,128)S(1)}, u32[]{:S(2)}, u32[]{:S(2)}) collective-permute-start(f32[144,128]{1,0:T(8,128)S(1)} %fixed.1.refs_4_), channel_id=1, source_target_pairs={{1,0},{2,1},{3,2},{4,3},{5,4},{6,5},{7,6},{0,7},{9,8},{10,9},{11,1... | collective-permute-start | bytes 221192 | tf_op jit(solution)/shard_map/ppermute | solution.py:479
  16.6 9.5 %collective-permute-start = (f32[144,128]{1,0:T(8,128)S(1)}, f32[144,128]{1,0:T(8,128)S(1)}, u32[]{:S(2)}, u32[]{:S(2)}) collective-permute-start(f32[144,128]{1,0:T(8,128)S(1)} %fixed.1.refs_4_), channel_id=1, source_target_pairs={{0,1},{1,2},{2,3},{3,4},{4,5},{5,6},{6,7},{7,0},{8,9},{9,10},{10,1... | collective-permute-start | bytes 221192 | tf_op jit(solution)/shard_map/ppermute | solution.py:479
  26.6 8.7 %collective-permute-start.2 = (f32[584,128]{1,0:T(8,128)S(1)}, f32[584,128]{1,0:T(8,128)S(1)}, u32[]{:S(2)}, u32[]{:S(2)}) collective-permute-start(f32[584,128]{1,0:T(8,128)S(1)} %get-tuple-element.18), channel_id=1, source_target_pairs={{0,1},{1,2},{2,3},{3,4},{4,5},{5,6},{6,7},{7,0},{8,9},{9,10},{10,1... | collective-permute-start | bytes 897032 | tf_op jit(solution)/shard_map/ppermute | solution.py:479
  28.5 8.3 %collective-permute-start.3 = (f32[584,128]{1,0:T(8,128)S(1)}, f32[584,128]{1,0:T(8,128)S(1)}, u32[]{:S(2)}, u32[]{:S(2)}) collective-permute-start(f32[584,128]{1,0:T(8,128)S(1)} %get-tuple-element.20), channel_id=1, source_target_pairs={{1,0},{2,1},{3,2},{4,3},{5,4},{6,5},{7,6},{0,7},{9,8},{10,9},{11,1... | collective-permute-start | bytes 897032 | tf_op jit(solution)/shard_map/ppermute | solution.py:479
  36.8 19.3 %collective-permute-start.4 = (f32[528,128]{1,0:T(8,128)S(1)}, f32[528,128]{1,0:T(8,128)S(1)}, u32[]{:S(2)}, u32[]{:S(2)}) collective-permute-start(f32[528,128]{1,0:T(8,128)S(1)} %get-tuple-element.21), channel_id=1, source_target_pairs={{0,8},{8,16},{16,24},{24,32},{32,40},{40,48},{48,56},{56,64},{64,7... | collective-permute-start | bytes 811016 | tf_op jit(solution)/shard_map/ppermute | solution.py:479
  48.3 7.7 %copy-start = (f32[128,128]{1,0:T(8,128)S(1)}, f32[128,128]{1,0:T(8,128)}, u32[]{:S(2)}) copy-start(f32[128,128]{1,0:T(8,128)} %factor_ref.1) | copy-start | bytes 196612
  48.3 7.7 %copy-start.1 = (f32[128,128]{1,0:T(8,128)S(1)}, f32[128,128]{1,0:T(8,128)}, u32[]{:S(2)}) copy-start(f32[128,128]{1,0:T(8,128)} %mixing_ref.1) | copy-start | bytes 196612
  48.3 7.9 %collective-permute-start.5 = (f32[528,128]{1,0:T(8,128)S(1)}, f32[528,128]{1,0:T(8,128)S(1)}, u32[]{:S(2)}, u32[]{:S(2)}) collective-permute-start(f32[528,128]{1,0:T(8,128)S(1)} %get-tuple-element.22), channel_id=1, source_target_pairs={{8,0},{16,8},{24,16},{32,24},{40,32},{48,40},{56,48},{64,56},{72,6... | collective-permute-start | bytes 811016 | tf_op jit(solution)/shard_map/ppermute | solution.py:479
  50.4 12.5 %collective-permute-start.8 = (f32[480,128]{1,0:T(8,128)S(1)}, f32[480,128]{1,0:T(8,128)S(1)}, u32[]{:S(2)}, u32[]{:S(2)}) collective-permute-start(f32[480,128]{1,0:T(8,128)S(1)} %get-tuple-element.27), channel_id=1, source_target_pairs={{0,8},{8,16},{16,24},{24,32},{32,40},{40,48},{48,56},{56,64},{64,7... | collective-permute-start | bytes 737288 | tf_op jit(solution)/shard_map/ppermute | solution.py:479
  54.0 8.9 %collective-permute-start.9 = (f32[480,128]{1,0:T(8,128)S(1)}, f32[480,128]{1,0:T(8,128)S(1)}, u32[]{:S(2)}, u32[]{:S(2)}) collective-permute-start(f32[480,128]{1,0:T(8,128)S(1)} %get-tuple-element.28), channel_id=1, source_target_pairs={{8,0},{16,8},{24,16},{32,24},{40,32},{48,40},{56,48},{64,56},{72,6... | collective-permute-start | bytes 737288 | tf_op jit(solution)/shard_map/ppermute | solution.py:479
  57.4 6.4 %collective-permute-start.6 = (f32[432,128]{1,0:T(8,128)S(1)}, f32[432,128]{1,0:T(8,128)S(1)}, u32[]{:S(2)}, u32[]{:S(2)}) collective-permute-start(f32[432,128]{1,0:T(8,128)S(1)} %get-tuple-element.25), channel_id=1, source_target_pairs={{0,8},{8,16},{16,24},{24,32},{32,40},{40,48},{48,56},{56,64},{64,7... | collective-permute-start | bytes 663560 | tf_op jit(solution)/shard_map/ppermute | solution.py:479
  61.0 7.3 %collective-permute-start.7 = (f32[432,128]{1,0:T(8,128)S(1)}, f32[432,128]{1,0:T(8,128)S(1)}, u32[]{:S(2)}, u32[]{:S(2)}) collective-permute-start(f32[432,128]{1,0:T(8,128)S(1)} %get-tuple-element.26), channel_id=1, source_target_pairs={{8,0},{16,8},{24,16},{32,24},{40,32},{48,40},{56,48},{64,56},{72,6... | collective-permute-start | bytes 663560 | tf_op jit(solution)/shard_map/ppermute | solution.py:479
  72.4 28.1 %all-to-all-start.1 = ((f32[24,4,128]{2,1,0:T(4,128)}), f32[24,4,128]{2,1,0:T(4,128)S(1)}, u32[]{:S(2)}, u32[]{:S(2)}) async-start(f32[24,4,128]{2,1,0:T(4,128)} %bitcast.4), calls=%async_computation.1 | async-start | bytes 98304 | tf_op jit(solution)/shard_map/all_to_all | solution.py:524
  90.5 18.3 %collective-permute-start.10 = (f32[192,128]{1,0:T(8,128)S(1)}, f32[192,128]{1,0:T(8,128)S(1)}, u32[]{:S(2)}, u32[]{:S(2)}) collective-permute-start(f32[192,128]{1,0:T(8,128)S(1)} %get-tuple-element.32), channel_id=1, source_target_pairs={{0,8},{8,16},{16,24},{24,32},{32,40},{40,48},{48,56},{56,64},{64,7... | collective-permute-start | bytes 294920 | tf_op jit(solution)/shard_map/ppermute | solution.py:479
  94.0 14.7 %collective-permute-start.11 = (f32[192,128]{1,0:T(8,128)S(1)}, f32[192,128]{1,0:T(8,128)S(1)}, u32[]{:S(2)}, u32[]{:S(2)}) collective-permute-start(f32[192,128]{1,0:T(8,128)S(1)} %get-tuple-element.33), channel_id=1, source_target_pairs={{8,0},{16,8},{24,16},{32,24},{40,32},{48,40},{56,48},{64,56},{72,6... | collective-permute-start | bytes 294920 | tf_op jit(solution)/shard_map/ppermute | solution.py:479
  101.2 16.1 %all-to-all-start.2 = ((f32[32,1,128]{2,1,0:T(1,128)}), f32[32,1,128]{2,1,0:T(1,128)S(1)}, u32[]{:S(2)}, u32[]{:S(2)}) async-start(f32[32,1,128]{2,1,0:T(1,128)} %bitcast.7), calls=%async_computation.2 | async-start | bytes 32768 | tf_op jit(solution)/shard_map/all_to_all | solution.py:528

commit v5 on v4

--- a/solution.py
+++ b/solution.py
@@ -216,36 +216,40 @@
 THIRD, THIRD_ROWS = places([(("g", t), h, INNER) for t in range(STEPS) for h in range(1, t + 2)])
 
 
-def send(low_ref, high_ref, found, kind, h, row):
-    start, width = found[kind, h]
-    for ref, r in ((low_ref, h - 1), (high_ref, ROWS - h)):
-        value = row(r)
-        ref[start : start + width] = inside(value) if width < value.shape[0] else value
-
-
-def taken(sides, found, kind, r):
-    below_ref, above_ref = sides
-    ref, h = (below_ref, -r) if r < 0 else (above_ref, r - ROWS + 1)
-    start, width = found[kind, h]
-    return ref[start : start + width]
+class Sides:
+    def __init__(self, parity_ref, core_ref, chip_ref, found):
+        self.even = parity_ref[0] == 0
+        self.core_ref, self.chip_ref, self.found = core_ref, chip_ref, found
+
+    def send(self, kind, h, row):
+        start, width = self.found[kind, h]
+        values = [row(r) for r in (h - 1, ROWS - h)]
+        low, high = [inside(v) if width < v.shape[0] else v for v in values]
+        self.core_ref[start : start + width] = jnp.where(self.even, high, low)
+        self.chip_ref[start : start + width] = jnp.where(self.even, low, high)
+
+    def taken(self, kind, r):
+        start, width = self.found[kind, -r if r < 0 else r - ROWS + 1]
+        core, chip = self.core_ref[start : start + width], self.chip_ref[start : start + width]
+        return jnp.where(self.even, chip, core) if r < 0 else jnp.where(self.even, core, chip)
 
 
 def sides_kernel(*refs):
-    tile, (low_ref, high_ref) = Tile(*refs[:6]), refs[6:]
+    tile, sides = Tile(*refs[1:7]), Sides(refs[0], *refs[7:], FIRST)
     for kind, h in FIRST:
         if kind == "std":
             row = tile.std
         elif kind == "diffusion":
             row = lambda r: tile.turned()
         else:
-            row = lambda r, t=kind[1]: tile.forcing(t, r)
-        send(low_ref, high_ref, FIRST, kind, h, row)
+            row = lambda r: tile.forcing(kind[1], r)
+        sides.send(kind, h, row)
 
 
 def weights_kernel(*refs):
-    tile, (low_ref, high_ref) = Tile(*refs[:6]), refs[6:]
+    tile, sides = Tile(*refs[1:7]), Sides(refs[0], *refs[7:], WEIGHTS)
     for kind, h in WEIGHTS:
-        send(low_ref, high_ref, WEIGHTS, kind, h, lambda r: jnp.concatenate(tile.inner_weights(kind[1], r), axis=0))
+        sides.send(kind, h, lambda r: jnp.concatenate(tile.inner_weights(kind[1], r), axis=0))
 
 
 def own(r):
@@ -274,7 +278,7 @@
         return self.v_ref[self.at(r)] + self.y_ref[self.at(r), :L] + self.y_ref[self.at(r), L:]
 
     def fill_diffusion(self, tile, sides, reach):
-        values = {0: tile.turned(), -1: taken(sides, FIRST, "diffusion", -1), 1: taken(sides, FIRST, "diffusion", ROWS)}
+        values = {0: tile.turned(), -1: sides.taken("diffusion", -1), 1: sides.taken("diffusion", ROWS)}
         skip = (WIDE - self.width) // 2
         for r in range(-reach, ROWS + reach):
             column = values[r // ROWS][skip : skip + self.width, r % ROWS : r % ROWS + 1]
@@ -335,15 +339,16 @@
 
 
 def std_rows(tile, sides):
-    return lambda r: tile.std(r) if own(r) else padded(taken(sides, FIRST, "std", r))
-
-
-def right_side_kernel(*refs):
-    tile, sides, m_ref = Tile(*refs[:6]), refs[6:8], refs[8]
-    b_ref, y_ref, low_ref, high_ref = refs[9:13]
+    return lambda r: tile.std(r) if own(r) else padded(sides.taken("std", r))
+
+
+def right_side_kernel(parity_ref, *refs):
+    tile, sides, m_ref = Tile(*refs[:6]), Sides(parity_ref, *refs[6:8], FIRST), refs[8]
+    b_ref, y_ref = refs[9:11]
+    out = Sides(parity_ref, *refs[11:13], SECOND)
     field = Field(WIDE, STEPS + 1, *refs[13:17], m_ref)
     field.fill_diffusion(tile, sides, STEPS + 1)
-    forcing = lambda t, r: tile.forcing(t, r) if own(r) else padded(taken(sides, FIRST, ("f", t), r))
+    forcing = lambda t, r: tile.forcing(t, r) if own(r) else padded(sides.taken(("f", t), r))
     std = std_rows(tile, sides)
     for r in range(-STEPS - 1, ROWS + STEPS + 1):
         field.put(r, forcing(STEPS - 1, r))
@@ -354,40 +359,38 @@
         if own(r):
             b_ref[r] = value
     field.mix(-1, ROWS + 1, FACTOR)
+    beyond = {}
     for r in range(-1, ROWS + 1):
         state = std(r) * field.get(r)
         if own(r):
             y_ref[r] = state
         else:
-            state = field.d_ref[field.at(r)] * state
-        for ref, h in ((low_ref, r + 1), (high_ref, ROWS - r)):
-            if 1 <= h <= REACH and own(r) == (h < REACH):
-                start, width = SECOND["state", h]
-                ref[start : start + width] = state if width == WIDE else inside(state)
-    for h in range(1, STEPS + 1):
-        send(low_ref, high_ref, SECOND, "b", h, lambda r: b_ref[r])
+            beyond[r] = field.d_ref[field.at(r)] * state
+    for kind, h in SECOND:
+        out.send(kind, h, lambda r: b_ref[r] if kind == "b" else y_ref[r] if own(r) else beyond[r])
 
 
 MIDDLE = slice(COLS, 2 * COLS)
 
 
-def first_image_kernel(*refs):
-    tile, sides, m_ref = Tile(*refs[:6]), refs[6:8], refs[8]
+def first_image_kernel(parity_ref, *refs):
+    tile, sides, m_ref = Tile(*refs[:6]), Sides(parity_ref, *refs[6:8], FIRST), refs[8]
     b_ref, y_ref = refs[9:11]
-    more, forced = refs[11:13], refs[13:15]
-    q_ref, g_ref, low_ref, high_ref, sums_ref = refs[15:20]
+    more, forced = Sides(parity_ref, *refs[11:13], SECOND), Sides(parity_ref, *refs[13:15], WEIGHTS)
+    q_ref, g_ref = refs[15:17]
+    out, sums_ref = Sides(parity_ref, *refs[17:19], THIRD), refs[19]
     field = Field(WIDE, REACH, *refs[20:24], m_ref)
     tops = refs[24:26]
     field.fill_diffusion(tile, sides, REACH - 1)
     std = std_rows(tile, sides)
 
     def weights(t, r):
-        return tile.weights(t, r) if own(r) else padded(taken(forced, WEIGHTS, ("w", t), r))
+        return tile.weights(t, r) if own(r) else padded(forced.taken(("w", t), r))
 
     def start(r):
         if own(r):
             return y_ref[r]
-        return padded(taken(more, SECOND, "state", r))
+        return padded(more.taken("state", r))
 
     def force(t, r, value):
         if -t - 4 <= r < ROWS + t + 4:
@@ -400,7 +403,7 @@
     field.adjoint(STEPS, lambda t, r: tops[t][field.at(r)], std)
     sums = [jnp.zeros((COLS, L), F32) for _ in range(4)]
     for r in range(-STEPS, ROWS + STEPS):
-        b = b_ref[r] if own(r) else padded(taken(more, SECOND, "b", r))
+        b = b_ref[r] if own(r) else padded(more.taken("b", r))
         q = b + field.get(r)
         field.put(r, q)
         if own(r):
@@ -412,16 +415,13 @@
 
     def keep(t, r, value):
         if own(r):
-            forced = tile.weights(t, r) * value
-            sums[3] = sums[3] + forced[MIDDLE] * value[MIDDLE]
-            forced = inside(forced)
-            g_ref[t, r] = forced
-            for ref, h in ((low_ref, r + 1), (high_ref, ROWS - r)):
-                if h <= t + 1:
-                    begin, width = THIRD[("g", t), h]
-                    ref[begin : begin + width] = forced
+            forcing = tile.weights(t, r) * value
+            sums[3] = sums[3] + forcing[MIDDLE] * value[MIDDLE]
+            g_ref[t, r] = inside(forcing)
 
     field.forward(STEPS, lambda r: std(r) * field.get(r), keep)
+    for kind, h in THIRD:
+        out.send(kind, h, lambda r: g_ref[kind[1], r])
     lane = lax.broadcasted_iota(jnp.int32, (1, L), 1)
     row = jnp.zeros((1, L), F32)
     for i, term in enumerate(sums):
@@ -430,14 +430,14 @@
     sums_ref[...] = jnp.broadcast_to(row, sums_ref.shape)
 
 
-def second_image_kernel(*refs):
-    tile, sides, m_ref = Tile(*refs[:6]), refs[6:8], refs[8]
+def second_image_kernel(parity_ref, *refs):
+    tile, sides, m_ref = Tile(*refs[:6]), Sides(parity_ref, *refs[6:8], FIRST), refs[8]
     q_ref, g_ref = refs[9:11]
-    more = refs[11:13]
+    more = Sides(parity_ref, *refs[11:13], THIRD)
     u_ref = refs[13]
     field = Field(INNER, STEPS, *refs[14:18], m_ref)
     field.fill_diffusion(tile, sides, STEPS)
-    forcing = lambda t, r: g_ref[t, r] if own(r) else taken(more, THIRD, ("g", t), r)
+    forcing = lambda t, r: g_ref[t, r] if own(r) else more.taken(("g", t), r)
     for r in range(-STEPS, ROWS + STEPS):
         field.put(r, forcing(STEPS - 1, r))
     field.adjoint(0, forcing, lambda r: inside(tile.std(r)))
@@ -472,17 +472,25 @@
         residual_ref[r] = b - along_b * q + along_q * u_ref[r]
 
 
-def exchange(to_before, to_after, axis, wrap):
-    size = lax.axis_size(axis)
-    up = [(i, (i + 1) % size) for i in range(size if wrap else size - 1)]
+def exchange(to_before, to_after):
+    size = lax.axis_size("lon")
+    up = [(i, (i + 1) % size) for i in range(size)]
     down = [(j, i) for i, j in up]
-    return lax.ppermute(to_after, axis, up), lax.ppermute(to_before, axis, down)
+    return lax.ppermute(to_after, "lon", up), lax.ppermute(to_before, "lon", down)
+
+
+def swap(core, chip):
+    size = lax.axis_size("lat")
+    pairs = [[(i, i + 1) for i in range(first, size - 1, 2)] for first in (0, 1)]
+    both = [p + [(j, i) for i, j in p] for p in pairs]
+    return lax.ppermute(core, "lat", both[0]), lax.ppermute(chip, "lat", both[1])
 
 
 def shards(
     departures, obs_weight, obs_columns, obs_owner, obs_counts, background_std, diffusion, level_factor, model_mixing
 ):
     parity = (lax.axis_index("lon") % 2).astype(jnp.int32).reshape(1)
+    side_of = (lax.axis_index("lat") % 2).astype(jnp.int32).reshape(1)
     slots = pltpu.VMEM((SLOTS, L), F32)
     buckets = call(
         bucket_kernel,
@@ -496,21 +504,23 @@
     received = lax.all_to_all(buckets, "lon", 0, 0)
     mats = call(matrices_kernel, "matrices", shape(4, 2 * L, 2 * L, dtype=BF16))(level_factor, model_mixing)
     fixed = call(fixed_kernel, "fixed", shape(CELLS + COLS, L))(background_std.reshape(CELLS, L), diffusion)
-    fixed_left, fixed_right = exchange(fixed, fixed, "lon", True)
+    fixed_left, fixed_right = exchange(fixed, fixed)
     beside = shape(PACKED + ROWS, L)
     tile, to_left, to_right = call(tile_kernel, "tile", (shape(2 * SIZE, L), beside, beside))(
         received, fixed_left, fixed_right
     )
-    left, right = exchange(to_left, to_right, "lon", True)
+    left, right = exchange(to_left, to_right)
     refs = (left, tile, right, fixed_left, fixed, fixed_right)
     side = shape(FIRST_ROWS, L)
-    below, above = exchange(*call(sides_kernel, "sides", (side, side))(*refs), "lat", False)
+    below, above = swap(*call(sides_kernel, "sides", (side, side), smem=(0,))(side_of, *refs))
     side = shape(WEIGHTS_ROWS, L)
-    weights = exchange(*call(weights_kernel, "weights", (side, side))(*refs), "lat", False)
+    weights = swap(*call(weights_kernel, "weights", (side, side), smem=(0,))(side_of, *refs))
     refs = (*refs, below, above, mats)
     field, side = shape(ROWS, WIDE, L), shape(SECOND_ROWS, L)
-    b, y, low, high = call(right_side_kernel, "right_side", (field, field, side, side), scratch(WIDE, STEPS + 1))(*refs)
-    south, north = exchange(low, high, "lat", False)
+    b, y, low, high = call(right_side_kernel, "right_side", (field, field, side, side), scratch(WIDE, STEPS + 1), smem=(0,))(
+        side_of, *refs
+    )
+    south, north = swap(low, high)
     lat, lon = lax.axis_size("lat"), lax.axis_size("lon")
     near, far = levels(lat, lon)
     small, side = shape(ROWS, COLS, L), shape(THIRD_ROWS, L)
@@ -520,10 +530,13 @@
         "first_image",
         (small, shape(STEPS, ROWS, INNER, L), side, side, shape(lat, L)),
         space + [space[0]] * 2,
-    )(*refs, b, y, south, north, *weights)
+        smem=(0,),
+    )(side_of, *refs, b, y, south, north, *weights)
     sums = lax.all_to_all(sums, "lat", 0, 0, axis_index_groups=near, tiled=True)
-    south, north = exchange(low, high, "lat", False)
-    u = call(second_image_kernel, "second_image", small, scratch(INNER, STEPS))(*refs, q, g, south, north)
+    south, north = swap(low, high)
+    u = call(second_image_kernel, "second_image", small, scratch(INNER, STEPS), smem=(0,))(
+        side_of, *refs, q, g, south, north
+    )
     sums = call(add_kernel, "add", shape(4 * lon, L))(sums)
     sums = lax.all_to_all(sums, ("lat", "lon"), 0, 0, axis_index_groups=far, tiled=True)
     return call(finish_kernel, "finish", (small, small))(sums, b, q, u)

time: 119 us -> 116 us (0.975)
  waiting for transfers between devices: 29.1 us -> 27.1 us
  starting transfers between devices: 76.4 us -> 75 us
    all_to_all x1, starting transfers between devices: 18 us -> 15 us  [shards(): sums = lax.all_to_all(sums, 'lat', 0, 0, axis_index_groups=near, tiled=True)]
    ppermute x12, waiting for transfers between devices: 16.7 us -> 14.9 us  [the longest x2 7.06 us: exchange(): lax.ppermute(to_after, 'lon', up)]
    ppermute x12, starting transfers between devices: 43 us -> 44.7 us  [the longest x4 16.8 us: swap(): lax.ppermute(chip, 'lat', both[1])]
  transfers between devices with their start and end apart: 15 -> 15, of which waited for: 9 -> 7; matrix products, arithmetic and copies ran while one was open for 0% -> 0% of each run, Pallas kernels for 2% -> 2%
where the time goes in v5:
time: 116 us; the launch traced here: 115 us
  starting transfers between devices  75 us (65%)
  waiting for transfers between devices  27.1 us (23%)
  Pallas kernels  11.1 us (10%)
  between operations  1.58 us (1%)
    ppermute x4, starting transfers between devices, swap(): lax.ppermute(chip, 'lat', both[1])  16.8 us
    all_to_all x1, starting transfers between devices, shards(): sums = lax.all_to_all(sums, 'lat', 0, 0, axis_index_groups=near, tiled=True)  15 us
    ppermute x4, starting transfers between devices, swap(): lax.ppermute(core, 'lat', both[0])  14.9 us
    pallas_call x11, Pallas kernels, run(): pl.pallas_call(kernel, name=name, out_shape=outs, in_specs=specs, out_spe...  11.1 us
    ppermute x2, starting transfers between devices, exchange(): lax.ppermute(to_before, 'lon', down)  9.15 us
    all_to_all x1, starting transfers between devices, shards(): received = lax.all_to_all(buckets, 'lon', 0, 0)  7.79 us
    all_to_all x1, waiting for transfers between devices, shards(): lax.all_to_all(sums, ('lat', 'lon'), 0, 0, axis_index_groups=far, tiled=T...  7.76 us
    all_to_all x1, starting transfers between devices, shards(): lax.all_to_all(sums, ('lat', 'lon'), 0, 0, axis_index_groups=far, tiled=T...  7.54 us
  transfers between devices with their start and end apart: 15, of which 7 were waited for; matrix products, arithmetic and copies ran while one was open for 0% of the time, Pallas kernels for 2%

profile of v5, /device:TPU:1, one launch (start us, length us, event | category | flops | bytes accessed | tf_op | source)
XLA Modules:
  0.0 114.8 jit_solution(2090074301005729083)
XLA Ops:
  1.3 2.8 %bucket.1 = f32[8,136,128]{2,1,0:T(8,128)} custom-call(f32[256,128]{1,0:T(8,128)} %departures_hbm.1, f32[256,128]{1,0:T(8,128)} %weight_hbm.1, s32[1,256]{1,0:T(1,128)} %bitcast.14, s32[1,256]{1,0:T(1,128)} %bitcast.15, s32[1]{0:T(128)S(6)} %copy.12.counts_ref, s32[1]{0:T(128)} %bitcast.3.parity_ref), custom_call_target="tpu_custom_call" | custom-call | tf_op jit(solution)/shard_map/bucket/pallas_call | solution.py:30
  4.1 0.0 copy-start.2
  4.1 0.0 copy-start.3
  4.1 7.8 %all-to-all-start = ((f32[8,136,128]{2,1,0:T(8,128)}), f32[8,136,128]{2,1,0:T(8,128)S(1)}, u32[]{:S(2)}, u32[]{:S(2)}) async-start(f32[8,136,128]{2,1,0:T(8,128)} %bucket.1), calls=%async_computation | async-start | bytes 1114112 | tf_op jit(solution)/shard_map/all_to_all | solution.py:504
  11.9 0.0 copy-done.2
  11.9 0.0 copy-done.3
  11.9 0.1 fixed.1.refs_5_.refs_4_
  12.0 4.6 %collective-permute-start.1 = (f32[144,128]{1,0:T(8,128)S(1)}, f32[144,128]{1,0:T(8,128)S(1)}, u32[]{:S(2)}, u32[]{:S(2)}) collective-permute-start(f32[144,128]{1,0:T(8,128)S(1)} %fixed.1.refs_5_.refs_4_), channel_id=1, source_target_pairs={{1,0},{2,1},{3,2},{4,3},{5,4},{6,5},{7,6},{0,7},{9,8},{10,9},{11,1... | collective-permute-start | bytes 221192 | tf_op jit(solution)/shard_map/ppermute | solution.py:479
  16.6 1.9 %collective-permute-start = (f32[144,128]{1,0:T(8,128)S(1)}, f32[144,128]{1,0:T(8,128)S(1)}, u32[]{:S(2)}, u32[]{:S(2)}) collective-permute-start(f32[144,128]{1,0:T(8,128)S(1)} %fixed.1.refs_5_.refs_4_), channel_id=1, source_target_pairs={{0,1},{1,2},{2,3},{3,4},{4,5},{5,6},{6,7},{7,0},{8,9},{9,10},{10,1... | collective-permute-start | bytes 221192 | tf_op jit(solution)/shard_map/ppermute | solution.py:479
  18.6 2.8 %collective-permute-done.1.fixed_right_ref.refs_6_.refs_5_ = f32[144,128]{1,0:T(8,128)S(1)} collective-permute-done((f32[144,128]{1,0:T(8,128)S(1)}, f32[144,128]{1,0:T(8,128)S(1)}, u32[]{:S(2)}, u32[]{:S(2)}) %collective-permute-start.1) | collective-permute-done | bytes 73760 | tf_op jit(solution)/shard_map/ppermute | solution.py:479
  21.3 4.9 %collective-permute-done.fixed_left_ref.refs_4_.refs_3_ = f32[144,128]{1,0:T(8,128)S(1)} collective-permute-done((f32[144,128]{1,0:T(8,128)S(1)}, f32[144,128]{1,0:T(8,128)S(1)}, u32[]{:S(2)}, u32[]{:S(2)}) %collective-permute-start) | collective-permute-done | bytes 73760 | tf_op jit(solution)/shard_map/ppermute | solution.py:479
  26.2 0.0 all-to-all-done.received_ref
  26.2 0.4 tile.1
  26.6 1.9 %collective-permute-start.2 = (f32[584,128]{1,0:T(8,128)S(1)}, f32[584,128]{1,0:T(8,128)S(1)}, u32[]{:S(2)}, u32[]{:S(2)}) collective-permute-start(f32[584,128]{1,0:T(8,128)S(1)} %get-tuple-element.18), channel_id=1, source_target_pairs={{0,1},{1,2},{2,3},{3,4},{4,5},{5,6},{6,7},{7,0},{8,9},{9,10},{10,1... | collective-permute-start | bytes 897032 | tf_op jit(solution)/shard_map/ppermute | solution.py:479
  28.5 4.6 %collective-permute-start.3 = (f32[584,128]{1,0:T(8,128)S(1)}, f32[584,128]{1,0:T(8,128)S(1)}, u32[]{:S(2)}, u32[]{:S(2)}) collective-permute-start(f32[584,128]{1,0:T(8,128)S(1)} %get-tuple-element.20), channel_id=1, source_target_pairs={{1,0},{2,1},{3,2},{4,3},{5,4},{6,5},{7,6},{0,7},{9,8},{10,9},{11,1... | collective-permute-start | bytes 897032 | tf_op jit(solution)/shard_map/ppermute | solution.py:479
  33.1 2.2 %collective-permute-done.2.refs_1_.refs_0_ = f32[584,128]{1,0:T(8,128)S(1)} collective-permute-done((f32[584,128]{1,0:T(8,128)S(1)}, f32[584,128]{1,0:T(8,128)S(1)}, u32[]{:S(2)}, u32[]{:S(2)}) %collective-permute-start.2) | collective-permute-done | bytes 299040 | tf_op jit(solution)/shard_map/ppermute | solution.py:479
  35.3 1.5 %collective-permute-done.3.refs_3_.refs_2_ = f32[584,128]{1,0:T(8,128)S(1)} collective-permute-done((f32[584,128]{1,0:T(8,128)S(1)}, f32[584,128]{1,0:T(8,128)S(1)}, u32[]{:S(2)}, u32[]{:S(2)}) %collective-permute-start.3) | collective-permute-done | bytes 299040 | tf_op jit(solution)/shard_map/ppermute | solution.py:479
  36.8 9.0 %collective-permute-start.4 = (f32[528,128]{1,0:T(8,128)S(1)}, f32[528,128]{1,0:T(8,128)S(1)}, u32[]{:S(2)}, u32[]{:S(2)}) collective-permute-start(f32[528,128]{1,0:T(8,128)S(1)} %get-tuple-element.21), channel_id=1, source_target_pairs={{0,8},{16,24},{32,40},{48,56},{64,72},{80,88},{96,104},{112,120},{... | collective-permute-start | bytes 811016 | tf_op jit(solution)/shard_map/ppermute | solution.py:486
  45.8 0.0 copy-start
  45.8 0.0 copy-start.1
  45.8 4.5 %collective-permute-start.5 = (f32[528,128]{1,0:T(8,128)S(1)}, f32[528,128]{1,0:T(8,128)S(1)}, u32[]{:S(2)}, u32[]{:S(2)}) collective-permute-start(f32[528,128]{1,0:T(8,128)S(1)} %get-tuple-element.22), channel_id=1, source_target_pairs={{8,16},{24,32},{40,48},{56,64},{72,80},{88,96},{104,112},{120,128}... | collective-permute-start | bytes 811016 | tf_op jit(solution)/shard_map/ppermute | solution.py:486
  50.4 1.9 %collective-permute-start.8 = (f32[480,128]{1,0:T(8,128)S(1)}, f32[480,128]{1,0:T(8,128)S(1)}, u32[]{:S(2)}, u32[]{:S(2)}) collective-permute-start(f32[480,128]{1,0:T(8,128)S(1)} %get-tuple-element.27), channel_id=1, source_target_pairs={{0,8},{16,24},{32,40},{48,56},{64,72},{80,88},{96,104},{112,120},{... | collective-permute-start | bytes 737288 | tf_op jit(solution)/shard_map/ppermute | solution.py:486
  52.3 4.4 %collective-permute-start.9 = (f32[480,128]{1,0:T(8,128)S(1)}, f32[480,128]{1,0:T(8,128)S(1)}, u32[]{:S(2)}, u32[]{:S(2)}) collective-permute-start(f32[480,128]{1,0:T(8,128)S(1)} %get-tuple-element.28), channel_id=1, source_target_pairs={{8,16},{24,32},{40,48},{56,64},{72,80},{88,96},{104,112},{120,128}... | collective-permute-start | bytes 737288 | tf_op jit(solution)/shard_map/ppermute | solution.py:486
  56.7 0.0 copy-done
  56.7 0.0 copy-done.1
  56.7 0.1 matrices.1.refs_8_
  56.8 0.0 collective-permute-done.4.refs_6_
  56.9 0.0 collective-permute-done.5.refs_7_
  56.9 1.2 %right_side.1 = (f32[8,48,128]{2,1,0:T(8,128)S(1)}, f32[8,48,128]{2,1,0:T(8,128)S(1)}, f32[432,128]{1,0:T(8,128)S(1)}, f32[432,128]{1,0:T(8,128)S(1)}) custom-call(s32[1]{0:T(128)} %bitcast.refs_0_.parity_ref, f32[584,128]{1,0:T(8,128)S(1)} %collective-permute-done.2.refs_1_.refs_0_, f32[768,128]{1,0:T(8,128)S(1)} %get-tuple-element.19.refs_2_.refs_1_, ...), custom_call_target="tpu_custom_call" | custom-call | tf_op jit(solution)/shard_map/right_side/pallas_call | solution.py:30
  58.1 1.9 %collective-permute-start.6 = (f32[432,128]{1,0:T(8,128)S(1)}, f32[432,128]{1,0:T(8,128)S(1)}, u32[]{:S(2)}, u32[]{:S(2)}) collective-permute-start(f32[432,128]{1,0:T(8,128)S(1)} %get-tuple-element.25), channel_id=1, source_target_pairs={{0,8},{16,24},{32,40},{48,56},{64,72},{80,88},{96,104},{112,120},{... | collective-permute-start | bytes 663560 | tf_op jit(solution)/shard_map/ppermute | solution.py:486
  60.0 4.4 %collective-permute-start.7 = (f32[432,128]{1,0:T(8,128)S(1)}, f32[432,128]{1,0:T(8,128)S(1)}, u32[]{:S(2)}, u32[]{:S(2)}) collective-permute-start(f32[432,128]{1,0:T(8,128)S(1)} %get-tuple-element.26), channel_id=1, source_target_pairs={{8,16},{24,32},{40,48},{56,64},{72,80},{88,96},{104,112},{120,128}... | collective-permute-start | bytes 663560 | tf_op jit(solution)/shard_map/ppermute | solution.py:486
  64.4 0.0 collective-permute-done.8.refs_13_
  64.4 0.0 collective-permute-done.9.refs_14_
  64.4 0.0 collective-permute-done.6.refs_11_
  64.4 3.6 %collective-permute-done.7.refs_12_ = f32[432,128]{1,0:T(8,128)S(1)} collective-permute-done((f32[432,128]{1,0:T(8,128)S(1)}, f32[432,128]{1,0:T(8,128)S(1)}, u32[]{:S(2)}, u32[]{:S(2)}) %collective-permute-start.7) | collective-permute-done | bytes 221216 | tf_op jit(solution)/shard_map/ppermute | solution.py:486
  68.0 4.2 %first_image.1 = (f32[8,16,128]{2,1,0:T(8,128)S(1)}, f32[3,8,32,128]{3,2,1,0:T(8,128)S(1)}, f32[192,128]{1,0:T(8,128)S(1)}, f32[192,128]{1,0:T(8,128)S(1)}, f32[96,128]{1,0:T(8,128)}) custom-call(s32[1]{0:T(128)} %bitcast.refs_0_.parity_ref, f32[584,128]{1,0:T(8,128)S(1)} %collective-permute-done.2.refs_1_.refs_0_, ...), custom_call_target="tpu_custom_call" | custom-call | tf_op jit(solution)/shard_map/first_image/pallas_call | solution.py:30
  72.2 15.0 %all-to-all-start.1 = ((f32[24,4,128]{2,1,0:T(4,128)}), f32[24,4,128]{2,1,0:T(4,128)S(1)}, u32[]{:S(2)}, u32[]{:S(2)}) async-start(f32[24,4,128]{2,1,0:T(4,128)} %bitcast.5), calls=%async_computation.1 | async-start | bytes 98304 | tf_op jit(solution)/shard_map/all_to_all | solution.py:535
  87.2 2.1 %collective-permute-start.10 = (f32[192,128]{1,0:T(8,128)S(1)}, f32[192,128]{1,0:T(8,128)S(1)}, u32[]{:S(2)}, u32[]{:S(2)}) collective-permute-start(f32[192,128]{1,0:T(8,128)S(1)} %get-tuple-element.32), channel_id=1, source_target_pairs={{0,8},{16,24},{32,40},{48,56},{64,72},{80,88},{96,104},{112,120},{... | collective-permute-start | bytes 294920 | tf_op jit(solution)/shard_map/ppermute | solution.py:486
  89.3 3.5 %collective-permute-start.11 = (f32[192,128]{1,0:T(8,128)S(1)}, f32[192,128]{1,0:T(8,128)S(1)}, u32[]{:S(2)}, u32[]{:S(2)}) collective-permute-start(f32[192,128]{1,0:T(8,128)S(1)} %get-tuple-element.33), channel_id=1, source_target_pairs={{8,16},{24,32},{40,48},{56,64},{72,80},{88,96},{104,112},{120,128}... | collective-permute-start | bytes 294920 | tf_op jit(solution)/shard_map/ppermute | solution.py:486
  92.8 4.5 %all-to-all-done.1 = f32[24,4,128]{2,1,0:T(4,128)S(1)} async-done(((f32[24,4,128]{2,1,0:T(4,128)}), f32[24,4,128]{2,1,0:T(4,128)S(1)}, u32[]{:S(2)}, u32[]{:S(2)}) %all-to-all-start.1) | async-done | bytes 49184 | tf_op jit(solution)/shard_map/all_to_all | solution.py:535
  97.3 0.6 add.10
  97.9 7.5 %all-to-all-start.2 = ((f32[32,1,128]{2,1,0:T(1,128)}), f32[32,1,128]{2,1,0:T(1,128)S(1)}, u32[]{:S(2)}, u32[]{:S(2)}) async-start(f32[32,1,128]{2,1,0:T(1,128)} %bitcast.8), calls=%async_computation.2 | async-start | bytes 32768 | tf_op jit(solution)/shard_map/all_to_all | solution.py:541
  105.4 0.0 collective-permute-done.10.refs_11_
  105.4 0.0 collective-permute-done.11.refs_12_
  105.5 0.8 second_image.1.u_ref
  106.2 7.8 %all-to-all-done.2 = f32[32,1,128]{2,1,0:T(1,128)S(1)} async-done(((f32[32,1,128]{2,1,0:T(1,128)}), f32[32,1,128]{2,1,0:T(1,128)S(1)}, u32[]{:S(2)}, u32[]{:S(2)}) %all-to-all-start.2) | async-done | bytes 16416 | tf_op jit(solution)/shard_map/all_to_all | solution.py:541
  114.0 0.8 finish.1
  (2 shorter events, 0.1 us)
Async XLA Ops:
  4.1 7.8 %copy-start.2 = (f32[8,16,128]{2,1,0:T(8,128)S(1)}, f32[8,16,128]{2,1,0:T(8,128)}, u32[]{:S(2)}) copy-start(f32[8,16,128]{2,1,0:T(8,128)} %param.14) | copy-start | bytes 196612
  4.1 7.8 %copy-start.3 = (f32[8,16]{1,0:T(8,128)S(1)}, f32[8,16]{1,0:T(8,128)}, u32[]{:S(2)}) copy-start(f32[8,16]{1,0:T(8,128)} %diffusion_ref.1) | copy-start | bytes 1540
  4.1 22.0 %all-to-all-start = ((f32[8,136,128]{2,1,0:T(8,128)}), f32[8,136,128]{2,1,0:T(8,128)S(1)}, u32[]{:S(2)}, u32[]{:S(2)}) async-start(f32[8,136,128]{2,1,0:T(8,128)} %bucket.1), calls=%async_computation | async-start | bytes 1114112 | tf_op jit(solution)/shard_map/all_to_all | solution.py:504
  12.0 9.3 %collective-permute-start.1 = (f32[144,128]{1,0:T(8,128)S(1)}, f32[144,128]{1,0:T(8,128)S(1)}, u32[]{:S(2)}, u32[]{:S(2)}) collective-permute-start(f32[144,128]{1,0:T(8,128)S(1)} %fixed.1.refs_5_.refs_4_), channel_id=1, source_target_pairs={{1,0},{2,1},{3,2},{4,3},{5,4},{6,5},{7,6},{0,7},{9,8},{10,9},{11,1... | collective-permute-start | bytes 221192 | tf_op jit(solution)/shard_map/ppermute | solution.py:479
  16.6 9.5 %collective-permute-start = (f32[144,128]{1,0:T(8,128)S(1)}, f32[144,128]{1,0:T(8,128)S(1)}, u32[]{:S(2)}, u32[]{:S(2)}) collective-permute-start(f32[144,128]{1,0:T(8,128)S(1)} %fixed.1.refs_5_.refs_4_), channel_id=1, source_target_pairs={{0,1},{1,2},{2,3},{3,4},{4,5},{5,6},{6,7},{7,0},{8,9},{9,10},{10,1... | collective-permute-start | bytes 221192 | tf_op jit(solution)/shard_map/ppermute | solution.py:479
  26.6 8.7 %collective-permute-start.2 = (f32[584,128]{1,0:T(8,128)S(1)}, f32[584,128]{1,0:T(8,128)S(1)}, u32[]{:S(2)}, u32[]{:S(2)}) collective-permute-start(f32[584,128]{1,0:T(8,128)S(1)} %get-tuple-element.18), channel_id=1, source_target_pairs={{0,1},{1,2},{2,3},{3,4},{4,5},{5,6},{6,7},{7,0},{8,9},{9,10},{10,1... | collective-permute-start | bytes 897032 | tf_op jit(solution)/shard_map/ppermute | solution.py:479
  28.5 8.3 %collective-permute-start.3 = (f32[584,128]{1,0:T(8,128)S(1)}, f32[584,128]{1,0:T(8,128)S(1)}, u32[]{:S(2)}, u32[]{:S(2)}) collective-permute-start(f32[584,128]{1,0:T(8,128)S(1)} %get-tuple-element.20), channel_id=1, source_target_pairs={{1,0},{2,1},{3,2},{4,3},{5,4},{6,5},{7,6},{0,7},{9,8},{10,9},{11,1... | collective-permute-start | bytes 897032 | tf_op jit(solution)/shard_map/ppermute | solution.py:479
  36.8 20.1 %collective-permute-start.4 = (f32[528,128]{1,0:T(8,128)S(1)}, f32[528,128]{1,0:T(8,128)S(1)}, u32[]{:S(2)}, u32[]{:S(2)}) collective-permute-start(f32[528,128]{1,0:T(8,128)S(1)} %get-tuple-element.21), channel_id=1, source_target_pairs={{0,8},{16,24},{32,40},{48,56},{64,72},{80,88},{96,104},{112,120},{... | collective-permute-start | bytes 811016 | tf_op jit(solution)/shard_map/ppermute | solution.py:486
  45.8 10.9 %copy-start = (f32[128,128]{1,0:T(8,128)S(1)}, f32[128,128]{1,0:T(8,128)}, u32[]{:S(2)}) copy-start(f32[128,128]{1,0:T(8,128)} %factor_ref.1) | copy-start | bytes 196612
  45.8 10.9 %copy-start.1 = (f32[128,128]{1,0:T(8,128)S(1)}, f32[128,128]{1,0:T(8,128)}, u32[]{:S(2)}) copy-start(f32[128,128]{1,0:T(8,128)} %mixing_ref.1) | copy-start | bytes 196612
  45.8 11.1 %collective-permute-start.5 = (f32[528,128]{1,0:T(8,128)S(1)}, f32[528,128]{1,0:T(8,128)S(1)}, u32[]{:S(2)}, u32[]{:S(2)}) collective-permute-start(f32[528,128]{1,0:T(8,128)S(1)} %get-tuple-element.22), channel_id=1, source_target_pairs={{8,16},{24,32},{40,48},{56,64},{72,80},{88,96},{104,112},{120,128}... | collective-permute-start | bytes 811016 | tf_op jit(solution)/shard_map/ppermute | solution.py:486
  50.4 14.0 %collective-permute-start.8 = (f32[480,128]{1,0:T(8,128)S(1)}, f32[480,128]{1,0:T(8,128)S(1)}, u32[]{:S(2)}, u32[]{:S(2)}) collective-permute-start(f32[480,128]{1,0:T(8,128)S(1)} %get-tuple-element.27), channel_id=1, source_target_pairs={{0,8},{16,24},{32,40},{48,56},{64,72},{80,88},{96,104},{112,120},{... | collective-permute-start | bytes 737288 | tf_op jit(solution)/shard_map/ppermute | solution.py:486
  52.3 12.1 %collective-permute-start.9 = (f32[480,128]{1,0:T(8,128)S(1)}, f32[480,128]{1,0:T(8,128)S(1)}, u32[]{:S(2)}, u32[]{:S(2)}) collective-permute-start(f32[480,128]{1,0:T(8,128)S(1)} %get-tuple-element.28), channel_id=1, source_target_pairs={{8,16},{24,32},{40,48},{56,64},{72,80},{88,96},{104,112},{120,128}... | collective-permute-start | bytes 737288 | tf_op jit(solution)/shard_map/ppermute | solution.py:486
  58.1 6.3 %collective-permute-start.6 = (f32[432,128]{1,0:T(8,128)S(1)}, f32[432,128]{1,0:T(8,128)S(1)}, u32[]{:S(2)}, u32[]{:S(2)}) collective-permute-start(f32[432,128]{1,0:T(8,128)S(1)} %get-tuple-element.25), channel_id=1, source_target_pairs={{0,8},{16,24},{32,40},{48,56},{64,72},{80,88},{96,104},{112,120},{... | collective-permute-start | bytes 663560 | tf_op jit(solution)/shard_map/ppermute | solution.py:486
  60.0 8.0 %collective-permute-start.7 = (f32[432,128]{1,0:T(8,128)S(1)}, f32[432,128]{1,0:T(8,128)S(1)}, u32[]{:S(2)}, u32[]{:S(2)}) collective-permute-start(f32[432,128]{1,0:T(8,128)S(1)} %get-tuple-element.26), channel_id=1, source_target_pairs={{8,16},{24,32},{40,48},{56,64},{72,80},{88,96},{104,112},{120,128}... | collective-permute-start | bytes 663560 | tf_op jit(solution)/shard_map/ppermute | solution.py:486
  72.2 25.1 %all-to-all-start.1 = ((f32[24,4,128]{2,1,0:T(4,128)}), f32[24,4,128]{2,1,0:T(4,128)S(1)}, u32[]{:S(2)}, u32[]{:S(2)}) async-start(f32[24,4,128]{2,1,0:T(4,128)} %bitcast.5), calls=%async_computation.1 | async-start | bytes 98304 | tf_op jit(solution)/shard_map/all_to_all | solution.py:535
  87.2 18.3 %collective-permute-start.10 = (f32[192,128]{1,0:T(8,128)S(1)}, f32[192,128]{1,0:T(8,128)S(1)}, u32[]{:S(2)}, u32[]{:S(2)}) collective-permute-start(f32[192,128]{1,0:T(8,128)S(1)} %get-tuple-element.32), channel_id=1, source_target_pairs={{0,8},{16,24},{32,40},{48,56},{64,72},{80,88},{96,104},{112,120},{... | collective-permute-start | bytes 294920 | tf_op jit(solution)/shard_map/ppermute | solution.py:486
  89.3 16.2 %collective-permute-start.11 = (f32[192,128]{1,0:T(8,128)S(1)}, f32[192,128]{1,0:T(8,128)S(1)}, u32[]{:S(2)}, u32[]{:S(2)}) collective-permute-start(f32[192,128]{1,0:T(8,128)S(1)} %get-tuple-element.33), channel_id=1, source_target_pairs={{8,16},{24,32},{40,48},{56,64},{72,80},{88,96},{104,112},{120,128}... | collective-permute-start | bytes 294920 | tf_op jit(solution)/shard_map/ppermute | solution.py:486
  97.9 16.1 %all-to-all-start.2 = ((f32[32,1,128]{2,1,0:T(1,128)}), f32[32,1,128]{2,1,0:T(1,128)S(1)}, u32[]{:S(2)}, u32[]{:S(2)}) async-start(f32[32,1,128]{2,1,0:T(1,128)} %bitcast.8), calls=%async_computation.2 | async-start | bytes 32768 | tf_op jit(solution)/shard_map/all_to_all | solution.py:541

commit v6 on v5

--- a/solution.py
+++ b/solution.py
@@ -217,7 +217,7 @@
 
 
 class Sides:
-    def __init__(self, parity_ref, core_ref, chip_ref, found):
+    def __init__(self, parity_ref, chip_ref, core_ref, found):
         self.even = parity_ref[0] == 0
         self.core_ref, self.chip_ref, self.found = core_ref, chip_ref, found
 
@@ -479,11 +479,11 @@
     return lax.ppermute(to_after, "lon", up), lax.ppermute(to_before, "lon", down)
 
 
-def swap(core, chip):
+def swap(chip, core):
     size = lax.axis_size("lat")
     pairs = [[(i, i + 1) for i in range(first, size - 1, 2)] for first in (0, 1)]
     both = [p + [(j, i) for i, j in p] for p in pairs]
-    return lax.ppermute(core, "lat", both[0]), lax.ppermute(chip, "lat", both[1])
+    return lax.ppermute(chip, "lat", both[1]), lax.ppermute(core, "lat", both[0])
 
 
 def shards(

time: 116 us -> 113 us (0.974)
  waiting for transfers between devices: 27.1 us -> 25.3 us
    ppermute x4, starting transfers between devices: 14.9 us -> 7.81 us  [swap(): lax.ppermute(core, 'lat', both[0])]
    ppermute x4, starting transfers between devices: 16.8 us -> 23.8 us  [swap(): lax.ppermute(chip, 'lat', both[1])]
    ppermute x4, waiting for transfers between devices: 3.58 us -> 1.66 us  [swap(): lax.ppermute(chip, 'lat', both[1])]
  transfers between devices with their start and end apart: 15 -> 15, of which waited for: 7 -> 7; matrix products, arithmetic and copies ran while one was open for 0% -> 0% of each run, Pallas kernels for 2% -> 3%
where the time goes in v6:
time: 113 us; the launch traced here: 112 us
  starting transfers between devices  73.9 us (65%)
  waiting for transfers between devices  25.3 us (22%)
  Pallas kernels  11.1 us (10%)
  between operations  1.58 us (1%)
    ppermute x4, starting transfers between devices, swap(): lax.ppermute(chip, 'lat', both[1])  23.8 us
    all_to_all x1, starting transfers between devices, shards(): sums = lax.all_to_all(sums, 'lat', 0, 0, axis_index_groups=near, tiled=True)  14 us
    pallas_call x11, Pallas kernels, run(): pl.pallas_call(kernel, name=name, out_shape=outs, in_specs=specs, out_spe...  11.1 us
    ppermute x2, starting transfers between devices, exchange(): lax.ppermute(to_before, 'lon', down)  9.15 us
    ppermute x4, starting transfers between devices, swap(): lax.ppermute(core, 'lat', both[0])  7.81 us
    all_to_all x1, starting transfers between devices, shards(): received = lax.all_to_all(buckets, 'lon', 0, 0)  7.79 us
    all_to_all x1, waiting for transfers between devices, shards(): lax.all_to_all(sums, ('lat', 'lon'), 0, 0, axis_index_groups=far, tiled=T...  7.76 us
    all_to_all x1, starting transfers between devices, shards(): lax.all_to_all(sums, ('lat', 'lon'), 0, 0, axis_index_groups=far, tiled=T...  7.55 us
  transfers between devices with their start and end apart: 15, of which 7 were waited for; matrix products, arithmetic and copies ran while one was open for 0% of the time, Pallas kernels for 3%

profile of v6, /device:TPU:1, one launch (start us, length us, event | category | flops | bytes accessed | tf_op | source)
XLA Modules:
  0.0 111.9 jit_solution(3066802920095633386)
XLA Ops:
  1.3 2.8 %bucket.1 = f32[8,136,128]{2,1,0:T(8,128)} custom-call(f32[256,128]{1,0:T(8,128)} %departures_hbm.1, f32[256,128]{1,0:T(8,128)} %weight_hbm.1, s32[1,256]{1,0:T(1,128)} %bitcast.14, s32[1,256]{1,0:T(1,128)} %bitcast.15, s32[1]{0:T(128)S(6)} %copy.12.counts_ref, s32[1]{0:T(128)} %bitcast.3.parity_ref), custom_call_target="tpu_custom_call" | custom-call | tf_op jit(solution)/shard_map/bucket/pallas_call | solution.py:30
  4.1 0.0 copy-start.2
  4.1 0.0 copy-start.3
  4.1 7.8 %all-to-all-start = ((f32[8,136,128]{2,1,0:T(8,128)}), f32[8,136,128]{2,1,0:T(8,128)S(1)}, u32[]{:S(2)}, u32[]{:S(2)}) async-start(f32[8,136,128]{2,1,0:T(8,128)} %bucket.1), calls=%async_computation | async-start | bytes 1114112 | tf_op jit(solution)/shard_map/all_to_all | solution.py:504
  11.9 0.0 copy-done.2
  11.9 0.0 copy-done.3
  11.9 0.1 fixed.1.refs_5_.refs_4_
  12.0 4.6 %collective-permute-start.1 = (f32[144,128]{1,0:T(8,128)S(1)}, f32[144,128]{1,0:T(8,128)S(1)}, u32[]{:S(2)}, u32[]{:S(2)}) collective-permute-start(f32[144,128]{1,0:T(8,128)S(1)} %fixed.1.refs_5_.refs_4_), channel_id=1, source_target_pairs={{1,0},{2,1},{3,2},{4,3},{5,4},{6,5},{7,6},{0,7},{9,8},{10,9},{11,1... | collective-permute-start | bytes 221192 | tf_op jit(solution)/shard_map/ppermute | solution.py:479
  16.6 1.9 %collective-permute-start = (f32[144,128]{1,0:T(8,128)S(1)}, f32[144,128]{1,0:T(8,128)S(1)}, u32[]{:S(2)}, u32[]{:S(2)}) collective-permute-start(f32[144,128]{1,0:T(8,128)S(1)} %fixed.1.refs_5_.refs_4_), channel_id=1, source_target_pairs={{0,1},{1,2},{2,3},{3,4},{4,5},{5,6},{6,7},{7,0},{8,9},{9,10},{10,1... | collective-permute-start | bytes 221192 | tf_op jit(solution)/shard_map/ppermute | solution.py:479
  18.6 2.8 %collective-permute-done.1.fixed_right_ref.refs_6_.refs_5_ = f32[144,128]{1,0:T(8,128)S(1)} collective-permute-done((f32[144,128]{1,0:T(8,128)S(1)}, f32[144,128]{1,0:T(8,128)S(1)}, u32[]{:S(2)}, u32[]{:S(2)}) %collective-permute-start.1) | collective-permute-done | bytes 73760 | tf_op jit(solution)/shard_map/ppermute | solution.py:479
  21.3 4.9 %collective-permute-done.fixed_left_ref.refs_4_.refs_3_ = f32[144,128]{1,0:T(8,128)S(1)} collective-permute-done((f32[144,128]{1,0:T(8,128)S(1)}, f32[144,128]{1,0:T(8,128)S(1)}, u32[]{:S(2)}, u32[]{:S(2)}) %collective-permute-start) | collective-permute-done | bytes 73760 | tf_op jit(solution)/shard_map/ppermute | solution.py:479
  26.2 0.0 all-to-all-done.received_ref
  26.2 0.4 tile.1
  26.6 1.9 %collective-permute-start.2 = (f32[584,128]{1,0:T(8,128)S(1)}, f32[584,128]{1,0:T(8,128)S(1)}, u32[]{:S(2)}, u32[]{:S(2)}) collective-permute-start(f32[584,128]{1,0:T(8,128)S(1)} %get-tuple-element.18), channel_id=1, source_target_pairs={{0,1},{1,2},{2,3},{3,4},{4,5},{5,6},{6,7},{7,0},{8,9},{9,10},{10,1... | collective-permute-start | bytes 897032 | tf_op jit(solution)/shard_map/ppermute | solution.py:479
  28.5 4.6 %collective-permute-start.3 = (f32[584,128]{1,0:T(8,128)S(1)}, f32[584,128]{1,0:T(8,128)S(1)}, u32[]{:S(2)}, u32[]{:S(2)}) collective-permute-start(f32[584,128]{1,0:T(8,128)S(1)} %get-tuple-element.20), channel_id=1, source_target_pairs={{1,0},{2,1},{3,2},{4,3},{5,4},{6,5},{7,6},{0,7},{9,8},{10,9},{11,1... | collective-permute-start | bytes 897032 | tf_op jit(solution)/shard_map/ppermute | solution.py:479
  33.1 2.2 %collective-permute-done.2.refs_1_.refs_0_ = f32[584,128]{1,0:T(8,128)S(1)} collective-permute-done((f32[584,128]{1,0:T(8,128)S(1)}, f32[584,128]{1,0:T(8,128)S(1)}, u32[]{:S(2)}, u32[]{:S(2)}) %collective-permute-start.2) | collective-permute-done | bytes 299040 | tf_op jit(solution)/shard_map/ppermute | solution.py:479
  35.3 1.5 %collective-permute-done.3.refs_3_.refs_2_ = f32[584,128]{1,0:T(8,128)S(1)} collective-permute-done((f32[584,128]{1,0:T(8,128)S(1)}, f32[584,128]{1,0:T(8,128)S(1)}, u32[]{:S(2)}, u32[]{:S(2)}) %collective-permute-start.3) | collective-permute-done | bytes 299040 | tf_op jit(solution)/shard_map/ppermute | solution.py:479
  36.8 11.5 %collective-permute-start.4 = (f32[528,128]{1,0:T(8,128)S(1)}, f32[528,128]{1,0:T(8,128)S(1)}, u32[]{:S(2)}, u32[]{:S(2)}) collective-permute-start(f32[528,128]{1,0:T(8,128)S(1)} %get-tuple-element.21), channel_id=1, source_target_pairs={{8,16},{24,32},{40,48},{56,64},{72,80},{88,96},{104,112},{120,128}... | collective-permute-start | bytes 811016 | tf_op jit(solution)/shard_map/ppermute | solution.py:486
  48.3 0.0 copy-start
  48.3 0.0 copy-start.1
  48.3 2.1 %collective-permute-start.5 = (f32[528,128]{1,0:T(8,128)S(1)}, f32[528,128]{1,0:T(8,128)S(1)}, u32[]{:S(2)}, u32[]{:S(2)}) collective-permute-start(f32[528,128]{1,0:T(8,128)S(1)} %get-tuple-element.22), channel_id=1, source_target_pairs={{0,8},{16,24},{32,40},{48,56},{64,72},{80,88},{96,104},{112,120},{... | collective-permute-start | bytes 811016 | tf_op jit(solution)/shard_map/ppermute | solution.py:486
  50.4 4.4 %collective-permute-start.8 = (f32[480,128]{1,0:T(8,128)S(1)}, f32[480,128]{1,0:T(8,128)S(1)}, u32[]{:S(2)}, u32[]{:S(2)}) collective-permute-start(f32[480,128]{1,0:T(8,128)S(1)} %get-tuple-element.27), channel_id=1, source_target_pairs={{8,16},{24,32},{40,48},{56,64},{72,80},{88,96},{104,112},{120,128}... | collective-permute-start | bytes 737288 | tf_op jit(solution)/shard_map/ppermute | solution.py:486
  54.8 1.9 %collective-permute-start.9 = (f32[480,128]{1,0:T(8,128)S(1)}, f32[480,128]{1,0:T(8,128)S(1)}, u32[]{:S(2)}, u32[]{:S(2)}) collective-permute-start(f32[480,128]{1,0:T(8,128)S(1)} %get-tuple-element.28), channel_id=1, source_target_pairs={{0,8},{16,24},{32,40},{48,56},{64,72},{80,88},{96,104},{112,120},{... | collective-permute-start | bytes 737288 | tf_op jit(solution)/shard_map/ppermute | solution.py:486
  56.7 0.0 copy-done
  56.7 0.0 copy-done.1
  56.7 0.1 matrices.1.refs_8_
  56.8 0.0 collective-permute-done.4.refs_6_
  56.9 0.0 collective-permute-done.5.refs_7_
  56.9 1.2 %right_side.1 = (f32[8,48,128]{2,1,0:T(8,128)S(1)}, f32[8,48,128]{2,1,0:T(8,128)S(1)}, f32[432,128]{1,0:T(8,128)S(1)}, f32[432,128]{1,0:T(8,128)S(1)}) custom-call(s32[1]{0:T(128)} %bitcast.refs_0_.parity_ref, f32[584,128]{1,0:T(8,128)S(1)} %collective-permute-done.2.refs_1_.refs_0_, f32[768,128]{1,0:T(8,128)S(1)} %get-tuple-element.19.refs_2_.refs_1_, ...), custom_call_target="tpu_custom_call" | custom-call | tf_op jit(solution)/shard_map/right_side/pallas_call | solution.py:30
  58.1 4.4 %collective-permute-start.6 = (f32[432,128]{1,0:T(8,128)S(1)}, f32[432,128]{1,0:T(8,128)S(1)}, u32[]{:S(2)}, u32[]{:S(2)}) collective-permute-start(f32[432,128]{1,0:T(8,128)S(1)} %get-tuple-element.25), channel_id=1, source_target_pairs={{8,16},{24,32},{40,48},{56,64},{72,80},{88,96},{104,112},{120,128}... | collective-permute-start | bytes 663560 | tf_op jit(solution)/shard_map/ppermute | solution.py:486
  62.5 1.9 %collective-permute-start.7 = (f32[432,128]{1,0:T(8,128)S(1)}, f32[432,128]{1,0:T(8,128)S(1)}, u32[]{:S(2)}, u32[]{:S(2)}) collective-permute-start(f32[432,128]{1,0:T(8,128)S(1)} %get-tuple-element.26), channel_id=1, source_target_pairs={{0,8},{16,24},{32,40},{48,56},{64,72},{80,88},{96,104},{112,120},{... | collective-permute-start | bytes 663560 | tf_op jit(solution)/shard_map/ppermute | solution.py:486
  64.4 0.0 collective-permute-done.8.refs_13_
  64.4 0.0 collective-permute-done.9.refs_14_
  64.4 1.7 %collective-permute-done.6.refs_11_ = f32[432,128]{1,0:T(8,128)S(1)} collective-permute-done((f32[432,128]{1,0:T(8,128)S(1)}, f32[432,128]{1,0:T(8,128)S(1)}, u32[]{:S(2)}, u32[]{:S(2)}) %collective-permute-start.6) | collective-permute-done | bytes 221216 | tf_op jit(solution)/shard_map/ppermute | solution.py:486
  66.1 0.0 collective-permute-done.7.refs_12_
  66.1 4.2 %first_image.1 = (f32[8,16,128]{2,1,0:T(8,128)S(1)}, f32[3,8,32,128]{3,2,1,0:T(8,128)S(1)}, f32[192,128]{1,0:T(8,128)S(1)}, f32[192,128]{1,0:T(8,128)S(1)}, f32[96,128]{1,0:T(8,128)}) custom-call(s32[1]{0:T(128)} %bitcast.refs_0_.parity_ref, f32[584,128]{1,0:T(8,128)S(1)} %collective-permute-done.2.refs_1_.refs_0_, ...), custom_call_target="tpu_custom_call" | custom-call | tf_op jit(solution)/shard_map/first_image/pallas_call | solution.py:30
  70.3 14.0 %all-to-all-start.1 = ((f32[24,4,128]{2,1,0:T(4,128)}), f32[24,4,128]{2,1,0:T(4,128)S(1)}, u32[]{:S(2)}, u32[]{:S(2)}) async-start(f32[24,4,128]{2,1,0:T(4,128)} %bitcast.5), calls=%async_computation.1 | async-start | bytes 98304 | tf_op jit(solution)/shard_map/all_to_all | solution.py:535
  84.3 3.5 %collective-permute-start.10 = (f32[192,128]{1,0:T(8,128)S(1)}, f32[192,128]{1,0:T(8,128)S(1)}, u32[]{:S(2)}, u32[]{:S(2)}) collective-permute-start(f32[192,128]{1,0:T(8,128)S(1)} %get-tuple-element.32), channel_id=1, source_target_pairs={{8,16},{24,32},{40,48},{56,64},{72,80},{88,96},{104,112},{120,128}... | collective-permute-start | bytes 294920 | tf_op jit(solution)/shard_map/ppermute | solution.py:486
  87.8 1.9 %collective-permute-start.11 = (f32[192,128]{1,0:T(8,128)S(1)}, f32[192,128]{1,0:T(8,128)S(1)}, u32[]{:S(2)}, u32[]{:S(2)}) collective-permute-start(f32[192,128]{1,0:T(8,128)S(1)} %get-tuple-element.33), channel_id=1, source_target_pairs={{0,8},{16,24},{32,40},{48,56},{64,72},{80,88},{96,104},{112,120},{... | collective-permute-start | bytes 294920 | tf_op jit(solution)/shard_map/ppermute | solution.py:486
  89.7 4.6 %all-to-all-done.1 = f32[24,4,128]{2,1,0:T(4,128)S(1)} async-done(((f32[24,4,128]{2,1,0:T(4,128)}), f32[24,4,128]{2,1,0:T(4,128)S(1)}, u32[]{:S(2)}, u32[]{:S(2)}) %all-to-all-start.1) | async-done | bytes 49184 | tf_op jit(solution)/shard_map/all_to_all | solution.py:535
  94.4 0.6 add.10
  95.0 7.5 %all-to-all-start.2 = ((f32[32,1,128]{2,1,0:T(1,128)}), f32[32,1,128]{2,1,0:T(1,128)S(1)}, u32[]{:S(2)}, u32[]{:S(2)}) async-start(f32[32,1,128]{2,1,0:T(1,128)} %bitcast.8), calls=%async_computation.2 | async-start | bytes 32768 | tf_op jit(solution)/shard_map/all_to_all | solution.py:541
  102.5 0.0 collective-permute-done.10.refs_11_
  102.5 0.0 collective-permute-done.11.refs_12_
  102.6 0.8 second_image.1.u_ref
  103.3 7.8 %all-to-all-done.2 = f32[32,1,128]{2,1,0:T(1,128)S(1)} async-done(((f32[32,1,128]{2,1,0:T(1,128)}), f32[32,1,128]{2,1,0:T(1,128)S(1)}, u32[]{:S(2)}, u32[]{:S(2)}) %all-to-all-start.2) | async-done | bytes 16416 | tf_op jit(solution)/shard_map/all_to_all | solution.py:541
  111.1 0.8 finish.1
  (2 shorter events, 0.1 us)
Async XLA Ops:
  4.1 7.8 %copy-start.2 = (f32[8,16,128]{2,1,0:T(8,128)S(1)}, f32[8,16,128]{2,1,0:T(8,128)}, u32[]{:S(2)}) copy-start(f32[8,16,128]{2,1,0:T(8,128)} %param.14) | copy-start | bytes 196612
  4.1 7.8 %copy-start.3 = (f32[8,16]{1,0:T(8,128)S(1)}, f32[8,16]{1,0:T(8,128)}, u32[]{:S(2)}) copy-start(f32[8,16]{1,0:T(8,128)} %diffusion_ref.1) | copy-start | bytes 1540
  4.1 22.0 %all-to-all-start = ((f32[8,136,128]{2,1,0:T(8,128)}), f32[8,136,128]{2,1,0:T(8,128)S(1)}, u32[]{:S(2)}, u32[]{:S(2)}) async-start(f32[8,136,128]{2,1,0:T(8,128)} %bucket.1), calls=%async_computation | async-start | bytes 1114112 | tf_op jit(solution)/shard_map/all_to_all | solution.py:504
  12.0 9.3 %collective-permute-start.1 = (f32[144,128]{1,0:T(8,128)S(1)}, f32[144,128]{1,0:T(8,128)S(1)}, u32[]{:S(2)}, u32[]{:S(2)}) collective-permute-start(f32[144,128]{1,0:T(8,128)S(1)} %fixed.1.refs_5_.refs_4_), channel_id=1, source_target_pairs={{1,0},{2,1},{3,2},{4,3},{5,4},{6,5},{7,6},{0,7},{9,8},{10,9},{11,1... | collective-permute-start | bytes 221192 | tf_op jit(solution)/shard_map/ppermute | solution.py:479
  16.6 9.5 %collective-permute-start = (f32[144,128]{1,0:T(8,128)S(1)}, f32[144,128]{1,0:T(8,128)S(1)}, u32[]{:S(2)}, u32[]{:S(2)}) collective-permute-start(f32[144,128]{1,0:T(8,128)S(1)} %fixed.1.refs_5_.refs_4_), channel_id=1, source_target_pairs={{0,1},{1,2},{2,3},{3,4},{4,5},{5,6},{6,7},{7,0},{8,9},{9,10},{10,1... | collective-permute-start | bytes 221192 | tf_op jit(solution)/shard_map/ppermute | solution.py:479
  26.6 8.7 %collective-permute-start.2 = (f32[584,128]{1,0:T(8,128)S(1)}, f32[584,128]{1,0:T(8,128)S(1)}, u32[]{:S(2)}, u32[]{:S(2)}) collective-permute-start(f32[584,128]{1,0:T(8,128)S(1)} %get-tuple-element.18), channel_id=1, source_target_pairs={{0,1},{1,2},{2,3},{3,4},{4,5},{5,6},{6,7},{7,0},{8,9},{9,10},{10,1... | collective-permute-start | bytes 897032 | tf_op jit(solution)/shard_map/ppermute | solution.py:479
  28.5 8.3 %collective-permute-start.3 = (f32[584,128]{1,0:T(8,128)S(1)}, f32[584,128]{1,0:T(8,128)S(1)}, u32[]{:S(2)}, u32[]{:S(2)}) collective-permute-start(f32[584,128]{1,0:T(8,128)S(1)} %get-tuple-element.20), channel_id=1, source_target_pairs={{1,0},{2,1},{3,2},{4,3},{5,4},{6,5},{7,6},{0,7},{9,8},{10,9},{11,1... | collective-permute-start | bytes 897032 | tf_op jit(solution)/shard_map/ppermute | solution.py:479
  36.8 20.1 %collective-permute-start.4 = (f32[528,128]{1,0:T(8,128)S(1)}, f32[528,128]{1,0:T(8,128)S(1)}, u32[]{:S(2)}, u32[]{:S(2)}) collective-permute-start(f32[528,128]{1,0:T(8,128)S(1)} %get-tuple-element.21), channel_id=1, source_target_pairs={{8,16},{24,32},{40,48},{56,64},{72,80},{88,96},{104,112},{120,128}... | collective-permute-start | bytes 811016 | tf_op jit(solution)/shard_map/ppermute | solution.py:486
  48.3 8.5 %copy-start = (f32[128,128]{1,0:T(8,128)S(1)}, f32[128,128]{1,0:T(8,128)}, u32[]{:S(2)}) copy-start(f32[128,128]{1,0:T(8,128)} %factor_ref.1) | copy-start | bytes 196612
  48.3 8.5 %copy-start.1 = (f32[128,128]{1,0:T(8,128)S(1)}, f32[128,128]{1,0:T(8,128)}, u32[]{:S(2)}) copy-start(f32[128,128]{1,0:T(8,128)} %mixing_ref.1) | copy-start | bytes 196612
  48.3 8.6 %collective-permute-start.5 = (f32[528,128]{1,0:T(8,128)S(1)}, f32[528,128]{1,0:T(8,128)S(1)}, u32[]{:S(2)}, u32[]{:S(2)}) collective-permute-start(f32[528,128]{1,0:T(8,128)S(1)} %get-tuple-element.22), channel_id=1, source_target_pairs={{0,8},{16,24},{32,40},{48,56},{64,72},{80,88},{96,104},{112,120},{... | collective-permute-start | bytes 811016 | tf_op jit(solution)/shard_map/ppermute | solution.py:486
  50.4 14.0 %collective-permute-start.8 = (f32[480,128]{1,0:T(8,128)S(1)}, f32[480,128]{1,0:T(8,128)S(1)}, u32[]{:S(2)}, u32[]{:S(2)}) collective-permute-start(f32[480,128]{1,0:T(8,128)S(1)} %get-tuple-element.27), channel_id=1, source_target_pairs={{8,16},{24,32},{40,48},{56,64},{72,80},{88,96},{104,112},{120,128}... | collective-permute-start | bytes 737288 | tf_op jit(solution)/shard_map/ppermute | solution.py:486
  54.8 9.7 %collective-permute-start.9 = (f32[480,128]{1,0:T(8,128)S(1)}, f32[480,128]{1,0:T(8,128)S(1)}, u32[]{:S(2)}, u32[]{:S(2)}) collective-permute-start(f32[480,128]{1,0:T(8,128)S(1)} %get-tuple-element.28), channel_id=1, source_target_pairs={{0,8},{16,24},{32,40},{48,56},{64,72},{80,88},{96,104},{112,120},{... | collective-permute-start | bytes 737288 | tf_op jit(solution)/shard_map/ppermute | solution.py:486
  58.1 8.0 %collective-permute-start.6 = (f32[432,128]{1,0:T(8,128)S(1)}, f32[432,128]{1,0:T(8,128)S(1)}, u32[]{:S(2)}, u32[]{:S(2)}) collective-permute-start(f32[432,128]{1,0:T(8,128)S(1)} %get-tuple-element.25), channel_id=1, source_target_pairs={{8,16},{24,32},{40,48},{56,64},{72,80},{88,96},{104,112},{120,128}... | collective-permute-start | bytes 663560 | tf_op jit(solution)/shard_map/ppermute | solution.py:486
  62.5 3.6 %collective-permute-start.7 = (f32[432,128]{1,0:T(8,128)S(1)}, f32[432,128]{1,0:T(8,128)S(1)}, u32[]{:S(2)}, u32[]{:S(2)}) collective-permute-start(f32[432,128]{1,0:T(8,128)S(1)} %get-tuple-element.26), channel_id=1, source_target_pairs={{0,8},{16,24},{32,40},{48,56},{64,72},{80,88},{96,104},{112,120},{... | collective-permute-start | bytes 663560 | tf_op jit(solution)/shard_map/ppermute | solution.py:486
  70.3 24.1 %all-to-all-start.1 = ((f32[24,4,128]{2,1,0:T(4,128)}), f32[24,4,128]{2,1,0:T(4,128)S(1)}, u32[]{:S(2)}, u32[]{:S(2)}) async-start(f32[24,4,128]{2,1,0:T(4,128)} %bitcast.5), calls=%async_computation.1 | async-start | bytes 98304 | tf_op jit(solution)/shard_map/all_to_all | solution.py:535
  84.3 18.3 %collective-permute-start.10 = (f32[192,128]{1,0:T(8,128)S(1)}, f32[192,128]{1,0:T(8,128)S(1)}, u32[]{:S(2)}, u32[]{:S(2)}) collective-permute-start(f32[192,128]{1,0:T(8,128)S(1)} %get-tuple-element.32), channel_id=1, source_target_pairs={{8,16},{24,32},{40,48},{56,64},{72,80},{88,96},{104,112},{120,128}... | collective-permute-start | bytes 294920 | tf_op jit(solution)/shard_map/ppermute | solution.py:486
  87.8 14.7 %collective-permute-start.11 = (f32[192,128]{1,0:T(8,128)S(1)}, f32[192,128]{1,0:T(8,128)S(1)}, u32[]{:S(2)}, u32[]{:S(2)}) collective-permute-start(f32[192,128]{1,0:T(8,128)S(1)} %get-tuple-element.33), channel_id=1, source_target_pairs={{0,8},{16,24},{32,40},{48,56},{64,72},{80,88},{96,104},{112,120},{... | collective-permute-start | bytes 294920 | tf_op jit(solution)/shard_map/ppermute | solution.py:486
  95.0 16.1 %all-to-all-start.2 = ((f32[32,1,128]{2,1,0:T(1,128)}), f32[32,1,128]{2,1,0:T(1,128)S(1)}, u32[]{:S(2)}, u32[]{:S(2)}) async-start(f32[32,1,128]{2,1,0:T(1,128)} %bitcast.8), calls=%async_computation.2 | async-start | bytes 32768 | tf_op jit(solution)/shard_map/all_to_all | solution.py:541

commit v7 on v6

--- a/solution.py
+++ b/solution.py
@@ -99,7 +99,7 @@
     marks = jnp.concatenate(
         [jnp.where(here, time, 0.0), jnp.where(here, columns_ref[...].astype(F32), 0.0)], axis=0
     )
-    target = rank_col + (CAP * parity_ref[0]).astype(F32)
+    target = rank_col + (CAP * (parity_ref[0] >> 1)).astype(F32)
     spread = jnp.where(lax.broadcasted_iota(jnp.int32, (SLOTS, L), 1).astype(F32) == target, 1.0, 0.0)
     codes = dot(marks.astype(BF16), spread.astype(BF16))
     codes = CELLS * codes[:8] + codes[8:]
@@ -126,7 +126,7 @@
 PACKED = SIZE + STEPS * ROWS * EDGE
 
 
-def tile_kernel(received_ref, fixed_left_ref, fixed_right_ref, own_ref, to_left_ref, to_right_ref):
+def tile_kernel(received_ref, fixed_first_ref, fixed_second_ref, parity_ref, own_ref, first_ref, second_ref):
     ones, data = [], []
     cell = lax.broadcasted_iota(jnp.int32, (SIZE, L), 0)
     for j in range(4):
@@ -139,49 +139,58 @@
     total = dot(jnp.concatenate(ones, axis=1), jnp.concatenate(data, axis=0))
     forcing = total[:, :L] + total[:, L : 2 * L]
     weights = total[:, 2 * L : 3 * L] + total[:, 3 * L :]
-    for ref in (own_ref, to_left_ref, to_right_ref):
+    for ref in (own_ref, first_ref, second_ref):
         ref[:SIZE] = forcing
     own_ref[SIZE:] = weights
+    even = (parity_ref[0] >> 1) == 0
     for k in range(STEPS * ROWS):
         to = pl.ds(SIZE + k * EDGE, EDGE)
-        to_left_ref[to] = weights[k * COLS : k * COLS + EDGE]
-        to_right_ref[to] = weights[k * COLS + EDGE : (k + 1) * COLS]
+        left, right = weights[k * COLS : k * COLS + EDGE], weights[k * COLS + EDGE : (k + 1) * COLS]
+        first_ref[to] = jnp.where(even, right, left)
+        second_ref[to] = jnp.where(even, left, right)
     for r in range(ROWS):
-        first = (STEPS - 1) * CELLS + r * COLS
-        to_left_ref[PACKED + r : PACKED + r + 1] = weights[first + EDGE : first + EDGE + 1]
-        to_right_ref[PACKED + r : PACKED + r + 1] = weights[first + EDGE - 1 : first + EDGE]
-
-
-def wide(refs, start):
-    return jnp.concatenate([ref[start : start + COLS] for ref in refs], axis=0)
+        start = (STEPS - 1) * CELLS + r * COLS + EDGE
+        left, right = weights[start : start + 1], weights[start - 1 : start]
+        first_ref[PACKED + r : PACKED + r + 1] = jnp.where(even, right, left)
+        second_ref[PACKED + r : PACKED + r + 1] = jnp.where(even, left, right)
 
 
 class Tile:
-    def __init__(self, left_ref, own_ref, right_ref, fixed_left_ref, fixed_ref, fixed_right_ref):
-        self.left, self.own, self.right = left_ref, own_ref, right_ref
-        self.fixed = (fixed_left_ref, fixed_ref, fixed_right_ref)
+    def __init__(self, parity_ref, first_ref, own_ref, second_ref, fixed_first_ref, fixed_ref, fixed_second_ref):
+        self.even = (parity_ref[0] >> 1) == 0
+        self.refs = (first_ref, own_ref, second_ref)
+        self.fixed = (fixed_first_ref, fixed_ref, fixed_second_ref)
+
+    def beside(self, refs, rows):
+        first, second = refs[0][rows], refs[2][rows]
+        return jnp.where(self.even, second, first), jnp.where(self.even, first, second)
+
+    def wide(self, refs, start):
+        rows = pl.ds(start, COLS)
+        left, right = self.beside(refs, rows)
+        return jnp.concatenate([left, refs[1][rows], right], axis=0)
 
     def forcing(self, t, r):
-        return wide((self.left, self.own, self.right), t * CELLS + r * COLS)
+        return self.wide(self.refs, t * CELLS + r * COLS)
 
     def inner_weights(self, t, r):
         start = SIZE + t * CELLS + r * COLS
-        packed = pl.ds(SIZE + (t * ROWS + r) * EDGE, EDGE)
-        return [self.left[packed], self.own[start : start + COLS], self.right[packed]]
+        left, right = self.beside(self.refs, pl.ds(SIZE + (t * ROWS + r) * EDGE, EDGE))
+        return [left, self.refs[1][start : start + COLS], right]
 
     def weights(self, t, r):
         inner = self.inner_weights(t, r)
         if t < STEPS - 1:
             edges = [jnp.zeros((EDGE, L), F32)] * 2
         else:
-            edges = [jnp.broadcast_to(ref[PACKED + r : PACKED + r + 1], (EDGE, L)) for ref in (self.left, self.right)]
+            edges = [jnp.broadcast_to(row, (EDGE, L)) for row in self.beside(self.refs, pl.ds(PACKED + r, 1))]
         return jnp.concatenate([edges[0], *inner, edges[1]], axis=0)
 
     def std(self, r):
-        return wide(self.fixed, r * COLS)
+        return self.wide(self.fixed, r * COLS)
 
     def turned(self):
-        return wide(self.fixed, CELLS)
+        return self.wide(self.fixed, CELLS)
 
 
 def inside(row):
@@ -218,7 +227,7 @@
 
 class Sides:
     def __init__(self, parity_ref, chip_ref, core_ref, found):
-        self.even = parity_ref[0] == 0
+        self.even = (parity_ref[0] & 1) == 0
         self.core_ref, self.chip_ref, self.found = core_ref, chip_ref, found
 
     def send(self, kind, h, row):
@@ -235,7 +244,7 @@
 
 
 def sides_kernel(*refs):
-    tile, sides = Tile(*refs[1:7]), Sides(refs[0], *refs[7:], FIRST)
+    tile, sides = Tile(*refs[:7]), Sides(refs[0], *refs[7:], FIRST)
     for kind, h in FIRST:
         if kind == "std":
             row = tile.std
@@ -247,7 +256,7 @@
 
 
 def weights_kernel(*refs):
-    tile, sides = Tile(*refs[1:7]), Sides(refs[0], *refs[7:], WEIGHTS)
+    tile, sides = Tile(*refs[:7]), Sides(refs[0], *refs[7:], WEIGHTS)
     for kind, h in WEIGHTS:
         sides.send(kind, h, lambda r: jnp.concatenate(tile.inner_weights(kind[1], r), axis=0))
 
@@ -343,7 +352,7 @@
 
 
 def right_side_kernel(parity_ref, *refs):
-    tile, sides, m_ref = Tile(*refs[:6]), Sides(parity_ref, *refs[6:8], FIRST), refs[8]
+    tile, sides, m_ref = Tile(parity_ref, *refs[:6]), Sides(parity_ref, *refs[6:8], FIRST), refs[8]
     b_ref, y_ref = refs[9:11]
     out = Sides(parity_ref, *refs[11:13], SECOND)
     field = Field(WIDE, STEPS + 1, *refs[13:17], m_ref)
@@ -374,7 +383,7 @@
 
 
 def first_image_kernel(parity_ref, *refs):
-    tile, sides, m_ref = Tile(*refs[:6]), Sides(parity_ref, *refs[6:8], FIRST), refs[8]
+    tile, sides, m_ref = Tile(parity_ref, *refs[:6]), Sides(parity_ref, *refs[6:8], FIRST), refs[8]
     b_ref, y_ref = refs[9:11]
     more, forced = Sides(parity_ref, *refs[11:13], SECOND), Sides(parity_ref, *refs[13:15], WEIGHTS)
     q_ref, g_ref = refs[15:17]
@@ -431,7 +440,7 @@
 
 
 def second_image_kernel(parity_ref, *refs):
-    tile, sides, m_ref = Tile(*refs[:6]), Sides(parity_ref, *refs[6:8], FIRST), refs[8]
+    tile, sides, m_ref = Tile(parity_ref, *refs[:6]), Sides(parity_ref, *refs[6:8], FIRST), refs[8]
     q_ref, g_ref = refs[9:11]
     more = Sides(parity_ref, *refs[11:13], THIRD)
     u_ref = refs[13]
@@ -472,11 +481,11 @@
         residual_ref[r] = b - along_b * q + along_q * u_ref[r]
 
 
-def exchange(to_before, to_after):
+def beside(first, second):
     size = lax.axis_size("lon")
-    up = [(i, (i + 1) % size) for i in range(size)]
-    down = [(j, i) for i, j in up]
-    return lax.ppermute(to_after, "lon", up), lax.ppermute(to_before, "lon", down)
+    pairs = [[(i, (i + 1) % size) for i in range(start, size, 2)] for start in (0, 1)]
+    both = [p + [(j, i) for i, j in p] for p in pairs]
+    return lax.ppermute(first, "lon", both[0]), lax.ppermute(second, "lon", both[1])
 
 
 def swap(chip, core):
@@ -489,8 +498,7 @@
 def shards(
     departures, obs_weight, obs_columns, obs_owner, obs_counts, background_std, diffusion, level_factor, model_mixing
 ):
-    parity = (lax.axis_index("lon") % 2).astype(jnp.int32).reshape(1)
-    side_of = (lax.axis_index("lat") % 2).astype(jnp.int32).reshape(1)
+    side_of = (lax.axis_index("lat") % 2 + 2 * (lax.axis_index("lon") % 2)).astype(jnp.int32).reshape(1)
     slots = pltpu.VMEM((SLOTS, L), F32)
     buckets = call(
         bucket_kernel,
@@ -500,17 +508,17 @@
         smem=(4, 5),
         hbm=(0, 1),
         vmem=60,
-    )(departures, obs_weight, obs_columns.reshape(1, SLOTS), obs_owner.reshape(1, SLOTS), obs_counts, parity)
+    )(departures, obs_weight, obs_columns.reshape(1, SLOTS), obs_owner.reshape(1, SLOTS), obs_counts, side_of)
     received = lax.all_to_all(buckets, "lon", 0, 0)
     mats = call(matrices_kernel, "matrices", shape(4, 2 * L, 2 * L, dtype=BF16))(level_factor, model_mixing)
     fixed = call(fixed_kernel, "fixed", shape(CELLS + COLS, L))(background_std.reshape(CELLS, L), diffusion)
-    fixed_left, fixed_right = exchange(fixed, fixed)
-    beside = shape(PACKED + ROWS, L)
-    tile, to_left, to_right = call(tile_kernel, "tile", (shape(2 * SIZE, L), beside, beside))(
-        received, fixed_left, fixed_right
+    fixed_first, fixed_second = beside(fixed, fixed)
+    edge = shape(PACKED + ROWS, L)
+    tile, first, second = call(tile_kernel, "tile", (shape(2 * SIZE, L), edge, edge), smem=(3,))(
+        received, fixed_first, fixed_second, side_of
     )
-    left, right = exchange(to_left, to_right)
-    refs = (left, tile, right, fixed_left, fixed, fixed_right)
+    first, second = beside(first, second)
+    refs = (first, tile, second, fixed_first, fixed, fixed_second)
     side = shape(FIRST_ROWS, L)
     below, above = swap(*call(sides_kernel, "sides", (side, side), smem=(0,))(side_of, *refs))
     side = shape(WEIGHTS_ROWS, L)

time: 113 us -> 114 us (level)
    ppermute x4, waiting for transfers between devices: 11.3 us -> 9.07 us  [the longest x2 5.89 us: beside(): lax.ppermute(second, 'lon', both[1])]
    all_to_all x1, waiting for transfers between devices: 0.01 us -> 2.07 us  [shards(): received = lax.all_to_all(buckets, 'lon', 0, 0)]
    ppermute x4, starting transfers between devices: 23.8 us -> 25.4 us  [swap(): lax.ppermute(chip, 'lat', both[1])]
  transfers between devices with their start and end apart: 15 -> 15, of which waited for: 7 -> 8; matrix products, arithmetic and copies ran while one was open for 0% -> 0% of each run, Pallas kernels for 3% -> 3%
where the time goes in v7:
time: 114 us; the launch traced here: 113 us
  starting transfers between devices  74.9 us (66%)
  waiting for transfers between devices  25.2 us (22%)
  Pallas kernels  11.2 us (10%)
  between operations  1.57 us (1%)
    ppermute x4, starting transfers between devices, swap(): lax.ppermute(chip, 'lat', both[1])  25.4 us
    all_to_all x1, starting transfers between devices, shards(): sums = lax.all_to_all(sums, 'lat', 0, 0, axis_index_groups=near, tiled=True)  14 us
    pallas_call x11, Pallas kernels, run(): pl.pallas_call(kernel, name=name, out_shape=outs, in_specs=specs, out_spe...  11.2 us
    ppermute x2, starting transfers between devices, beside(): lax.ppermute(second, 'lon', both[1])  8.18 us
    ppermute x4, starting transfers between devices, swap(): lax.ppermute(core, 'lat', both[0])  7.81 us
    all_to_all x1, starting transfers between devices, shards(): received = lax.all_to_all(buckets, 'lon', 0, 0)  7.79 us
    all_to_all x1, waiting for transfers between devices, shards(): lax.all_to_all(sums, ('lat', 'lon'), 0, 0, axis_index_groups=far, tiled=T...  7.76 us
    all_to_all x1, starting transfers between devices, shards(): lax.all_to_all(sums, ('lat', 'lon'), 0, 0, axis_index_groups=far, tiled=T...  7.61 us
  transfers between devices with their start and end apart: 15, of which 8 were waited for; matrix products, arithmetic and copies ran while one was open for 0% of the time, Pallas kernels for 3%

profile of v7, /device:TPU:1, one launch (start us, length us, event | category | flops | bytes accessed | tf_op | source)
XLA Modules:
  0.0 112.8 jit_solution(10681636766446341928)
XLA Ops:
  1.3 2.8 %bucket.1 = f32[8,136,128]{2,1,0:T(8,128)} custom-call(f32[256,128]{1,0:T(8,128)} %departures_hbm.1, f32[256,128]{1,0:T(8,128)} %weight_hbm.1, s32[1,256]{1,0:T(1,128)} %bitcast.13, s32[1,256]{1,0:T(1,128)} %bitcast.14, s32[1]{0:T(128)S(6)} %copy.12.counts_ref, s32[1]{0:T(128)} %bitcast.parity_ref.refs_0_), custom_call_target="tpu_custom_call" | custom-call | tf_op jit(solution)/shard_map/bucket/pallas_call | solution.py:30
  4.1 0.0 copy-start.2
  4.1 0.0 copy-start.3
  4.2 7.8 %all-to-all-start = ((f32[8,136,128]{2,1,0:T(8,128)}), f32[8,136,128]{2,1,0:T(8,128)S(1)}, u32[]{:S(2)}, u32[]{:S(2)}) async-start(f32[8,136,128]{2,1,0:T(8,128)} %bucket.1), calls=%async_computation | async-start | bytes 1114112 | tf_op jit(solution)/shard_map/all_to_all | solution.py:512
  11.9 0.0 copy-done.2
  11.9 0.0 copy-done.3
  12.0 0.1 fixed.1.refs_5_.refs_4_
  12.1 4.6 %collective-permute-start.1 = (f32[144,128]{1,0:T(8,128)S(1)}, f32[144,128]{1,0:T(8,128)S(1)}, u32[]{:S(2)}, u32[]{:S(2)}) collective-permute-start(f32[144,128]{1,0:T(8,128)S(1)} %fixed.1.refs_5_.refs_4_), channel_id=1, source_target_pairs={{1,2},{3,4},{5,6},{7,0},{2,1},{4,3},{6,5},{0,7},{9,10},{11,12},{13... | collective-permute-start | bytes 221192 | tf_op jit(solution)/shard_map/ppermute | solution.py:488
  16.6 1.9 %collective-permute-start = (f32[144,128]{1,0:T(8,128)S(1)}, f32[144,128]{1,0:T(8,128)S(1)}, u32[]{:S(2)}, u32[]{:S(2)}) collective-permute-start(f32[144,128]{1,0:T(8,128)S(1)} %fixed.1.refs_5_.refs_4_), channel_id=1, source_target_pairs={{0,1},{2,3},{4,5},{6,7},{1,0},{3,2},{5,4},{7,6},{8,9},{10,11},{12,... | collective-permute-start | bytes 221192 | tf_op jit(solution)/shard_map/ppermute | solution.py:488
  18.6 2.5 %collective-permute-done.1.fixed_second_ref.refs_6_.refs_5_ = f32[144,128]{1,0:T(8,128)S(1)} collective-permute-done((f32[144,128]{1,0:T(8,128)S(1)}, f32[144,128]{1,0:T(8,128)S(1)}, u32[]{:S(2)}, u32[]{:S(2)}) %collective-permute-start.1) | collective-permute-done | bytes 73760 | tf_op jit(solution)/shard_map/ppermute | solution.py:488
  21.0 1.5 %collective-permute-done.fixed_first_ref.refs_4_.refs_3_ = f32[144,128]{1,0:T(8,128)S(1)} collective-permute-done((f32[144,128]{1,0:T(8,128)S(1)}, f32[144,128]{1,0:T(8,128)S(1)}, u32[]{:S(2)}, u32[]{:S(2)}) %collective-permute-start) | collective-permute-done | bytes 73760 | tf_op jit(solution)/shard_map/ppermute | solution.py:488
  22.5 2.1 %all-to-all-done.received_ref = f32[8,136,128]{2,1,0:T(8,128)S(1)} async-done(((f32[8,136,128]{2,1,0:T(8,128)}), f32[8,136,128]{2,1,0:T(8,128)S(1)}, u32[]{:S(2)}, u32[]{:S(2)}) %all-to-all-start) | async-done | bytes 557088 | tf_op jit(solution)/shard_map/all_to_all | solution.py:512
  24.6 0.4 tile.1
  25.0 2.2 %collective-permute-start.2 = (f32[584,128]{1,0:T(8,128)S(1)}, f32[584,128]{1,0:T(8,128)S(1)}, u32[]{:S(2)}, u32[]{:S(2)}) collective-permute-start(f32[584,128]{1,0:T(8,128)S(1)} %get-tuple-element.18), channel_id=1, source_target_pairs={{0,1},{2,3},{4,5},{6,7},{1,0},{3,2},{5,4},{7,6},{8,9},{10,11},{12,... | collective-permute-start | bytes 897032 | tf_op jit(solution)/shard_map/ppermute | solution.py:488
  27.2 3.6 %collective-permute-start.3 = (f32[584,128]{1,0:T(8,128)S(1)}, f32[584,128]{1,0:T(8,128)S(1)}, u32[]{:S(2)}, u32[]{:S(2)}) collective-permute-start(f32[584,128]{1,0:T(8,128)S(1)} %get-tuple-element.20), channel_id=1, source_target_pairs={{1,2},{3,4},{5,6},{7,0},{2,1},{4,3},{6,5},{0,7},{9,10},{11,12},{13... | collective-permute-start | bytes 897032 | tf_op jit(solution)/shard_map/ppermute | solution.py:488
  30.8 1.7 %collective-permute-done.2.refs_1_.refs_0_ = f32[584,128]{1,0:T(8,128)S(1)} collective-permute-done((f32[584,128]{1,0:T(8,128)S(1)}, f32[584,128]{1,0:T(8,128)S(1)}, u32[]{:S(2)}, u32[]{:S(2)}) %collective-permute-start.2) | collective-permute-done | bytes 299040 | tf_op jit(solution)/shard_map/ppermute | solution.py:488
  32.5 3.4 %collective-permute-done.3.refs_3_.refs_2_ = f32[584,128]{1,0:T(8,128)S(1)} collective-permute-done((f32[584,128]{1,0:T(8,128)S(1)}, f32[584,128]{1,0:T(8,128)S(1)}, u32[]{:S(2)}, u32[]{:S(2)}) %collective-permute-start.3) | collective-permute-done | bytes 299040 | tf_op jit(solution)/shard_map/ppermute | solution.py:488
  36.0 13.1 %collective-permute-start.4 = (f32[528,128]{1,0:T(8,128)S(1)}, f32[528,128]{1,0:T(8,128)S(1)}, u32[]{:S(2)}, u32[]{:S(2)}) collective-permute-start(f32[528,128]{1,0:T(8,128)S(1)} %get-tuple-element.21), channel_id=1, source_target_pairs={{8,16},{24,32},{40,48},{56,64},{72,80},{88,96},{104,112},{120,128}... | collective-permute-start | bytes 811016 | tf_op jit(solution)/shard_map/ppermute | solution.py:495
  49.0 0.0 copy-start
  49.0 0.0 copy-start.1
  49.0 2.1 %collective-permute-start.5 = (f32[528,128]{1,0:T(8,128)S(1)}, f32[528,128]{1,0:T(8,128)S(1)}, u32[]{:S(2)}, u32[]{:S(2)}) collective-permute-start(f32[528,128]{1,0:T(8,128)S(1)} %get-tuple-element.22), channel_id=1, source_target_pairs={{0,8},{16,24},{32,40},{48,56},{64,72},{80,88},{96,104},{112,120},{... | collective-permute-start | bytes 811016 | tf_op jit(solution)/shard_map/ppermute | solution.py:495
  51.2 4.4 %collective-permute-start.8 = (f32[480,128]{1,0:T(8,128)S(1)}, f32[480,128]{1,0:T(8,128)S(1)}, u32[]{:S(2)}, u32[]{:S(2)}) collective-permute-start(f32[480,128]{1,0:T(8,128)S(1)} %get-tuple-element.27), channel_id=1, source_target_pairs={{8,16},{24,32},{40,48},{56,64},{72,80},{88,96},{104,112},{120,128}... | collective-permute-start | bytes 737288 | tf_op jit(solution)/shard_map/ppermute | solution.py:495
  55.6 1.9 %collective-permute-start.9 = (f32[480,128]{1,0:T(8,128)S(1)}, f32[480,128]{1,0:T(8,128)S(1)}, u32[]{:S(2)}, u32[]{:S(2)}) collective-permute-start(f32[480,128]{1,0:T(8,128)S(1)} %get-tuple-element.28), channel_id=1, source_target_pairs={{0,8},{16,24},{32,40},{48,56},{64,72},{80,88},{96,104},{112,120},{... | collective-permute-start | bytes 737288 | tf_op jit(solution)/shard_map/ppermute | solution.py:495
  57.5 0.0 copy-done
  57.5 0.0 copy-done.1
  57.5 0.1 matrices.1.refs_8_
  57.6 0.0 collective-permute-done.4.refs_6_
  57.6 0.0 collective-permute-done.5.refs_7_
  57.6 1.2 %right_side.1 = (f32[8,48,128]{2,1,0:T(8,128)S(1)}, f32[8,48,128]{2,1,0:T(8,128)S(1)}, f32[432,128]{1,0:T(8,128)S(1)}, f32[432,128]{1,0:T(8,128)S(1)}) custom-call(s32[1]{0:T(128)} %bitcast.parity_ref.refs_0_, f32[584,128]{1,0:T(8,128)S(1)} %collective-permute-done.2.refs_1_.refs_0_, f32[768,128]{1,0:T(8,128)S(1)} %get-tuple-element.19.refs_2_.refs_1_, ...), custom_call_target="tpu_custom_call" | custom-call | tf_op jit(solution)/shard_map/right_side/pallas_call | solution.py:30
  58.9 4.4 %collective-permute-start.6 = (f32[432,128]{1,0:T(8,128)S(1)}, f32[432,128]{1,0:T(8,128)S(1)}, u32[]{:S(2)}, u32[]{:S(2)}) collective-permute-start(f32[432,128]{1,0:T(8,128)S(1)} %get-tuple-element.25), channel_id=1, source_target_pairs={{8,16},{24,32},{40,48},{56,64},{72,80},{88,96},{104,112},{120,128}... | collective-permute-start | bytes 663560 | tf_op jit(solution)/shard_map/ppermute | solution.py:495
  63.3 1.9 %collective-permute-start.7 = (f32[432,128]{1,0:T(8,128)S(1)}, f32[432,128]{1,0:T(8,128)S(1)}, u32[]{:S(2)}, u32[]{:S(2)}) collective-permute-start(f32[432,128]{1,0:T(8,128)S(1)} %get-tuple-element.26), channel_id=1, source_target_pairs={{0,8},{16,24},{32,40},{48,56},{64,72},{80,88},{96,104},{112,120},{... | collective-permute-start | bytes 663560 | tf_op jit(solution)/shard_map/ppermute | solution.py:495
  65.2 0.0 collective-permute-done.8.refs_13_
  65.2 0.0 collective-permute-done.9.refs_14_
  65.2 1.7 %collective-permute-done.6.refs_11_ = f32[432,128]{1,0:T(8,128)S(1)} collective-permute-done((f32[432,128]{1,0:T(8,128)S(1)}, f32[432,128]{1,0:T(8,128)S(1)}, u32[]{:S(2)}, u32[]{:S(2)}) %collective-permute-start.6) | collective-permute-done | bytes 221216 | tf_op jit(solution)/shard_map/ppermute | solution.py:495
  66.9 0.0 collective-permute-done.7.refs_12_
  66.9 4.3 %first_image.1 = (f32[8,16,128]{2,1,0:T(8,128)S(1)}, f32[3,8,32,128]{3,2,1,0:T(8,128)S(1)}, f32[192,128]{1,0:T(8,128)S(1)}, f32[192,128]{1,0:T(8,128)S(1)}, f32[96,128]{1,0:T(8,128)}) custom-call(s32[1]{0:T(128)} %bitcast.parity_ref.refs_0_, f32[584,128]{1,0:T(8,128)S(1)} %collective-permute-done.2.refs_1_.refs_0_, ...), custom_call_target="tpu_custom_call" | custom-call | tf_op jit(solution)/shard_map/first_image/pallas_call | solution.py:30
  71.1 14.0 %all-to-all-start.1 = ((f32[24,4,128]{2,1,0:T(4,128)}), f32[24,4,128]{2,1,0:T(4,128)S(1)}, u32[]{:S(2)}, u32[]{:S(2)}) async-start(f32[24,4,128]{2,1,0:T(4,128)} %bitcast.4), calls=%async_computation.1 | async-start | bytes 98304 | tf_op jit(solution)/shard_map/all_to_all | solution.py:543
  85.1 3.5 %collective-permute-start.10 = (f32[192,128]{1,0:T(8,128)S(1)}, f32[192,128]{1,0:T(8,128)S(1)}, u32[]{:S(2)}, u32[]{:S(2)}) collective-permute-start(f32[192,128]{1,0:T(8,128)S(1)} %get-tuple-element.32), channel_id=1, source_target_pairs={{8,16},{24,32},{40,48},{56,64},{72,80},{88,96},{104,112},{120,128}... | collective-permute-start | bytes 294920 | tf_op jit(solution)/shard_map/ppermute | solution.py:495
  88.7 1.9 %collective-permute-start.11 = (f32[192,128]{1,0:T(8,128)S(1)}, f32[192,128]{1,0:T(8,128)S(1)}, u32[]{:S(2)}, u32[]{:S(2)}) collective-permute-start(f32[192,128]{1,0:T(8,128)S(1)} %get-tuple-element.33), channel_id=1, source_target_pairs={{0,8},{16,24},{32,40},{48,56},{64,72},{80,88},{96,104},{112,120},{... | collective-permute-start | bytes 294920 | tf_op jit(solution)/shard_map/ppermute | solution.py:495
  90.6 4.6 %all-to-all-done.1 = f32[24,4,128]{2,1,0:T(4,128)S(1)} async-done(((f32[24,4,128]{2,1,0:T(4,128)}), f32[24,4,128]{2,1,0:T(4,128)S(1)}, u32[]{:S(2)}, u32[]{:S(2)}) %all-to-all-start.1) | async-done | bytes 49184 | tf_op jit(solution)/shard_map/all_to_all | solution.py:543
  95.2 0.6 add.14
  95.8 7.6 %all-to-all-start.2 = ((f32[32,1,128]{2,1,0:T(1,128)}), f32[32,1,128]{2,1,0:T(1,128)S(1)}, u32[]{:S(2)}, u32[]{:S(2)}) async-start(f32[32,1,128]{2,1,0:T(1,128)} %bitcast.7), calls=%async_computation.2 | async-start | bytes 32768 | tf_op jit(solution)/shard_map/all_to_all | solution.py:549
  103.4 0.0 collective-permute-done.10.refs_11_
  103.5 0.0 collective-permute-done.11.refs_12_
  103.5 0.8 second_image.1.u_ref
  104.2 7.8 %all-to-all-done.2 = f32[32,1,128]{2,1,0:T(1,128)S(1)} async-done(((f32[32,1,128]{2,1,0:T(1,128)}), f32[32,1,128]{2,1,0:T(1,128)S(1)}, u32[]{:S(2)}, u32[]{:S(2)}) %all-to-all-start.2) | async-done | bytes 16416 | tf_op jit(solution)/shard_map/all_to_all | solution.py:549
  112.0 0.8 finish.1
  (2 shorter events, 0.1 us)
Async XLA Ops:
  4.1 7.8 %copy-start.2 = (f32[8,16,128]{2,1,0:T(8,128)S(1)}, f32[8,16,128]{2,1,0:T(8,128)}, u32[]{:S(2)}) copy-start(f32[8,16,128]{2,1,0:T(8,128)} %param.14) | copy-start | bytes 196612
  4.1 7.8 %copy-start.3 = (f32[8,16]{1,0:T(8,128)S(1)}, f32[8,16]{1,0:T(8,128)}, u32[]{:S(2)}) copy-start(f32[8,16]{1,0:T(8,128)} %diffusion_ref.1) | copy-start | bytes 1540
  4.2 20.4 %all-to-all-start = ((f32[8,136,128]{2,1,0:T(8,128)}), f32[8,136,128]{2,1,0:T(8,128)S(1)}, u32[]{:S(2)}, u32[]{:S(2)}) async-start(f32[8,136,128]{2,1,0:T(8,128)} %bucket.1), calls=%async_computation | async-start | bytes 1114112 | tf_op jit(solution)/shard_map/all_to_all | solution.py:512
  12.1 9.0 %collective-permute-start.1 = (f32[144,128]{1,0:T(8,128)S(1)}, f32[144,128]{1,0:T(8,128)S(1)}, u32[]{:S(2)}, u32[]{:S(2)}) collective-permute-start(f32[144,128]{1,0:T(8,128)S(1)} %fixed.1.refs_5_.refs_4_), channel_id=1, source_target_pairs={{1,2},{3,4},{5,6},{7,0},{2,1},{4,3},{6,5},{0,7},{9,10},{11,12},{13... | collective-permute-start | bytes 221192 | tf_op jit(solution)/shard_map/ppermute | solution.py:488
  16.6 5.9 %collective-permute-start = (f32[144,128]{1,0:T(8,128)S(1)}, f32[144,128]{1,0:T(8,128)S(1)}, u32[]{:S(2)}, u32[]{:S(2)}) collective-permute-start(f32[144,128]{1,0:T(8,128)S(1)} %fixed.1.refs_5_.refs_4_), channel_id=1, source_target_pairs={{0,1},{2,3},{4,5},{6,7},{1,0},{3,2},{5,4},{7,6},{8,9},{10,11},{12,... | collective-permute-start | bytes 221192 | tf_op jit(solution)/shard_map/ppermute | solution.py:488
  25.0 7.5 %collective-permute-start.2 = (f32[584,128]{1,0:T(8,128)S(1)}, f32[584,128]{1,0:T(8,128)S(1)}, u32[]{:S(2)}, u32[]{:S(2)}) collective-permute-start(f32[584,128]{1,0:T(8,128)S(1)} %get-tuple-element.18), channel_id=1, source_target_pairs={{0,1},{2,3},{4,5},{6,7},{1,0},{3,2},{5,4},{7,6},{8,9},{10,11},{12,... | collective-permute-start | bytes 897032 | tf_op jit(solution)/shard_map/ppermute | solution.py:488
  27.2 8.7 %collective-permute-start.3 = (f32[584,128]{1,0:T(8,128)S(1)}, f32[584,128]{1,0:T(8,128)S(1)}, u32[]{:S(2)}, u32[]{:S(2)}) collective-permute-start(f32[584,128]{1,0:T(8,128)S(1)} %get-tuple-element.20), channel_id=1, source_target_pairs={{1,2},{3,4},{5,6},{7,0},{2,1},{4,3},{6,5},{0,7},{9,10},{11,12},{13... | collective-permute-start | bytes 897032 | tf_op jit(solution)/shard_map/ppermute | solution.py:488
  36.0 21.7 %collective-permute-start.4 = (f32[528,128]{1,0:T(8,128)S(1)}, f32[528,128]{1,0:T(8,128)S(1)}, u32[]{:S(2)}, u32[]{:S(2)}) collective-permute-start(f32[528,128]{1,0:T(8,128)S(1)} %get-tuple-element.21), channel_id=1, source_target_pairs={{8,16},{24,32},{40,48},{56,64},{72,80},{88,96},{104,112},{120,128}... | collective-permute-start | bytes 811016 | tf_op jit(solution)/shard_map/ppermute | solution.py:495
  49.0 8.5 %copy-start = (f32[128,128]{1,0:T(8,128)S(1)}, f32[128,128]{1,0:T(8,128)}, u32[]{:S(2)}) copy-start(f32[128,128]{1,0:T(8,128)} %factor_ref.1) | copy-start | bytes 196612
  49.0 8.5 %copy-start.1 = (f32[128,128]{1,0:T(8,128)S(1)}, f32[128,128]{1,0:T(8,128)}, u32[]{:S(2)}) copy-start(f32[128,128]{1,0:T(8,128)} %mixing_ref.1) | copy-start | bytes 196612
  49.0 8.6 %collective-permute-start.5 = (f32[528,128]{1,0:T(8,128)S(1)}, f32[528,128]{1,0:T(8,128)S(1)}, u32[]{:S(2)}, u32[]{:S(2)}) collective-permute-start(f32[528,128]{1,0:T(8,128)S(1)} %get-tuple-element.22), channel_id=1, source_target_pairs={{0,8},{16,24},{32,40},{48,56},{64,72},{80,88},{96,104},{112,120},{... | collective-permute-start | bytes 811016 | tf_op jit(solution)/shard_map/ppermute | solution.py:495
  51.2 14.0 %collective-permute-start.8 = (f32[480,128]{1,0:T(8,128)S(1)}, f32[480,128]{1,0:T(8,128)S(1)}, u32[]{:S(2)}, u32[]{:S(2)}) collective-permute-start(f32[480,128]{1,0:T(8,128)S(1)} %get-tuple-element.27), channel_id=1, source_target_pairs={{8,16},{24,32},{40,48},{56,64},{72,80},{88,96},{104,112},{120,128}... | collective-permute-start | bytes 737288 | tf_op jit(solution)/shard_map/ppermute | solution.py:495
  55.6 9.6 %collective-permute-start.9 = (f32[480,128]{1,0:T(8,128)S(1)}, f32[480,128]{1,0:T(8,128)S(1)}, u32[]{:S(2)}, u32[]{:S(2)}) collective-permute-start(f32[480,128]{1,0:T(8,128)S(1)} %get-tuple-element.28), channel_id=1, source_target_pairs={{0,8},{16,24},{32,40},{48,56},{64,72},{80,88},{96,104},{112,120},{... | collective-permute-start | bytes 737288 | tf_op jit(solution)/shard_map/ppermute | solution.py:495
  58.9 8.0 %collective-permute-start.6 = (f32[432,128]{1,0:T(8,128)S(1)}, f32[432,128]{1,0:T(8,128)S(1)}, u32[]{:S(2)}, u32[]{:S(2)}) collective-permute-start(f32[432,128]{1,0:T(8,128)S(1)} %get-tuple-element.25), channel_id=1, source_target_pairs={{8,16},{24,32},{40,48},{56,64},{72,80},{88,96},{104,112},{120,128}... | collective-permute-start | bytes 663560 | tf_op jit(solution)/shard_map/ppermute | solution.py:495
  63.3 3.6 %collective-permute-start.7 = (f32[432,128]{1,0:T(8,128)S(1)}, f32[432,128]{1,0:T(8,128)S(1)}, u32[]{:S(2)}, u32[]{:S(2)}) collective-permute-start(f32[432,128]{1,0:T(8,128)S(1)} %get-tuple-element.26), channel_id=1, source_target_pairs={{0,8},{16,24},{32,40},{48,56},{64,72},{80,88},{96,104},{112,120},{... | collective-permute-start | bytes 663560 | tf_op jit(solution)/shard_map/ppermute | solution.py:495
  71.1 24.1 %all-to-all-start.1 = ((f32[24,4,128]{2,1,0:T(4,128)}), f32[24,4,128]{2,1,0:T(4,128)S(1)}, u32[]{:S(2)}, u32[]{:S(2)}) async-start(f32[24,4,128]{2,1,0:T(4,128)} %bitcast.4), calls=%async_computation.1 | async-start | bytes 98304 | tf_op jit(solution)/shard_map/all_to_all | solution.py:543
  85.1 18.3 %collective-permute-start.10 = (f32[192,128]{1,0:T(8,128)S(1)}, f32[192,128]{1,0:T(8,128)S(1)}, u32[]{:S(2)}, u32[]{:S(2)}) collective-permute-start(f32[192,128]{1,0:T(8,128)S(1)} %get-tuple-element.32), channel_id=1, source_target_pairs={{8,16},{24,32},{40,48},{56,64},{72,80},{88,96},{104,112},{120,128}... | collective-permute-start | bytes 294920 | tf_op jit(solution)/shard_map/ppermute | solution.py:495
  88.7 14.8 %collective-permute-start.11 = (f32[192,128]{1,0:T(8,128)S(1)}, f32[192,128]{1,0:T(8,128)S(1)}, u32[]{:S(2)}, u32[]{:S(2)}) collective-permute-start(f32[192,128]{1,0:T(8,128)S(1)} %get-tuple-element.33), channel_id=1, source_target_pairs={{0,8},{16,24},{32,40},{48,56},{64,72},{80,88},{96,104},{112,120},{... | collective-permute-start | bytes 294920 | tf_op jit(solution)/shard_map/ppermute | solution.py:495
  95.8 16.2 %all-to-all-start.2 = ((f32[32,1,128]{2,1,0:T(1,128)}), f32[32,1,128]{2,1,0:T(1,128)S(1)}, u32[]{:S(2)}, u32[]{:S(2)}) async-start(f32[32,1,128]{2,1,0:T(1,128)} %bitcast.7), calls=%async_computation.2 | async-start | bytes 32768 | tf_op jit(solution)/shard_map/all_to_all | solution.py:549

commit v8 on v6

--- a/solution.py
+++ b/solution.py
@@ -23,7 +23,7 @@
 MIB = 1024 * 1024
 
 
-def call(kernel, name, outs, scratch=(), smem=(), hbm=(), vmem=40):
+def call(kernel, name, outs, scratch=(), smem=(), hbm=(), vmem=40, out_space=pltpu.VMEM):
     def run(*args):
         spaces = [pltpu.SMEM if i in smem else pltpu.HBM if i in hbm else pltpu.VMEM for i in range(len(args))]
         specs = [pl.BlockSpec(memory_space=space) for space in spaces]
@@ -32,7 +32,7 @@
             name=name,
             out_shape=outs,
             in_specs=specs,
-            out_specs=jax.tree.map(lambda _: pl.BlockSpec(memory_space=pltpu.VMEM), outs),
+            out_specs=jax.tree.map(lambda _: pl.BlockSpec(memory_space=out_space), outs),
             scratch_shapes=scratch,
             compiler_params=pltpu.CompilerParams(vmem_limit_bytes=vmem * MIB),
         )(*args)
@@ -66,7 +66,8 @@
 
 
 def bucket_kernel(
-    departures_hbm, weight_hbm, columns_ref, owner_ref, counts_ref, parity_ref, out_ref, departures_ref, weight_ref, sems
+    departures_hbm, weight_hbm, columns_ref, owner_ref, counts_ref, parity_ref, out_hbm,
+    departures_ref, weight_ref, out_ref, sems,
 ):
     copies = [
         pltpu.make_async_copy(departures_hbm, departures_ref, sems.at[0]),
@@ -89,9 +90,7 @@
         copy.wait()
     weights = jnp.where(slot < counts_ref[0], weight_ref[...], 0.0)
     parts = halves(weights * departures_ref[...]) + halves(weights)
-    moved = dot(pick, jnp.concatenate(parts, axis=1))
-    forcing = moved[:, :L] + moved[:, L : 2 * L]
-    weights = moved[:, 2 * L : 3 * L] + moved[:, 3 * L :]
+    data = jnp.concatenate(parts, axis=1)
     number = lax.broadcasted_iota(jnp.int32, (1, SLOTS), 1)
     time = (number - STEPS * ((number * 171) >> 9)).astype(F32)
     tile = lax.broadcasted_iota(jnp.int32, (8, SLOTS), 0).astype(F32)
@@ -103,10 +102,20 @@
     spread = jnp.where(lax.broadcasted_iota(jnp.int32, (SLOTS, L), 1).astype(F32) == target, 1.0, 0.0)
     codes = dot(marks.astype(BF16), spread.astype(BF16))
     codes = CELLS * codes[:8] + codes[8:]
-    for d in range(8):
-        out_ref[d, :CAP] = forcing[d * CAP : (d + 1) * CAP]
-        out_ref[d, CAP : 2 * CAP] = weights[d * CAP : (d + 1) * CAP]
-        out_ref[d, 2 * CAP :] = jnp.broadcast_to(codes[d : d + 1], (8, L))
+    sends = []
+    for j in range(4):
+        moved = dot(pick[2 * j * CAP : 2 * (j + 1) * CAP], data)
+        forcing = moved[:, :L] + moved[:, L : 2 * L]
+        weights = moved[:, 2 * L : 3 * L] + moved[:, 3 * L :]
+        for k in range(2):
+            d, rows = 2 * j + k, slice(k * CAP, (k + 1) * CAP)
+            out_ref[d, :CAP] = forcing[rows]
+            out_ref[d, CAP : 2 * CAP] = weights[rows]
+            out_ref[d, 2 * CAP :] = jnp.broadcast_to(codes[d : d + 1], (8, L))
+            sends.append(pltpu.make_async_copy(out_ref.at[d], out_hbm.at[d], sems.at[2 + d]))
+            sends[-1].start()
+    for copy in sends:
+        copy.wait()
 
 
 def fixed_kernel(std_ref, diffusion_ref, out_ref):
@@ -126,7 +135,7 @@
 PACKED = SIZE + STEPS * ROWS * EDGE
 
 
-def tile_kernel(received_ref, fixed_left_ref, fixed_right_ref, own_ref, to_left_ref, to_right_ref):
+def tile_kernel(received_ref, fixed_left_ref, fixed_right_ref, m_ref, own_ref, to_left_ref, to_right_ref):
     ones, data = [], []
     cell = lax.broadcasted_iota(jnp.int32, (SIZE, L), 0)
     for j in range(4):
@@ -496,10 +505,11 @@
         bucket_kernel,
         "bucket",
         shape(8, BUCKET, L),
-        [slots, slots, pltpu.SemaphoreType.DMA((2,))],
+        [slots, slots, pltpu.VMEM((8, BUCKET, L), F32), pltpu.SemaphoreType.DMA((10,))],
         smem=(4, 5),
         hbm=(0, 1),
         vmem=60,
+        out_space=pltpu.HBM,
     )(departures, obs_weight, obs_columns.reshape(1, SLOTS), obs_owner.reshape(1, SLOTS), obs_counts, parity)
     received = lax.all_to_all(buckets, "lon", 0, 0)
     mats = call(matrices_kernel, "matrices", shape(4, 2 * L, 2 * L, dtype=BF16))(level_factor, model_mixing)
@@ -507,7 +517,7 @@
     fixed_left, fixed_right = exchange(fixed, fixed)
     beside = shape(PACKED + ROWS, L)
     tile, to_left, to_right = call(tile_kernel, "tile", (shape(2 * SIZE, L), beside, beside))(
-        received, fixed_left, fixed_right
+        received, fixed_left, fixed_right, mats
     )
     left, right = exchange(to_left, to_right)
     refs = (left, tile, right, fixed_left, fixed, fixed_right)

time: 113 us -> 112 us (level)
  no operation moved by 1% of the time
where the time goes in v8:
time: 112 us
  starting transfers between devices  73.7 us (66%)
  waiting for transfers between devices  25.2 us (22%)
  Pallas kernels  11.1 us (10%)
  between operations  1.58 us (1%)
    ppermute x4, starting transfers between devices, swap(): lax.ppermute(chip, 'lat', both[1])  23.7 us
    all_to_all x1, starting transfers between devices, shards(): sums = lax.all_to_all(sums, 'lat', 0, 0, axis_index_groups=near, tiled=True)  14 us
    pallas_call x11, Pallas kernels, run(): pl.pallas_call(kernel, name=name, out_shape=outs, in_specs=specs, out_spe...  11.1 us
    ppermute x2, starting transfers between devices, exchange(): lax.ppermute(to_before, 'lon', down)  9.15 us
    all_to_all x1, starting transfers between devices, shards(): received = lax.all_to_all(buckets, 'lon', 0, 0)  7.8 us
    all_to_all x1, waiting for transfers between devices, shards(): lax.all_to_all(sums, ('lat', 'lon'), 0, 0, axis_index_groups=far, tiled=T...  7.75 us
    ppermute x4, starting transfers between devices, swap(): lax.ppermute(core, 'lat', both[0])  7.68 us
    all_to_all x1, starting transfers between devices, shards(): lax.all_to_all(sums, ('lat', 'lon'), 0, 0, axis_index_groups=far, tiled=T...  7.54 us
  transfers between devices with their start and end apart: 15, of which 7 were waited for; matrix products, arithmetic and copies ran while one was open for 0% of the time, Pallas kernels for 3%

profile of v8, /device:TPU:1, one launch (start us, length us, event | category | flops | bytes accessed | tf_op | source)
XLA Modules:
  0.0 111.6 jit_solution(5872973578621019886)
XLA Ops:
  1.3 2.8 %bucket.1 = f32[8,136,128]{2,1,0:T(8,128)} custom-call(f32[256,128]{1,0:T(8,128)} %departures_hbm.1, f32[256,128]{1,0:T(8,128)} %weight_hbm.1, s32[1,256]{1,0:T(1,128)} %bitcast.14, s32[1,256]{1,0:T(1,128)} %bitcast.15, s32[1]{0:T(128)S(6)} %copy.12.counts_ref, s32[1]{0:T(128)} %bitcast.3.parity_ref), custom_call_target="tpu_custom_call" | custom-call | tf_op jit(solution)/shard_map/bucket/pallas_call | solution.py:30
  4.1 0.0 copy-start.2
  4.1 0.0 copy-start.3
  4.1 7.8 %all-to-all-start = ((f32[8,136,128]{2,1,0:T(8,128)}), f32[8,136,128]{2,1,0:T(8,128)S(1)}, u32[]{:S(2)}, u32[]{:S(2)}) async-start(f32[8,136,128]{2,1,0:T(8,128)} %bucket.1), calls=%async_computation | async-start | bytes 1114112 | tf_op jit(solution)/shard_map/all_to_all | solution.py:514
  11.9 0.0 copy-done.2
  11.9 0.0 copy-done.3
  11.9 0.0 copy-start
  11.9 0.0 copy-start.1
  11.9 0.1 fixed.1.refs_5_.refs_4_
  12.0 4.6 %collective-permute-start.1 = (f32[144,128]{1,0:T(8,128)S(1)}, f32[144,128]{1,0:T(8,128)S(1)}, u32[]{:S(2)}, u32[]{:S(2)}) collective-permute-start(f32[144,128]{1,0:T(8,128)S(1)} %fixed.1.refs_5_.refs_4_), channel_id=1, source_target_pairs={{1,0},{2,1},{3,2},{4,3},{5,4},{6,5},{7,6},{0,7},{9,8},{10,9},{11,1... | collective-permute-start | bytes 221192 | tf_op jit(solution)/shard_map/ppermute | solution.py:488
  16.6 1.9 %collective-permute-start = (f32[144,128]{1,0:T(8,128)S(1)}, f32[144,128]{1,0:T(8,128)S(1)}, u32[]{:S(2)}, u32[]{:S(2)}) collective-permute-start(f32[144,128]{1,0:T(8,128)S(1)} %fixed.1.refs_5_.refs_4_), channel_id=1, source_target_pairs={{0,1},{1,2},{2,3},{3,4},{4,5},{5,6},{6,7},{7,0},{8,9},{9,10},{10,1... | collective-permute-start | bytes 221192 | tf_op jit(solution)/shard_map/ppermute | solution.py:488
  18.6 0.0 copy-done
  18.6 0.0 copy-done.1
  18.6 0.1 matrices.1.m_ref.refs_8_
  18.7 2.6 %collective-permute-done.1.fixed_right_ref.refs_6_.refs_5_ = f32[144,128]{1,0:T(8,128)S(1)} collective-permute-done((f32[144,128]{1,0:T(8,128)S(1)}, f32[144,128]{1,0:T(8,128)S(1)}, u32[]{:S(2)}, u32[]{:S(2)}) %collective-permute-start.1) | collective-permute-done | bytes 73760 | tf_op jit(solution)/shard_map/ppermute | solution.py:488
  21.3 4.9 %collective-permute-done.fixed_left_ref.refs_4_.refs_3_ = f32[144,128]{1,0:T(8,128)S(1)} collective-permute-done((f32[144,128]{1,0:T(8,128)S(1)}, f32[144,128]{1,0:T(8,128)S(1)}, u32[]{:S(2)}, u32[]{:S(2)}) %collective-permute-start) | collective-permute-done | bytes 73760 | tf_op jit(solution)/shard_map/ppermute | solution.py:488
  26.2 0.0 all-to-all-done.received_ref
  26.2 0.4 tile.1
  26.6 1.9 %collective-permute-start.2 = (f32[584,128]{1,0:T(8,128)S(1)}, f32[584,128]{1,0:T(8,128)S(1)}, u32[]{:S(2)}, u32[]{:S(2)}) collective-permute-start(f32[584,128]{1,0:T(8,128)S(1)} %get-tuple-element.18), channel_id=1, source_target_pairs={{0,1},{1,2},{2,3},{3,4},{4,5},{5,6},{6,7},{7,0},{8,9},{9,10},{10,1... | collective-permute-start | bytes 897032 | tf_op jit(solution)/shard_map/ppermute | solution.py:488
  28.5 4.6 %collective-permute-start.3 = (f32[584,128]{1,0:T(8,128)S(1)}, f32[584,128]{1,0:T(8,128)S(1)}, u32[]{:S(2)}, u32[]{:S(2)}) collective-permute-start(f32[584,128]{1,0:T(8,128)S(1)} %get-tuple-element.20), channel_id=1, source_target_pairs={{1,0},{2,1},{3,2},{4,3},{5,4},{6,5},{7,6},{0,7},{9,8},{10,9},{11,1... | collective-permute-start | bytes 897032 | tf_op jit(solution)/shard_map/ppermute | solution.py:488
  33.1 2.2 %collective-permute-done.2.refs_1_.refs_0_ = f32[584,128]{1,0:T(8,128)S(1)} collective-permute-done((f32[584,128]{1,0:T(8,128)S(1)}, f32[584,128]{1,0:T(8,128)S(1)}, u32[]{:S(2)}, u32[]{:S(2)}) %collective-permute-start.2) | collective-permute-done | bytes 299040 | tf_op jit(solution)/shard_map/ppermute | solution.py:488
  35.3 1.5 %collective-permute-done.3.refs_3_.refs_2_ = f32[584,128]{1,0:T(8,128)S(1)} collective-permute-done((f32[584,128]{1,0:T(8,128)S(1)}, f32[584,128]{1,0:T(8,128)S(1)}, u32[]{:S(2)}, u32[]{:S(2)}) %collective-permute-start.3) | collective-permute-done | bytes 299040 | tf_op jit(solution)/shard_map/ppermute | solution.py:488
  36.8 11.4 %collective-permute-start.4 = (f32[528,128]{1,0:T(8,128)S(1)}, f32[528,128]{1,0:T(8,128)S(1)}, u32[]{:S(2)}, u32[]{:S(2)}) collective-permute-start(f32[528,128]{1,0:T(8,128)S(1)} %get-tuple-element.21), channel_id=1, source_target_pairs={{8,16},{24,32},{40,48},{56,64},{72,80},{88,96},{104,112},{120,128}... | collective-permute-start | bytes 811016 | tf_op jit(solution)/shard_map/ppermute | solution.py:495
  48.2 1.9 %collective-permute-start.5 = (f32[528,128]{1,0:T(8,128)S(1)}, f32[528,128]{1,0:T(8,128)S(1)}, u32[]{:S(2)}, u32[]{:S(2)}) collective-permute-start(f32[528,128]{1,0:T(8,128)S(1)} %get-tuple-element.22), channel_id=1, source_target_pairs={{0,8},{16,24},{32,40},{48,56},{64,72},{80,88},{96,104},{112,120},{... | collective-permute-start | bytes 811016 | tf_op jit(solution)/shard_map/ppermute | solution.py:495
  50.2 4.4 %collective-permute-start.8 = (f32[480,128]{1,0:T(8,128)S(1)}, f32[480,128]{1,0:T(8,128)S(1)}, u32[]{:S(2)}, u32[]{:S(2)}) collective-permute-start(f32[480,128]{1,0:T(8,128)S(1)} %get-tuple-element.27), channel_id=1, source_target_pairs={{8,16},{24,32},{40,48},{56,64},{72,80},{88,96},{104,112},{120,128}... | collective-permute-start | bytes 737288 | tf_op jit(solution)/shard_map/ppermute | solution.py:495
  54.6 1.9 %collective-permute-start.9 = (f32[480,128]{1,0:T(8,128)S(1)}, f32[480,128]{1,0:T(8,128)S(1)}, u32[]{:S(2)}, u32[]{:S(2)}) collective-permute-start(f32[480,128]{1,0:T(8,128)S(1)} %get-tuple-element.28), channel_id=1, source_target_pairs={{0,8},{16,24},{32,40},{48,56},{64,72},{80,88},{96,104},{112,120},{... | collective-permute-start | bytes 737288 | tf_op jit(solution)/shard_map/ppermute | solution.py:495
  56.5 0.0 collective-permute-done.4.refs_6_
  56.5 0.0 collective-permute-done.5.refs_7_
  56.6 1.2 %right_side.1 = (f32[8,48,128]{2,1,0:T(8,128)S(1)}, f32[8,48,128]{2,1,0:T(8,128)S(1)}, f32[432,128]{1,0:T(8,128)S(1)}, f32[432,128]{1,0:T(8,128)S(1)}) custom-call(s32[1]{0:T(128)} %bitcast.refs_0_.parity_ref, f32[584,128]{1,0:T(8,128)S(1)} %collective-permute-done.2.refs_1_.refs_0_, f32[768,128]{1,0:T(8,128)S(1)} %get-tuple-element.19.refs_2_.refs_1_, ...), custom_call_target="tpu_custom_call" | custom-call | tf_op jit(solution)/shard_map/right_side/pallas_call | solution.py:30
  57.8 4.4 %collective-permute-start.6 = (f32[432,128]{1,0:T(8,128)S(1)}, f32[432,128]{1,0:T(8,128)S(1)}, u32[]{:S(2)}, u32[]{:S(2)}) collective-permute-start(f32[432,128]{1,0:T(8,128)S(1)} %get-tuple-element.25), channel_id=1, source_target_pairs={{8,16},{24,32},{40,48},{56,64},{72,80},{88,96},{104,112},{120,128}... | collective-permute-start | bytes 663560 | tf_op jit(solution)/shard_map/ppermute | solution.py:495
  62.2 1.9 %collective-permute-start.7 = (f32[432,128]{1,0:T(8,128)S(1)}, f32[432,128]{1,0:T(8,128)S(1)}, u32[]{:S(2)}, u32[]{:S(2)}) collective-permute-start(f32[432,128]{1,0:T(8,128)S(1)} %get-tuple-element.26), channel_id=1, source_target_pairs={{0,8},{16,24},{32,40},{48,56},{64,72},{80,88},{96,104},{112,120},{... | collective-permute-start | bytes 663560 | tf_op jit(solution)/shard_map/ppermute | solution.py:495
  64.1 0.0 collective-permute-done.8.refs_13_
  64.1 0.0 collective-permute-done.9.refs_14_
  64.1 1.7 %collective-permute-done.6.refs_11_ = f32[432,128]{1,0:T(8,128)S(1)} collective-permute-done((f32[432,128]{1,0:T(8,128)S(1)}, f32[432,128]{1,0:T(8,128)S(1)}, u32[]{:S(2)}, u32[]{:S(2)}) %collective-permute-start.6) | collective-permute-done | bytes 221216 | tf_op jit(solution)/shard_map/ppermute | solution.py:495
  65.8 0.0 collective-permute-done.7.refs_12_
  65.8 4.2 %first_image.1 = (f32[8,16,128]{2,1,0:T(8,128)S(1)}, f32[3,8,32,128]{3,2,1,0:T(8,128)S(1)}, f32[192,128]{1,0:T(8,128)S(1)}, f32[192,128]{1,0:T(8,128)S(1)}, f32[96,128]{1,0:T(8,128)}) custom-call(s32[1]{0:T(128)} %bitcast.refs_0_.parity_ref, f32[584,128]{1,0:T(8,128)S(1)} %collective-permute-done.2.refs_1_.refs_0_, ...), custom_call_target="tpu_custom_call" | custom-call | tf_op jit(solution)/shard_map/first_image/pallas_call | solution.py:30
  70.0 14.0 %all-to-all-start.1 = ((f32[24,4,128]{2,1,0:T(4,128)}), f32[24,4,128]{2,1,0:T(4,128)S(1)}, u32[]{:S(2)}, u32[]{:S(2)}) async-start(f32[24,4,128]{2,1,0:T(4,128)} %bitcast.5), calls=%async_computation.1 | async-start | bytes 98304 | tf_op jit(solution)/shard_map/all_to_all | solution.py:545
  84.0 3.5 %collective-permute-start.10 = (f32[192,128]{1,0:T(8,128)S(1)}, f32[192,128]{1,0:T(8,128)S(1)}, u32[]{:S(2)}, u32[]{:S(2)}) collective-permute-start(f32[192,128]{1,0:T(8,128)S(1)} %get-tuple-element.32), channel_id=1, source_target_pairs={{8,16},{24,32},{40,48},{56,64},{72,80},{88,96},{104,112},{120,128}... | collective-permute-start | bytes 294920 | tf_op jit(solution)/shard_map/ppermute | solution.py:495
  87.5 1.9 %collective-permute-start.11 = (f32[192,128]{1,0:T(8,128)S(1)}, f32[192,128]{1,0:T(8,128)S(1)}, u32[]{:S(2)}, u32[]{:S(2)}) collective-permute-start(f32[192,128]{1,0:T(8,128)S(1)} %get-tuple-element.33), channel_id=1, source_target_pairs={{0,8},{16,24},{32,40},{48,56},{64,72},{80,88},{96,104},{112,120},{... | collective-permute-start | bytes 294920 | tf_op jit(solution)/shard_map/ppermute | solution.py:495
  89.5 4.6 %all-to-all-done.1 = f32[24,4,128]{2,1,0:T(4,128)S(1)} async-done(((f32[24,4,128]{2,1,0:T(4,128)}), f32[24,4,128]{2,1,0:T(4,128)S(1)}, u32[]{:S(2)}, u32[]{:S(2)}) %all-to-all-start.1) | async-done | bytes 49184 | tf_op jit(solution)/shard_map/all_to_all | solution.py:545
  94.1 0.6 add.10
  94.7 7.5 %all-to-all-start.2 = ((f32[32,1,128]{2,1,0:T(1,128)}), f32[32,1,128]{2,1,0:T(1,128)S(1)}, u32[]{:S(2)}, u32[]{:S(2)}) async-start(f32[32,1,128]{2,1,0:T(1,128)} %bitcast.8), calls=%async_computation.2 | async-start | bytes 32768 | tf_op jit(solution)/shard_map/all_to_all | solution.py:551
  102.3 0.0 collective-permute-done.10.refs_11_
  102.3 0.0 collective-permute-done.11.refs_12_
  102.3 0.8 second_image.1.u_ref
  103.1 7.8 %all-to-all-done.2 = f32[32,1,128]{2,1,0:T(1,128)S(1)} async-done(((f32[32,1,128]{2,1,0:T(1,128)}), f32[32,1,128]{2,1,0:T(1,128)S(1)}, u32[]{:S(2)}, u32[]{:S(2)}) %all-to-all-start.2) | async-done | bytes 16416 | tf_op jit(solution)/shard_map/all_to_all | solution.py:551
  110.8 0.8 finish.1
  (2 shorter events, 0.1 us)
Async XLA Ops:
  4.1 7.8 %copy-start.2 = (f32[8,16,128]{2,1,0:T(8,128)S(1)}, f32[8,16,128]{2,1,0:T(8,128)}, u32[]{:S(2)}) copy-start(f32[8,16,128]{2,1,0:T(8,128)} %param.14) | copy-start | bytes 196612
  4.1 7.8 %copy-start.3 = (f32[8,16]{1,0:T(8,128)S(1)}, f32[8,16]{1,0:T(8,128)}, u32[]{:S(2)}) copy-start(f32[8,16]{1,0:T(8,128)} %diffusion_ref.1) | copy-start | bytes 1540
  4.1 22.1 %all-to-all-start = ((f32[8,136,128]{2,1,0:T(8,128)}), f32[8,136,128]{2,1,0:T(8,128)S(1)}, u32[]{:S(2)}, u32[]{:S(2)}) async-start(f32[8,136,128]{2,1,0:T(8,128)} %bucket.1), calls=%async_computation | async-start | bytes 1114112 | tf_op jit(solution)/shard_map/all_to_all | solution.py:514
  11.9 6.6 %copy-start = (f32[128,128]{1,0:T(8,128)S(1)}, f32[128,128]{1,0:T(8,128)}, u32[]{:S(2)}) copy-start(f32[128,128]{1,0:T(8,128)} %factor_ref.1) | copy-start | bytes 196612
  11.9 6.6 %copy-start.1 = (f32[128,128]{1,0:T(8,128)S(1)}, f32[128,128]{1,0:T(8,128)}, u32[]{:S(2)}) copy-start(f32[128,128]{1,0:T(8,128)} %mixing_ref.1) | copy-start | bytes 196612
  12.0 9.2 %collective-permute-start.1 = (f32[144,128]{1,0:T(8,128)S(1)}, f32[144,128]{1,0:T(8,128)S(1)}, u32[]{:S(2)}, u32[]{:S(2)}) collective-permute-start(f32[144,128]{1,0:T(8,128)S(1)} %fixed.1.refs_5_.refs_4_), channel_id=1, source_target_pairs={{1,0},{2,1},{3,2},{4,3},{5,4},{6,5},{7,6},{0,7},{9,8},{10,9},{11,1... | collective-permute-start | bytes 221192 | tf_op jit(solution)/shard_map/ppermute | solution.py:488
  16.6 9.6 %collective-permute-start = (f32[144,128]{1,0:T(8,128)S(1)}, f32[144,128]{1,0:T(8,128)S(1)}, u32[]{:S(2)}, u32[]{:S(2)}) collective-permute-start(f32[144,128]{1,0:T(8,128)S(1)} %fixed.1.refs_5_.refs_4_), channel_id=1, source_target_pairs={{0,1},{1,2},{2,3},{3,4},{4,5},{5,6},{6,7},{7,0},{8,9},{9,10},{10,1... | collective-permute-start | bytes 221192 | tf_op jit(solution)/shard_map/ppermute | solution.py:488
  26.6 8.7 %collective-permute-start.2 = (f32[584,128]{1,0:T(8,128)S(1)}, f32[584,128]{1,0:T(8,128)S(1)}, u32[]{:S(2)}, u32[]{:S(2)}) collective-permute-start(f32[584,128]{1,0:T(8,128)S(1)} %get-tuple-element.18), channel_id=1, source_target_pairs={{0,1},{1,2},{2,3},{3,4},{4,5},{5,6},{6,7},{7,0},{8,9},{9,10},{10,1... | collective-permute-start | bytes 897032 | tf_op jit(solution)/shard_map/ppermute | solution.py:488
  28.5 8.3 %collective-permute-start.3 = (f32[584,128]{1,0:T(8,128)S(1)}, f32[584,128]{1,0:T(8,128)S(1)}, u32[]{:S(2)}, u32[]{:S(2)}) collective-permute-start(f32[584,128]{1,0:T(8,128)S(1)} %get-tuple-element.20), channel_id=1, source_target_pairs={{1,0},{2,1},{3,2},{4,3},{5,4},{6,5},{7,6},{0,7},{9,8},{10,9},{11,1... | collective-permute-start | bytes 897032 | tf_op jit(solution)/shard_map/ppermute | solution.py:488
  36.8 19.7 %collective-permute-start.4 = (f32[528,128]{1,0:T(8,128)S(1)}, f32[528,128]{1,0:T(8,128)S(1)}, u32[]{:S(2)}, u32[]{:S(2)}) collective-permute-start(f32[528,128]{1,0:T(8,128)S(1)} %get-tuple-element.21), channel_id=1, source_target_pairs={{8,16},{24,32},{40,48},{56,64},{72,80},{88,96},{104,112},{120,128}... | collective-permute-start | bytes 811016 | tf_op jit(solution)/shard_map/ppermute | solution.py:495
  48.2 8.3 %collective-permute-start.5 = (f32[528,128]{1,0:T(8,128)S(1)}, f32[528,128]{1,0:T(8,128)S(1)}, u32[]{:S(2)}, u32[]{:S(2)}) collective-permute-start(f32[528,128]{1,0:T(8,128)S(1)} %get-tuple-element.22), channel_id=1, source_target_pairs={{0,8},{16,24},{32,40},{48,56},{64,72},{80,88},{96,104},{112,120},{... | collective-permute-start | bytes 811016 | tf_op jit(solution)/shard_map/ppermute | solution.py:495
  50.2 13.9 %collective-permute-start.8 = (f32[480,128]{1,0:T(8,128)S(1)}, f32[480,128]{1,0:T(8,128)S(1)}, u32[]{:S(2)}, u32[]{:S(2)}) collective-permute-start(f32[480,128]{1,0:T(8,128)S(1)} %get-tuple-element.27), channel_id=1, source_target_pairs={{8,16},{24,32},{40,48},{56,64},{72,80},{88,96},{104,112},{120,128}... | collective-permute-start | bytes 737288 | tf_op jit(solution)/shard_map/ppermute | solution.py:495
  54.6 9.5 %collective-permute-start.9 = (f32[480,128]{1,0:T(8,128)S(1)}, f32[480,128]{1,0:T(8,128)S(1)}, u32[]{:S(2)}, u32[]{:S(2)}) collective-permute-start(f32[480,128]{1,0:T(8,128)S(1)} %get-tuple-element.28), channel_id=1, source_target_pairs={{0,8},{16,24},{32,40},{48,56},{64,72},{80,88},{96,104},{112,120},{... | collective-permute-start | bytes 737288 | tf_op jit(solution)/shard_map/ppermute | solution.py:495
  57.8 8.0 %collective-permute-start.6 = (f32[432,128]{1,0:T(8,128)S(1)}, f32[432,128]{1,0:T(8,128)S(1)}, u32[]{:S(2)}, u32[]{:S(2)}) collective-permute-start(f32[432,128]{1,0:T(8,128)S(1)} %get-tuple-element.25), channel_id=1, source_target_pairs={{8,16},{24,32},{40,48},{56,64},{72,80},{88,96},{104,112},{120,128}... | collective-permute-start | bytes 663560 | tf_op jit(solution)/shard_map/ppermute | solution.py:495
  62.2 3.6 %collective-permute-start.7 = (f32[432,128]{1,0:T(8,128)S(1)}, f32[432,128]{1,0:T(8,128)S(1)}, u32[]{:S(2)}, u32[]{:S(2)}) collective-permute-start(f32[432,128]{1,0:T(8,128)S(1)} %get-tuple-element.26), channel_id=1, source_target_pairs={{0,8},{16,24},{32,40},{48,56},{64,72},{80,88},{96,104},{112,120},{... | collective-permute-start | bytes 663560 | tf_op jit(solution)/shard_map/ppermute | solution.py:495
  70.0 24.1 %all-to-all-start.1 = ((f32[24,4,128]{2,1,0:T(4,128)}), f32[24,4,128]{2,1,0:T(4,128)S(1)}, u32[]{:S(2)}, u32[]{:S(2)}) async-start(f32[24,4,128]{2,1,0:T(4,128)} %bitcast.5), calls=%async_computation.1 | async-start | bytes 98304 | tf_op jit(solution)/shard_map/all_to_all | solution.py:545
  84.0 18.3 %collective-permute-start.10 = (f32[192,128]{1,0:T(8,128)S(1)}, f32[192,128]{1,0:T(8,128)S(1)}, u32[]{:S(2)}, u32[]{:S(2)}) collective-permute-start(f32[192,128]{1,0:T(8,128)S(1)} %get-tuple-element.32), channel_id=1, source_target_pairs={{8,16},{24,32},{40,48},{56,64},{72,80},{88,96},{104,112},{120,128}... | collective-permute-start | bytes 294920 | tf_op jit(solution)/shard_map/ppermute | solution.py:495
  87.5 14.7 %collective-permute-start.11 = (f32[192,128]{1,0:T(8,128)S(1)}, f32[192,128]{1,0:T(8,128)S(1)}, u32[]{:S(2)}, u32[]{:S(2)}) collective-permute-start(f32[192,128]{1,0:T(8,128)S(1)} %get-tuple-element.33), channel_id=1, source_target_pairs={{0,8},{16,24},{32,40},{48,56},{64,72},{80,88},{96,104},{112,120},{... | collective-permute-start | bytes 294920 | tf_op jit(solution)/shard_map/ppermute | solution.py:495
  94.7 16.1 %all-to-all-start.2 = ((f32[32,1,128]{2,1,0:T(1,128)}), f32[32,1,128]{2,1,0:T(1,128)S(1)}, u32[]{:S(2)}, u32[]{:S(2)}) async-start(f32[32,1,128]{2,1,0:T(1,128)} %bitcast.8), calls=%async_computation.2 | async-start | bytes 32768 | tf_op jit(solution)/shard_map/all_to_all | solution.py:551

commit v9 on v8

--- a/solution.py
+++ b/solution.py
@@ -455,14 +455,14 @@
 
 
 def levels(lat, lon):
-    quarter = lat // 4
-    near = [[i * quarter + k for k in range(quarter)] for i in range(4)]
-    far = [[(i * quarter + k) * lon + j for i in range(4) for j in range(lon)] for k in range(quarter)]
-    return near, far
+    row = 2 * lon
+    first = [[2 * i + core for i in range(lat // 2)] for core in range(2)]
+    second = [[i * row + k for k in range(row)] for i in range(lat // 2)]
+    return first, second
 
 
 def add_kernel(parts_ref, out_ref):
-    out_ref[...] = jnp.broadcast_to(0.25 * jnp.sum(parts_ref[...], axis=0, keepdims=True), out_ref.shape)
+    out_ref[...] = jnp.broadcast_to(0.5 * jnp.sum(parts_ref[...], axis=0, keepdims=True), out_ref.shape)
 
 
 def finish_kernel(parts_ref, b_ref, q_ref, u_ref, solution_ref, residual_ref):
@@ -532,7 +532,7 @@
     )
     south, north = swap(low, high)
     lat, lon = lax.axis_size("lat"), lax.axis_size("lon")
-    near, far = levels(lat, lon)
+    alike, row = levels(lat, lon)
     small, side = shape(ROWS, COLS, L), shape(THIRD_ROWS, L)
     space = scratch(WIDE, REACH)
     q, g, low, high, sums = call(
@@ -542,13 +542,13 @@
         space + [space[0]] * 2,
         smem=(0,),
     )(side_of, *refs, b, y, south, north, *weights)
-    sums = lax.all_to_all(sums, "lat", 0, 0, axis_index_groups=near, tiled=True)
+    sums = lax.all_to_all(sums, "lat", 0, 0, axis_index_groups=alike, tiled=True)
     south, north = swap(low, high)
     u = call(second_image_kernel, "second_image", small, scratch(INNER, STEPS), smem=(0,))(
         side_of, *refs, q, g, south, north
     )
-    sums = call(add_kernel, "add", shape(4 * lon, L))(sums)
-    sums = lax.all_to_all(sums, ("lat", "lon"), 0, 0, axis_index_groups=far, tiled=True)
+    sums = call(add_kernel, "add", shape(2 * lon, L))(sums)
+    sums = lax.all_to_all(sums, ("lat", "lon"), 0, 0, axis_index_groups=row, tiled=True)
     return call(finish_kernel, "finish", (small, small))(sums, b, q, u)
 
 

time: 112 us -> 113 us (level)
  no operation moved by 1% of the time
where the time goes in v9:
time: 113 us
  starting transfers between devices  73.8 us (65%)
  waiting for transfers between devices  26.1 us (23%)
  Pallas kernels  11.1 us (10%)
  between operations  1.56 us (1%)
    ppermute x4, starting transfers between devices, swap(): lax.ppermute(chip, 'lat', both[1])  22.9 us
    all_to_all x1, starting transfers between devices, shards(): lax.all_to_all(sums, 'lat', 0, 0, axis_index_groups=alike, tiled=True)  16.7 us
    pallas_call x11, Pallas kernels, run(): pl.pallas_call(kernel, name=name, out_shape=outs, in_specs=specs, out_spe...  11.1 us
    ppermute x2, starting transfers between devices, exchange(): lax.ppermute(to_before, 'lon', down)  9.15 us
    all_to_all x1, starting transfers between devices, shards(): received = lax.all_to_all(buckets, 'lon', 0, 0)  7.8 us
    ppermute x4, starting transfers between devices, swap(): lax.ppermute(core, 'lat', both[0])  7.68 us
    all_to_all x1, waiting for transfers between devices, shards(): lax.all_to_all(sums, 'lat', 0, 0, axis_index_groups=alike, tiled=True)  7.18 us
    ppermute x2, waiting for transfers between devices, exchange(): lax.ppermute(to_after, 'lon', up)  7.12 us
  transfers between devices with their start and end apart: 15, of which 7 were waited for; matrix products, arithmetic and copies ran while one was open for 0% of the time, Pallas kernels for 3%

profile of v9, /device:TPU:1, one launch (start us, length us, event | category | flops | bytes accessed | tf_op | source)
XLA Modules:
  0.0 112.6 jit_solution(10753797065322369395)
XLA Ops:
  1.3 2.8 %bucket.1 = f32[8,136,128]{2,1,0:T(8,128)} custom-call(f32[256,128]{1,0:T(8,128)} %departures_hbm.1, f32[256,128]{1,0:T(8,128)} %weight_hbm.1, s32[1,256]{1,0:T(1,128)} %bitcast.14, s32[1,256]{1,0:T(1,128)} %bitcast.15, s32[1]{0:T(128)S(6)} %copy.12.counts_ref, s32[1]{0:T(128)} %bitcast.3.parity_ref), custom_call_target="tpu_custom_call" | custom-call | tf_op jit(solution)/shard_map/bucket/pallas_call | solution.py:30
  4.1 0.0 copy-start.2
  4.1 0.0 copy-start.3
  4.1 7.8 %all-to-all-start = ((f32[8,136,128]{2,1,0:T(8,128)}), f32[8,136,128]{2,1,0:T(8,128)S(1)}, u32[]{:S(2)}, u32[]{:S(2)}) async-start(f32[8,136,128]{2,1,0:T(8,128)} %bucket.1), calls=%async_computation | async-start | bytes 1114112 | tf_op jit(solution)/shard_map/all_to_all | solution.py:514
  11.9 0.0 copy-done.2
  11.9 0.0 copy-done.3
  11.9 0.0 copy-start
  11.9 0.0 copy-start.1
  11.9 0.1 fixed.1.refs_5_.refs_4_
  12.0 4.6 %collective-permute-start.1 = (f32[144,128]{1,0:T(8,128)S(1)}, f32[144,128]{1,0:T(8,128)S(1)}, u32[]{:S(2)}, u32[]{:S(2)}) collective-permute-start(f32[144,128]{1,0:T(8,128)S(1)} %fixed.1.refs_5_.refs_4_), channel_id=1, source_target_pairs={{1,0},{2,1},{3,2},{4,3},{5,4},{6,5},{7,6},{0,7},{9,8},{10,9},{11,1... | collective-permute-start | bytes 221192 | tf_op jit(solution)/shard_map/ppermute | solution.py:488
  16.6 1.9 %collective-permute-start = (f32[144,128]{1,0:T(8,128)S(1)}, f32[144,128]{1,0:T(8,128)S(1)}, u32[]{:S(2)}, u32[]{:S(2)}) collective-permute-start(f32[144,128]{1,0:T(8,128)S(1)} %fixed.1.refs_5_.refs_4_), channel_id=1, source_target_pairs={{0,1},{1,2},{2,3},{3,4},{4,5},{5,6},{6,7},{7,0},{8,9},{9,10},{10,1... | collective-permute-start | bytes 221192 | tf_op jit(solution)/shard_map/ppermute | solution.py:488
  18.6 0.0 copy-done
  18.6 0.0 copy-done.1
  18.6 0.1 matrices.1.m_ref.refs_8_
  18.7 2.6 %collective-permute-done.1.fixed_right_ref.refs_6_.refs_5_ = f32[144,128]{1,0:T(8,128)S(1)} collective-permute-done((f32[144,128]{1,0:T(8,128)S(1)}, f32[144,128]{1,0:T(8,128)S(1)}, u32[]{:S(2)}, u32[]{:S(2)}) %collective-permute-start.1) | collective-permute-done | bytes 73760 | tf_op jit(solution)/shard_map/ppermute | solution.py:488
  21.3 4.9 %collective-permute-done.fixed_left_ref.refs_4_.refs_3_ = f32[144,128]{1,0:T(8,128)S(1)} collective-permute-done((f32[144,128]{1,0:T(8,128)S(1)}, f32[144,128]{1,0:T(8,128)S(1)}, u32[]{:S(2)}, u32[]{:S(2)}) %collective-permute-start) | collective-permute-done | bytes 73760 | tf_op jit(solution)/shard_map/ppermute | solution.py:488
  26.2 0.0 all-to-all-done.received_ref
  26.2 0.4 tile.1
  26.6 1.9 %collective-permute-start.2 = (f32[584,128]{1,0:T(8,128)S(1)}, f32[584,128]{1,0:T(8,128)S(1)}, u32[]{:S(2)}, u32[]{:S(2)}) collective-permute-start(f32[584,128]{1,0:T(8,128)S(1)} %get-tuple-element.18), channel_id=1, source_target_pairs={{0,1},{1,2},{2,3},{3,4},{4,5},{5,6},{6,7},{7,0},{8,9},{9,10},{10,1... | collective-permute-start | bytes 897032 | tf_op jit(solution)/shard_map/ppermute | solution.py:488
  28.5 4.6 %collective-permute-start.3 = (f32[584,128]{1,0:T(8,128)S(1)}, f32[584,128]{1,0:T(8,128)S(1)}, u32[]{:S(2)}, u32[]{:S(2)}) collective-permute-start(f32[584,128]{1,0:T(8,128)S(1)} %get-tuple-element.20), channel_id=1, source_target_pairs={{1,0},{2,1},{3,2},{4,3},{5,4},{6,5},{7,6},{0,7},{9,8},{10,9},{11,1... | collective-permute-start | bytes 897032 | tf_op jit(solution)/shard_map/ppermute | solution.py:488
  33.1 2.2 %collective-permute-done.2.refs_1_.refs_0_ = f32[584,128]{1,0:T(8,128)S(1)} collective-permute-done((f32[584,128]{1,0:T(8,128)S(1)}, f32[584,128]{1,0:T(8,128)S(1)}, u32[]{:S(2)}, u32[]{:S(2)}) %collective-permute-start.2) | collective-permute-done | bytes 299040 | tf_op jit(solution)/shard_map/ppermute | solution.py:488
  35.3 1.5 %collective-permute-done.3.refs_3_.refs_2_ = f32[584,128]{1,0:T(8,128)S(1)} collective-permute-done((f32[584,128]{1,0:T(8,128)S(1)}, f32[584,128]{1,0:T(8,128)S(1)}, u32[]{:S(2)}, u32[]{:S(2)}) %collective-permute-start.3) | collective-permute-done | bytes 299040 | tf_op jit(solution)/shard_map/ppermute | solution.py:488
  36.8 11.4 %collective-permute-start.4 = (f32[528,128]{1,0:T(8,128)S(1)}, f32[528,128]{1,0:T(8,128)S(1)}, u32[]{:S(2)}, u32[]{:S(2)}) collective-permute-start(f32[528,128]{1,0:T(8,128)S(1)} %get-tuple-element.21), channel_id=1, source_target_pairs={{8,16},{24,32},{40,48},{56,64},{72,80},{88,96},{104,112},{120,128}... | collective-permute-start | bytes 811016 | tf_op jit(solution)/shard_map/ppermute | solution.py:495
  48.2 1.9 %collective-permute-start.5 = (f32[528,128]{1,0:T(8,128)S(1)}, f32[528,128]{1,0:T(8,128)S(1)}, u32[]{:S(2)}, u32[]{:S(2)}) collective-permute-start(f32[528,128]{1,0:T(8,128)S(1)} %get-tuple-element.22), channel_id=1, source_target_pairs={{0,8},{16,24},{32,40},{48,56},{64,72},{80,88},{96,104},{112,120},{... | collective-permute-start | bytes 811016 | tf_op jit(solution)/shard_map/ppermute | solution.py:495
  50.2 4.4 %collective-permute-start.8 = (f32[480,128]{1,0:T(8,128)S(1)}, f32[480,128]{1,0:T(8,128)S(1)}, u32[]{:S(2)}, u32[]{:S(2)}) collective-permute-start(f32[480,128]{1,0:T(8,128)S(1)} %get-tuple-element.27), channel_id=1, source_target_pairs={{8,16},{24,32},{40,48},{56,64},{72,80},{88,96},{104,112},{120,128}... | collective-permute-start | bytes 737288 | tf_op jit(solution)/shard_map/ppermute | solution.py:495
  54.6 1.9 %collective-permute-start.9 = (f32[480,128]{1,0:T(8,128)S(1)}, f32[480,128]{1,0:T(8,128)S(1)}, u32[]{:S(2)}, u32[]{:S(2)}) collective-permute-start(f32[480,128]{1,0:T(8,128)S(1)} %get-tuple-element.28), channel_id=1, source_target_pairs={{0,8},{16,24},{32,40},{48,56},{64,72},{80,88},{96,104},{112,120},{... | collective-permute-start | bytes 737288 | tf_op jit(solution)/shard_map/ppermute | solution.py:495
  56.5 0.0 collective-permute-done.4.refs_6_
  56.5 0.0 collective-permute-done.5.refs_7_
  56.6 1.2 %right_side.1 = (f32[8,48,128]{2,1,0:T(8,128)S(1)}, f32[8,48,128]{2,1,0:T(8,128)S(1)}, f32[432,128]{1,0:T(8,128)S(1)}, f32[432,128]{1,0:T(8,128)S(1)}) custom-call(s32[1]{0:T(128)} %bitcast.refs_0_.parity_ref, f32[584,128]{1,0:T(8,128)S(1)} %collective-permute-done.2.refs_1_.refs_0_, f32[768,128]{1,0:T(8,128)S(1)} %get-tuple-element.19.refs_2_.refs_1_, ...), custom_call_target="tpu_custom_call" | custom-call | tf_op jit(solution)/shard_map/right_side/pallas_call | solution.py:30
  57.8 4.4 %collective-permute-start.6 = (f32[432,128]{1,0:T(8,128)S(1)}, f32[432,128]{1,0:T(8,128)S(1)}, u32[]{:S(2)}, u32[]{:S(2)}) collective-permute-start(f32[432,128]{1,0:T(8,128)S(1)} %get-tuple-element.25), channel_id=1, source_target_pairs={{8,16},{24,32},{40,48},{56,64},{72,80},{88,96},{104,112},{120,128}... | collective-permute-start | bytes 663560 | tf_op jit(solution)/shard_map/ppermute | solution.py:495
  62.2 1.9 %collective-permute-start.7 = (f32[432,128]{1,0:T(8,128)S(1)}, f32[432,128]{1,0:T(8,128)S(1)}, u32[]{:S(2)}, u32[]{:S(2)}) collective-permute-start(f32[432,128]{1,0:T(8,128)S(1)} %get-tuple-element.26), channel_id=1, source_target_pairs={{0,8},{16,24},{32,40},{48,56},{64,72},{80,88},{96,104},{112,120},{... | collective-permute-start | bytes 663560 | tf_op jit(solution)/shard_map/ppermute | solution.py:495
  64.1 0.0 collective-permute-done.8.refs_13_
  64.1 0.0 collective-permute-done.9.refs_14_
  64.1 1.7 %collective-permute-done.6.refs_11_ = f32[432,128]{1,0:T(8,128)S(1)} collective-permute-done((f32[432,128]{1,0:T(8,128)S(1)}, f32[432,128]{1,0:T(8,128)S(1)}, u32[]{:S(2)}, u32[]{:S(2)}) %collective-permute-start.6) | collective-permute-done | bytes 221216 | tf_op jit(solution)/shard_map/ppermute | solution.py:495
  65.8 0.0 collective-permute-done.7.refs_12_
  65.8 4.2 %first_image.1 = (f32[8,16,128]{2,1,0:T(8,128)S(1)}, f32[3,8,32,128]{3,2,1,0:T(8,128)S(1)}, f32[192,128]{1,0:T(8,128)S(1)}, f32[192,128]{1,0:T(8,128)S(1)}, f32[96,128]{1,0:T(8,128)}) custom-call(s32[1]{0:T(128)} %bitcast.refs_0_.parity_ref, f32[584,128]{1,0:T(8,128)S(1)} %collective-permute-done.2.refs_1_.refs_0_, ...), custom_call_target="tpu_custom_call" | custom-call | tf_op jit(solution)/shard_map/first_image/pallas_call | solution.py:30
  70.0 16.7 %all-to-all-start.1 = ((f32[48,2,128]{2,1,0:T(2,128)}), f32[48,2,128]{2,1,0:T(2,128)S(1)}, u32[]{:S(2)}, u32[]{:S(2)}) async-start(f32[48,2,128]{2,1,0:T(2,128)} %bitcast.5), calls=%async_computation.1 | async-start | bytes 98304 | tf_op jit(solution)/shard_map/all_to_all | solution.py:545
  86.7 2.8 %collective-permute-start.10 = (f32[192,128]{1,0:T(8,128)S(1)}, f32[192,128]{1,0:T(8,128)S(1)}, u32[]{:S(2)}, u32[]{:S(2)}) collective-permute-start(f32[192,128]{1,0:T(8,128)S(1)} %get-tuple-element.32), channel_id=1, source_target_pairs={{8,16},{24,32},{40,48},{56,64},{72,80},{88,96},{104,112},{120,128}... | collective-permute-start | bytes 294920 | tf_op jit(solution)/shard_map/ppermute | solution.py:495
  89.5 1.9 %collective-permute-start.11 = (f32[192,128]{1,0:T(8,128)S(1)}, f32[192,128]{1,0:T(8,128)S(1)}, u32[]{:S(2)}, u32[]{:S(2)}) collective-permute-start(f32[192,128]{1,0:T(8,128)S(1)} %get-tuple-element.33), channel_id=1, source_target_pairs={{0,8},{16,24},{32,40},{48,56},{64,72},{80,88},{96,104},{112,120},{... | collective-permute-start | bytes 294920 | tf_op jit(solution)/shard_map/ppermute | solution.py:495
  91.4 7.2 %all-to-all-done.1 = f32[48,2,128]{2,1,0:T(2,128)S(1)} async-done(((f32[48,2,128]{2,1,0:T(2,128)}), f32[48,2,128]{2,1,0:T(2,128)S(1)}, u32[]{:S(2)}, u32[]{:S(2)}) %all-to-all-start.1) | async-done | bytes 49184 | tf_op jit(solution)/shard_map/all_to_all | solution.py:545
  98.6 0.6 add.10
  99.2 5.7 %all-to-all-start.2 = ((f32[16,1,128]{2,1,0:T(1,128)}), f32[16,1,128]{2,1,0:T(1,128)S(1)}, u32[]{:S(2)}, u32[]{:S(2)}) async-start(f32[16,1,128]{2,1,0:T(1,128)} %bitcast.8), calls=%async_computation.2 | async-start | bytes 16384 | tf_op jit(solution)/shard_map/all_to_all | solution.py:551
  104.9 0.0 collective-permute-done.10.refs_11_
  104.9 0.0 collective-permute-done.11.refs_12_
  104.9 0.8 second_image.1.u_ref
  105.7 6.1 %all-to-all-done.2 = f32[16,1,128]{2,1,0:T(1,128)S(1)} async-done(((f32[16,1,128]{2,1,0:T(1,128)}), f32[16,1,128]{2,1,0:T(1,128)S(1)}, u32[]{:S(2)}, u32[]{:S(2)}) %all-to-all-start.2) | async-done | bytes 8224 | tf_op jit(solution)/shard_map/all_to_all | solution.py:551
  111.8 0.8 finish.1
  (2 shorter events, 0.1 us)
Async XLA Ops:
  4.1 7.8 %copy-start.2 = (f32[8,16,128]{2,1,0:T(8,128)S(1)}, f32[8,16,128]{2,1,0:T(8,128)}, u32[]{:S(2)}) copy-start(f32[8,16,128]{2,1,0:T(8,128)} %param.14) | copy-start | bytes 196612
  4.1 7.8 %copy-start.3 = (f32[8,16]{1,0:T(8,128)S(1)}, f32[8,16]{1,0:T(8,128)}, u32[]{:S(2)}) copy-start(f32[8,16]{1,0:T(8,128)} %diffusion_ref.1) | copy-start | bytes 1540
  4.1 22.1 %all-to-all-start = ((f32[8,136,128]{2,1,0:T(8,128)}), f32[8,136,128]{2,1,0:T(8,128)S(1)}, u32[]{:S(2)}, u32[]{:S(2)}) async-start(f32[8,136,128]{2,1,0:T(8,128)} %bucket.1), calls=%async_computation | async-start | bytes 1114112 | tf_op jit(solution)/shard_map/all_to_all | solution.py:514
  11.9 6.6 %copy-start = (f32[128,128]{1,0:T(8,128)S(1)}, f32[128,128]{1,0:T(8,128)}, u32[]{:S(2)}) copy-start(f32[128,128]{1,0:T(8,128)} %factor_ref.1) | copy-start | bytes 196612
  11.9 6.6 %copy-start.1 = (f32[128,128]{1,0:T(8,128)S(1)}, f32[128,128]{1,0:T(8,128)}, u32[]{:S(2)}) copy-start(f32[128,128]{1,0:T(8,128)} %mixing_ref.1) | copy-start | bytes 196612
  12.0 9.2 %collective-permute-start.1 = (f32[144,128]{1,0:T(8,128)S(1)}, f32[144,128]{1,0:T(8,128)S(1)}, u32[]{:S(2)}, u32[]{:S(2)}) collective-permute-start(f32[144,128]{1,0:T(8,128)S(1)} %fixed.1.refs_5_.refs_4_), channel_id=1, source_target_pairs={{1,0},{2,1},{3,2},{4,3},{5,4},{6,5},{7,6},{0,7},{9,8},{10,9},{11,1... | collective-permute-start | bytes 221192 | tf_op jit(solution)/shard_map/ppermute | solution.py:488
  16.6 9.6 %collective-permute-start = (f32[144,128]{1,0:T(8,128)S(1)}, f32[144,128]{1,0:T(8,128)S(1)}, u32[]{:S(2)}, u32[]{:S(2)}) collective-permute-start(f32[144,128]{1,0:T(8,128)S(1)} %fixed.1.refs_5_.refs_4_), channel_id=1, source_target_pairs={{0,1},{1,2},{2,3},{3,4},{4,5},{5,6},{6,7},{7,0},{8,9},{9,10},{10,1... | collective-permute-start | bytes 221192 | tf_op jit(solution)/shard_map/ppermute | solution.py:488
  26.6 8.7 %collective-permute-start.2 = (f32[584,128]{1,0:T(8,128)S(1)}, f32[584,128]{1,0:T(8,128)S(1)}, u32[]{:S(2)}, u32[]{:S(2)}) collective-permute-start(f32[584,128]{1,0:T(8,128)S(1)} %get-tuple-element.18), channel_id=1, source_target_pairs={{0,1},{1,2},{2,3},{3,4},{4,5},{5,6},{6,7},{7,0},{8,9},{9,10},{10,1... | collective-permute-start | bytes 897032 | tf_op jit(solution)/shard_map/ppermute | solution.py:488
  28.5 8.3 %collective-permute-start.3 = (f32[584,128]{1,0:T(8,128)S(1)}, f32[584,128]{1,0:T(8,128)S(1)}, u32[]{:S(2)}, u32[]{:S(2)}) collective-permute-start(f32[584,128]{1,0:T(8,128)S(1)} %get-tuple-element.20), channel_id=1, source_target_pairs={{1,0},{2,1},{3,2},{4,3},{5,4},{6,5},{7,6},{0,7},{9,8},{10,9},{11,1... | collective-permute-start | bytes 897032 | tf_op jit(solution)/shard_map/ppermute | solution.py:488
  36.8 19.7 %collective-permute-start.4 = (f32[528,128]{1,0:T(8,128)S(1)}, f32[528,128]{1,0:T(8,128)S(1)}, u32[]{:S(2)}, u32[]{:S(2)}) collective-permute-start(f32[528,128]{1,0:T(8,128)S(1)} %get-tuple-element.21), channel_id=1, source_target_pairs={{8,16},{24,32},{40,48},{56,64},{72,80},{88,96},{104,112},{120,128}... | collective-permute-start | bytes 811016 | tf_op jit(solution)/shard_map/ppermute | solution.py:495
  48.2 8.3 %collective-permute-start.5 = (f32[528,128]{1,0:T(8,128)S(1)}, f32[528,128]{1,0:T(8,128)S(1)}, u32[]{:S(2)}, u32[]{:S(2)}) collective-permute-start(f32[528,128]{1,0:T(8,128)S(1)} %get-tuple-element.22), channel_id=1, source_target_pairs={{0,8},{16,24},{32,40},{48,56},{64,72},{80,88},{96,104},{112,120},{... | collective-permute-start | bytes 811016 | tf_op jit(solution)/shard_map/ppermute | solution.py:495
  50.2 13.9 %collective-permute-start.8 = (f32[480,128]{1,0:T(8,128)S(1)}, f32[480,128]{1,0:T(8,128)S(1)}, u32[]{:S(2)}, u32[]{:S(2)}) collective-permute-start(f32[480,128]{1,0:T(8,128)S(1)} %get-tuple-element.27), channel_id=1, source_target_pairs={{8,16},{24,32},{40,48},{56,64},{72,80},{88,96},{104,112},{120,128}... | collective-permute-start | bytes 737288 | tf_op jit(solution)/shard_map/ppermute | solution.py:495
  54.6 9.5 %collective-permute-start.9 = (f32[480,128]{1,0:T(8,128)S(1)}, f32[480,128]{1,0:T(8,128)S(1)}, u32[]{:S(2)}, u32[]{:S(2)}) collective-permute-start(f32[480,128]{1,0:T(8,128)S(1)} %get-tuple-element.28), channel_id=1, source_target_pairs={{0,8},{16,24},{32,40},{48,56},{64,72},{80,88},{96,104},{112,120},{... | collective-permute-start | bytes 737288 | tf_op jit(solution)/shard_map/ppermute | solution.py:495
  57.8 8.0 %collective-permute-start.6 = (f32[432,128]{1,0:T(8,128)S(1)}, f32[432,128]{1,0:T(8,128)S(1)}, u32[]{:S(2)}, u32[]{:S(2)}) collective-permute-start(f32[432,128]{1,0:T(8,128)S(1)} %get-tuple-element.25), channel_id=1, source_target_pairs={{8,16},{24,32},{40,48},{56,64},{72,80},{88,96},{104,112},{120,128}... | collective-permute-start | bytes 663560 | tf_op jit(solution)/shard_map/ppermute | solution.py:495
  62.2 3.6 %collective-permute-start.7 = (f32[432,128]{1,0:T(8,128)S(1)}, f32[432,128]{1,0:T(8,128)S(1)}, u32[]{:S(2)}, u32[]{:S(2)}) collective-permute-start(f32[432,128]{1,0:T(8,128)S(1)} %get-tuple-element.26), channel_id=1, source_target_pairs={{0,8},{16,24},{32,40},{48,56},{64,72},{80,88},{96,104},{112,120},{... | collective-permute-start | bytes 663560 | tf_op jit(solution)/shard_map/ppermute | solution.py:495
  70.0 28.6 %all-to-all-start.1 = ((f32[48,2,128]{2,1,0:T(2,128)}), f32[48,2,128]{2,1,0:T(2,128)S(1)}, u32[]{:S(2)}, u32[]{:S(2)}) async-start(f32[48,2,128]{2,1,0:T(2,128)} %bitcast.5), calls=%async_computation.1 | async-start | bytes 98304 | tf_op jit(solution)/shard_map/all_to_all | solution.py:545
  86.7 18.2 %collective-permute-start.10 = (f32[192,128]{1,0:T(8,128)S(1)}, f32[192,128]{1,0:T(8,128)S(1)}, u32[]{:S(2)}, u32[]{:S(2)}) collective-permute-start(f32[192,128]{1,0:T(8,128)S(1)} %get-tuple-element.32), channel_id=1, source_target_pairs={{8,16},{24,32},{40,48},{56,64},{72,80},{88,96},{104,112},{120,128}... | collective-permute-start | bytes 294920 | tf_op jit(solution)/shard_map/ppermute | solution.py:495
  89.5 15.5 %collective-permute-start.11 = (f32[192,128]{1,0:T(8,128)S(1)}, f32[192,128]{1,0:T(8,128)S(1)}, u32[]{:S(2)}, u32[]{:S(2)}) collective-permute-start(f32[192,128]{1,0:T(8,128)S(1)} %get-tuple-element.33), channel_id=1, source_target_pairs={{0,8},{16,24},{32,40},{48,56},{64,72},{80,88},{96,104},{112,120},{... | collective-permute-start | bytes 294920 | tf_op jit(solution)/shard_map/ppermute | solution.py:495
  99.2 12.6 %all-to-all-start.2 = ((f32[16,1,128]{2,1,0:T(1,128)}), f32[16,1,128]{2,1,0:T(1,128)S(1)}, u32[]{:S(2)}, u32[]{:S(2)}) async-start(f32[16,1,128]{2,1,0:T(1,128)} %bitcast.8), calls=%async_computation.2 | async-start | bytes 16384 | tf_op jit(solution)/shard_map/all_to_all | solution.py:551

commit v10 on v8

--- a/solution.py
+++ b/solution.py
@@ -325,16 +325,18 @@
                 for r in range(first, stop):
                     get(r)
 
-    def adjoint(self, h, forcing, std):
+    def adjoint(self, h, forcing, std, last=None):
         for t in range(STEPS - 1, -1, -1):
             first, stop = -h - t - 1, ROWS + h + t + 1
             self.mix(first, stop, MIX_T)
             if t > 0:
                 put = lambda r, value, t=t: self.put(r, value + forcing(t - 1, r))
+            elif last is None:
+                put = lambda r, value: self.put(r, std(r) * value)
             else:
-                put = lambda r, value: self.put(r, std(r) * value)
+                put = lambda r, value: last.put(r, std(r) * inside(value))
             self.smooth(first, stop, self.get, put)
-        self.mix(-h, ROWS + h, FACTOR_T)
+        (last or self).mix(-h, ROWS + h, FACTOR_T)
 
 
 def scratch(width, reach):
@@ -390,8 +392,12 @@
     out, sums_ref = Sides(parity_ref, *refs[17:19], THIRD), refs[19]
     field = Field(WIDE, REACH, *refs[20:24], m_ref)
     tops = refs[24:26]
+    inner = Field(INNER, STEPS, *refs[26:30], m_ref)
     field.fill_diffusion(tile, sides, REACH - 1)
-    std = std_rows(tile, sides)
+    for r in range(-STEPS, ROWS + STEPS):
+        inner.d_ref[inner.at(r)] = inside(field.d_ref[field.at(r)])
+    wide_std = std_rows(tile, sides)
+    std = lambda r: inside(wide_std(r))
 
     def weights(t, r):
         return tile.weights(t, r) if own(r) else padded(forced.taken(("w", t), r))
@@ -409,26 +415,26 @@
                 field.put(r, weights(t, r) * value)
 
     field.forward(REACH, start, force, scaled=True)
-    field.adjoint(STEPS, lambda t, r: tops[t][field.at(r)], std)
+    field.adjoint(STEPS, lambda t, r: tops[t][field.at(r)], std, inner)
     sums = [jnp.zeros((COLS, L), F32) for _ in range(4)]
     for r in range(-STEPS, ROWS + STEPS):
-        b = b_ref[r] if own(r) else padded(more.taken("b", r))
-        q = b + field.get(r)
-        field.put(r, q)
+        b = inside(b_ref[r]) if own(r) else more.taken("b", r)
+        q = b + inner.get(r)
+        inner.put(r, q)
         if own(r):
-            b, q = b[MIDDLE], q[MIDDLE]
+            b, q = b[EDGE : EDGE + COLS], q[EDGE : EDGE + COLS]
             q_ref[r] = q
             for i, term in enumerate((b * b, b * q, q * q, q * q)):
                 sums[i] = sums[i] + term
-    field.mix(-STEPS, ROWS + STEPS, FACTOR)
+    inner.mix(-STEPS, ROWS + STEPS, FACTOR)
 
     def keep(t, r, value):
         if own(r):
-            forcing = tile.weights(t, r) * value
-            sums[3] = sums[3] + forcing[MIDDLE] * value[MIDDLE]
-            g_ref[t, r] = inside(forcing)
-
-    field.forward(STEPS, lambda r: std(r) * field.get(r), keep)
+            forcing = jnp.concatenate(tile.inner_weights(t, r), axis=0) * value
+            sums[3] = sums[3] + forcing[EDGE : EDGE + COLS] * value[EDGE : EDGE + COLS]
+            g_ref[t, r] = forcing
+
+    inner.forward(STEPS, lambda r: std(r) * inner.get(r), keep)
     for kind, h in THIRD:
         out.send(kind, h, lambda r: g_ref[kind[1], r])
     lane = lax.broadcasted_iota(jnp.int32, (1, L), 1)
@@ -539,7 +545,7 @@
         first_image_kernel,
         "first_image",
         (small, shape(STEPS, ROWS, INNER, L), side, side, shape(lat, L)),
-        space + [space[0]] * 2,
+        space + [space[0]] * 2 + scratch(INNER, STEPS),
         smem=(0,),
     )(side_of, *refs, b, y, south, north, *weights)
     sums = lax.all_to_all(sums, "lat", 0, 0, axis_index_groups=near, tiled=True)

time: 112 us -> 112 us (level)
  no operation moved by 1% of the time
where the time goes in v10:
time: 112 us; the launch traced here: 111 us
  starting transfers between devices  73.7 us (66%)
  waiting for transfers between devices  25.2 us (22%)
  Pallas kernels  10.9 us (10%)
  between operations  1.58 us (1%)
    ppermute x4, starting transfers between devices, swap(): lax.ppermute(chip, 'lat', both[1])  23.7 us
    all_to_all x1, starting transfers between devices, shards(): sums = lax.all_to_all(sums, 'lat', 0, 0, axis_index_groups=near, tiled=True)  14 us
    pallas_call x11, Pallas kernels, run(): pl.pallas_call(kernel, name=name, out_shape=outs, in_specs=specs, out_spe...  10.9 us
    ppermute x2, starting transfers between devices, exchange(): lax.ppermute(to_before, 'lon', down)  9.15 us
    all_to_all x1, starting transfers between devices, shards(): received = lax.all_to_all(buckets, 'lon', 0, 0)  7.8 us
    all_to_all x1, waiting for transfers between devices, shards(): lax.all_to_all(sums, ('lat', 'lon'), 0, 0, axis_index_groups=far, tiled=T...  7.75 us
    ppermute x4, starting transfers between devices, swap(): lax.ppermute(core, 'lat', both[0])  7.68 us
    all_to_all x1, starting transfers between devices, shards(): lax.all_to_all(sums, ('lat', 'lon'), 0, 0, axis_index_groups=far, tiled=T...  7.54 us
  transfers between devices with their start and end apart: 15, of which 7 were waited for; matrix products, arithmetic and copies ran while one was open for 0% of the time, Pallas kernels for 3%

profile of v10, /device:TPU:1, one launch (start us, length us, event | category | flops | bytes accessed | tf_op | source)
XLA Modules:
  0.0 111.4 jit_solution(1657879285088985308)
XLA Ops:
  1.3 2.8 %bucket.1 = f32[8,136,128]{2,1,0:T(8,128)} custom-call(f32[256,128]{1,0:T(8,128)} %departures_hbm.1, f32[256,128]{1,0:T(8,128)} %weight_hbm.1, s32[1,256]{1,0:T(1,128)} %bitcast.14, s32[1,256]{1,0:T(1,128)} %bitcast.15, s32[1]{0:T(128)S(6)} %copy.12.counts_ref, s32[1]{0:T(128)} %bitcast.3.parity_ref), custom_call_target="tpu_custom_call" | custom-call | tf_op jit(solution)/shard_map/bucket/pallas_call | solution.py:30
  4.1 0.0 copy-start.2
  4.1 0.0 copy-start.3
  4.1 7.8 %all-to-all-start = ((f32[8,136,128]{2,1,0:T(8,128)}), f32[8,136,128]{2,1,0:T(8,128)S(1)}, u32[]{:S(2)}, u32[]{:S(2)}) async-start(f32[8,136,128]{2,1,0:T(8,128)} %bucket.1), calls=%async_computation | async-start | bytes 1114112 | tf_op jit(solution)/shard_map/all_to_all | solution.py:520
  11.9 0.0 copy-done.2
  11.9 0.0 copy-done.3
  11.9 0.0 copy-start
  11.9 0.0 copy-start.1
  11.9 0.1 fixed.1.refs_5_.refs_4_
  12.0 4.6 %collective-permute-start.1 = (f32[144,128]{1,0:T(8,128)S(1)}, f32[144,128]{1,0:T(8,128)S(1)}, u32[]{:S(2)}, u32[]{:S(2)}) collective-permute-start(f32[144,128]{1,0:T(8,128)S(1)} %fixed.1.refs_5_.refs_4_), channel_id=1, source_target_pairs={{1,0},{2,1},{3,2},{4,3},{5,4},{6,5},{7,6},{0,7},{9,8},{10,9},{11,1... | collective-permute-start | bytes 221192 | tf_op jit(solution)/shard_map/ppermute | solution.py:494
  16.6 1.9 %collective-permute-start = (f32[144,128]{1,0:T(8,128)S(1)}, f32[144,128]{1,0:T(8,128)S(1)}, u32[]{:S(2)}, u32[]{:S(2)}) collective-permute-start(f32[144,128]{1,0:T(8,128)S(1)} %fixed.1.refs_5_.refs_4_), channel_id=1, source_target_pairs={{0,1},{1,2},{2,3},{3,4},{4,5},{5,6},{6,7},{7,0},{8,9},{9,10},{10,1... | collective-permute-start | bytes 221192 | tf_op jit(solution)/shard_map/ppermute | solution.py:494
  18.6 0.0 copy-done
  18.6 0.0 copy-done.1
  18.6 0.1 matrices.1.m_ref.refs_8_
  18.7 2.6 %collective-permute-done.1.fixed_right_ref.refs_6_.refs_5_ = f32[144,128]{1,0:T(8,128)S(1)} collective-permute-done((f32[144,128]{1,0:T(8,128)S(1)}, f32[144,128]{1,0:T(8,128)S(1)}, u32[]{:S(2)}, u32[]{:S(2)}) %collective-permute-start.1) | collective-permute-done | bytes 73760 | tf_op jit(solution)/shard_map/ppermute | solution.py:494
  21.3 4.9 %collective-permute-done.fixed_left_ref.refs_4_.refs_3_ = f32[144,128]{1,0:T(8,128)S(1)} collective-permute-done((f32[144,128]{1,0:T(8,128)S(1)}, f32[144,128]{1,0:T(8,128)S(1)}, u32[]{:S(2)}, u32[]{:S(2)}) %collective-permute-start) | collective-permute-done | bytes 73760 | tf_op jit(solution)/shard_map/ppermute | solution.py:494
  26.2 0.0 all-to-all-done.received_ref
  26.2 0.4 tile.1
  26.6 1.9 %collective-permute-start.2 = (f32[584,128]{1,0:T(8,128)S(1)}, f32[584,128]{1,0:T(8,128)S(1)}, u32[]{:S(2)}, u32[]{:S(2)}) collective-permute-start(f32[584,128]{1,0:T(8,128)S(1)} %get-tuple-element.18), channel_id=1, source_target_pairs={{0,1},{1,2},{2,3},{3,4},{4,5},{5,6},{6,7},{7,0},{8,9},{9,10},{10,1... | collective-permute-start | bytes 897032 | tf_op jit(solution)/shard_map/ppermute | solution.py:494
  28.5 4.6 %collective-permute-start.3 = (f32[584,128]{1,0:T(8,128)S(1)}, f32[584,128]{1,0:T(8,128)S(1)}, u32[]{:S(2)}, u32[]{:S(2)}) collective-permute-start(f32[584,128]{1,0:T(8,128)S(1)} %get-tuple-element.20), channel_id=1, source_target_pairs={{1,0},{2,1},{3,2},{4,3},{5,4},{6,5},{7,6},{0,7},{9,8},{10,9},{11,1... | collective-permute-start | bytes 897032 | tf_op jit(solution)/shard_map/ppermute | solution.py:494
  33.1 2.2 %collective-permute-done.2.refs_1_.refs_0_ = f32[584,128]{1,0:T(8,128)S(1)} collective-permute-done((f32[584,128]{1,0:T(8,128)S(1)}, f32[584,128]{1,0:T(8,128)S(1)}, u32[]{:S(2)}, u32[]{:S(2)}) %collective-permute-start.2) | collective-permute-done | bytes 299040 | tf_op jit(solution)/shard_map/ppermute | solution.py:494
  35.3 1.5 %collective-permute-done.3.refs_3_.refs_2_ = f32[584,128]{1,0:T(8,128)S(1)} collective-permute-done((f32[584,128]{1,0:T(8,128)S(1)}, f32[584,128]{1,0:T(8,128)S(1)}, u32[]{:S(2)}, u32[]{:S(2)}) %collective-permute-start.3) | collective-permute-done | bytes 299040 | tf_op jit(solution)/shard_map/ppermute | solution.py:494
  36.8 11.4 %collective-permute-start.4 = (f32[528,128]{1,0:T(8,128)S(1)}, f32[528,128]{1,0:T(8,128)S(1)}, u32[]{:S(2)}, u32[]{:S(2)}) collective-permute-start(f32[528,128]{1,0:T(8,128)S(1)} %get-tuple-element.21), channel_id=1, source_target_pairs={{8,16},{24,32},{40,48},{56,64},{72,80},{88,96},{104,112},{120,128}... | collective-permute-start | bytes 811016 | tf_op jit(solution)/shard_map/ppermute | solution.py:501
  48.2 1.9 %collective-permute-start.5 = (f32[528,128]{1,0:T(8,128)S(1)}, f32[528,128]{1,0:T(8,128)S(1)}, u32[]{:S(2)}, u32[]{:S(2)}) collective-permute-start(f32[528,128]{1,0:T(8,128)S(1)} %get-tuple-element.22), channel_id=1, source_target_pairs={{0,8},{16,24},{32,40},{48,56},{64,72},{80,88},{96,104},{112,120},{... | collective-permute-start | bytes 811016 | tf_op jit(solution)/shard_map/ppermute | solution.py:501
  50.2 4.4 %collective-permute-start.8 = (f32[480,128]{1,0:T(8,128)S(1)}, f32[480,128]{1,0:T(8,128)S(1)}, u32[]{:S(2)}, u32[]{:S(2)}) collective-permute-start(f32[480,128]{1,0:T(8,128)S(1)} %get-tuple-element.27), channel_id=1, source_target_pairs={{8,16},{24,32},{40,48},{56,64},{72,80},{88,96},{104,112},{120,128}... | collective-permute-start | bytes 737288 | tf_op jit(solution)/shard_map/ppermute | solution.py:501
  54.6 1.9 %collective-permute-start.9 = (f32[480,128]{1,0:T(8,128)S(1)}, f32[480,128]{1,0:T(8,128)S(1)}, u32[]{:S(2)}, u32[]{:S(2)}) collective-permute-start(f32[480,128]{1,0:T(8,128)S(1)} %get-tuple-element.28), channel_id=1, source_target_pairs={{0,8},{16,24},{32,40},{48,56},{64,72},{80,88},{96,104},{112,120},{... | collective-permute-start | bytes 737288 | tf_op jit(solution)/shard_map/ppermute | solution.py:501
  56.5 0.0 collective-permute-done.4.refs_6_
  56.5 0.0 collective-permute-done.5.refs_7_
  56.6 1.2 %right_side.1 = (f32[8,48,128]{2,1,0:T(8,128)S(1)}, f32[8,48,128]{2,1,0:T(8,128)S(1)}, f32[432,128]{1,0:T(8,128)S(1)}, f32[432,128]{1,0:T(8,128)S(1)}) custom-call(s32[1]{0:T(128)} %bitcast.refs_0_.parity_ref, f32[584,128]{1,0:T(8,128)S(1)} %collective-permute-done.2.refs_1_.refs_0_, f32[768,128]{1,0:T(8,128)S(1)} %get-tuple-element.19.refs_2_.refs_1_, ...), custom_call_target="tpu_custom_call" | custom-call | tf_op jit(solution)/shard_map/right_side/pallas_call | solution.py:30
  57.8 4.4 %collective-permute-start.6 = (f32[432,128]{1,0:T(8,128)S(1)}, f32[432,128]{1,0:T(8,128)S(1)}, u32[]{:S(2)}, u32[]{:S(2)}) collective-permute-start(f32[432,128]{1,0:T(8,128)S(1)} %get-tuple-element.25), channel_id=1, source_target_pairs={{8,16},{24,32},{40,48},{56,64},{72,80},{88,96},{104,112},{120,128}... | collective-permute-start | bytes 663560 | tf_op jit(solution)/shard_map/ppermute | solution.py:501
  62.2 1.9 %collective-permute-start.7 = (f32[432,128]{1,0:T(8,128)S(1)}, f32[432,128]{1,0:T(8,128)S(1)}, u32[]{:S(2)}, u32[]{:S(2)}) collective-permute-start(f32[432,128]{1,0:T(8,128)S(1)} %get-tuple-element.26), channel_id=1, source_target_pairs={{0,8},{16,24},{32,40},{48,56},{64,72},{80,88},{96,104},{112,120},{... | collective-permute-start | bytes 663560 | tf_op jit(solution)/shard_map/ppermute | solution.py:501
  64.1 0.0 collective-permute-done.8.refs_13_
  64.1 0.0 collective-permute-done.9.refs_14_
  64.1 1.7 %collective-permute-done.6.refs_11_ = f32[432,128]{1,0:T(8,128)S(1)} collective-permute-done((f32[432,128]{1,0:T(8,128)S(1)}, f32[432,128]{1,0:T(8,128)S(1)}, u32[]{:S(2)}, u32[]{:S(2)}) %collective-permute-start.6) | collective-permute-done | bytes 221216 | tf_op jit(solution)/shard_map/ppermute | solution.py:501
  65.8 0.0 collective-permute-done.7.refs_12_
  65.8 4.0 %first_image.1 = (f32[8,16,128]{2,1,0:T(8,128)S(1)}, f32[3,8,32,128]{3,2,1,0:T(8,128)S(1)}, f32[192,128]{1,0:T(8,128)S(1)}, f32[192,128]{1,0:T(8,128)S(1)}, f32[96,128]{1,0:T(8,128)}) custom-call(s32[1]{0:T(128)} %bitcast.refs_0_.parity_ref, f32[584,128]{1,0:T(8,128)S(1)} %collective-permute-done.2.refs_1_.refs_0_, ...), custom_call_target="tpu_custom_call" | custom-call | tf_op jit(solution)/shard_map/first_image/pallas_call | solution.py:30
  69.8 14.0 %all-to-all-start.1 = ((f32[24,4,128]{2,1,0:T(4,128)}), f32[24,4,128]{2,1,0:T(4,128)S(1)}, u32[]{:S(2)}, u32[]{:S(2)}) async-start(f32[24,4,128]{2,1,0:T(4,128)} %bitcast.5), calls=%async_computation.1 | async-start | bytes 98304 | tf_op jit(solution)/shard_map/all_to_all | solution.py:551
  83.8 3.5 %collective-permute-start.10 = (f32[192,128]{1,0:T(8,128)S(1)}, f32[192,128]{1,0:T(8,128)S(1)}, u32[]{:S(2)}, u32[]{:S(2)}) collective-permute-start(f32[192,128]{1,0:T(8,128)S(1)} %get-tuple-element.32), channel_id=1, source_target_pairs={{8,16},{24,32},{40,48},{56,64},{72,80},{88,96},{104,112},{120,128}... | collective-permute-start | bytes 294920 | tf_op jit(solution)/shard_map/ppermute | solution.py:501
  87.3 1.9 %collective-permute-start.11 = (f32[192,128]{1,0:T(8,128)S(1)}, f32[192,128]{1,0:T(8,128)S(1)}, u32[]{:S(2)}, u32[]{:S(2)}) collective-permute-start(f32[192,128]{1,0:T(8,128)S(1)} %get-tuple-element.33), channel_id=1, source_target_pairs={{0,8},{16,24},{32,40},{48,56},{64,72},{80,88},{96,104},{112,120},{... | collective-permute-start | bytes 294920 | tf_op jit(solution)/shard_map/ppermute | solution.py:501
  89.2 4.6 %all-to-all-done.1 = f32[24,4,128]{2,1,0:T(4,128)S(1)} async-done(((f32[24,4,128]{2,1,0:T(4,128)}), f32[24,4,128]{2,1,0:T(4,128)S(1)}, u32[]{:S(2)}, u32[]{:S(2)}) %all-to-all-start.1) | async-done | bytes 49184 | tf_op jit(solution)/shard_map/all_to_all | solution.py:551
  93.8 0.6 add.10
  94.5 7.5 %all-to-all-start.2 = ((f32[32,1,128]{2,1,0:T(1,128)}), f32[32,1,128]{2,1,0:T(1,128)S(1)}, u32[]{:S(2)}, u32[]{:S(2)}) async-start(f32[32,1,128]{2,1,0:T(1,128)} %bitcast.8), calls=%async_computation.2 | async-start | bytes 32768 | tf_op jit(solution)/shard_map/all_to_all | solution.py:557
  102.0 0.0 collective-permute-done.10.refs_11_
  102.0 0.0 collective-permute-done.11.refs_12_
  102.0 0.8 second_image.1.u_ref
  102.8 7.8 %all-to-all-done.2 = f32[32,1,128]{2,1,0:T(1,128)S(1)} async-done(((f32[32,1,128]{2,1,0:T(1,128)}), f32[32,1,128]{2,1,0:T(1,128)S(1)}, u32[]{:S(2)}, u32[]{:S(2)}) %all-to-all-start.2) | async-done | bytes 16416 | tf_op jit(solution)/shard_map/all_to_all | solution.py:557
  110.6 0.8 finish.1
  (2 shorter events, 0.1 us)
Async XLA Ops:
  4.1 7.8 %copy-start.2 = (f32[8,16,128]{2,1,0:T(8,128)S(1)}, f32[8,16,128]{2,1,0:T(8,128)}, u32[]{:S(2)}) copy-start(f32[8,16,128]{2,1,0:T(8,128)} %param.14) | copy-start | bytes 196612
  4.1 7.8 %copy-start.3 = (f32[8,16]{1,0:T(8,128)S(1)}, f32[8,16]{1,0:T(8,128)}, u32[]{:S(2)}) copy-start(f32[8,16]{1,0:T(8,128)} %diffusion_ref.1) | copy-start | bytes 1540
  4.1 22.1 %all-to-all-start = ((f32[8,136,128]{2,1,0:T(8,128)}), f32[8,136,128]{2,1,0:T(8,128)S(1)}, u32[]{:S(2)}, u32[]{:S(2)}) async-start(f32[8,136,128]{2,1,0:T(8,128)} %bucket.1), calls=%async_computation | async-start | bytes 1114112 | tf_op jit(solution)/shard_map/all_to_all | solution.py:520
  11.9 6.6 %copy-start = (f32[128,128]{1,0:T(8,128)S(1)}, f32[128,128]{1,0:T(8,128)}, u32[]{:S(2)}) copy-start(f32[128,128]{1,0:T(8,128)} %factor_ref.1) | copy-start | bytes 196612
  11.9 6.6 %copy-start.1 = (f32[128,128]{1,0:T(8,128)S(1)}, f32[128,128]{1,0:T(8,128)}, u32[]{:S(2)}) copy-start(f32[128,128]{1,0:T(8,128)} %mixing_ref.1) | copy-start | bytes 196612
  12.0 9.2 %collective-permute-start.1 = (f32[144,128]{1,0:T(8,128)S(1)}, f32[144,128]{1,0:T(8,128)S(1)}, u32[]{:S(2)}, u32[]{:S(2)}) collective-permute-start(f32[144,128]{1,0:T(8,128)S(1)} %fixed.1.refs_5_.refs_4_), channel_id=1, source_target_pairs={{1,0},{2,1},{3,2},{4,3},{5,4},{6,5},{7,6},{0,7},{9,8},{10,9},{11,1... | collective-permute-start | bytes 221192 | tf_op jit(solution)/shard_map/ppermute | solution.py:494
  16.6 9.6 %collective-permute-start = (f32[144,128]{1,0:T(8,128)S(1)}, f32[144,128]{1,0:T(8,128)S(1)}, u32[]{:S(2)}, u32[]{:S(2)}) collective-permute-start(f32[144,128]{1,0:T(8,128)S(1)} %fixed.1.refs_5_.refs_4_), channel_id=1, source_target_pairs={{0,1},{1,2},{2,3},{3,4},{4,5},{5,6},{6,7},{7,0},{8,9},{9,10},{10,1... | collective-permute-start | bytes 221192 | tf_op jit(solution)/shard_map/ppermute | solution.py:494
  26.6 8.7 %collective-permute-start.2 = (f32[584,128]{1,0:T(8,128)S(1)}, f32[584,128]{1,0:T(8,128)S(1)}, u32[]{:S(2)}, u32[]{:S(2)}) collective-permute-start(f32[584,128]{1,0:T(8,128)S(1)} %get-tuple-element.18), channel_id=1, source_target_pairs={{0,1},{1,2},{2,3},{3,4},{4,5},{5,6},{6,7},{7,0},{8,9},{9,10},{10,1... | collective-permute-start | bytes 897032 | tf_op jit(solution)/shard_map/ppermute | solution.py:494
  28.5 8.3 %collective-permute-start.3 = (f32[584,128]{1,0:T(8,128)S(1)}, f32[584,128]{1,0:T(8,128)S(1)}, u32[]{:S(2)}, u32[]{:S(2)}) collective-permute-start(f32[584,128]{1,0:T(8,128)S(1)} %get-tuple-element.20), channel_id=1, source_target_pairs={{1,0},{2,1},{3,2},{4,3},{5,4},{6,5},{7,6},{0,7},{9,8},{10,9},{11,1... | collective-permute-start | bytes 897032 | tf_op jit(solution)/shard_map/ppermute | solution.py:494
  36.8 19.7 %collective-permute-start.4 = (f32[528,128]{1,0:T(8,128)S(1)}, f32[528,128]{1,0:T(8,128)S(1)}, u32[]{:S(2)}, u32[]{:S(2)}) collective-permute-start(f32[528,128]{1,0:T(8,128)S(1)} %get-tuple-element.21), channel_id=1, source_target_pairs={{8,16},{24,32},{40,48},{56,64},{72,80},{88,96},{104,112},{120,128}... | collective-permute-start | bytes 811016 | tf_op jit(solution)/shard_map/ppermute | solution.py:501
  48.2 8.3 %collective-permute-start.5 = (f32[528,128]{1,0:T(8,128)S(1)}, f32[528,128]{1,0:T(8,128)S(1)}, u32[]{:S(2)}, u32[]{:S(2)}) collective-permute-start(f32[528,128]{1,0:T(8,128)S(1)} %get-tuple-element.22), channel_id=1, source_target_pairs={{0,8},{16,24},{32,40},{48,56},{64,72},{80,88},{96,104},{112,120},{... | collective-permute-start | bytes 811016 | tf_op jit(solution)/shard_map/ppermute | solution.py:501
  50.2 13.9 %collective-permute-start.8 = (f32[480,128]{1,0:T(8,128)S(1)}, f32[480,128]{1,0:T(8,128)S(1)}, u32[]{:S(2)}, u32[]{:S(2)}) collective-permute-start(f32[480,128]{1,0:T(8,128)S(1)} %get-tuple-element.27), channel_id=1, source_target_pairs={{8,16},{24,32},{40,48},{56,64},{72,80},{88,96},{104,112},{120,128}... | collective-permute-start | bytes 737288 | tf_op jit(solution)/shard_map/ppermute | solution.py:501
  54.6 9.5 %collective-permute-start.9 = (f32[480,128]{1,0:T(8,128)S(1)}, f32[480,128]{1,0:T(8,128)S(1)}, u32[]{:S(2)}, u32[]{:S(2)}) collective-permute-start(f32[480,128]{1,0:T(8,128)S(1)} %get-tuple-element.28), channel_id=1, source_target_pairs={{0,8},{16,24},{32,40},{48,56},{64,72},{80,88},{96,104},{112,120},{... | collective-permute-start | bytes 737288 | tf_op jit(solution)/shard_map/ppermute | solution.py:501
  57.8 8.0 %collective-permute-start.6 = (f32[432,128]{1,0:T(8,128)S(1)}, f32[432,128]{1,0:T(8,128)S(1)}, u32[]{:S(2)}, u32[]{:S(2)}) collective-permute-start(f32[432,128]{1,0:T(8,128)S(1)} %get-tuple-element.25), channel_id=1, source_target_pairs={{8,16},{24,32},{40,48},{56,64},{72,80},{88,96},{104,112},{120,128}... | collective-permute-start | bytes 663560 | tf_op jit(solution)/shard_map/ppermute | solution.py:501
  62.2 3.6 %collective-permute-start.7 = (f32[432,128]{1,0:T(8,128)S(1)}, f32[432,128]{1,0:T(8,128)S(1)}, u32[]{:S(2)}, u32[]{:S(2)}) collective-permute-start(f32[432,128]{1,0:T(8,128)S(1)} %get-tuple-element.26), channel_id=1, source_target_pairs={{0,8},{16,24},{32,40},{48,56},{64,72},{80,88},{96,104},{112,120},{... | collective-permute-start | bytes 663560 | tf_op jit(solution)/shard_map/ppermute | solution.py:501
  69.8 24.1 %all-to-all-start.1 = ((f32[24,4,128]{2,1,0:T(4,128)}), f32[24,4,128]{2,1,0:T(4,128)S(1)}, u32[]{:S(2)}, u32[]{:S(2)}) async-start(f32[24,4,128]{2,1,0:T(4,128)} %bitcast.5), calls=%async_computation.1 | async-start | bytes 98304 | tf_op jit(solution)/shard_map/all_to_all | solution.py:551
  83.8 18.3 %collective-permute-start.10 = (f32[192,128]{1,0:T(8,128)S(1)}, f32[192,128]{1,0:T(8,128)S(1)}, u32[]{:S(2)}, u32[]{:S(2)}) collective-permute-start(f32[192,128]{1,0:T(8,128)S(1)} %get-tuple-element.32), channel_id=1, source_target_pairs={{8,16},{24,32},{40,48},{56,64},{72,80},{88,96},{104,112},{120,128}... | collective-permute-start | bytes 294920 | tf_op jit(solution)/shard_map/ppermute | solution.py:501
  87.3 14.7 %collective-permute-start.11 = (f32[192,128]{1,0:T(8,128)S(1)}, f32[192,128]{1,0:T(8,128)S(1)}, u32[]{:S(2)}, u32[]{:S(2)}) collective-permute-start(f32[192,128]{1,0:T(8,128)S(1)} %get-tuple-element.33), channel_id=1, source_target_pairs={{0,8},{16,24},{32,40},{48,56},{64,72},{80,88},{96,104},{112,120},{... | collective-permute-start | bytes 294920 | tf_op jit(solution)/shard_map/ppermute | solution.py:501
  94.5 16.1 %all-to-all-start.2 = ((f32[32,1,128]{2,1,0:T(1,128)}), f32[32,1,128]{2,1,0:T(1,128)S(1)}, u32[]{:S(2)}, u32[]{:S(2)}) async-start(f32[32,1,128]{2,1,0:T(1,128)} %bitcast.8), calls=%async_computation.2 | async-start | bytes 32768 | tf_op jit(solution)/shard_map/all_to_all | solution.py:557

commit v11 on v10

--- a/solution.py
+++ b/solution.py
@@ -135,7 +135,7 @@
 PACKED = SIZE + STEPS * ROWS * EDGE
 
 
-def tile_kernel(received_ref, fixed_left_ref, fixed_right_ref, m_ref, own_ref, to_left_ref, to_right_ref):
+def tile_kernel(received_ref, fixed_ref, m_ref, own_ref, to_left_ref, to_right_ref):
     ones, data = [], []
     cell = lax.broadcasted_iota(jnp.int32, (SIZE, L), 0)
     for j in range(4):
@@ -523,7 +523,7 @@
     fixed_left, fixed_right = exchange(fixed, fixed)
     beside = shape(PACKED + ROWS, L)
     tile, to_left, to_right = call(tile_kernel, "tile", (shape(2 * SIZE, L), beside, beside))(
-        received, fixed_left, fixed_right, mats
+        received, fixed, mats
     )
     left, right = exchange(to_left, to_right)
     refs = (left, tile, right, fixed_left, fixed, fixed_right)

time: 112 us -> 114 us (1.018)
  waiting for transfers between devices: 25.2 us -> 29.4 us
  starting transfers between devices: 73.7 us -> 70.8 us
    all_to_all x1, waiting for transfers between devices: 0.01 us -> 11.6 us  [shards(): received = lax.all_to_all(buckets, 'lon', 0, 0)]
    ppermute x2, waiting for transfers between devices: 4.06 us -> 0.01 us  [exchange(): lax.ppermute(to_before, 'lon', down)]
    ppermute x2, waiting for transfers between devices: 7.12 us -> 3.69 us  [exchange(): lax.ppermute(to_after, 'lon', up)]
    ppermute x2, starting transfers between devices: 9.15 us -> 6.18 us  [exchange(): lax.ppermute(to_before, 'lon', down)]
    ppermute x2, starting transfers between devices: 3.84 us -> 5.6 us  [exchange(): lax.ppermute(to_after, 'lon', up)]
    all_to_all x1, starting transfers between devices: 7.54 us -> 5.98 us  [shards(): lax.all_to_all(sums, ('lat', 'lon'), 0, 0, axis_index_groups=far, tiled=T...]
  transfers between devices with their start and end apart: 15 -> 15, of which waited for: 7 -> 5; matrix products, arithmetic and copies ran while one was open for 0% -> 0% of each run, Pallas kernels for 3% -> 3%
where the time goes in v11:
time: 114 us; the launch traced here: 113 us
  starting transfers between devices  70.8 us (62%)
  waiting for transfers between devices  29.4 us (26%)
  Pallas kernels  10.9 us (10%)
  between operations  1.57 us (1%)
    ppermute x4, starting transfers between devices, swap(): lax.ppermute(chip, 'lat', both[1])  23.6 us
    all_to_all x1, starting transfers between devices, shards(): sums = lax.all_to_all(sums, 'lat', 0, 0, axis_index_groups=near, tiled=True)  14 us
    all_to_all x1, waiting for transfers between devices, shards(): received = lax.all_to_all(buckets, 'lon', 0, 0)  11.6 us
    pallas_call x11, Pallas kernels, run(): pl.pallas_call(kernel, name=name, out_shape=outs, in_specs=specs, out_spe...  10.9 us
    all_to_all x1, starting transfers between devices, shards(): received = lax.all_to_all(buckets, 'lon', 0, 0)  7.8 us
    all_to_all x1, waiting for transfers between devices, shards(): lax.all_to_all(sums, ('lat', 'lon'), 0, 0, axis_index_groups=far, tiled=T...  7.75 us
    ppermute x4, starting transfers between devices, swap(): lax.ppermute(core, 'lat', both[0])  7.68 us
    ppermute x2, starting transfers between devices, exchange(): lax.ppermute(to_before, 'lon', down)  6.18 us
  transfers between devices with their start and end apart: 15, of which 5 were waited for; matrix products, arithmetic and copies ran while one was open for 0% of the time, Pallas kernels for 3%

profile of v11, /device:TPU:1, one launch (start us, length us, event | category | flops | bytes accessed | tf_op | source)
XLA Modules:
  0.0 113.4 jit_solution(14248762199234435042)
XLA Ops:
  1.3 2.8 %bucket.1 = f32[8,136,128]{2,1,0:T(8,128)} custom-call(f32[256,128]{1,0:T(8,128)} %departures_hbm.1, f32[256,128]{1,0:T(8,128)} %weight_hbm.1, s32[1,256]{1,0:T(1,128)} %bitcast.14, s32[1,256]{1,0:T(1,128)} %bitcast.15, s32[1]{0:T(128)S(6)} %copy.12.counts_ref, s32[1]{0:T(128)} %bitcast.3.parity_ref), custom_call_target="tpu_custom_call" | custom-call | tf_op jit(solution)/shard_map/bucket/pallas_call | solution.py:30
  4.1 0.0 copy-start.2
  4.1 0.0 copy-start.3
  4.1 7.8 %all-to-all-start = ((f32[8,136,128]{2,1,0:T(8,128)}), f32[8,136,128]{2,1,0:T(8,128)S(1)}, u32[]{:S(2)}, u32[]{:S(2)}) async-start(f32[8,136,128]{2,1,0:T(8,128)} %bucket.1), calls=%async_computation | async-start | bytes 1114112 | tf_op jit(solution)/shard_map/all_to_all | solution.py:520
  11.9 0.0 copy-done.2
  11.9 0.0 copy-done.3
  11.9 0.0 copy-start
  11.9 0.0 copy-start.1
  11.9 0.1 fixed.1.fixed_ref.refs_5_.refs_4_
  12.0 0.7 copy-done
  12.8 0.0 copy-done.1
  12.8 0.1 matrices.1.m_ref.refs_8_
  12.9 11.6 %all-to-all-done.received_ref = f32[8,136,128]{2,1,0:T(8,128)S(1)} async-done(((f32[8,136,128]{2,1,0:T(8,128)}), f32[8,136,128]{2,1,0:T(8,128)S(1)}, u32[]{:S(2)}, u32[]{:S(2)}) %all-to-all-start) | async-done | bytes 557088 | tf_op jit(solution)/shard_map/all_to_all | solution.py:520
  24.6 0.4 tile.1
  24.9 2.2 %collective-permute-start = (f32[584,128]{1,0:T(8,128)S(1)}, f32[584,128]{1,0:T(8,128)S(1)}, u32[]{:S(2)}, u32[]{:S(2)}) collective-permute-start(f32[584,128]{1,0:T(8,128)S(1)} %get-tuple-element.18), channel_id=1, source_target_pairs={{0,1},{1,2},{2,3},{3,4},{4,5},{5,6},{6,7},{7,0},{8,9},{9,10},{10,1... | collective-permute-start | bytes 897032 | tf_op jit(solution)/shard_map/ppermute | solution.py:494
  27.2 4.3 %collective-permute-start.1 = (f32[584,128]{1,0:T(8,128)S(1)}, f32[584,128]{1,0:T(8,128)S(1)}, u32[]{:S(2)}, u32[]{:S(2)}) collective-permute-start(f32[584,128]{1,0:T(8,128)S(1)} %get-tuple-element.20), channel_id=1, source_target_pairs={{1,0},{2,1},{3,2},{4,3},{5,4},{6,5},{7,6},{0,7},{9,8},{10,9},{11,1... | collective-permute-start | bytes 897032 | tf_op jit(solution)/shard_map/ppermute | solution.py:494
  31.5 1.9 %collective-permute-start.3 = (f32[144,128]{1,0:T(8,128)S(1)}, f32[144,128]{1,0:T(8,128)S(1)}, u32[]{:S(2)}, u32[]{:S(2)}) collective-permute-start(f32[144,128]{1,0:T(8,128)S(1)} %fixed.1.fixed_ref.refs_5_.refs_4_), channel_id=1, source_target_pairs={{1,0},{2,1},{3,2},{4,3},{5,4},{6,5},{7,6},{0,7},{9,8},{10,9},{11,1... | collective-permute-start | bytes 221192 | tf_op jit(solution)/shard_map/ppermute | solution.py:494
  33.4 3.4 %collective-permute-start.2 = (f32[144,128]{1,0:T(8,128)S(1)}, f32[144,128]{1,0:T(8,128)S(1)}, u32[]{:S(2)}, u32[]{:S(2)}) collective-permute-start(f32[144,128]{1,0:T(8,128)S(1)} %fixed.1.fixed_ref.refs_5_.refs_4_), channel_id=1, source_target_pairs={{0,1},{1,2},{2,3},{3,4},{4,5},{5,6},{6,7},{7,0},{8,9},{9,10},{10,1... | collective-permute-start | bytes 221192 | tf_op jit(solution)/shard_map/ppermute | solution.py:494
  36.8 0.0 collective-permute-done.3.refs_6_.refs_5_
  36.8 3.7 %collective-permute-done.2.refs_4_.refs_3_ = f32[144,128]{1,0:T(8,128)S(1)} collective-permute-done((f32[144,128]{1,0:T(8,128)S(1)}, f32[144,128]{1,0:T(8,128)S(1)}, u32[]{:S(2)}, u32[]{:S(2)}) %collective-permute-start.2) | collective-permute-done | bytes 73760 | tf_op jit(solution)/shard_map/ppermute | solution.py:494
  40.5 0.0 collective-permute-done.refs_1_.refs_0_
  40.5 0.0 collective-permute-done.1.refs_3_.refs_2_
  40.5 11.3 %collective-permute-start.4 = (f32[528,128]{1,0:T(8,128)S(1)}, f32[528,128]{1,0:T(8,128)S(1)}, u32[]{:S(2)}, u32[]{:S(2)}) collective-permute-start(f32[528,128]{1,0:T(8,128)S(1)} %get-tuple-element.21), channel_id=1, source_target_pairs={{8,16},{24,32},{40,48},{56,64},{72,80},{88,96},{104,112},{120,128}... | collective-permute-start | bytes 811016 | tf_op jit(solution)/shard_map/ppermute | solution.py:501
  51.8 1.9 %collective-permute-start.5 = (f32[528,128]{1,0:T(8,128)S(1)}, f32[528,128]{1,0:T(8,128)S(1)}, u32[]{:S(2)}, u32[]{:S(2)}) collective-permute-start(f32[528,128]{1,0:T(8,128)S(1)} %get-tuple-element.22), channel_id=1, source_target_pairs={{0,8},{16,24},{32,40},{48,56},{64,72},{80,88},{96,104},{112,120},{... | collective-permute-start | bytes 811016 | tf_op jit(solution)/shard_map/ppermute | solution.py:501
  53.8 4.4 %collective-permute-start.8 = (f32[480,128]{1,0:T(8,128)S(1)}, f32[480,128]{1,0:T(8,128)S(1)}, u32[]{:S(2)}, u32[]{:S(2)}) collective-permute-start(f32[480,128]{1,0:T(8,128)S(1)} %get-tuple-element.27), channel_id=1, source_target_pairs={{8,16},{24,32},{40,48},{56,64},{72,80},{88,96},{104,112},{120,128}... | collective-permute-start | bytes 737288 | tf_op jit(solution)/shard_map/ppermute | solution.py:501
  58.2 1.9 %collective-permute-start.9 = (f32[480,128]{1,0:T(8,128)S(1)}, f32[480,128]{1,0:T(8,128)S(1)}, u32[]{:S(2)}, u32[]{:S(2)}) collective-permute-start(f32[480,128]{1,0:T(8,128)S(1)} %get-tuple-element.28), channel_id=1, source_target_pairs={{0,8},{16,24},{32,40},{48,56},{64,72},{80,88},{96,104},{112,120},{... | collective-permute-start | bytes 737288 | tf_op jit(solution)/shard_map/ppermute | solution.py:501
  60.1 0.0 collective-permute-done.4.refs_6_
  60.2 0.0 collective-permute-done.5.refs_7_
  60.2 1.2 %right_side.1 = (f32[8,48,128]{2,1,0:T(8,128)S(1)}, f32[8,48,128]{2,1,0:T(8,128)S(1)}, f32[432,128]{1,0:T(8,128)S(1)}, f32[432,128]{1,0:T(8,128)S(1)}) custom-call(s32[1]{0:T(128)} %bitcast.refs_0_.parity_ref, f32[584,128]{1,0:T(8,128)S(1)} %collective-permute-done.refs_1_.refs_0_, f32[768,128]{1,0:T(8,128)S(1)} %get-tuple-element.19.refs_2_.refs_1_, ...), custom_call_target="tpu_custom_call" | custom-call | tf_op jit(solution)/shard_map/right_side/pallas_call | solution.py:30
  61.4 4.4 %collective-permute-start.6 = (f32[432,128]{1,0:T(8,128)S(1)}, f32[432,128]{1,0:T(8,128)S(1)}, u32[]{:S(2)}, u32[]{:S(2)}) collective-permute-start(f32[432,128]{1,0:T(8,128)S(1)} %get-tuple-element.25), channel_id=1, source_target_pairs={{8,16},{24,32},{40,48},{56,64},{72,80},{88,96},{104,112},{120,128}... | collective-permute-start | bytes 663560 | tf_op jit(solution)/shard_map/ppermute | solution.py:501
  65.8 1.9 %collective-permute-start.7 = (f32[432,128]{1,0:T(8,128)S(1)}, f32[432,128]{1,0:T(8,128)S(1)}, u32[]{:S(2)}, u32[]{:S(2)}) collective-permute-start(f32[432,128]{1,0:T(8,128)S(1)} %get-tuple-element.26), channel_id=1, source_target_pairs={{0,8},{16,24},{32,40},{48,56},{64,72},{80,88},{96,104},{112,120},{... | collective-permute-start | bytes 663560 | tf_op jit(solution)/shard_map/ppermute | solution.py:501
  67.7 0.0 collective-permute-done.8.refs_13_
  67.7 0.0 collective-permute-done.9.refs_14_
  67.7 1.7 %collective-permute-done.6.refs_11_ = f32[432,128]{1,0:T(8,128)S(1)} collective-permute-done((f32[432,128]{1,0:T(8,128)S(1)}, f32[432,128]{1,0:T(8,128)S(1)}, u32[]{:S(2)}, u32[]{:S(2)}) %collective-permute-start.6) | collective-permute-done | bytes 221216 | tf_op jit(solution)/shard_map/ppermute | solution.py:501
  69.4 0.0 collective-permute-done.7.refs_12_
  69.4 4.0 %first_image.1 = (f32[8,16,128]{2,1,0:T(8,128)S(1)}, f32[3,8,32,128]{3,2,1,0:T(8,128)S(1)}, f32[192,128]{1,0:T(8,128)S(1)}, f32[192,128]{1,0:T(8,128)S(1)}, f32[96,128]{1,0:T(8,128)}) custom-call(s32[1]{0:T(128)} %bitcast.refs_0_.parity_ref, f32[584,128]{1,0:T(8,128)S(1)} %collective-permute-done.refs_1_.refs_0_, ...), custom_call_target="tpu_custom_call" | custom-call | tf_op jit(solution)/shard_map/first_image/pallas_call | solution.py:30
  73.4 14.0 %all-to-all-start.1 = ((f32[24,4,128]{2,1,0:T(4,128)}), f32[24,4,128]{2,1,0:T(4,128)S(1)}, u32[]{:S(2)}, u32[]{:S(2)}) async-start(f32[24,4,128]{2,1,0:T(4,128)} %bitcast.5), calls=%async_computation.1 | async-start | bytes 98304 | tf_op jit(solution)/shard_map/all_to_all | solution.py:551
  87.4 3.5 %collective-permute-start.10 = (f32[192,128]{1,0:T(8,128)S(1)}, f32[192,128]{1,0:T(8,128)S(1)}, u32[]{:S(2)}, u32[]{:S(2)}) collective-permute-start(f32[192,128]{1,0:T(8,128)S(1)} %get-tuple-element.32), channel_id=1, source_target_pairs={{8,16},{24,32},{40,48},{56,64},{72,80},{88,96},{104,112},{120,128}... | collective-permute-start | bytes 294920 | tf_op jit(solution)/shard_map/ppermute | solution.py:501
  90.9 1.9 %collective-permute-start.11 = (f32[192,128]{1,0:T(8,128)S(1)}, f32[192,128]{1,0:T(8,128)S(1)}, u32[]{:S(2)}, u32[]{:S(2)}) collective-permute-start(f32[192,128]{1,0:T(8,128)S(1)} %get-tuple-element.33), channel_id=1, source_target_pairs={{0,8},{16,24},{32,40},{48,56},{64,72},{80,88},{96,104},{112,120},{... | collective-permute-start | bytes 294920 | tf_op jit(solution)/shard_map/ppermute | solution.py:501
  92.8 4.6 %all-to-all-done.1 = f32[24,4,128]{2,1,0:T(4,128)S(1)} async-done(((f32[24,4,128]{2,1,0:T(4,128)}), f32[24,4,128]{2,1,0:T(4,128)S(1)}, u32[]{:S(2)}, u32[]{:S(2)}) %all-to-all-start.1) | async-done | bytes 49184 | tf_op jit(solution)/shard_map/all_to_all | solution.py:551
  97.5 0.6 add.10
  98.1 6.0 %all-to-all-start.2 = ((f32[32,1,128]{2,1,0:T(1,128)}), f32[32,1,128]{2,1,0:T(1,128)S(1)}, u32[]{:S(2)}, u32[]{:S(2)}) async-start(f32[32,1,128]{2,1,0:T(1,128)} %bitcast.8), calls=%async_computation.2 | async-start | bytes 32768 | tf_op jit(solution)/shard_map/all_to_all | solution.py:557
  104.1 0.0 collective-permute-done.10.refs_11_
  104.1 0.0 collective-permute-done.11.refs_12_
  104.1 0.8 second_image.1.u_ref
  104.9 7.8 %all-to-all-done.2 = f32[32,1,128]{2,1,0:T(1,128)S(1)} async-done(((f32[32,1,128]{2,1,0:T(1,128)}), f32[32,1,128]{2,1,0:T(1,128)S(1)}, u32[]{:S(2)}, u32[]{:S(2)}) %all-to-all-start.2) | async-done | bytes 16416 | tf_op jit(solution)/shard_map/all_to_all | solution.py:557
  112.6 0.8 finish.1
  (2 shorter events, 0.1 us)
Async XLA Ops:
  4.1 7.8 %copy-start.2 = (f32[8,16,128]{2,1,0:T(8,128)S(1)}, f32[8,16,128]{2,1,0:T(8,128)}, u32[]{:S(2)}) copy-start(f32[8,16,128]{2,1,0:T(8,128)} %param.14) | copy-start | bytes 196612
  4.1 7.8 %copy-start.3 = (f32[8,16]{1,0:T(8,128)S(1)}, f32[8,16]{1,0:T(8,128)}, u32[]{:S(2)}) copy-start(f32[8,16]{1,0:T(8,128)} %diffusion_ref.1) | copy-start | bytes 1540
  4.1 20.5 %all-to-all-start = ((f32[8,136,128]{2,1,0:T(8,128)}), f32[8,136,128]{2,1,0:T(8,128)S(1)}, u32[]{:S(2)}, u32[]{:S(2)}) async-start(f32[8,136,128]{2,1,0:T(8,128)} %bucket.1), calls=%async_computation | async-start | bytes 1114112 | tf_op jit(solution)/shard_map/all_to_all | solution.py:520
  11.9 0.8 copy-start
  11.9 0.9 copy-start.1
  24.9 15.5 %collective-permute-start = (f32[584,128]{1,0:T(8,128)S(1)}, f32[584,128]{1,0:T(8,128)S(1)}, u32[]{:S(2)}, u32[]{:S(2)}) collective-permute-start(f32[584,128]{1,0:T(8,128)S(1)} %get-tuple-element.18), channel_id=1, source_target_pairs={{0,1},{1,2},{2,3},{3,4},{4,5},{5,6},{6,7},{7,0},{8,9},{9,10},{10,1... | collective-permute-start | bytes 897032 | tf_op jit(solution)/shard_map/ppermute | solution.py:494
  27.2 13.3 %collective-permute-start.1 = (f32[584,128]{1,0:T(8,128)S(1)}, f32[584,128]{1,0:T(8,128)S(1)}, u32[]{:S(2)}, u32[]{:S(2)}) collective-permute-start(f32[584,128]{1,0:T(8,128)S(1)} %get-tuple-element.20), channel_id=1, source_target_pairs={{1,0},{2,1},{3,2},{4,3},{5,4},{6,5},{7,6},{0,7},{9,8},{10,9},{11,1... | collective-permute-start | bytes 897032 | tf_op jit(solution)/shard_map/ppermute | solution.py:494
  31.5 5.3 %collective-permute-start.3 = (f32[144,128]{1,0:T(8,128)S(1)}, f32[144,128]{1,0:T(8,128)S(1)}, u32[]{:S(2)}, u32[]{:S(2)}) collective-permute-start(f32[144,128]{1,0:T(8,128)S(1)} %fixed.1.fixed_ref.refs_5_.refs_4_), channel_id=1, source_target_pairs={{1,0},{2,1},{3,2},{4,3},{5,4},{6,5},{7,6},{0,7},{9,8},{10,9},{11,1... | collective-permute-start | bytes 221192 | tf_op jit(solution)/shard_map/ppermute | solution.py:494
  33.4 7.1 %collective-permute-start.2 = (f32[144,128]{1,0:T(8,128)S(1)}, f32[144,128]{1,0:T(8,128)S(1)}, u32[]{:S(2)}, u32[]{:S(2)}) collective-permute-start(f32[144,128]{1,0:T(8,128)S(1)} %fixed.1.fixed_ref.refs_5_.refs_4_), channel_id=1, source_target_pairs={{0,1},{1,2},{2,3},{3,4},{4,5},{5,6},{6,7},{7,0},{8,9},{9,10},{10,1... | collective-permute-start | bytes 221192 | tf_op jit(solution)/shard_map/ppermute | solution.py:494
  40.5 19.6 %collective-permute-start.4 = (f32[528,128]{1,0:T(8,128)S(1)}, f32[528,128]{1,0:T(8,128)S(1)}, u32[]{:S(2)}, u32[]{:S(2)}) collective-permute-start(f32[528,128]{1,0:T(8,128)S(1)} %get-tuple-element.21), channel_id=1, source_target_pairs={{8,16},{24,32},{40,48},{56,64},{72,80},{88,96},{104,112},{120,128}... | collective-permute-start | bytes 811016 | tf_op jit(solution)/shard_map/ppermute | solution.py:501
  51.8 8.3 %collective-permute-start.5 = (f32[528,128]{1,0:T(8,128)S(1)}, f32[528,128]{1,0:T(8,128)S(1)}, u32[]{:S(2)}, u32[]{:S(2)}) collective-permute-start(f32[528,128]{1,0:T(8,128)S(1)} %get-tuple-element.22), channel_id=1, source_target_pairs={{0,8},{16,24},{32,40},{48,56},{64,72},{80,88},{96,104},{112,120},{... | collective-permute-start | bytes 811016 | tf_op jit(solution)/shard_map/ppermute | solution.py:501
  53.8 13.9 %collective-permute-start.8 = (f32[480,128]{1,0:T(8,128)S(1)}, f32[480,128]{1,0:T(8,128)S(1)}, u32[]{:S(2)}, u32[]{:S(2)}) collective-permute-start(f32[480,128]{1,0:T(8,128)S(1)} %get-tuple-element.27), channel_id=1, source_target_pairs={{8,16},{24,32},{40,48},{56,64},{72,80},{88,96},{104,112},{120,128}... | collective-permute-start | bytes 737288 | tf_op jit(solution)/shard_map/ppermute | solution.py:501
  58.2 9.5 %collective-permute-start.9 = (f32[480,128]{1,0:T(8,128)S(1)}, f32[480,128]{1,0:T(8,128)S(1)}, u32[]{:S(2)}, u32[]{:S(2)}) collective-permute-start(f32[480,128]{1,0:T(8,128)S(1)} %get-tuple-element.28), channel_id=1, source_target_pairs={{0,8},{16,24},{32,40},{48,56},{64,72},{80,88},{96,104},{112,120},{... | collective-permute-start | bytes 737288 | tf_op jit(solution)/shard_map/ppermute | solution.py:501
  61.4 8.0 %collective-permute-start.6 = (f32[432,128]{1,0:T(8,128)S(1)}, f32[432,128]{1,0:T(8,128)S(1)}, u32[]{:S(2)}, u32[]{:S(2)}) collective-permute-start(f32[432,128]{1,0:T(8,128)S(1)} %get-tuple-element.25), channel_id=1, source_target_pairs={{8,16},{24,32},{40,48},{56,64},{72,80},{88,96},{104,112},{120,128}... | collective-permute-start | bytes 663560 | tf_op jit(solution)/shard_map/ppermute | solution.py:501
  65.8 3.6 %collective-permute-start.7 = (f32[432,128]{1,0:T(8,128)S(1)}, f32[432,128]{1,0:T(8,128)S(1)}, u32[]{:S(2)}, u32[]{:S(2)}) collective-permute-start(f32[432,128]{1,0:T(8,128)S(1)} %get-tuple-element.26), channel_id=1, source_target_pairs={{0,8},{16,24},{32,40},{48,56},{64,72},{80,88},{96,104},{112,120},{... | collective-permute-start | bytes 663560 | tf_op jit(solution)/shard_map/ppermute | solution.py:501
  73.4 24.1 %all-to-all-start.1 = ((f32[24,4,128]{2,1,0:T(4,128)}), f32[24,4,128]{2,1,0:T(4,128)S(1)}, u32[]{:S(2)}, u32[]{:S(2)}) async-start(f32[24,4,128]{2,1,0:T(4,128)} %bitcast.5), calls=%async_computation.1 | async-start | bytes 98304 | tf_op jit(solution)/shard_map/all_to_all | solution.py:551
  87.4 16.7 %collective-permute-start.10 = (f32[192,128]{1,0:T(8,128)S(1)}, f32[192,128]{1,0:T(8,128)S(1)}, u32[]{:S(2)}, u32[]{:S(2)}) collective-permute-start(f32[192,128]{1,0:T(8,128)S(1)} %get-tuple-element.32), channel_id=1, source_target_pairs={{8,16},{24,32},{40,48},{56,64},{72,80},{88,96},{104,112},{120,128}... | collective-permute-start | bytes 294920 | tf_op jit(solution)/shard_map/ppermute | solution.py:501
  90.9 13.2 %collective-permute-start.11 = (f32[192,128]{1,0:T(8,128)S(1)}, f32[192,128]{1,0:T(8,128)S(1)}, u32[]{:S(2)}, u32[]{:S(2)}) collective-permute-start(f32[192,128]{1,0:T(8,128)S(1)} %get-tuple-element.33), channel_id=1, source_target_pairs={{0,8},{16,24},{32,40},{48,56},{64,72},{80,88},{96,104},{112,120},{... | collective-permute-start | bytes 294920 | tf_op jit(solution)/shard_map/ppermute | solution.py:501
  98.1 14.6 %all-to-all-start.2 = ((f32[32,1,128]{2,1,0:T(1,128)}), f32[32,1,128]{2,1,0:T(1,128)S(1)}, u32[]{:S(2)}, u32[]{:S(2)}) async-start(f32[32,1,128]{2,1,0:T(1,128)} %bitcast.8), calls=%async_computation.2 | async-start | bytes 32768 | tf_op jit(solution)/shard_map/all_to_all | solution.py:557
